TPU v7x, 32 devices: a whole 2x2x4 slice. The times are simulated.
32 devices in a mesh: ctx: 16 (over z, y, x), fsdp: 2 (over core).
Axes of the slice: x: 2, y: 2, z: 4, core: 2. Of those that a mesh axis runs over, the one named last changes fastest.
Arguments:
- inputs: bfloat16 [2, 8192, 1024], P('fsdp', 'ctx'), may hold values from -6 to 6
- segments: int32 [2, 8192], P('fsdp'), may hold values from 0 to 8, as said below
- cotangent: bfloat16 [2, 8192, 1024], P('fsdp', 'ctx'), may hold values from -6 to 6
- qkv_weight: bfloat16 [1024, 3072], P(('ctx', 'fsdp')), may hold values from -0.25 to 0.25
- query_bias: bfloat16 [1024], P(('ctx', 'fsdp')), may hold values from -3 to 3
- value_bias: bfloat16 [1024], P(('ctx', 'fsdp')), may hold values from -3 to 3
- out_weight: bfloat16 [1024, 1024], P(('ctx', 'fsdp')), may hold values from -0.75 to 0.75
- out_bias: bfloat16 [1024], P(('ctx', 'fsdp')), may hold values from -3 to 3
- first_gain: bfloat16 [1024], P(('ctx', 'fsdp')), may hold values from 0.099609375 to 1.8984375
- first_shift: bfloat16 [1024], P(('ctx', 'fsdp')), may hold values from -3 to 3
- up_weight: bfloat16 [1024, 4096], P(('ctx', 'fsdp')), may hold values from -0.1875 to 0.1875
- up_bias: bfloat16 [4096], P(('ctx', 'fsdp')), may hold values from -3 to 3
- down_weight: bfloat16 [4096, 1024], P(('ctx', 'fsdp')), may hold values from -0.125 to 0.125
- down_bias: bfloat16 [1024], P(('ctx', 'fsdp')), may hold values from -3 to 3
- second_gain: bfloat16 [1024], P(('ctx', 'fsdp')), may hold values from 0.099609375 to 1.8984375
- second_shift: bfloat16 [1024], P(('ctx', 'fsdp')), may hold values from -3 to 3
Outputs:
- result: bfloat16 [2, 8192, 1024], P('fsdp', 'ctx')
- inputs_grad: bfloat16 [2, 8192, 1024], P('fsdp', 'ctx')
- qkv_weight_grad: float32 [1024, 3072], P(('ctx', 'fsdp'))
- query_bias_grad: float32 [1024], P(('ctx', 'fsdp'))
- value_bias_grad: float32 [1024], P(('ctx', 'fsdp'))
- out_weight_grad: float32 [1024, 1024], P(('ctx', 'fsdp'))
- out_bias_grad: float32 [1024], P(('ctx', 'fsdp'))
- first_gain_grad: float32 [1024], P(('ctx', 'fsdp'))
- first_shift_grad: float32 [1024], P(('ctx', 'fsdp'))
- up_weight_grad: float32 [1024, 4096], P(('ctx', 'fsdp'))
- up_bias_grad: float32 [4096], P(('ctx', 'fsdp'))
- down_weight_grad: float32 [4096, 1024], P(('ctx', 'fsdp'))
- down_bias_grad: float32 [1024], P(('ctx', 'fsdp'))
- second_gain_grad: float32 [1024], P(('ctx', 'fsdp'))
- second_shift_grad: float32 [1024], P(('ctx', 'fsdp'))
Inputs may be any that keep to these rules, and one draw needn't show every extreme that they name: `segments`: along each sequence the numbers start at 0, never fall and rise by at most one from a token to the next; each sequence holds 9 documents of any lengths.
All inputs are finite; a program needn't handle non-finite values.
Results may differ from a plain program's by a relative error of at most 0.015.
Values may be sent and summed in bfloat16 or wider, within the bound.
No kernel may reach another device: no remote copies, remote signals or barrier semaphores. Data moves between devices by JAX's collectives and lax.ppermute only.
A program may use at most 192 MiB of HBM per device.

v0:
```python
import jax
import jax.numpy as jnp
from jax import lax
from jax.sharding import PartitionSpec as P

H = 16
HD = 64
WINDOW = 1024


masked_fill = -1e30
norm_epsilon = 1e-05


def extended(block, sides, width):
    for axis, dim in sides:
        count = lax.axis_size(axis)
        forward = [(i, i + 1) for i in range(count - 1)]
        backward = [(target, source) for source, target in forward]
        low = lax.ppermute(
            lax.slice_in_dim(block, block.shape[dim] - width, None, axis=dim), axis, forward
        )
        high = lax.ppermute(lax.slice_in_dim(block, 0, width, axis=dim), axis, backward)
        block = jnp.concatenate([low, block, high], axis=dim)
    return block


def norm_rows(values, gain, shift):
    average = jnp.mean(values, axis=-1, keepdims=True)
    centered = values - average
    spread = jnp.mean(centered * centered, axis=-1, keepdims=True)
    return centered * lax.rsqrt(spread + norm_epsilon) * gain + shift


def gelu_exact(values):
    return jax.nn.gelu(values, approximate=False)


def window_mask(seg_query, seg_keys, row_start, block_rows, half_width):
    query_pos = row_start + jnp.arange(block_rows, dtype=jnp.int32)
    key_pos = row_start - half_width + jnp.arange(block_rows + 2 * half_width, dtype=jnp.int32)
    distance = key_pos[None, :] - query_pos[:, None]
    return (seg_query[:, None] == seg_keys[None, :]) & (jnp.abs(distance) < half_width)


def shards(
    inputs,
    segments,
    cotangent,
    qkv_weight,
    query_bias,
    value_bias,
    out_weight,
    out_bias,
    first_gain,
    first_shift,
    up_weight,
    up_bias,
    down_weight,
    down_bias,
    second_gain,
    second_shift,
):
    tokens = inputs.shape[1]
    width = inputs.shape[2]
    half_width = WINDOW // 2
    block_rows = min(512, tokens)
    group_heads = min(4, H)
    head_groups = H // group_heads
    turns = tokens // block_rows * head_groups
    span_rows = block_rows + 2 * half_width
    score_scale = HD ** (-0.5)
    gathered = (
        lax.all_gather(qkv_weight, ("ctx", "fsdp"), axis=0, tiled=True),
        lax.all_gather(query_bias, ("ctx", "fsdp"), axis=0, tiled=True),
        lax.all_gather(value_bias, ("ctx", "fsdp"), axis=0, tiled=True),
        lax.all_gather(out_weight, ("ctx", "fsdp"), axis=0, tiled=True),
        lax.all_gather(out_bias, ("ctx", "fsdp"), axis=0, tiled=True),
        lax.all_gather(first_gain, ("ctx", "fsdp"), axis=0, tiled=True),
        lax.all_gather(first_shift, ("ctx", "fsdp"), axis=0, tiled=True),
        lax.all_gather(up_weight, ("ctx", "fsdp"), axis=0, tiled=True),
        lax.all_gather(up_bias, ("ctx", "fsdp"), axis=0, tiled=True),
        lax.all_gather(down_weight, ("ctx", "fsdp"), axis=0, tiled=True),
        lax.all_gather(down_bias, ("ctx", "fsdp"), axis=0, tiled=True),
        lax.all_gather(second_gain, ("ctx", "fsdp"), axis=0, tiled=True),
        lax.all_gather(second_shift, ("ctx", "fsdp"), axis=0, tiled=True),
    )
    (
        qkv_full,
        query_full,
        value_full,
        out_full,
        outb_full,
        gain_one,
        shift_one,
        up_full,
        upb_full,
        down_full,
        downb_full,
        gain_two,
        shift_two,
    ) = gathered
    row_input = inputs[0]
    row_float = row_input.astype(jnp.float32)
    mixed = jnp.dot(row_input, qkv_full, preferred_element_type=jnp.float32)
    query_rows = (mixed[:, :width] + query_full).astype(jnp.bfloat16)
    key_rows = mixed[:, width : 2 * width].astype(jnp.bfloat16)
    value_rows = (mixed[:, 2 * width :] + value_full).astype(jnp.bfloat16)
    paired = jnp.concatenate([key_rows, value_rows], axis=1)
    paired_ext = extended(paired, (("ctx", 0),), half_width)
    key_ext = paired_ext[:, :width].reshape(-1, H, HD)
    value_ext = paired_ext[:, width:].reshape(-1, H, HD)
    query_heads = query_rows.reshape(tokens, H, HD)
    padding = jnp.full((half_width,), -1, jnp.int32)
    seg_line = jnp.concatenate([padding, segments[0], padding])
    seg_ext = lax.dynamic_slice_in_dim(
        seg_line, lax.axis_index("ctx") * tokens, tokens + 2 * half_width
    )

    def block_parts(block_index):
        row_start = block_index // head_groups * block_rows
        head_start = block_index % head_groups * group_heads
        query_block = lax.dynamic_slice(
            query_heads, (row_start, head_start, 0), (block_rows, group_heads, HD)
        )
        key_block = lax.dynamic_slice(
            key_ext, (row_start, head_start, 0), (span_rows, group_heads, HD)
        )
        value_block = lax.dynamic_slice(
            value_ext, (row_start, head_start, 0), (span_rows, group_heads, HD)
        )
        seg_query = lax.dynamic_slice_in_dim(seg_ext, row_start + half_width, block_rows)
        allowed = window_mask(seg_query, seg_ext, row_start, block_rows, half_width)
        scores = (
            jnp.einsum("qhd,khd->hqk", query_block, key_block, preferred_element_type=jnp.float32)
            * score_scale
        )
        scores = jnp.where(allowed[None], scores, masked_fill)
        return (row_start, head_start, query_block, key_block, value_block, scores)

    def forward_turn(block_index, carry):
        attended, log_totals = carry
        row_start, head_start, query_block, key_block, value_block, scores = block_parts(
            block_index
        )
        peak = jnp.max(scores, axis=-1, keepdims=True)
        expo = jnp.exp(scores - peak)
        total = jnp.sum(expo, axis=-1, keepdims=True)
        soft = expo / total
        block_out = jnp.einsum(
            "hqk,khd->qhd",
            soft.astype(jnp.bfloat16),
            value_block,
            preferred_element_type=jnp.float32,
        )
        attended = lax.dynamic_update_slice(attended, block_out, (row_start, head_start, 0))
        log_totals = lax.dynamic_update_slice(
            log_totals, (peak + jnp.log(total))[..., 0], (head_start, row_start)
        )
        return (attended, log_totals)

    attended, log_totals = lax.fori_loop(
        0,
        turns,
        forward_turn,
        (jnp.zeros((tokens, H, HD), jnp.float32), jnp.zeros((H, tokens), jnp.float32)),
    )
    heads_low = attended.reshape(tokens, width).astype(jnp.bfloat16)
    branch = jnp.dot(heads_low, out_full, preferred_element_type=jnp.float32) + outb_full
    residual_one = row_float + branch
    first_rows = norm_rows(residual_one, gain_one, shift_one)
    first_low = first_rows.astype(jnp.bfloat16)
    lifted = jnp.dot(first_low, up_full, preferred_element_type=jnp.float32) + upb_full
    active = gelu_exact(lifted).astype(jnp.bfloat16)
    second = jnp.dot(active, down_full, preferred_element_type=jnp.float32) + downb_full
    residual_two = first_rows + second
    result = norm_rows(residual_two, gain_two, shift_two).astype(jnp.bfloat16)[None]
    regathered = (
        lax.all_gather(qkv_weight, ("ctx", "fsdp"), axis=0, tiled=True),
        lax.all_gather(query_bias, ("ctx", "fsdp"), axis=0, tiled=True),
        lax.all_gather(value_bias, ("ctx", "fsdp"), axis=0, tiled=True),
        lax.all_gather(out_weight, ("ctx", "fsdp"), axis=0, tiled=True),
        lax.all_gather(out_bias, ("ctx", "fsdp"), axis=0, tiled=True),
        lax.all_gather(first_gain, ("ctx", "fsdp"), axis=0, tiled=True),
        lax.all_gather(first_shift, ("ctx", "fsdp"), axis=0, tiled=True),
        lax.all_gather(up_weight, ("ctx", "fsdp"), axis=0, tiled=True),
        lax.all_gather(up_bias, ("ctx", "fsdp"), axis=0, tiled=True),
        lax.all_gather(down_weight, ("ctx", "fsdp"), axis=0, tiled=True),
        lax.all_gather(down_bias, ("ctx", "fsdp"), axis=0, tiled=True),
        lax.all_gather(second_gain, ("ctx", "fsdp"), axis=0, tiled=True),
        lax.all_gather(second_shift, ("ctx", "fsdp"), axis=0, tiled=True),
    )
    (
        qkv_full,
        query_full,
        value_full,
        out_full,
        outb_full,
        gain_one,
        shift_one,
        up_full,
        upb_full,
        down_full,
        downb_full,
        gain_two,
        shift_two,
    ) = regathered
    upstream = cotangent[0].astype(jnp.float32)
    unused_two, norm_back_two = jax.vjp(
        norm_rows, residual_two, gain_two.astype(jnp.float32), shift_two.astype(jnp.float32)
    )
    grad_two, gain_two_part, shift_two_part = norm_back_two(upstream)
    grad_second = grad_two.astype(jnp.bfloat16)
    down_bias_part = jnp.sum(grad_second, axis=0, dtype=jnp.float32)
    down_weight_part = jnp.einsum(
        "tf,td->fd", active, grad_second, preferred_element_type=jnp.float32
    )
    grad_active = jnp.einsum(
        "td,fd->tf", grad_second, down_full, preferred_element_type=jnp.float32
    )
    unused_gelu, gelu_back = jax.vjp(gelu_exact, lifted)
    grad_lifted = gelu_back(grad_active)[0].astype(jnp.bfloat16)
    up_bias_part = jnp.sum(grad_lifted, axis=0, dtype=jnp.float32)
    up_weight_part = jnp.einsum(
        "td,tf->df", first_low, grad_lifted, preferred_element_type=jnp.float32
    )
    grad_first = grad_two + jnp.einsum(
        "tf,df->td", grad_lifted, up_full, preferred_element_type=jnp.float32
    )
    unused_one, norm_back_one = jax.vjp(
        norm_rows, residual_one, gain_one.astype(jnp.float32), shift_one.astype(jnp.float32)
    )
    grad_one, gain_one_part, shift_one_part = norm_back_one(grad_first)
    grad_branch = grad_one.astype(jnp.bfloat16)
    out_bias_part = jnp.sum(grad_branch, axis=0, dtype=jnp.float32)
    out_weight_part = jnp.einsum(
        "te,td->ed", heads_low, grad_branch, preferred_element_type=jnp.float32
    )
    grad_heads = (
        jnp.einsum("td,ed->te", grad_branch, out_full, preferred_element_type=jnp.float32)
        .astype(jnp.bfloat16)
        .reshape(tokens, H, HD)
    )

    def backward_turn(block_index, carry):
        grad_query, grad_key_ext, grad_value_ext = carry
        row_start, head_start, query_block, key_block, value_block, scores = block_parts(
            block_index
        )
        log_block = lax.dynamic_slice(
            log_totals, (head_start, row_start), (group_heads, block_rows)
        )
        soft = jnp.exp(scores - log_block[..., None])
        grad_block = lax.dynamic_slice(
            grad_heads, (row_start, head_start, 0), (block_rows, group_heads, HD)
        )
        grad_soft = jnp.einsum(
            "qhd,khd->hqk", grad_block, value_block, preferred_element_type=jnp.float32
        )
        grad_scores = (
            soft * (grad_soft - jnp.sum(soft * grad_soft, axis=-1, keepdims=True))
        ).astype(jnp.bfloat16)
        query_part = (
            jnp.einsum("hqk,khd->qhd", grad_scores, key_block, preferred_element_type=jnp.float32)
            * score_scale
        )
        key_part = (
            jnp.einsum("hqk,qhd->khd", grad_scores, query_block, preferred_element_type=jnp.float32)
            * score_scale
        )
        value_part = jnp.einsum(
            "hqk,qhd->khd",
            soft.astype(jnp.bfloat16),
            grad_block,
            preferred_element_type=jnp.float32,
        )
        grad_query = lax.dynamic_update_slice(grad_query, query_part, (row_start, head_start, 0))
        key_before = lax.dynamic_slice(
            grad_key_ext, (row_start, head_start, 0), (span_rows, group_heads, HD)
        )
        grad_key_ext = lax.dynamic_update_slice(
            grad_key_ext, key_before + key_part, (row_start, head_start, 0)
        )
        value_before = lax.dynamic_slice(
            grad_value_ext, (row_start, head_start, 0), (span_rows, group_heads, HD)
        )
        grad_value_ext = lax.dynamic_update_slice(
            grad_value_ext, value_before + value_part, (row_start, head_start, 0)
        )
        return (grad_query, grad_key_ext, grad_value_ext)

    ext_rows = tokens + 2 * half_width
    grad_query, grad_key_ext, grad_value_ext = lax.fori_loop(
        0,
        turns,
        backward_turn,
        (
            jnp.zeros((tokens, H, HD), jnp.float32),
            jnp.zeros((ext_rows, H, HD), jnp.float32),
            jnp.zeros((ext_rows, H, HD), jnp.float32),
        ),
    )
    grad_pair_ext = jnp.concatenate(
        [grad_key_ext.reshape(ext_rows, width), grad_value_ext.reshape(ext_rows, width)], axis=1
    )
    outer_rims = jnp.concatenate(
        [grad_pair_ext[:half_width], grad_pair_ext[half_width + tokens :]], axis=0
    )
    arrived = extended(outer_rims.astype(jnp.bfloat16), (("ctx", 0),), half_width).astype(
        outer_rims.dtype
    )
    own_rows = grad_pair_ext[half_width : half_width + tokens]
    own_rows = own_rows + arrived[:half_width]
    own_rows = own_rows + arrived[arrived.shape[0] - half_width :]
    grad_key_rows = own_rows[:, :width].astype(jnp.bfloat16)
    grad_value_rows = own_rows[:, width:].astype(jnp.bfloat16)
    grad_query_rows = grad_query.reshape(tokens, width).astype(jnp.bfloat16)
    grad_mixed = jnp.concatenate([grad_query_rows, grad_key_rows, grad_value_rows], axis=1)
    query_bias_part = jnp.sum(grad_query_rows, axis=0, dtype=jnp.float32)
    value_bias_part = jnp.sum(grad_value_rows, axis=0, dtype=jnp.float32)
    qkv_weight_part = jnp.einsum(
        "td,te->de", row_input, grad_mixed, preferred_element_type=jnp.float32
    )
    inputs_grad = (
        grad_one + jnp.einsum("te,de->td", grad_mixed, qkv_full, preferred_element_type=jnp.float32)
    ).astype(jnp.bfloat16)[None]
    summed = (
        lax.psum_scatter(qkv_weight_part, ("ctx", "fsdp"), scatter_dimension=0, tiled=True),
        lax.psum_scatter(query_bias_part, ("ctx", "fsdp"), scatter_dimension=0, tiled=True),
        lax.psum_scatter(value_bias_part, ("ctx", "fsdp"), scatter_dimension=0, tiled=True),
        lax.psum_scatter(out_weight_part, ("ctx", "fsdp"), scatter_dimension=0, tiled=True),
        lax.psum_scatter(out_bias_part, ("ctx", "fsdp"), scatter_dimension=0, tiled=True),
        lax.psum_scatter(gain_one_part, ("ctx", "fsdp"), scatter_dimension=0, tiled=True),
        lax.psum_scatter(shift_one_part, ("ctx", "fsdp"), scatter_dimension=0, tiled=True),
        lax.psum_scatter(up_weight_part, ("ctx", "fsdp"), scatter_dimension=0, tiled=True),
        lax.psum_scatter(up_bias_part, ("ctx", "fsdp"), scatter_dimension=0, tiled=True),
        lax.psum_scatter(down_weight_part, ("ctx", "fsdp"), scatter_dimension=0, tiled=True),
        lax.psum_scatter(down_bias_part, ("ctx", "fsdp"), scatter_dimension=0, tiled=True),
        lax.psum_scatter(gain_two_part, ("ctx", "fsdp"), scatter_dimension=0, tiled=True),
        lax.psum_scatter(shift_two_part, ("ctx", "fsdp"), scatter_dimension=0, tiled=True),
    )
    return (
        result,
        inputs_grad,
        summed[0],
        summed[1],
        summed[2],
        summed[3],
        summed[4],
        summed[5],
        summed[6],
        summed[7],
        summed[8],
        summed[9],
        summed[10],
        summed[11],
        summed[12],
    )


def solution(mesh):
    placed = (
        P("fsdp", "ctx", None),
        P("fsdp", None),
        P("fsdp", "ctx", None),
        P(("ctx", "fsdp"), None),
        P(("ctx", "fsdp")),
        P(("ctx", "fsdp")),
        P(("ctx", "fsdp"), None),
        P(("ctx", "fsdp")),
        P(("ctx", "fsdp")),
        P(("ctx", "fsdp")),
        P(("ctx", "fsdp"), None),
        P(("ctx", "fsdp")),
        P(("ctx", "fsdp"), None),
        P(("ctx", "fsdp")),
        P(("ctx", "fsdp")),
        P(("ctx", "fsdp")),
    )
    return jax.shard_map(
        shards,
        mesh=mesh,
        in_specs=placed,
        out_specs=(
            P("fsdp", "ctx", None),
            P("fsdp", "ctx", None),
            P(("ctx", "fsdp"), None),
            P(("ctx", "fsdp")),
            P(("ctx", "fsdp")),
            P(("ctx", "fsdp"), None),
            P(("ctx", "fsdp")),
            P(("ctx", "fsdp")),
            P(("ctx", "fsdp")),
            P(("ctx", "fsdp"), None),
            P(("ctx", "fsdp")),
            P(("ctx", "fsdp"), None),
            P(("ctx", "fsdp")),
            P(("ctx", "fsdp")),
            P(("ctx", "fsdp")),
        ),
        check_vma=False,
    )
```

profile of v0, /device:TPU:25, one launch (start us, length us, event | category | flops | bytes accessed | tf_op | source)
XLA Modules:
  0.0 1211.2 jit_solution(11110229297390891250)
XLA Ops:
  16.2 38.7 %all-reduce.18 = (bf16[1024]{0:T(1024)(128)(2,1)S(1)}, bf16[1024]{0:T(1024)(128)(2,1)S(1)}, bf16[1024]{0:T(1024)(128)(2,1)S(1)}, bf16[1024]{0:T(1024)(128)(2,1)S...) all-reduce(bf16[1024]{0:T(1024)(128)(2,1)S(1)} %dynamic-update-slic, ...), channel_id=1, replica_groups=mesh['ctx'=16,'fsdp'=2] {'ctx','fsdp'}, use_global_device_ids=true, to_apply=%add | all-reduce | flops 8192 | bytes 32768
  54.9 25.5 %all-gather.6.cloned.1.call-done = bf16[1024,3072]{1,0:T(8,128)(2,1)} async-done(((bf16[32,3072]{1,0:T(8,128)(2,1)}), bf16[1024,3072]{1,0:T(8,128)(2,1)}) %all-gather.6.cloned.1.call-update) | async-done | bytes 6291472 | tf_op jit(solution)/shard_map/all_gather | solution.py:74
  97.7 119.4 %all-gather = bf16[32,1,128]{2,1,0:T(2,128)(2,1)S(1)} all-gather(bf16[1,1,128]{2,1,0:T(2,128)(2,1)S(1)} %bitcast.110), channel_id=1, replica_groups=mesh['ctx'=16,'fsdp'=2] {'ctx','fsdp'}, dimensions={0}, use_global_device_ids=true | all-gather | bytes 8448 | tf_op jit(solution)/shard_map/all_gather | solution.py:82
  237.6 53.7 %while.36 = (s32[]{:T(128)}, bf16[512,16,64]{0,2,1:T(8,128)(2,1)S(1)}, f32[16,512]{1,0:T(8,128)S(1)}, bf16[1536,16,64]{0,2,1:T(8,128)(2,1)}, s32[1536]{0:T(1024)...) while((s32[]{:T(128)}, ...), condition=%wide.region_3.4_spmd, body=%wide.region_0.3_spmd.sunk | while | flops 846987264 | bytes 43350420 | solution.py:162
  296.4 28.3 %multiply_convert_fusion.1 = (bf16[512,4096]{1,0:T(8,128)(2,1)}, f32[512,4096]{1,0:T(8,128)}, f32[512,4096]{1,0:T(8,128)}) fusion(f32[4096]{0:T(1024)S(1)} %bitcast.108, bf16[1024,4096]{1,0:T(8,128)(2,1)} %all-gather.10.cloned.1.call-done, f32[512,1024]{1,0:T(8,128)} %copy-done.3, f32[1024]{0:T(1024)S(1)} %convert_element_type.143, ...), kind=kOutput, calls=%fused_computation.62 | convolution fusion | flops 4436000768 | bytes 31485952 | tf_op jit(solution)/shard_map/dot_general | solution.py:173
  324.7 10.5 all-gather.12.cloned.1.call-done
  335.2 10.0 fusion.86
  349.7 15.9 %convert_reduce_fusion = (f32[4096]{0:T(1024)}, bf16[512,4096]{1,0:T(8,128)(2,1)}) fusion(f32[512,4096]{1,0:T(8,128)} %get-tuple-element.580, f32[512,4096]{1,0:T(8,128)} %get-tuple-element.594, f32[4096]{0:T(1024)S(1)} %bitcast.109, bf16[512,1024]{1,0:T(8,128)(2,1)S(1)} %get-tuple-element.570, bf16[4096,1024]{1,0:T(8,128)(2,1)} %all-gather.12.cloned.1.call-done), kind=kOutput, calls=%fused_computation.60 | convolution fusion | flops 4330614784 | bytes 30441472 | tf_op jit(solution)/shard_map/td,fd->tf/dot_general | solution.py:218
  365.6 9.5 multiply_reduce_fusion.1
  395.9 146.8 %while.37 = (s32[]{:T(128)}, bf16[512,16,64]{0,2,1:T(8,128)(2,1)}, f32[1536,16,64]{0,2,1:T(8,128)}, f32[1536,16,64]{0,2,1:T(8,128)}, bf16[1536,16,64]{0,2,1:T(8,...) while((s32[]{:T(128)}, bf16[512,16,64]{0,2,1:T(8,128)(2,1)}, ...), condition=%wide.region_14.15_spmd, body=%wide.region_12.14_spmd.sunk | while | flops 2046820352 | bytes 194324176 | solution.py:293
  396.1 8.1 fusion.140
  406.3 7.9 multiply_reduce_fusion.6
  418.8 5.8 fusion.143
  432.8 8.1 fusion.140
  443.0 7.9 multiply_reduce_fusion.6
  469.4 8.0 fusion.140
  479.6 7.9 multiply_reduce_fusion.6
  492.1 5.8 fusion.143
  506.1 8.0 fusion.140
  516.3 7.9 multiply_reduce_fusion.6
  542.7 8.1 fusion.44
  560.5 43.5 %collective-permute-done.2 = bf16[512,2048]{0,1:T(8,128)(2,1)S(1)} collective-permute-done((bf16[512,2048]{0,1:T(8,128)(2,1)S(1)}, bf16[512,2048]{0,1:T(8,128)(2,1)S(1)}, u32[]{:S(2)}, u32[]{:S(2)}) %collective-permute-start.2) | collective-permute-done | bytes 2097184 | tf_op jit(solution)/shard_map/ppermute | solution.py:20
  603.9 44.0 %collective-permute-done.3 = bf16[512,2048]{0,1:T(8,128)(2,1)S(1)} collective-permute-done((bf16[512,2048]{0,1:T(8,128)(2,1)S(1)}, bf16[512,2048]{0,1:T(8,128)(2,1)S(1)}, u32[]{:S(2)}, u32[]{:S(2)}) %collective-permute-start.3) | collective-permute-done | bytes 2097184 | tf_op jit(solution)/shard_map/ppermute | solution.py:23
  654.3 7.8 convolution_bitcast_fusion
  662.1 12.6 %copy.49 = f32[1024,3072]{1,0:T(8,128)} copy(f32[1024,3072]{0,1:T(8,128)} %convolution_bitcast_fusion) | data formatting | bytes 25165824
  676.3 10.9 fusion.76
  688.5 11.2 fusion.88
  704.3 43.0 %all-reduce.17 = (f32[1024]{0:T(1024)S(1)}, f32[1024]{0:T(1024)S(1)}, f32[1024]{0:T(1024)S(1)}, f32[1024]{0:T(1024)S(1)}, f32[1024]{0:T(1024)S(1)}, /*index=5*/f...) all-reduce(f32[1024]{0:T(1024)S(1)} %reduce_sum.212, ...), channel_id=3, replica_groups=mesh['ctx'=16,'fsdp'=2] {'ctx','fsdp'}, use_global_device_ids=true, to_apply=%region_17.18.clone | all-reduce | flops 12288 | bytes 98304
  752.6 8.4 fusion.65
  761.0 67.1 %reduce-scatter.13.cloned.1.call-done = f32[32,3072]{1,0:T(8,128)} async-done(((f32[1024,3072]{1,0:T(8,128)}), f32[32,3072]{1,0:T(8,128)}) %reduce-scatter.13.cloned.1.call-update) | async-done | bytes 393232
  828.1 188.3 %reduce-scatter.9.cloned.1.call-done = f32[32,4096]{1,0:T(8,128)} async-done(((f32[1024,4096]{1,0:T(8,128)}), f32[32,4096]{1,0:T(8,128)}) %reduce-scatter.9.cloned.1.call-update) | async-done | bytes 524304 | tf_op jit(solution)/shard_map/reduce_scatter | solution.py:335
  1016.4 187.5 %reduce-scatter.11.cloned.1.call-done = f32[128,1024]{1,0:T(8,128)} async-done(((f32[4096,1024]{1,0:T(8,128)}), f32[128,1024]{1,0:T(8,128)}) %reduce-scatter.11.cloned.1.call-update) | async-done | bytes 524304 | tf_op jit(solution)/shard_map/reduce_scatter | solution.py:337
  (320 shorter events, 229.6 us)
Async XLA Ops:
  7.2 73.2 %all-gather.6.cloned.1.call-start = ((), (), s32[]{:S(2)}) async-start(), calls=%async_computation.4 | async-start | bytes 6488064 | tf_op jit(solution)/shard_map/all_gather | solution.py:74
  7.9 283.5 %all-gather.8.cloned.1.call-start = ((), (), s32[]{:S(2)}) async-start(), calls=%async_computation.5 | async-start | bytes 2162688 | tf_op jit(solution)/shard_map/all_gather | solution.py:77
  8.7 287.7 %all-gather.10.cloned.1.call-start = ((), (), s32[]{:S(2)}) async-start(), calls=%async_computation.6 | async-start | bytes 8650752 | tf_op jit(solution)/shard_map/all_gather | solution.py:81
  9.4 325.8 %all-gather.12.cloned.1.call-start = ((), (), s32[]{:S(2)}) async-start(), calls=%async_computation.7 | async-start | bytes 8650752 | tf_op jit(solution)/shard_map/all_gather | solution.py:83
  86.4 11.3 copy-start.41
  86.4 132.5 %copy-start.22 = (s32[1,8192]{1,0:T(1,128)S(1)}, s32[1,8192]{1,0:T(1,128)}, u32[]{:S(2)}) copy-start(s32[1,8192]{1,0:T(1,128)} %param.21) | copy-start | bytes 98308
  90.5 130.0 %collective-permute-start = (bf16[512,2048]{1,0:T(8,128)(2,1)}, bf16[512,2048]{1,0:T(8,128)(2,1)}, u32[]{:S(2)}, u32[]{:S(2)}) collective-permute-start(bf16[512,2048]{1,0:T(8,128)(2,1)} %pad_maximum_fusion.6), channel_id=1, source_target_pairs={{0,2},{2,4},{4,6},{6,8},{8,10},{10,12},{12,14},{14,16},{16,18},{18... | collective-permute-start | bytes 6291464 | tf_op jit(solution)/shard_map/ppermute | solution.py:20
  93.5 127.0 %collective-permute-start.1 = (bf16[512,2048]{1,0:T(8,128)(2,1)}, bf16[512,2048]{1,0:T(8,128)(2,1)}, u32[]{:S(2)}, u32[]{:S(2)}) collective-permute-start(bf16[512,2048]{1,0:T(8,128)(2,1)} %pad_maximum_fusion.6), channel_id=1, source_target_pairs={{2,0},{4,2},{6,4},{8,6},{10,8},{12,10},{14,12},{16,14},{18,16},{20... | collective-permute-start | bytes 6291464 | tf_op jit(solution)/shard_map/ppermute | solution.py:23
  97.6 663.4 %reduce-scatter.7.cloned.1.call-start = ((), (), s32[]{:S(2)}) async-start(), calls=%async_computation.8 | async-start | bytes 4325376 | tf_op jit(solution)/shard_map/reduce_scatter | solution.py:331
  97.6 277.5 %copy-start.30 = (f32[1024]{0:T(1024)}, f32[1024]{0:T(1024)S(1)}, u32[]{:S(2)}) copy-start(f32[1024]{0:T(1024)S(1)} %convert_element_type.142) | copy-start | bytes 12292
  97.7 237.6 %copy-start.38 = (f32[1024]{0:T(1024)}, f32[1024]{0:T(1024)S(1)}, u32[]{:S(2)}) copy-start(f32[1024]{0:T(1024)S(1)} %convert_element_type.143) | copy-start | bytes 12292
  294.7 80.4 %copy-start.23 = (f32[512]{0:T(512)}, f32[512]{0:T(512)S(1)}, u32[]{:S(2)}) copy-start(f32[512]{0:T(512)S(1)} %broadcast_multiply_fusion.1) | copy-start | bytes 6148
  296.3 78.8 %copy-start.32 = (f32[512]{0:T(512)}, f32[512]{0:T(512)S(1)}, u32[]{:S(2)}) copy-start(f32[512]{0:T(512)S(1)} %fusion.72) | copy-start | bytes 6148
  296.4 38.9 %copy-start.40 = (f32[1024]{0:T(1024)S(1)}, f32[1024]{0:T(1024)}, u32[]{:S(2)}) copy-start(f32[1024]{0:T(1024)} %convert_element_type.147) | copy-start | bytes 12292
  335.2 10.4 copy-start.8
  335.2 10.4 copy-start.21
  349.7 15.9 %copy-start.17 = (bf16[512,1024]{1,0:T(8,128)(2,1)}, bf16[512,1024]{1,0:T(8,128)(2,1)S(1)}, u32[]{:S(2)}) copy-start(bf16[512,1024]{1,0:T(8,128)(2,1)S(1)} %get-tuple-element.570) | copy-start | bytes 3145732
  349.7 15.9 %copy-start.4 = (f32[512,1024]{1,0:T(8,128)S(1)}, f32[512,1024]{1,0:T(8,128)}, u32[]{:S(2)}) copy-start(f32[512,1024]{1,0:T(8,128)} %copy-done.3) | copy-start | bytes 6291460
  387.9 440.2 %reduce-scatter.13.cloned.1.call-start = ((), (), s32[]{:S(2)}) async-start(), calls=%async_computation.11 | async-start | bytes 12976128
  396.1 8.1 copy-start.1
  406.3 8.9 slice-start.2
  443.0 8.9 slice-start.2
  479.6 8.9 slice-start.2
  516.3 8.8 slice-start.2
  553.2 50.7 %collective-permute-start.2 = (bf16[512,2048]{0,1:T(8,128)(2,1)S(1)}, bf16[512,2048]{0,1:T(8,128)(2,1)S(1)}, u32[]{:S(2)}, u32[]{:S(2)}) collective-permute-start(bf16[512,2048]{0,1:T(8,128)(2,1)S(1)} %get-tuple-element.585), channel_id=1, source_target_pairs={{0,2},{2,4},{4,6},{6,8},{8,10},{10,12},{12,14},{14,16},{16,18},{18... | collective-permute-start | bytes 6291464 | tf_op jit(solution)/shard_map/ppermute | solution.py:20
  556.3 98.0 %copy-start.16 = (bf16[512,16,64]{0,2,1:T(8,128)(2,1)S(1)}, bf16[512,16,64]{0,2,1:T(8,128)(2,1)}, u32[]{:S(2)}) copy-start(bf16[512,16,64]{0,2,1:T(8,128)(2,1)} %get-tuple-element.448) | copy-start | bytes 3145732
  556.3 98.0 %copy-start.20 = (bf16[1,512,1024]{2,1,0:T(8,128)(2,1)S(1)}, bf16[1,512,1024]{2,1,0:T(8,128)(2,1)}, u32[]{:S(2)}) copy-start(bf16[1,512,1024]{2,1,0:T(8,128)(2,1)} %param.20) | copy-start | bytes 3145732
  556.3 91.6 %collective-permute-start.3 = (bf16[512,2048]{0,1:T(8,128)(2,1)S(1)}, bf16[512,2048]{0,1:T(8,128)(2,1)S(1)}, u32[]{:S(2)}, u32[]{:S(2)}) collective-permute-start(bf16[512,2048]{0,1:T(8,128)(2,1)S(1)} %get-tuple-element.586), channel_id=1, source_target_pairs={{2,0},{4,2},{6,4},{8,6},{10,8},{12,10},{14,12},{16,14},{18,16},{20... | collective-permute-start | bytes 6291464 | tf_op jit(solution)/shard_map/ppermute | solution.py:23
  674.7 341.6 %reduce-scatter.9.cloned.1.call-start = ((), (), s32[]{:S(2)}) async-start(), calls=%async_computation.9 | async-start | bytes 17301504 | tf_op jit(solution)/shard_map/reduce_scatter | solution.py:335
  687.3 516.6 %reduce-scatter.11.cloned.1.call-start = ((), (), s32[]{:S(2)}) async-start(), calls=%async_computation.10 | async-start | bytes 17301504 | tf_op jit(solution)/shard_map/reduce_scatter | solution.py:337
  699.7 52.8 %copy-start.12 = (f32[512,1024]{1,0:T(8,128)S(1)}, f32[512,1024]{1,0:T(8,128)}, u32[]{:S(2)}) copy-start(f32[512,1024]{1,0:T(8,128)} %copy-done.11) | copy-start | bytes 6291460
  699.7 52.8 %copy-start.35 = (f32[512]{0:T(512)S(1)}, f32[512]{0:T(512)}, u32[]{:S(2)}) copy-start(f32[512]{0:T(512)} %copy-done.34) | copy-start | bytes 6148
  (55 other events, 255.5 us)
Sparse Core Ops, SparseCore 0:
  10.9 69.4 all-gather.5
  83.3 94.1 all-gather.7
  180.3 76.0 all-gather.9
  259.1 76.0 all-gather.11
  388.0 122.7 reduce-scatter.6
  674.9 153.1 reduce-scatter.12
  831.1 185.2 reduce-scatter.8
  1019.3 184.4 reduce-scatter.10
where the time goes:
time: 1220 us; the launch traced here: 1210 us
  waiting for transfers between devices  569 us (47%)
  matrix products  269 us (22%)
  blocking collectives  201 us (16%)
  other arithmetic  72.8 us (6%)
  local copies, waits for them, and re-layouts  69.7 us (6%)
  between operations  15.2 us (1%)
  starting transfers between devices  14.6 us (1%)
    reduce_scatter x1, waiting for transfers between devices, shards(): lax.psum_scatter(up_weight_part, ('ctx', 'fsdp'), scatter_dimension=0, ti...  188 us
    reduce_scatter x1, waiting for transfers between devices, shards(): lax.psum_scatter(down_weight_part, ('ctx', 'fsdp'), scatter_dimension=0,...  187 us
    all_gather x1, blocking collectives, shards(): lax.all_gather(up_bias, ('ctx', 'fsdp'), axis=0, tiled=True)  119 us
    unnamed x2, blocking collectives  81.7 us
    unnamed x9, waiting for transfers between devices  69.3 us
    dot_general x8, matrix products, block_parts(): jnp.einsum('qhd,khd->hqk', query_block, key_block, preferred_element_type...  46.2 us
    ppermute x2, waiting for transfers between devices, extended(): lax.ppermute(lax.slice_in_dim(block, 0, width, axis=dim), axis, backward)  44 us
    ppermute x2, waiting for transfers between devices, extended(): lax.ppermute(lax.slice_in_dim(block, block.shape[dim] - width, None, axis...  43.5 us
  transfers between devices with their start and end apart: 12, of which 7 were waited for; matrix products, arithmetic and copies ran while one was open for 28% of the time, Pallas kernels for 0%

commit v1 on v0

v1 whole, which is shorter than its diff:
```python
import functools

import jax
import jax.numpy as jnp
from jax import lax
from jax.experimental import pallas as pl
from jax.experimental.pallas import tpu as pltpu
from jax.sharding import PartitionSpec as P

H = 16
HD = 64
WINDOW = 1024
HALF = WINDOW // 2
ROWS = 128
PAIR = 2 * HD
FILL = -1e30
EPS = 1e-05
F32 = jnp.float32
BF16 = jnp.bfloat16
VMEM_BYTES = 56 * 1024 * 1024


def nn(a, b):
    return lax.dot_general(a, b, (((1,), (0,)), ((), ())), preferred_element_type=F32)


def nt(a, b):
    return lax.dot_general(a, b, (((1,), (1,)), ((), ())), preferred_element_type=F32)


def tn(a, b):
    return lax.dot_general(a, b, (((0,), (0,)), ((), ())), preferred_element_type=F32)


def cat(parts, axis):
    return jnp.concatenate(parts, axis=axis)


def cost(flops, bytes_accessed, exps=0):
    return pl.CostEstimate(flops=flops, bytes_accessed=bytes_accessed, transcendentals=exps)


def params():
    return pltpu.CompilerParams(vmem_limit_bytes=VMEM_BYTES)


def head_masks(scale):
    lane = lax.broadcasted_iota(jnp.int32, (1, PAIR), 1)
    first = jnp.where(lane < HD, scale, 0.0).astype(F32)
    second = jnp.where(lane < HD, 0.0, scale).astype(F32)
    return first.astype(BF16), second.astype(BF16)


def stacked(values, masks):
    return cat([values * masks[0], values * masks[1]], 0)


def strip(i, tokens):
    return slice(ROWS * i, ROWS * i + tokens + ROWS)


def attend_kernel(q_ref, ko_ref, kp_ref, kn_ref, vo_ref, vp_ref, vn_ref, bo_ref, bh_ref, out_ref, lse_ref, kh, vh):
    tokens = q_ref.shape[0]
    kh[:tokens] = kp_ref[...]
    kh[tokens:] = kn_ref[...]
    ones = head_masks(1.0)
    vh[:tokens] = vp_ref[...]
    vh[tokens:] = vn_ref[...]
    vo = stacked(vo_ref[...], ones)
    scaled = head_masks(HD ** -0.5)
    lane = lax.broadcasted_iota(jnp.int32, (ROWS, PAIR), 1)
    for i in range(tokens // ROWS):
        rows = slice(ROWS * i, ROWS * i + ROWS)
        window = strip(i, tokens)
        q = q_ref[rows]
        own_parts, halo_parts, totals, logs = [], [], [], []
        for mask in scaled:
            qm = q * mask
            so = nt(qm, ko_ref[...]) + bo_ref[rows]
            sh = nt(qm, kh[window]) + bh_ref[i]
            peak = jnp.maximum(jnp.max(so, axis=1, keepdims=True), jnp.max(sh, axis=1, keepdims=True))
            po = jnp.exp(so - peak)
            ph = jnp.exp(sh - peak)
            total = jnp.sum(po, axis=1, keepdims=True) + jnp.sum(ph, axis=1, keepdims=True)
            own_parts.append(po.astype(BF16))
            halo_parts.append(ph.astype(BF16))
            totals.append(1.0 / total)
            logs.append(peak + jnp.log(total))
        out = nn(cat(own_parts, 1), vo) + nn(cat(halo_parts, 1), stacked(vh[window], ones))
        out = out * jnp.where(lane < HD, totals[0], totals[1])
        out_ref[rows] = out.astype(BF16)
        lse_ref[0, rows] = cat(logs, 1)


def attend(mixed, before, after, bias_own, bias_halo):
    tokens, width = mixed.shape[0], mixed.shape[1] // 3
    pairs = width // PAIR

    def column(part):
        return pl.BlockSpec((tokens, PAIR), lambda p: (0, part * pairs + p))

    whole = lambda shape: pl.BlockSpec(shape, lambda p: (0,) * len(shape))
    return pl.pallas_call(
        attend_kernel,
        grid=(pairs,),
        in_specs=[column(0), column(1), column(1), column(1), column(2), column(2), column(2), whole(bias_own.shape), whole(bias_halo.shape)],
        out_specs=[pl.BlockSpec((tokens, PAIR), lambda p: (0, p)), pl.BlockSpec((1, tokens, 2), lambda p: (p, 0, 0))],
        out_shape=[jax.ShapeDtypeStruct((tokens, width), BF16), jax.ShapeDtypeStruct((pairs, tokens, 2), F32)],
        scratch_shapes=[pltpu.VMEM((2 * tokens, PAIR), BF16), pltpu.VMEM((2 * tokens, PAIR), BF16)],
        compiler_params=params(),
        cost_estimate=cost(4 * tokens * 9 * ROWS * width * 4, 16 * tokens * width, H * tokens * 9 * ROWS),
        name="attend",
    )(mixed, mixed, before, after, mixed, before, after, bias_own, bias_halo)


def own_grad_kernel(q_ref, ko_ref, kp_ref, kn_ref, vo_ref, vp_ref, vn_ref, do_ref, lc_ref, dc_ref, lr_ref, dr_ref, bo_ref, bh_ref, dq_ref, dk_ref, dv_ref, kh, vh):
    tokens = q_ref.shape[0]
    kh[:tokens] = kp_ref[...]
    kh[tokens:] = kn_ref[...]
    vh[:tokens] = vp_ref[...]
    vh[tokens:] = vn_ref[...]
    ones = head_masks(1.0)
    scaled = head_masks(HD ** -0.5)
    k_own = ko_ref[...]
    v_own = vo_ref[...]
    k_pair = stacked(k_own, scaled)
    chunk = 2 * ROWS
    for c in range(tokens // chunk):
        cols = slice(chunk * c, chunk * c + chunk)
        q = q_ref[cols]
        do = do_ref[cols]
        probs, grads, qs, dos = [], [], [], []
        for h in range(2):
            qm = q * scaled[h]
            dm = do * ones[h]
            st = nt(k_own, qm) + bo_ref[:, cols]
            pt = jnp.exp(st - lr_ref[0, h : h + 1, cols])
            gt = pt * (nt(v_own, dm) - dr_ref[0, h : h + 1, cols])
            probs.append(pt.astype(BF16))
            grads.append(gt.astype(BF16))
            qs.append(qm)
            dos.append(dm)
        dv = nn(cat(probs, 1), cat(dos, 0))
        dk = nn(cat(grads, 1), cat(qs, 0))
        if c == 0:
            dv_ref[...] = dv
            dk_ref[...] = dk
        else:
            dv_ref[...] += dv
            dk_ref[...] += dk
        dq_own = tn(cat(grads, 0), k_pair)
        for r in range(chunk // ROWS):
            i = c * (chunk // ROWS) + r
            rows = slice(ROWS * i, ROWS * i + ROWS)
            window = strip(i, tokens)
            halo = []
            for h in range(2):
                qm = q[ROWS * r : ROWS * r + ROWS] * scaled[h]
                dm = do[ROWS * r : ROWS * r + ROWS] * ones[h]
                s = nt(qm, kh[window]) + bh_ref[i]
                p = jnp.exp(s - lc_ref[0, rows, h : h + 1])
                halo.append((p * (nt(dm, vh[window]) - dc_ref[0, rows, h : h + 1])).astype(BF16))
            dq = dq_own[ROWS * r : ROWS * r + ROWS] + nn(cat(halo, 1), stacked(kh[window], scaled))
            dq_ref[rows] = dq.astype(BF16)


def own_grads(mixed, before, after, grad_heads, log_cols, mean_cols, log_rows, mean_rows, bias_own, bias_halo):
    tokens, width = grad_heads.shape
    pairs = width // PAIR

    def column(part):
        return pl.BlockSpec((tokens, PAIR), lambda p: (0, part * pairs + p))

    whole = lambda shape: pl.BlockSpec(shape, lambda p: (0,) * len(shape))
    cols = pl.BlockSpec((1, tokens, 2), lambda p: (p, 0, 0))
    rows = pl.BlockSpec((1, 2, tokens), lambda p: (p, 0, 0))
    block = pl.BlockSpec((tokens, PAIR), lambda p: (0, p))
    return pl.pallas_call(
        own_grad_kernel,
        grid=(pairs,),
        in_specs=[column(0), column(1), column(1), column(1), column(2), column(2), column(2), block, cols, cols, rows, rows, whole(bias_own.shape), whole(bias_halo.shape)],
        out_specs=[block, block, block],
        out_shape=[
            jax.ShapeDtypeStruct((tokens, width), BF16),
            jax.ShapeDtypeStruct((tokens, width), F32),
            jax.ShapeDtypeStruct((tokens, width), F32),
        ],
        scratch_shapes=[pltpu.VMEM((2 * tokens, PAIR), BF16), pltpu.VMEM((2 * tokens, PAIR), BF16)],
        compiler_params=params(),
        cost_estimate=cost(10 * tokens * 9 * ROWS * width * 4, 30 * tokens * width, H * tokens * 9 * ROWS),
        name="own_grads",
    )(mixed, mixed, before, after, mixed, before, after, grad_heads, log_cols, mean_cols, log_rows, mean_rows, bias_own, bias_halo)


def halo_grad_kernel(ko_ref, vo_ref, qp_ref, qn_ref, dp_ref, dn_ref, lp_ref, ln_ref, bh_ref, dk_in, dv_in, dk_ref, dv_ref, qh, dh, lh):
    tokens = ko_ref.shape[0]
    qh[:tokens] = qp_ref[...]
    qh[tokens:] = qn_ref[...]
    dh[:tokens] = dp_ref[...]
    dh[tokens:] = dn_ref[...]
    lh[:, :, :tokens] = lp_ref[:, 0]
    lh[:, :, tokens:] = ln_ref[:, 0]
    ones = head_masks(1.0)
    scaled = head_masks(HD ** -0.5)
    for j in range(tokens // ROWS):
        rows = slice(ROWS * j, ROWS * j + ROWS)
        window = strip(j, tokens)
        q = qh[window]
        do = dh[window]
        k = ko_ref[rows]
        v = vo_ref[rows]
        probs, grads, qs, dos = [], [], [], []
        for h in range(2):
            qm = q * scaled[h]
            dm = do * ones[h]
            st = nt(k, qm) + bh_ref[j]
            pt = jnp.exp(st - lh[0, h : h + 1, window])
            gt = pt * (nt(v, dm) - lh[1, h : h + 1, window])
            probs.append(pt.astype(BF16))
            grads.append(gt.astype(BF16))
            qs.append(qm)
            dos.append(dm)
        dk_ref[rows] = (dk_in[rows] + nn(cat(grads, 1), cat(qs, 0))).astype(BF16)
        dv_ref[rows] = (dv_in[rows] + nn(cat(probs, 1), cat(dos, 0))).astype(BF16)


def halo_grads(mixed, before, after, grad_before, grad_after, rows_before, rows_after, bias_halo, dk, dv):
    tokens, width = dk.shape
    pairs = width // PAIR

    def column(part):
        return pl.BlockSpec((tokens, PAIR), lambda p: (0, part * pairs + p))

    whole = lambda shape: pl.BlockSpec(shape, lambda p: (0,) * len(shape))
    rows = pl.BlockSpec((2, 1, 2, tokens), lambda p: (0, p, 0, 0))
    block = pl.BlockSpec((tokens, PAIR), lambda p: (0, p))
    return pl.pallas_call(
        halo_grad_kernel,
        grid=(pairs,),
        in_specs=[column(1), column(2), column(0), column(0), block, block, rows, rows, whole(bias_halo.shape), block, block],
        out_specs=[block, block],
        out_shape=[jax.ShapeDtypeStruct((tokens, width), BF16)] * 2,
        scratch_shapes=[pltpu.VMEM((2 * tokens, PAIR), BF16), pltpu.VMEM((2 * tokens, PAIR), BF16), pltpu.VMEM((2, 2, 2 * tokens), F32)],
        compiler_params=params(),
        cost_estimate=cost(8 * tokens * 5 * ROWS * width * 4, 20 * tokens * width, H * tokens * 5 * ROWS),
        name="halo_grads",
    )(mixed, mixed, before, after, grad_before, grad_after, rows_before, rows_after, bias_halo, dk, dv)


def mask_biases(segments, place, blocks, tokens):
    line = cat([jnp.full((tokens,), -1, jnp.int32), segments, jnp.full((tokens,), -1, jnp.int32)], 0)
    near = lax.dynamic_slice_in_dim(line, place * tokens, 3 * tokens)
    own = near[tokens : 2 * tokens]
    bias_own = jnp.where(own[:, None] == own[None, :], 0.0, FILL).astype(F32)
    halo = cat([near[:tokens], near[2 * tokens :]], 0)
    at = jnp.arange(tokens, dtype=jnp.int32)
    halo_at = cat([at - tokens, at + tokens], 0)
    allowed = (own[:, None] == halo[None, :]) & (jnp.abs(halo_at[None, :] - at[:, None]) < HALF)
    bias = jnp.where(allowed, 0.0, FILL).astype(F32)
    bias_halo = jnp.stack([bias[ROWS * i : ROWS * i + ROWS, strip(i, tokens)] for i in range(tokens // ROWS)])
    return bias_own, bias_halo


def normalized(values):
    average = jnp.mean(values, axis=1, keepdims=True)
    centered = values - average
    spread = jnp.mean(centered * centered, axis=1, keepdims=True)
    inverse = lax.rsqrt(spread + EPS)
    return centered * inverse, inverse


def norm_back(grad, gain, hat, inverse):
    scaled = grad * gain
    return inverse * (
        scaled
        - jnp.mean(scaled, axis=1, keepdims=True)
        - hat * jnp.mean(scaled * hat, axis=1, keepdims=True)
    )


def column_sum(values):
    return jnp.sum(values, axis=0, keepdims=True)


def part_blocks(at_ref, order, second, far):
    for first in range(2):
        rel = {order[0]: first, order[1]: second}
        y = jnp.bitwise_xor(at_ref[0], rel["y"])
        x = jnp.bitwise_xor(at_ref[1], rel["x"])
        for z in range(far):
            yield first, z, (z * 2 + y) * 2 + x


def start_all(copies):
    for copy in copies:
        copy.start()


def wait_all(copies):
    for copy in copies:
        copy.wait()


def flipped_rows(values, flipped, at_ref, far):
    turned = values.T
    if far is None:
        flipped[...] = turned
        return
    rows = turned.shape[0] // (4 * far)
    for z in range(far):
        for y in range(2):
            for x in range(2):
                a = (z * 2 + y) * 2 + x
                to = (jnp.bitwise_xor(at_ref[1], x) * 2 + jnp.bitwise_xor(at_ref[0], y)) * far + z
                flipped[pl.ds(pl.multiple_of(to * rows, rows), rows)] = turned[a * rows : a * rows + rows]


def qkv_copies(refs, full, sems, at_ref, far):
    if far is None:
        return [pltpu.make_async_copy(refs[0], full, sems.at[0])]
    width, columns = full.shape
    rows, half = width // (8 * far), columns // 2
    copies = []
    for core in range(2):
        at_half = jnp.bitwise_xor(at_ref[2], core)
        for color, order in enumerate(("yx", "xy")):
            for second in range(2):
                ref = refs[core * 4 + color * 2 + second]
                for first, z, block in part_blocks(at_ref, order, second, far):
                    row = pl.multiple_of((block * 2 + color) * rows, rows)
                    to = full.at[pl.ds(row, rows), pl.ds(pl.multiple_of(at_half * half, half), half)]
                    copies.append(pltpu.make_async_copy(ref.at[first, z, :, pl.ds(0, half)], to, sems.at[len(copies)]))
    return copies


def project_kernel(far, parts, *refs):
    at_ref, refs = refs[0], refs[1:]
    part_refs, refs = refs[:parts], refs[parts:]
    own_ref, before_ref, after_ref, row_ref, own_out, before_out, after_out, full_out, full, sems, out_sem = refs
    copies = qkv_copies(part_refs, full, sems, at_ref, far)
    start_all(copies)
    wait_all(copies)
    keep = pltpu.make_async_copy(full, full_out, out_sem)
    keep.start()
    chunk = 512
    for source, target in ((own_ref, own_out), (before_ref, before_out), (after_ref, after_out)):

        def body(j, carry, source=source, target=target):
            cols = pl.ds(pl.multiple_of(j * chunk, chunk), chunk)
            target[:, cols] = (nn(source[...], full[:, cols]) + row_ref[:, cols]).astype(BF16)
            return carry

        lax.fori_loop(0, full.shape[1] // chunk, body, 0)
    keep.wait()


SMEM = pl.BlockSpec(memory_space=pltpu.SMEM)
ANY = pl.BlockSpec(memory_space=pl.ANY)
VMEM = pl.BlockSpec(memory_space=pltpu.VMEM)


def copy_count(far, each):
    return 1 if far is None else 8 * far * each


def project(far, at, parts, x, before, after, row):
    tokens, width = x.shape
    columns = row.shape[1]
    mixed = jax.ShapeDtypeStruct((tokens, columns), BF16)
    return pl.pallas_call(
        functools.partial(project_kernel, far, len(parts)),
        in_specs=[SMEM] + [ANY] * len(parts) + [VMEM] * 4,
        out_specs=[VMEM, VMEM, VMEM, ANY],
        out_shape=[mixed, mixed, mixed, jax.ShapeDtypeStruct((width, columns), BF16)],
        scratch_shapes=[
            pltpu.VMEM((width, columns), BF16),
            pltpu.SemaphoreType.DMA((copy_count(far, 4),)),
            pltpu.SemaphoreType.DMA,
        ],
        compiler_params=params(),
        cost_estimate=cost(6 * tokens * width * columns, 4 * width * columns + 8 * tokens * columns),
        name="project",
    )(at, *parts, x, before, after, row)


def out_copies(refs, full, sems, at_ref, far):
    if far is None:
        return [pltpu.make_async_copy(refs[0], full, sems.at[0])]
    width = full.shape[0]
    rows, half = width // (8 * far), width // 2
    copies = []
    for core in range(2):
        col = pl.multiple_of(jnp.bitwise_xor(at_ref[2], core) * half, half)
        for second in range(2):
            ref = refs[core * 2 + second]
            skip = ref.shape[2] - rows
            for first, z, block in part_blocks(at_ref, "xy", second, far):
                for side in range(2):
                    row = pl.multiple_of((block * 2 + side) * rows, rows)
                    copies.append(
                        pltpu.make_async_copy(
                            ref.at[first, z, pl.ds(skip, rows), pl.ds(side * half, half)],
                            full.at[pl.ds(row, rows), pl.ds(col, half)],
                            sems.at[len(copies)],
                        )
                    )
    return copies


def out_kernel(far, parts, *refs):
    at_ref, refs = refs[0], refs[1:]
    part_refs, refs = refs[:parts], refs[parts:]
    heads_ref, x_ref, vec_ref, hat_ref, inv_ref, first_ref, low_ref, full_out, full, sems, out_sem = refs
    copies = out_copies(part_refs, full, sems, at_ref, far)
    keep = pltpu.make_async_copy(full, full_out, out_sem)

    @pl.when(pl.program_id(0) == 0)
    def _():
        start_all(copies)
        wait_all(copies)
        keep.start()

    branch = nn(heads_ref[...], full[...]) + vec_ref[0:1]
    hat, inverse = normalized(x_ref[...].astype(F32) + branch)
    first = hat * vec_ref[1:2] + vec_ref[2:3]
    hat_ref[...] = hat
    inv_ref[...] = inverse
    first_ref[...] = first
    low_ref[...] = first.astype(BF16)

    @pl.when(pl.program_id(0) == pl.num_programs(0) - 1)
    def _():
        keep.wait()


def out_project(far, at, parts, heads, x, vectors):
    tokens, width = heads.shape
    rows = tokens // 4
    block = pl.BlockSpec((rows, width), lambda i: (i, 0))
    return pl.pallas_call(
        functools.partial(out_kernel, far, len(parts)),
        grid=(4,),
        in_specs=[SMEM] + [ANY] * len(parts) + [block, block, pl.BlockSpec(vectors.shape, lambda i: (0, 0))],
        out_specs=[block, pl.BlockSpec((rows, 1), lambda i: (i, 0)), block, block, ANY],
        out_shape=[
            jax.ShapeDtypeStruct((tokens, width), F32),
            jax.ShapeDtypeStruct((tokens, 1), F32),
            jax.ShapeDtypeStruct((tokens, width), F32),
            jax.ShapeDtypeStruct((tokens, width), BF16),
            jax.ShapeDtypeStruct((width, width), BF16),
        ],
        scratch_shapes=[
            pltpu.VMEM((width, width), BF16),
            pltpu.SemaphoreType.DMA((copy_count(far, 4),)),
            pltpu.SemaphoreType.DMA,
        ],
        compiler_params=params(),
        cost_estimate=cost(2 * tokens * width * width, 16 * tokens * width),
        name="out_project",
    )(at, *parts, heads, x, vectors)


def up_copies(refs, full, sems, at_ref, far):
    if far is None:
        return [pltpu.make_async_copy(refs[0], full, sems.at[0])]
    width, hidden = full.shape
    rows, half = width // (4 * far), hidden // 2
    copies = []
    for core in range(2):
        col = pl.multiple_of(jnp.bitwise_xor(at_ref[2], core) * half, half)
        for second in range(2):
            ref = refs[core * 2 + second]
            for first, z, block in part_blocks(at_ref, "yx", second, far):
                to = full.at[pl.ds(pl.multiple_of(block * rows, rows), rows), pl.ds(col, half)]
                copies.append(pltpu.make_async_copy(ref.at[first, z], to, sems.at[len(copies)]))
    return copies


def down_copies(refs, full, sems, at_ref, far):
    if far is None:
        return [pltpu.make_async_copy(refs[0], full, sems.at[0])]
    rows = full.shape[0] // (8 * far)
    copies = []
    for core in range(2):
        side = jnp.bitwise_xor(at_ref[2], core)
        for second in range(2):
            ref = refs[core * 2 + second]
            for first, z, block in part_blocks(at_ref, "xy", second, far):
                to = full.at[pl.ds(pl.multiple_of((block * 2 + side) * rows, rows), rows)]
                copies.append(pltpu.make_async_copy(ref.at[first, z, pl.ds(0, rows)], to, sems.at[len(copies)]))
    return copies


def forward_kernel(far, ups, downs, *refs):
    at_ref, refs = refs[0], refs[1:]
    up_refs, down_refs, refs = refs[:ups], refs[ups : ups + downs], refs[ups + downs :]
    low_ref, first_ref, upb_ref, vec_ref, dy_ref, act_ref, slope_ref, result_ref, grad_ref, glow_ref, sums_ref, up_out, down_out = refs[:13]
    total, up_full, down_full, up_sems, down_sems, out_sems = refs[13:]
    step = pl.program_id(0)
    chunk = act_ref.shape[1]
    cols = pl.ds(pl.multiple_of(step * chunk, chunk), chunk)
    from_up = up_copies(up_refs, up_full, up_sems, at_ref, far)
    from_down = down_copies(down_refs, down_full, down_sems, at_ref, far)
    keep_up = pltpu.make_async_copy(up_full, up_out, out_sems.at[0])
    keep_down = pltpu.make_async_copy(down_full, down_out, out_sems.at[1])

    @pl.when(step == 0)
    def _():
        start_all(from_up)
        start_all(from_down)
        wait_all(from_up)
        keep_up.start()

    lifted = nn(low_ref[...], up_full[:, cols]) + upb_ref[...]
    phi = 0.5 * (1.0 + lax.erf(lifted * (0.5 ** 0.5)))
    density = jnp.exp(lifted * lifted * -0.5) * 0.3989422804014327
    active = (lifted * phi).astype(BF16)
    act_ref[...] = active
    slope_ref[...] = phi + lifted * density

    @pl.when(step == 0)
    def _():
        wait_all(from_down)
        keep_down.start()

    part = nn(active, down_full[cols])

    @pl.when(step == 0)
    def _():
        total[...] = part

    @pl.when(step > 0)
    def _():
        total[...] += part

    @pl.when(step == pl.num_programs(0) - 1)
    def _():
        rows = total.shape[0] // 4
        sums = None
        for i in range(4):
            at = slice(rows * i, rows * i + rows)
            hat, inverse = normalized(first_ref[at] + (total[at] + vec_ref[0:1]))
            result_ref[at] = (hat * vec_ref[1:2] + vec_ref[2:3]).astype(BF16)
            dy = dy_ref[at].astype(F32)
            grad = norm_back(dy, vec_ref[1:2], hat, inverse)
            low = grad.astype(BF16)
            grad_ref[at] = grad
            glow_ref[at] = low
            part = cat([column_sum(dy * hat), column_sum(dy), column_sum(low.astype(F32))], 0)
            sums = part if sums is None else sums + part
        sums_ref[...] = sums
        keep_up.wait()
        keep_down.wait()


def forward(far, at, up_parts, down_parts, low, first, up_bias, vectors, dy, chunk=512):
    tokens, width = low.shape
    hidden = up_bias.shape[1]
    whole = lambda shape: pl.BlockSpec(shape, lambda i: (0, 0))
    return pl.pallas_call(
        functools.partial(forward_kernel, far, len(up_parts), len(down_parts)),
        grid=(hidden // chunk,),
        in_specs=[SMEM]
        + [ANY] * (len(up_parts) + len(down_parts))
        + [
            whole((tokens, width)),
            whole((tokens, width)),
            pl.BlockSpec((1, chunk), lambda i: (0, i)),
            whole(vectors.shape),
            whole((tokens, width)),
        ],
        out_specs=[
            pl.BlockSpec((tokens, chunk), lambda i: (0, i)),
            pl.BlockSpec((tokens, chunk), lambda i: (0, i)),
            whole((tokens, width)),
            whole((tokens, width)),
            whole((tokens, width)),
            whole((3, width)),
            ANY,
            ANY,
        ],
        out_shape=[
            jax.ShapeDtypeStruct((tokens, hidden), BF16),
            jax.ShapeDtypeStruct((tokens, hidden), F32),
            jax.ShapeDtypeStruct((tokens, width), BF16),
            jax.ShapeDtypeStruct((tokens, width), F32),
            jax.ShapeDtypeStruct((tokens, width), BF16),
            jax.ShapeDtypeStruct((3, width), F32),
            jax.ShapeDtypeStruct((width, hidden), BF16),
            jax.ShapeDtypeStruct((hidden, width), BF16),
        ],
        scratch_shapes=[
            pltpu.VMEM((tokens, width), F32),
            pltpu.VMEM((width, hidden), BF16),
            pltpu.VMEM((hidden, width), BF16),
            pltpu.SemaphoreType.DMA((copy_count(far, 2),)),
            pltpu.SemaphoreType.DMA((copy_count(far, 2),)),
            pltpu.SemaphoreType.DMA((2,)),
        ],
        compiler_params=params(),
        cost_estimate=cost(4 * tokens * width * hidden, 8 * width * hidden + 6 * tokens * hidden, 2 * tokens * hidden),
        name="feed_forward",
    )(at, *up_parts, *down_parts, low, first, up_bias, vectors, dy)


def down_grad_kernel(far, at_ref, glow_ref, down_ref, slope_ref, act_ref, lift_ref, keep_ref, send_ref, ub_ref):
    step = pl.program_id(0)
    glow = glow_ref[...]
    lift = (nt(glow, down_ref[...]) * slope_ref[...]).astype(BF16)
    lift_ref[...] = lift
    ub_ref[...] = column_sum(lift.astype(F32))
    dw = tn(act_ref[...], glow).astype(BF16)
    chunk = dw.shape[0]
    if far is None:
        half = keep_ref.shape[0] // chunk

        @pl.when(step < half)
        def _():
            keep_ref[pl.ds(pl.multiple_of(step * chunk, chunk), chunk)] = dw

        @pl.when(step >= half)
        def _():
            send_ref[pl.ds(pl.multiple_of((step - half) * chunk, chunk), chunk)] = dw

        return
    rows = keep_ref.shape[0] // (4 * far)
    for j in range(chunk // rows):
        block, side = step * (chunk // rows // 2) + j // 2, j % 2
        z, y, x = block // 4, block // 2 % 2, block % 2
        to = (jnp.bitwise_xor(at_ref[0], y) * 2 + jnp.bitwise_xor(at_ref[1], x)) * far + z
        rows_to = pl.ds(pl.multiple_of(to * rows, rows), rows)
        value = dw[j * rows : j * rows + rows]

        @pl.when(at_ref[2] == side)
        def _(value=value, rows_to=rows_to):
            keep_ref[rows_to] = value

        @pl.when(at_ref[2] != side)
        def _(value=value, rows_to=rows_to):
            send_ref[rows_to] = value


def down_grads(far, at, glow, down_full, slope, active, chunk=512):
    tokens, width = glow.shape
    hidden = down_full.shape[0]
    block = pl.BlockSpec((tokens, chunk), lambda i: (0, i))
    half = pl.BlockSpec((hidden // 2, width), lambda i: (0, 0))
    return pl.pallas_call(
        functools.partial(down_grad_kernel, far),
        grid=(hidden // chunk,),
        in_specs=[SMEM, pl.BlockSpec((tokens, width), lambda i: (0, 0)), pl.BlockSpec((chunk, width), lambda i: (i, 0)), block, block],
        out_specs=[block, half, half, pl.BlockSpec((1, chunk), lambda i: (0, i))],
        out_shape=[
            jax.ShapeDtypeStruct((tokens, hidden), BF16),
            jax.ShapeDtypeStruct((hidden // 2, width), BF16),
            jax.ShapeDtypeStruct((hidden // 2, width), BF16),
            jax.ShapeDtypeStruct((1, hidden), F32),
        ],
        compiler_params=params(),
        cost_estimate=cost(4 * tokens * width * hidden, 4 * width * hidden + 8 * tokens * hidden),
        name="down_grads",
    )(at, glow, down_full, slope, active)


def split_store(at_ref, half, keep_ref, send_ref, cols, value):
    @pl.when(at_ref[2] == half)
    def _():
        keep_ref[:, cols] = value

    @pl.when(at_ref[2] != half)
    def _():
        send_ref[:, cols] = value


def up_grad_kernel(far, at_ref, low_ref, lift_ref, up_ref, grad_ref, hat_ref, inv_ref, gain_ref, keep_ref, send_ref, one_ref, branch_ref, sums_ref, total, flipped):
    step = pl.program_id(0)

    @pl.when(step == 0)
    def _():
        flipped_rows(low_ref[...], flipped, at_ref, far)

    lift = lift_ref[...]
    dw = nn(flipped[...], lift).astype(BF16)
    chunk = dw.shape[1]
    steps = keep_ref.shape[1] // chunk
    cols = pl.ds(pl.multiple_of(step % steps * chunk, chunk), chunk)
    split_store(at_ref, step // steps, keep_ref, send_ref, cols, dw)
    part = nt(lift, up_ref[...])

    @pl.when(step == 0)
    def _():
        total[...] = grad_ref[...] + part

    @pl.when(step > 0)
    def _():
        total[...] += part

    @pl.when(step == pl.num_programs(0) - 1)
    def _():
        rows = total.shape[0] // 4
        sums = None
        for i in range(4):
            at = slice(rows * i, rows * i + rows)
            grad = total[at]
            hat = hat_ref[at]
            one = norm_back(grad, gain_ref[...], hat, inv_ref[at])
            branch = one.astype(BF16)
            one_ref[at] = one
            branch_ref[at] = branch
            part = cat([column_sum(grad * hat), column_sum(grad), column_sum(branch.astype(F32))], 0)
            sums = part if sums is None else sums + part
        sums_ref[...] = sums


def up_grads(far, at, low, lift, up_full, grad_two, hat, inverse, gain, chunk=512):
    tokens, width = low.shape
    hidden = up_full.shape[1]
    whole = lambda shape: pl.BlockSpec(shape, lambda i: (0, 0))
    half = whole((width, hidden // 2))
    return pl.pallas_call(
        functools.partial(up_grad_kernel, far),
        grid=(hidden // chunk,),
        in_specs=[
            SMEM,
            whole((tokens, width)),
            pl.BlockSpec((tokens, chunk), lambda i: (0, i)),
            pl.BlockSpec((width, chunk), lambda i: (0, i)),
            whole((tokens, width)),
            whole((tokens, width)),
            whole((tokens, 1)),
            whole((1, width)),
        ],
        out_specs=[half, half, whole((tokens, width)), whole((tokens, width)), whole((3, width))],
        out_shape=[
            jax.ShapeDtypeStruct((width, hidden // 2), BF16),
            jax.ShapeDtypeStruct((width, hidden // 2), BF16),
            jax.ShapeDtypeStruct((tokens, width), F32),
            jax.ShapeDtypeStruct((tokens, width), BF16),
            jax.ShapeDtypeStruct((3, width), F32),
        ],
        scratch_shapes=[pltpu.VMEM((tokens, width), F32), pltpu.VMEM((width, tokens), BF16)],
        compiler_params=params(),
        cost_estimate=cost(4 * tokens * width * hidden, 4 * width * hidden + 2 * tokens * hidden),
        name="up_grads",
    )(at, low, lift, up_full, grad_two, hat, inverse, gain)


def out_grad_kernel(far, at_ref, branch_ref, w_ref, heads_ref, gh_ref, mean_ref, keep_ref, send_ref, flipped):
    width = branch_ref.shape[1]
    branch = branch_ref[...]
    heads = heads_ref[...]
    grad = nt(branch, w_ref[...]).astype(BF16)
    gh_ref[...] = grad
    flipped_rows(heads, flipped, at_ref, far)
    half = width // 2
    for j in range(2):
        dw = nn(flipped[...], branch[:, j * half : j * half + half]).astype(BF16)
        split_store(at_ref, j, keep_ref, send_ref, slice(None), dw)
    product = grad.astype(F32) * heads.astype(F32)
    head = lax.broadcasted_iota(jnp.int32, (width, H), 0) // HD
    pick = jnp.where(head == lax.broadcasted_iota(jnp.int32, (width, H), 1), 1.0, 0.0).astype(F32)
    mean_ref[...] = lax.dot_general(product, pick, (((1,), (0,)), ((), ())), precision=lax.Precision.HIGHEST, preferred_element_type=F32)


def out_grads(far, at, branch, out_full, heads):
    tokens, width = branch.shape
    half = jax.ShapeDtypeStruct((width, width // 2), BF16)
    return pl.pallas_call(
        functools.partial(out_grad_kernel, far),
        in_specs=[SMEM, VMEM, VMEM, VMEM],
        out_shape=[jax.ShapeDtypeStruct((tokens, width), BF16), jax.ShapeDtypeStruct((tokens, H), F32), half, half],
        scratch_shapes=[pltpu.VMEM((width, tokens), BF16)],
        compiler_params=params(),
        cost_estimate=cost(4 * tokens * width * width, 4 * width * width + 6 * tokens * width),
        name="out_grads",
    )(at, branch, out_full, heads)


def qkv_grad_kernel(far, at_ref, x_ref, dq_ref, dk_ref, dv_ref, keep_ref, send_ref, sums_ref, flipped):
    flipped_rows(x_ref[...], flipped, at_ref, far)
    chunk = 512
    parts = [(ref, j) for ref in (dq_ref, dk_ref, dv_ref) for j in range(ref.shape[1] // chunk)]
    for n, (ref, j) in enumerate(parts):
        dw = nn(flipped[...], ref[:, j * chunk : j * chunk + chunk]).astype(BF16)
        half = n // (len(parts) // 2)
        to = n % (len(parts) // 2) * chunk
        split_store(at_ref, half, keep_ref, send_ref, slice(to, to + chunk), dw)
    sums_ref[...] = cat([column_sum(dq_ref[...].astype(F32)), column_sum(dv_ref[...].astype(F32))], 0)


def qkv_grads(far, at, x, dq, dk, dv):
    tokens, width = x.shape
    half = jax.ShapeDtypeStruct((width, 3 * width // 2), BF16)
    return pl.pallas_call(
        functools.partial(qkv_grad_kernel, far),
        in_specs=[SMEM] + [VMEM] * 4,
        out_shape=[half, half, jax.ShapeDtypeStruct((2, width), F32)],
        scratch_shapes=[pltpu.VMEM((width, tokens), BF16)],
        compiler_params=params(),
        cost_estimate=cost(6 * tokens * width * width, 12 * width * width + 8 * tokens * width),
        name="qkv_grads",
    )(at, x, dq, dk, dv)


FAR, Y, X, CORE = "far", "y", "x", "fsdp"
CTX = (FAR, Y, X)
ALL = CTX + (CORE,)


def swap(values, axis):
    return lax.ppermute(values, axis, [(0, 1), (1, 0)])


def choose(core, left, right):
    return jnp.where(core == 0, left, right), jnp.where(core == 0, right, left)


def halves(values):
    middle = values.shape[1] // 2
    return values[:, :middle], values[:, middle:]


def added(*terms):
    total = terms[0].astype(F32)
    for term in terms[1:]:
        total = total + term.astype(F32)
    return total.astype(BF16)


def gather_first(block):
    wide = lax.all_gather(block, FAR, axis=0)
    parts = []
    for color, (one, two) in enumerate(((Y, X), (X, Y))):
        mine = wide[:, color]
        pair = jnp.stack([mine, swap(mine, one)])
        parts += [pair, swap(pair, two)]
    return parts


def gather_up(block):
    wide = lax.all_gather(block, FAR, axis=0)
    pair = jnp.stack([wide, swap(wide, Y)])
    return [pair, swap(pair, X)]


def gather_down(block):
    pair = jnp.stack([block, swap(block, X)])
    wide = lax.all_gather(pair, FAR, axis=1)
    return [wide, swap(wide, Y)]


def scatter_up(keep, got):
    there = swap(added(keep[1], got[1]), X)
    there_y = swap(added(keep[0, 1], got[0, 1], there[1]), Y)
    mine = added(keep[0, 0], got[0, 0], there[0], there_y)
    return lax.psum_scatter(mine, FAR, scatter_dimension=0, tiled=False)


def scatter_down(keep, got):
    there = swap(added(keep[1], got[1]), Y)
    mine = added(keep[0], got[0], there)
    wide = lax.psum_scatter(mine.swapaxes(0, 1), FAR, scatter_dimension=0, tiled=False)
    return wide[0].astype(F32) + swap(wide[1], X).astype(F32)


def scatter_last(keep, got):
    a, b = keep[:, :, :, 0], got[:, :, :, 0]
    there = swap(added(a[1], b[1]), X)
    there_y = swap(added(a[0, 1], b[0, 1], there[1]), Y)
    first = added(a[0, 0], b[0, 0], there[0], there_y)
    a, b = keep[:, :, :, 1], got[:, :, :, 1]
    there = swap(added(a[:, 1], b[:, 1]), Y)
    there_x = swap(added(a[1, 0], b[1, 0], there[1]), X)
    second = added(a[0, 0], b[0, 0], there[0], there_x)
    return lax.psum_scatter(jnp.stack([first, second], 1), FAR, scatter_dimension=0, tiled=False)


def own_rows(core, summed):
    mine, send = choose(core, summed[0], summed[1])
    got = swap(send, CORE)
    left, right = choose(core, mine, got)
    return left, right


def shards(inputs, segments, cotangent, qkv_weight, query_bias, value_bias, out_weight, out_bias, first_gain, first_shift, up_weight, up_bias, down_weight, down_bias, second_gain, second_shift):
    tokens, width = inputs.shape[1:]
    hidden = up_weight.shape[1]
    pairs = width // PAIR
    blocks = lax.axis_size(CTX)
    place = lax.axis_index(CTX)
    core = lax.axis_index(CORE)
    at = jnp.stack([lax.axis_index(Y), lax.axis_index(X), core]).astype(jnp.int32)
    rows = qkv_weight.shape[0]
    far = lax.axis_size(FAR) if rows % 16 == 0 else None
    onward = [(i, i + 1) for i in range(blocks - 1)]
    back = [(i + 1, i) for i in range(blocks - 1)]

    def from_before(v):
        return lax.ppermute(v, CTX, onward)

    def from_after(v):
        return lax.ppermute(v, CTX, back)

    x = inputs[0]
    vector = cat([query_bias, value_bias, out_bias, first_gain, first_shift, down_bias, second_gain, second_shift, up_bias], 0)
    if far is None:
        at = jnp.zeros_like(at)
        whole = lambda v: [lax.all_gather(v, ALL, axis=0, tiled=True)]
        qkv_parts, out_parts, up_parts, down_parts = whole(qkv_weight), whole(out_weight), whole(up_weight), whole(down_weight)
        table = whole(vector[None])[0]
    else:
        pieces = [choose(core, *halves(w)) for w in (qkv_weight, out_weight, up_weight)]
        mine = cat([p[0] for p in pieces], 1)
        got = swap(cat([p[1] for p in pieces], 1), CORE)
        both = jnp.stack(choose(core, mine, got))
        cut = 3 * width // 2
        cut_out = cut + width // 2
        lines = vector.shape[0] // 128
        note = jnp.zeros((rows, 128), BF16).at[:lines].set(vector.reshape(lines, 128))
        note = jnp.stack([note, jnp.zeros_like(note)])
        first_parts = gather_first(cat([both[:, :, :cut], note], 2))
        qkv_parts = first_parts + [swap(p, CORE) for p in first_parts]
        up_own = gather_up(both[:, :, cut_out:].reshape(2 * rows, hidden // 2))
        up_parts = up_own + [swap(p, CORE) for p in up_own]
        out_block = cat([both[0, :, cut:cut_out], both[1, :, cut:cut_out]], 1)
        down_own = gather_down(cat([down_weight, out_block], 0))
        down_parts = down_own + [swap(p, CORE) for p in down_own]
        out_parts = down_parts
        notes = jnp.stack([jnp.stack([qkv_parts[4 * c + s][:, :, :lines, cut:] for s in range(2)]) for c in range(2)])
        notes = notes.reshape(2, 2, 2, far, -1)
        for axis, index in ((0, at[2]), (1, at[1]), (2, at[0])):
            notes = jnp.where(index == 0, notes, jnp.flip(notes, axis))
        table = notes.transpose(3, 2, 1, 0, 4).reshape(2 * blocks, -1)

    each = query_bias.shape[0]
    rows_of = [table[:, each * i : each * i + each].reshape(1, width).astype(F32) for i in range(8)]
    query_row, value_row, out_row, gain_one, shift_one, down_row, gain_two, shift_two = rows_of
    up_row = table[:, 8 * each :].reshape(1, hidden).astype(F32)

    x_before = from_before(x)
    x_after = from_after(x)
    bias_own, bias_halo = mask_biases(segments[0], place, blocks, tokens)
    qkv_row = cat([query_row, jnp.zeros_like(query_row), value_row], 1)
    mixed, before, after, qkv_full = project(far, at, qkv_parts, x, x_before, x_after, qkv_row)
    heads, log_cols = attend(mixed, before, after, bias_own, bias_halo)
    hat, inverse, first, low, out_full = out_project(far, at, out_parts, heads, x, cat([out_row, gain_one, shift_one], 0))
    active, slope, result, grad_two, glow, sums_two, up_full, down_full = forward(
        far, at, up_parts, down_parts, low, first, up_row, cat([down_row, gain_two, shift_two], 0), cotangent[0]
    )
    lift, down_keep, down_send, up_bias_part = down_grads(far, at, glow, down_full, slope, active)
    down_got = None if far is None else swap(down_send, CORE)
    up_keep, up_send, grad_one, branch, sums_one = up_grads(far, at, low, lift, up_full, grad_two, hat, inverse, gain_one)
    up_got = None if far is None else swap(up_send, CORE)
    grad_heads, means, out_keep, out_send = out_grads(far, at, branch, out_full, heads)
    out_got = None if far is None else swap(out_send, CORE)
    mean_cols = means.reshape(tokens, pairs, 2).transpose(1, 0, 2)
    row_pair = jnp.stack([log_cols.transpose(0, 2, 1), mean_cols.transpose(0, 2, 1)])
    grad_before = from_before(grad_heads)
    grad_after = from_after(grad_heads)
    rows_before = from_before(row_pair)
    rows_after = from_after(row_pair)
    dq, dk, dv = own_grads(mixed, before, after, grad_heads, log_cols, mean_cols, row_pair[0], row_pair[1], bias_own, bias_halo)
    dk, dv = halo_grads(mixed, before, after, grad_before, grad_after, rows_before, rows_after, bias_halo, dk, dv)
    qkv_keep, qkv_send, sums_qkv = qkv_grads(far, at, x, dq, dk, dv)
    inputs_grad = (grad_one + nt(cat([dq, dk, dv], 1), qkv_full)).astype(BF16)[None]

    small_parts = (sums_qkv[0], sums_qkv[1], sums_one[2], sums_one[0], sums_one[1], sums_two[2], sums_two[0], sums_two[1])
    small = cat([v.reshape(2 * blocks, each) for v in small_parts] + [up_bias_part.reshape(2 * blocks, -1)], 1)
    if far is None:
        total = lambda keep, send, axis: lax.psum_scatter(cat([keep, send], axis), ALL, scatter_dimension=0, tiled=True).astype(F32)
        down_sum = total(down_keep, down_send, 0)
        up_sum = total(up_keep, up_send, 1)
        out_sum = total(out_keep, out_send, 1)
        qkv_sum = total(qkv_keep, qkv_send, 1)
        small_sum = lax.psum_scatter(small, ALL, scatter_dimension=0, tiled=True)[0]
    else:
        by = lambda v: v.reshape(2, 2, far, -1, v.shape[-1])
        down_sum = scatter_down(by(down_keep), by(down_got))
        up_out = scatter_up(cat([by(up_keep), by(out_keep)], 4), cat([by(up_got), by(out_got)], 4))
        small = small.reshape(far, 2, 2, 2, lines, 128).transpose(3, 2, 1, 0, 4, 5)
        for axis, index in ((0, at[2]), (1, at[1]), (2, at[0])):
            small = jnp.where(index == 0, small, jnp.flip(small, axis))
        note = jnp.zeros((2, 2, 2, far, 2, rows, 128), BF16).at[:, :, :, :, 0, :lines].set(small.astype(BF16))
        note_got = swap(note[1], CORE)
        qkv_got = swap(qkv_send, CORE)
        colors = lambda v: v.reshape(2, 2, far, 2, rows, v.shape[-1])
        last = scatter_last(cat([colors(qkv_keep), note[0]], 5), cat([colors(qkv_got), note_got], 5))
        qkv_left, qkv_right = own_rows(core, last[:, :, :cut])
        qkv_sum = cat([qkv_left, qkv_right], 1).astype(F32)
        small_sum = last[0, :lines, cut:].reshape(-1).astype(F32)
        left, right = own_rows(core, up_out.reshape(2, rows, -1))
        cut_up = hidden // 2
        up_sum = cat([left[:, :cut_up], right[:, :cut_up]], 1).astype(F32)
        out_sum = cat([left[:, cut_up:], right[:, cut_up:]], 1).astype(F32)
    s = [small_sum[each * i : each * i + each] for i in range(8)]
    return (
        result[None], inputs_grad, qkv_sum, s[0], s[1], out_sum, s[2], s[3], s[4], up_sum, small_sum[8 * each :], down_sum, s[5], s[6], s[7],
    )


def solution(mesh):
    devices = mesh.devices
    split = jax.sharding.Mesh(devices.reshape(devices.shape[0] // 4, 2, 2, devices.shape[1]), ALL)
    rows, vec = P(ALL, None), P(ALL)
    tokens = P(CORE, CTX, None)
    return jax.shard_map(
        shards,
        mesh=split,
        in_specs=(tokens, P(CORE, None), tokens, rows, vec, vec, rows, vec, vec, vec, rows, vec, rows, vec, vec, vec),
        out_specs=(tokens, tokens, rows, vec, vec, rows, vec, vec, vec, rows, vec, rows, vec, vec, vec),
        check_vma=False,
    )
```

time: 1220 us -> 689 us (0.56)
  waiting for transfers between devices: 569 us -> 306 us
  matrix products: 269 us -> 7.01 us
  Pallas kernels: 0 us -> 199 us
  blocking collectives: 201 us -> 30.1 us
  local copies, waits for them, and re-layouts: 69.7 us -> 21 us
  starting transfers between devices: 14.6 us -> 51.9 us
  other arithmetic: 72.8 us -> 49.6 us
    reduce_scatter x3, waiting for transfers between devices: 376 us -> 16.3 us  [the longest x1 16.3 us: scatter_up(): return lax.psum_scatter(mine, FAR, scatter_dimension=0, tiled=False)]
    dot_general x40 -> x1, matrix products: 269 us -> 7.01 us  [nt(): lax.dot_general(a, b, (((1,), (1,)), ((), ())), preferred_element_type=F32)]
    pallas_call x0 -> x10, Pallas kernels: none -> 199 us  [the longest x1 32.9 us: forward(): pl.pallas_call(functools.partial(forward_kernel, far, len(up_parts), len(...]
    ppermute x4 -> x38, waiting for transfers between devices: 87.5 us -> 248 us  [the longest x32 181 us: swap(): return lax.ppermute(values, axis, [(0, 1), (1, 0)])]
    all_gather x1, blocking collectives: 119 us -> 30.1 us  [gather_first(): wide = lax.all_gather(block, FAR, axis=0)]
    unnamed x2 -> x0, blocking collectives: 81.7 us -> none
    unnamed x9 -> x5, waiting for transfers between devices: 69.3 us -> 0.08 us
    ppermute x4 -> x38, starting transfers between devices: 14.3 us -> 51.5 us  [the longest x32 30.3 us: swap(): return lax.ppermute(values, axis, [(0, 1), (1, 0)])]
  transfers between devices with their start and end apart: 12 -> 43, of which waited for: 7 -> 17; matrix products, arithmetic and copies ran while one was open for 28% -> 10% of each run, Pallas kernels for 0% -> 12%
where the time goes in v1:
time: 689 us; the launch traced here: 680 us
  waiting for transfers between devices  306 us (44%)
  Pallas kernels  199 us (29%)
  starting transfers between devices  51.9 us (8%)
  other arithmetic  49.6 us (7%)
  blocking collectives  30.1 us (4%)
  local copies, waits for them, and re-layouts  21 us (3%)
  between operations  14.9 us (2%)
  matrix products  7.01 us (1%)
    ppermute x32, waiting for transfers between devices, swap(): return lax.ppermute(values, axis, [(0, 1), (1, 0)])  181 us
    ppermute x3, waiting for transfers between devices, from_before(): return lax.ppermute(v, CTX, onward)  54.1 us
    all_gather x1, waiting for transfers between devices, gather_down(): wide = lax.all_gather(pair, FAR, axis=1)  41.6 us
    pallas_call x1, Pallas kernels, forward(): pl.pallas_call(functools.partial(forward_kernel, far, len(up_parts), len(...  32.9 us
    ppermute x32, starting transfers between devices, swap(): return lax.ppermute(values, axis, [(0, 1), (1, 0)])  30.3 us
    all_gather x1, blocking collectives, gather_first(): wide = lax.all_gather(block, FAR, axis=0)  30.1 us
    pallas_call x1, Pallas kernels, own_grads(): pl.pallas_call(own_grad_kernel, grid=(pairs,), in_specs=[column(0), colum...  28.9 us
    pallas_call x1, Pallas kernels, attend(): pl.pallas_call(attend_kernel, grid=(pairs,), in_specs=[column(0), column(...  23.7 us
  transfers between devices with their start and end apart: 43, of which 17 were waited for; matrix products, arithmetic and copies ran while one was open for 10% of the time, Pallas kernels for 12%

profile of v1, /device:TPU:25, one launch (start us, length us, event | category | flops | bytes accessed | tf_op | source)
XLA Modules:
  0.0 680.1 jit_solution(11663738082247999495)
XLA Ops:
  14.3 7.7 %collective-permute-done.5 = bf16[160,1024]{1,0:T(8,128)(2,1)S(1)} collective-permute-done((bf16[160,1024]{1,0:T(8,128)(2,1)S(1)}, bf16[160,1024]{1,0:T(8,128)(2,1)S(1)}, u32[]{:S(2)}, u32[]{:S(2)}) %collective-permute-start.5) | collective-permute-done | bytes 327712 | tf_op jit(solution)/shard_map/ppermute | solution.py:811
  23.2 30.1 %all-gather.1 = bf16[8,32,1664]{2,1,0:T(8,128)(2,1)S(1)} all-gather(bf16[2,32,1664]{2,1,0:T(8,128)(2,1)S(1)} %fusion.33), channel_id=3, replica_groups=mesh['far'=4,'y'=2,'x'=2,'fsdp'=2] {'far'}, dimensions={0}, use_global_device_ids=true | all-gather | bytes 1064960 | tf_op jit(solution)/shard_map/all_gather | solution.py:831
  55.4 9.2 %collective-permute-done.9 = bf16[4,32,1664]{2,1,0:T(8,128)(2,1)S(1)} collective-permute-done((bf16[4,32,1664]{2,1,0:T(8,128)(2,1)S(1)}, bf16[4,32,1664]{2,1,0:T(8,128)(2,1)S(1)}, u32[]{:S(2)}, u32[]{:S(2)}) %collective-permute-start.9) | collective-permute-done | bytes 426016 | tf_op jit(solution)/shard_map/ppermute | solution.py:811
  67.9 41.6 %all-gather.7.cloned.1.call-done = bf16[2,640,1024]{2,1,0:T(8,128)(2,1)} async-done(((bf16[2,160,1024]{2,1,0:T(8,128)(2,1)}), bf16[2,640,1024]{2,1,0:T(8,128)(2,1)}) %all-gather.7.cloned.1.call-update) | async-done | bytes 2621456 | tf_op jit(solution)/shard_map/all_gather | solution.py:848
  119.7 5.3 collective-permute-done.11
  130.0 4.0 collective-permute-start.18
  137.2 54.1 %collective-permute-done.17.refs_10_ = bf16[512,1024]{1,0:T(8,128)(2,1)} collective-permute-done((bf16[512,1024]{1,0:T(8,128)(2,1)}, bf16[512,1024]{1,0:T(8,128)(2,1)}, u32[]{:S(2)}, u32[]{:S(2)}) %collective-permute-start.17) | collective-permute-done | bytes 1048608 | tf_op jit(solution)/shard_map/ppermute | solution.py:899
  192.6 16.0 %collective-permute-done.12.refs_4_ = bf16[2,4,32,1664]{3,2,1,0:T(8,128)(2,1)} collective-permute-done((bf16[2,4,32,1664]{3,2,1,0:T(8,128)(2,1)}, bf16[2,4,32,1664]{3,2,1,0:T(8,128)(2,1)}, u32[]{:S(2)}, u32[]{:S(2)}) %collective-permute-start.12) | collective-permute-done | bytes 852000 | tf_op jit(solution)/shard_map/ppermute | solution.py:811
  210.6 4.3 collective-permute-done.18.refs_11_
  217.3 22.6 %project.1 = (bf16[512,3072]{1,0:T(8,128)(2,1)}, bf16[512,3072]{1,0:T(8,128)(2,1)}, bf16[512,3072]{1,0:T(8,128)(2,1)}, bf16[1024,3072]{1,0:T(8,128)(2,1)}) custom-call(s32[3]{0:T(128)} %pad_add_fusion.2.refs_0_.at_ref, bf16[2,4,32,1664]{3,2,1,0:T(8,128)(2,1)} %pad_maximum_fusion.4.refs_1_, bf16[2,4,32,1664]{3,2,1,0:T(8,128)(2,1)} %collective-permute-done.10.refs_2_, ...), custom_call_target="tpu_custom_call" | custom-call | flops 9663676416 | bytes 25165824 | tf_op jit(solution)/shard_map/project/pallas_call | solution.py:370
  239.9 23.7 %attend.1 = (bf16[512,1024]{1,0:T(8,128)(2,1)}, f32[8,512,2]{2,1,0:T(8,128)}) custom-call(bf16[512,3072]{1,0:T(8,128)(2,1)} %get-tuple-element.79.q_ref.ko_ref.vo_ref, bf16[512,3072]{1,0:T(8,128)(2,1)} %get-tuple-element.79.q_ref.ko_ref.vo_ref, bf16[512,3072]{1,0:T(8,128)(2,1)} %get-tuple-element.80.kp_ref.vp_ref.qp_ref, ...), custom_call_target="tpu_custom_call" | custom-call | flops 9663676416 | bytes 8388608 | tf_op jit(solution)/shard_map/attend/pallas_call | solution.py:103
  267.7 8.5 %out_project.1 = (f32[512,1024]{1,0:T(8,128)}, f32[512,1]{1,0:T(8,128)}, f32[512,1024]{1,0:T(8,128)}, bf16[512,1024]{1,0:T(8,128)(2,1)}, bf16[1024,1024]{1,0:T(8,128)(2,1)}) custom-call(s32[3]{0:T(128)} %pad_add_fusion.2.refs_0_.at_ref, bf16[2,4,160,1024]{3,2,1,0:T(8,128)(2,1)} %bitcast.184, ...), custom_call_target="tpu_custom_call" | custom-call | flops 1073741824 | bytes 8388608 | tf_op jit(solution)/shard_map/out_project/pallas_call | solution.py:440
  276.2 32.9 %feed_forward.1 = (bf16[512,4096]{1,0:T(8,128)(2,1)}, f32[512,4096]{1,0:T(8,128)}, bf16[512,1024]{1,0:T(8,128)(2,1)}, f32[512,1024]{1,0:T(8,128)}, bf16[512,1024...) custom-call(s32[3]{0:T(128)} %pad_add_fusion.2.refs_0_.at_ref, ...), custom_call_target="tpu_custom_call" | custom-call | flops 8589934592 | bytes 46137344 | tf_op jit(solution)/shard_map/feed_forward/pallas_call | solution.py:560
  309.1 18.9 %down_grads.1 = (bf16[512,4096]{1,0:T(8,128)(2,1)}, bf16[2048,1024]{1,0:T(8,128)(2,1)}, bf16[2048,1024]{1,0:T(8,128)(2,1)}, f32[1,4096]{1,0:T(1,128)}) custom-call(s32[3]{0:T(128)} %pad_add_fusion.2.refs_0_.at_ref, bf16[512,1024]{1,0:T(8,128)(2,1)} %get-tuple-element.86.glow_ref, bf16[4096,1024]{1,0:T(8,128)(2,1)} %get-tuple-element.87.down_ref, ...), custom_call_target="tpu_custom_call" | custom-call | flops 8589934592 | bytes 33554432 | tf_op jit(solution)/shard_map/down_grads/pallas_call | solution.py:648
  328.0 23.6 %up_grads.1 = (bf16[1024,2048]{1,0:T(8,128)(2,1)}, bf16[1024,2048]{1,0:T(8,128)(2,1)}, f32[512,1024]{1,0:T(8,128)}, bf16[512,1024]{1,0:T(8,128)(2,1)}, f32[3,1024]{1,0:T(4,128)}) custom-call(s32[3]{0:T(128)} %pad_add_fusion.2.refs_0_.at_ref, bf16[512,1024]{1,0:T(8,128)(2,1)} %get-tuple-element.83.refs_9_.low_ref, ...), custom_call_target="tpu_custom_call" | custom-call | flops 8589934592 | bytes 20971520 | tf_op jit(solution)/shard_map/up_grads/pallas_call | solution.py:720
  351.7 11.0 %out_grads.1 = (bf16[512,1024]{1,0:T(8,128)(2,1)}, f32[512,16]{1,0:T(8,128)}, bf16[1024,512]{1,0:T(8,128)(2,1)}, bf16[1024,512]{1,0:T(8,128)(2,1)}) custom-call(s32[3]{0:T(128)} %pad_add_fusion.2.refs_0_.at_ref, bf16[512,1024]{1,0:T(8,128)(2,1)} %get-tuple-element.96.branch_ref, bf16[1024,1024]{1,0:T(8,128)(2,1)} %get-tuple-element.97.w_ref, ...), custom_call_target="tpu_custom_call" | custom-call | flops 2147483648 | bytes 7340032 | tf_op jit(solution)/shard_map/out_grads/pallas_call | solution.py:768
  366.9 4.0 collective-permute-start.22
  372.8 5.2 collective-permute-start.20
  380.0 28.9 %own_grads.1 = (bf16[512,1024]{1,0:T(8,128)(2,1)}, f32[512,1024]{1,0:T(8,128)}, f32[512,1024]{1,0:T(8,128)}) custom-call(bf16[512,3072]{1,0:T(8,128)(2,1)} %get-tuple-element.79.q_ref.ko_ref.vo_ref, bf16[512,3072]{1,0:T(8,128)(2,1)} %get-tuple-element.79.q_ref.ko_ref.vo_ref, bf16[512,3072]{1,0:T(8,128)(2,1)} %get-tuple-element.80.kp_ref.vp_ref.qp_ref, ...), custom_call_target="tpu_custom_call" | custom-call | flops 24159191040 | bytes 15728640 | tf_op jit(solution)/shard_map/own_grads/pallas_call | solution.py:178
  409.0 9.0 %collective-permute-done.20.dn_ref = bf16[512,1024]{1,0:T(8,128)(2,1)S(1)} collective-permute-done((bf16[512,1024]{1,0:T(8,128)(2,1)}, bf16[512,1024]{1,0:T(8,128)(2,1)S(1)}, u32[]{:S(2)}, u32[]{:S(2)}) %collective-permute-start.20) | collective-permute-done | bytes 1048608 | tf_op jit(solution)/shard_map/ppermute | solution.py:902
  418.9 18.9 %halo_grads.1 = (bf16[512,1024]{1,0:T(8,128)(2,1)}, bf16[512,1024]{1,0:T(8,128)(2,1)}) custom-call(bf16[512,3072]{1,0:T(8,128)(2,1)} %get-tuple-element.79.q_ref.ko_ref.vo_ref, bf16[512,3072]{1,0:T(8,128)(2,1)} %get-tuple-element.79.q_ref.ko_ref.vo_ref, bf16[512,3072]{1,0:T(8,128)(2,1)} %get-tuple-element.80.kp_ref.vp_ref.qp_ref, ...), custom_call_target="tpu_custom_call" | custom-call | flops 10737418240 | bytes 10485760 | tf_op jit(solution)/shard_map/halo_grads/pallas_call | solution.py:237
  437.9 10.3 %qkv_grads.1 = (bf16[1024,1536]{1,0:T(8,128)(2,1)}, bf16[1024,1536]{1,0:T(8,128)(2,1)}, f32[2,1024]{1,0:T(2,128)}) custom-call(s32[3]{0:T(128)} %pad_add_fusion.2.refs_0_.at_ref, bf16[512,1024]{1,0:T(8,128)(2,1)} %bitcast.193, bf16[512,1024]{1,0:T(8,128)(2,1)} %get-tuple-element.101.dq_ref, bf16[512,1024]{1,0:T(8,128)(2,1)} %get-tuple-element.104.dk_ref, ...), custom_call_target="tpu_custom_call" | custom-call | flops 3221225472 | bytes 16777216 | tf_op jit(solution)/shard_map/qkv_grads/pallas_call | solution.py:794
  463.6 6.3 convert_add_fusion
  473.6 6.0 collective-permute-done.25
  482.7 52.7 %collective-permute-done.26 = bf16[4,32,1664]{2,1,0:T(8,128)(2,1)S(1)} collective-permute-done((bf16[4,32,1664]{2,1,0:T(8,128)(2,1)S(1)}, bf16[4,32,1664]{2,1,0:T(8,128)(2,1)S(1)}, u32[]{:S(2)}, u32[]{:S(2)}) %collective-permute-start.26) | collective-permute-done | bytes 426016 | tf_op jit(solution)/shard_map/ppermute | solution.py:811
  537.0 3.8 fusion.7
  542.0 3.8 fusion.13
  546.1 52.6 %collective-permute-done.32 = bf16[2,4,64,2560]{3,2,1,0:T(8,128)(2,1)} collective-permute-done((bf16[2,4,64,2560]{3,2,1,0:T(8,128)(2,1)}, bf16[2,4,64,2560]{3,2,1,0:T(8,128)(2,1)}, u32[]{:S(2)}, u32[]{:S(2)}) %collective-permute-start.32) | collective-permute-done | bytes 2621472 | tf_op jit(solution)/shard_map/ppermute | solution.py:811
  602.2 27.7 %collective-permute-done.33 = bf16[4,64,2560]{2,1,0:T(8,128)(2,1)S(1)} collective-permute-done((bf16[4,64,2560]{2,1,0:T(8,128)(2,1)S(1)}, bf16[4,64,2560]{2,1,0:T(8,128)(2,1)S(1)}, u32[]{:S(2)}, u32[]{:S(2)}) %collective-permute-start.33) | collective-permute-done | bytes 1310752 | tf_op jit(solution)/shard_map/ppermute | solution.py:811
  629.9 3.5 fusion.12
  633.4 7.0 %fusion.1 = f32[512,1024]{1,0:T(8,128)S(1)} fusion(bf16[1024,3072]{1,0:T(8,128)(2,1)} %get-tuple-element.106, bf16[512,1024]{1,0:T(8,128)(2,1)} %get-tuple-element.105.dv_ref, bf16[512,1024]{1,0:T(8,128)(2,1)} %get-tuple-element.104.dk_ref, bf16[512,1024]{1,0:T(8,128)(2,1)S(1)} %copy-done.30), kind=kOutput, calls=%fused_computation.9 | convolution fusion | flops 3230662656 | bytes 11534336 | tf_op jit(solution)/shard_map/dot_general | solution.py:28
  650.8 16.3 %reduce-scatter.6.cloned.1.call-done = bf16[1,64,2560]{2,1,0:T(8,128)(2,1)} async-done(((bf16[4,64,2560]{2,1,0:T(8,128)(2,1)}), bf16[1,64,2560]{2,1,0:T(8,128)(2,1)}) %reduce-scatter.6.cloned.1.call-update) | async-done | bytes 327696 | tf_op jit(solution)/shard_map/reduce_scatter | solution.py:856
  (246 shorter events, 95.8 us)
Async XLA Ops:
  7.2 59.4 %all-gather.5.cloned.1.call-start = ((), (), s32[]{:S(2)}) async-start(), calls=%async_computation.3 | async-start | bytes 1310720 | tf_op jit(solution)/shard_map/all_gather | solution.py:841
  12.9 96.6 %all-gather.7.cloned.1.call-start = ((), (), s32[]{:S(2)}) async-start(), calls=%async_computation.7 | async-start | bytes 3276800 | tf_op jit(solution)/shard_map/all_gather | solution.py:848
  23.0 618.8 %reduce-scatter.4.cloned.1.call-start = ((), (), s32[]{:S(2)}) async-start(), calls=%async_computation.4 | async-start | bytes 1064960 | tf_op jit(solution)/shard_map/reduce_scatter | solution.py:875
  65.6 46.8 %collective-permute-start.10 = (bf16[2,4,32,1664]{3,2,1,0:T(8,128)(2,1)}, bf16[2,4,32,1664]{3,2,1,0:T(8,128)(2,1)}, u32[]{:S(2)}, u32[]{:S(2)}) collective-permute-start(bf16[2,4,32,1664]{3,2,1,0:T(8,128)(2,1)} %pad_maximum_fusion.4.refs_1_), channel_id=1, source_target_pairs={{0,2},{2,0},{1,3},{3,1},{4,6},{6,4},{5,7},{7,5},{8,10},{10,8},{9,1... | collective-permute-start | bytes 2555912 | tf_op jit(solution)/shard_map/ppermute | solution.py:811
  66.6 49.4 %collective-permute-start.1 = (bf16[4,64,2048]{2,1,0:T(8,128)(2,1)}, bf16[4,64,2048]{2,1,0:T(8,128)(2,1)}, u32[]{:S(2)}, u32[]{:S(2)}) collective-permute-start(bf16[4,64,2048]{2,1,0:T(8,128)(2,1)} %all-gather.5.cloned.1.call-done), channel_id=1, source_target_pairs={{0,4},{4,0},{1,5},{5,1},{2,6},{6,2},{3,7},{7,3},{8,12},{12,8},{9,1... | collective-permute-start | bytes 3145736 | tf_op jit(solution)/shard_map/ppermute | solution.py:811
  109.5 106.6 %collective-permute-start.6 = (bf16[2,4,160,1024]{3,2,1,0:T(8,128)(2,1)}, bf16[2,4,160,1024]{3,2,1,0:T(8,128)(2,1)}, u32[]{:S(2)}, u32[]{:S(2)}) collective-permute-start(bf16[2,4,160,1024]{3,2,1,0:T(8,128)(2,1)} %bitcast.183), channel_id=1, source_target_pairs={{0,4},{4,0},{1,5},{5,1},{2,6},{6,2},{3,7},{7,3},{8,12},{12,8},{9,1... | collective-permute-start | bytes 7864328 | tf_op jit(solution)/shard_map/ppermute | solution.py:811
  112.5 21.6 %collective-permute-start.14 = (bf16[2,4,32,1664]{3,2,1,0:T(8,128)(2,1)}, bf16[2,4,32,1664]{3,2,1,0:T(8,128)(2,1)}, u32[]{:S(2)}, u32[]{:S(2)}) collective-permute-start(bf16[2,4,32,1664]{3,2,1,0:T(8,128)(2,1)} %collective-permute-done.10.refs_2_), channel_id=1, source_target_pairs={{0,1},{1,0},{2,3},{3,2},{4,5},{5,4},{6,7},{7,6},{8,9},{9,8},{10,11... | collective-permute-start | bytes 2555912 | tf_op jit(solution)/shard_map/ppermute | solution.py:811
  118.8 98.5 %collective-permute-start.2 = (bf16[2,4,64,2048]{3,2,1,0:T(8,128)(2,1)}, bf16[2,4,64,2048]{3,2,1,0:T(8,128)(2,1)}, u32[]{:S(2)}, u32[]{:S(2)}) collective-permute-start(bf16[2,4,64,2048]{3,2,1,0:T(8,128)(2,1)} %pad_maximum_fusion.refs_1_), channel_id=1, source_target_pairs={{0,2},{2,0},{1,3},{3,1},{4,6},{6,4},{5,7},{7,5},{8,10},{10,8},{9,1... | collective-permute-start | bytes 6291464 | tf_op jit(solution)/shard_map/ppermute | solution.py:811
  124.9 66.4 %collective-permute-start.17 = (bf16[512,1024]{1,0:T(8,128)(2,1)}, bf16[512,1024]{1,0:T(8,128)(2,1)}, u32[]{:S(2)}, u32[]{:S(2)}) collective-permute-start(bf16[512,1024]{1,0:T(8,128)(2,1)} %bitcast.189), channel_id=1, source_target_pairs={{0,2},{2,4},{4,6},{6,8},{8,10},{10,12},{12,14},{14,16},{16,18},{18... | collective-permute-start | bytes 3145736 | tf_op jit(solution)/shard_map/ppermute | solution.py:899
  130.0 84.8 %collective-permute-start.18 = (bf16[512,1024]{1,0:T(8,128)(2,1)}, bf16[512,1024]{1,0:T(8,128)(2,1)}, u32[]{:S(2)}, u32[]{:S(2)}) collective-permute-start(bf16[512,1024]{1,0:T(8,128)(2,1)} %bitcast.190), channel_id=1, source_target_pairs={{2,0},{4,2},{6,4},{8,6},{10,8},{12,10},{14,12},{16,14},{18,16},{20... | collective-permute-start | bytes 3145736 | tf_op jit(solution)/shard_map/ppermute | solution.py:902
  134.0 74.5 %collective-permute-start.12 = (bf16[2,4,32,1664]{3,2,1,0:T(8,128)(2,1)}, bf16[2,4,32,1664]{3,2,1,0:T(8,128)(2,1)}, u32[]{:S(2)}, u32[]{:S(2)}) collective-permute-start(bf16[2,4,32,1664]{3,2,1,0:T(8,128)(2,1)} %pad_maximum_fusion.5.refs_3_), channel_id=1, source_target_pairs={{0,4},{4,0},{1,5},{5,1},{2,6},{6,2},{3,7},{7,3},{8,12},{12,8},{9,1... | collective-permute-start | bytes 2555912 | tf_op jit(solution)/shard_map/ppermute | solution.py:811
  191.3 25.5 %collective-permute-start.15 = (bf16[2,4,32,1664]{3,2,1,0:T(8,128)(2,1)}, bf16[2,4,32,1664]{3,2,1,0:T(8,128)(2,1)}, u32[]{:S(2)}, u32[]{:S(2)}) collective-permute-start(bf16[2,4,32,1664]{3,2,1,0:T(8,128)(2,1)} %pad_maximum_fusion.5.refs_3_), channel_id=1, source_target_pairs={{0,1},{1,0},{2,3},{3,2},{4,5},{5,4},{6,7},{7,6},{8,9},{9,8},{10,11... | collective-permute-start | bytes 2555912 | tf_op jit(solution)/shard_map/ppermute | solution.py:811
  214.9 52.8 %collective-permute-start.7 = (bf16[2,4,160,1024]{3,2,1,0:T(8,128)(2,1)S(1)}, bf16[2,4,160,1024]{3,2,1,0:T(8,128)(2,1)}, u32[]{:S(2)}, u32[]{:S(2)}) collective-permute-start(bf16[2,4,160,1024]{3,2,1,0:T(8,128)(2,1)S(1)} %bitcast.186), channel_id=1, source_target_pairs={{0,1},{1,0},{2,3},{3,2},{4,5},{5,4},{6,7},{7,6},{8,9},{9,8},{10,11... | collective-permute-start | bytes 7864328 | tf_op jit(solution)/shard_map/ppermute | solution.py:811
  216.1 51.5 %collective-permute-start.8 = (bf16[2,4,160,1024]{3,2,1,0:T(8,128)(2,1)}, bf16[2,4,160,1024]{3,2,1,0:T(8,128)(2,1)}, u32[]{:S(2)}, u32[]{:S(2)}) collective-permute-start(bf16[2,4,160,1024]{3,2,1,0:T(8,128)(2,1)} %collective-permute-done.6.refs_2_.refs_6_), channel_id=1, source_target_pairs={{0,1},{1,0},{2,3},{3,2},{4,5},{5,4},{6,7},{7,6},{8,9},{9,8},{10,11... | collective-permute-start | bytes 7864328 | tf_op jit(solution)/shard_map/ppermute | solution.py:811
  216.8 59.3 %collective-permute-start.3 = (bf16[2,4,64,2048]{3,2,1,0:T(8,128)(2,1)}, bf16[2,4,64,2048]{3,2,1,0:T(8,128)(2,1)}, u32[]{:S(2)}, u32[]{:S(2)}) collective-permute-start(bf16[2,4,64,2048]{3,2,1,0:T(8,128)(2,1)} %pad_maximum_fusion.refs_1_), channel_id=1, source_target_pairs={{0,1},{1,0},{2,3},{3,2},{4,5},{5,4},{6,7},{7,6},{8,9},{9,8},{10,11... | collective-permute-start | bytes 6291464 | tf_op jit(solution)/shard_map/ppermute | solution.py:811
  217.3 58.9 %collective-permute-start.4 = (bf16[2,4,64,2048]{3,2,1,0:T(8,128)(2,1)}, bf16[2,4,64,2048]{3,2,1,0:T(8,128)(2,1)}, u32[]{:S(2)}, u32[]{:S(2)}) collective-permute-start(bf16[2,4,64,2048]{3,2,1,0:T(8,128)(2,1)} %collective-permute-done.2.refs_2_), channel_id=1, source_target_pairs={{0,1},{1,0},{2,3},{3,2},{4,5},{5,4},{6,7},{7,6},{8,9},{9,8},{10,11... | collective-permute-start | bytes 6291464 | tf_op jit(solution)/shard_map/ppermute | solution.py:811
  363.8 45.1 %collective-permute-start.21 = (f32[2,8,2,512]{3,2,1,0:T(2,128)S(1)}, f32[2,8,2,512]{3,2,1,0:T(2,128)S(1)}, u32[]{:S(2)}, u32[]{:S(2)}) collective-permute-start(f32[2,8,2,512]{3,2,1,0:T(2,128)S(1)} %pad_maximum_fusion.10), channel_id=1, source_target_pairs={{0,2},{2,4},{4,6},{6,8},{8,10},{10,12},{12,14},{14,16},{16,18},{18... | collective-permute-start | bytes 196616 | tf_op jit(solution)/shard_map/ppermute | solution.py:899
  366.9 42.1 %collective-permute-start.22 = (f32[2,8,2,512]{3,2,1,0:T(2,128)S(1)}, f32[2,8,2,512]{3,2,1,0:T(2,128)S(1)}, u32[]{:S(2)}, u32[]{:S(2)}) collective-permute-start(f32[2,8,2,512]{3,2,1,0:T(2,128)S(1)} %pad_maximum_fusion.10), channel_id=1, source_target_pairs={{2,0},{4,2},{6,4},{8,6},{10,8},{12,10},{14,12},{16,14},{18,16},{20... | collective-permute-start | bytes 196616 | tf_op jit(solution)/shard_map/ppermute | solution.py:902
  370.9 38.0 %collective-permute-start.19 = (bf16[512,1024]{1,0:T(8,128)(2,1)}, bf16[512,1024]{1,0:T(8,128)(2,1)S(1)}, u32[]{:S(2)}, u32[]{:S(2)}) collective-permute-start(bf16[512,1024]{1,0:T(8,128)(2,1)} %get-tuple-element.98.do_ref), channel_id=1, source_target_pairs={{0,2},{2,4},{4,6},{6,8},{8,10},{10,12},{12,14},{14,16},{16,18},{18... | collective-permute-start | bytes 3145736 | tf_op jit(solution)/shard_map/ppermute | solution.py:899
  372.8 45.1 %collective-permute-start.20 = (bf16[512,1024]{1,0:T(8,128)(2,1)}, bf16[512,1024]{1,0:T(8,128)(2,1)S(1)}, u32[]{:S(2)}, u32[]{:S(2)}) collective-permute-start(bf16[512,1024]{1,0:T(8,128)(2,1)} %get-tuple-element.98.do_ref), channel_id=1, source_target_pairs={{2,0},{4,2},{6,4},{8,6},{10,8},{12,10},{14,12},{16,14},{18,16},{20... | collective-permute-start | bytes 3145736 | tf_op jit(solution)/shard_map/ppermute | solution.py:902
  450.1 86.9 %collective-permute-start.31 = (bf16[1024,512]{1,0:T(8,128)(2,1)S(1)}, bf16[1024,512]{1,0:T(8,128)(2,1)S(1)}, u32[]{:S(2)}, u32[]{:S(2)}) collective-permute-start(bf16[1024,512]{1,0:T(8,128)(2,1)S(1)} %copy-done.25), channel_id=1, source_target_pairs={{0,1},{1,0},{2,3},{3,2},{4,5},{5,4},{6,7},{7,6},{8,9},{9,8},{10,11... | collective-permute-start | bytes 3145736 | tf_op jit(solution)/shard_map/ppermute | solution.py:811
  450.6 86.4 %collective-permute-start.30 = (bf16[1024,2048]{1,0:T(8,128)(2,1)}, bf16[1024,2048]{1,0:T(8,128)(2,1)}, u32[]{:S(2)}, u32[]{:S(2)}) collective-permute-start(bf16[1024,2048]{1,0:T(8,128)(2,1)} %get-tuple-element.115), channel_id=1, source_target_pairs={{0,1},{1,0},{2,3},{3,2},{4,5},{5,4},{6,7},{7,6},{8,9},{9,8},{10,11... | collective-permute-start | bytes 12582920 | tf_op jit(solution)/shard_map/ppermute | solution.py:811
  459.4 20.2 %collective-permute-start.25 = (bf16[2,4,32,1664]{3,2,1,0:T(8,128)(2,1)S(1)}, bf16[2,4,32,1664]{3,2,1,0:T(8,128)(2,1)S(1)}, u32[]{:S(2)}, u32[]{:S(2)}) collective-permute-start(bf16[2,4,32,1664]{3,2,1,0:T(8,128)(2,1)S(1)} %fusion.17), channel_id=1, source_target_pairs={{0,2},{2,0},{1,3},{3,1},{4,6},{6,4},{5,7},{7,5},{8,10},{10,8},{9,1... | collective-permute-start | bytes 2555912 | tf_op jit(solution)/shard_map/ppermute | solution.py:811
  460.1 22.0 %collective-permute-start.27 = (bf16[2,4,32,1664]{3,2,1,0:T(8,128)(2,1)S(1)}, bf16[2,4,32,1664]{3,2,1,0:T(8,128)(2,1)S(1)}, u32[]{:S(2)}, u32[]{:S(2)}) collective-permute-start(bf16[2,4,32,1664]{3,2,1,0:T(8,128)(2,1)S(1)} %fusion.18), channel_id=1, source_target_pairs={{0,4},{4,0},{1,5},{5,1},{2,6},{6,2},{3,7},{7,3},{8,12},{12,8},{9,1... | collective-permute-start | bytes 2555912 | tf_op jit(solution)/shard_map/ppermute | solution.py:811
  471.4 70.5 %collective-permute-start.36 = (bf16[2,4,128,1024]{3,2,0,1:T(8,128)(2,1)}, bf16[2,4,128,1024]{3,2,0,1:T(8,128)(2,1)}, u32[]{:S(2)}, u32[]{:S(2)}) collective-permute-start(bf16[2,4,128,1024]{3,2,0,1:T(8,128)(2,1)} %copy.74), channel_id=1, source_target_pairs={{0,4},{4,0},{1,5},{5,1},{2,6},{6,2},{3,7},{7,3},{8,12},{12,8},{9,1... | collective-permute-start | bytes 6291464 | tf_op jit(solution)/shard_map/ppermute | solution.py:811
  479.8 55.6 %collective-permute-start.26 = (bf16[4,32,1664]{2,1,0:T(8,128)(2,1)S(1)}, bf16[4,32,1664]{2,1,0:T(8,128)(2,1)S(1)}, u32[]{:S(2)}, u32[]{:S(2)}) collective-permute-start(bf16[4,32,1664]{2,1,0:T(8,128)(2,1)S(1)} %fusion.22), channel_id=1, source_target_pairs={{0,4},{4,0},{1,5},{5,1},{2,6},{6,2},{3,7},{7,3},{8,12},{12,8},{9,1... | collective-permute-start | bytes 1277960 | tf_op jit(solution)/shard_map/ppermute | solution.py:811
  482.3 53.4 %collective-permute-start.28 = (bf16[4,32,1664]{2,1,0:T(8,128)(2,1)S(1)}, bf16[4,32,1664]{2,1,0:T(8,128)(2,1)S(1)}, u32[]{:S(2)}, u32[]{:S(2)}) collective-permute-start(bf16[4,32,1664]{2,1,0:T(8,128)(2,1)S(1)} %fusion.19), channel_id=1, source_target_pairs={{0,2},{2,0},{1,3},{3,1},{4,6},{6,4},{5,7},{7,5},{8,10},{10,8},{9,1... | collective-permute-start | bytes 1277960 | tf_op jit(solution)/shard_map/ppermute | solution.py:811
  536.9 112.1 %reduce-scatter.8.cloned.1.call-start = ((), (), s32[]{:S(2)}) async-start(), calls=%async_computation.6 | async-start | bytes 2621440 | tf_op jit(solution)/shard_map/reduce_scatter | solution.py:862
  540.8 57.8 %collective-permute-start.32 = (bf16[2,4,64,2560]{3,2,1,0:T(8,128)(2,1)}, bf16[2,4,64,2560]{3,2,1,0:T(8,128)(2,1)}, u32[]{:S(2)}, u32[]{:S(2)}) collective-permute-start(bf16[2,4,64,2560]{3,2,1,0:T(8,128)(2,1)} %fusion.7), channel_id=1, source_target_pairs={{0,2},{2,0},{1,3},{3,1},{4,6},{6,4},{5,7},{7,5},{8,10},{10,8},{9,1... | collective-permute-start | bytes 7864328 | tf_op jit(solution)/shard_map/ppermute | solution.py:811
  545.8 121.3 %reduce-scatter.6.cloned.1.call-start = ((), (), s32[]{:S(2)}) async-start(), calls=%async_computation.5 | async-start | bytes 1638400 | tf_op jit(solution)/shard_map/reduce_scatter | solution.py:856
  601.3 28.5 %collective-permute-start.33 = (bf16[4,64,2560]{2,1,0:T(8,128)(2,1)S(1)}, bf16[4,64,2560]{2,1,0:T(8,128)(2,1)S(1)}, u32[]{:S(2)}, u32[]{:S(2)}) collective-permute-start(bf16[4,64,2560]{2,1,0:T(8,128)(2,1)S(1)} %fusion.10), channel_id=1, source_target_pairs={{0,4},{4,0},{1,5},{5,1},{2,6},{6,2},{3,7},{7,3},{8,12},{12,8},{9,1... | collective-permute-start | bytes 3932168 | tf_op jit(solution)/shard_map/ppermute | solution.py:811
  650.0 19.0 %collective-permute-start.37 = (bf16[128,1024]{1,0:T(8,128)(2,1)S(1)}, bf16[128,1024]{1,0:T(8,128)(2,1)S(1)}, u32[]{:S(2)}, u32[]{:S(2)}) collective-permute-start(bf16[128,1024]{1,0:T(8,128)(2,1)S(1)} %slice_bitcast_fusion.18), channel_id=1, source_target_pairs={{0,2},{2,0},{1,3},{3,1},{4,6},{6,4},{5,7},{7,5},{8,10},{10,8},{9,1... | collective-permute-start | bytes 786440 | tf_op jit(solution)/shard_map/ppermute | solution.py:811
  (42 other events, 728.0 us)
Sparse Core Ops, SparseCore 0:
  13.0 39.7 all-gather.4
  54.9 54.5 all-gather.6
  537.0 26.1 reduce-scatter.3
  565.4 43.4 reduce-scatter.7
  633.5 33.5 reduce-scatter.5

commit v2 on v1

v2 whole, which is shorter than its diff:
```python
import functools

import jax
import jax.numpy as jnp
from jax import lax
from jax.experimental import pallas as pl
from jax.experimental.pallas import tpu as pltpu
from jax.sharding import PartitionSpec as P

H = 16
HD = 64
WINDOW = 1024
HALF = WINDOW // 2
ROWS = 128
PAIR = 2 * HD
FILL = -1e30
EPS = 1e-05
HIDDEN_BLOCK = 128
F32 = jnp.float32
BF16 = jnp.bfloat16
VMEM_BYTES = 56 * 1024 * 1024
SMEM = pl.BlockSpec(memory_space=pltpu.SMEM)
ANY = pl.BlockSpec(memory_space=pl.ANY)
VMEM = pl.BlockSpec(memory_space=pltpu.VMEM)


def nn(a, b):
    return lax.dot_general(a, b, (((1,), (0,)), ((), ())), preferred_element_type=F32)


def nt(a, b):
    return lax.dot_general(a, b, (((1,), (1,)), ((), ())), preferred_element_type=F32)


def tn(a, b):
    return lax.dot_general(a, b, (((0,), (0,)), ((), ())), preferred_element_type=F32)


def cat(parts, axis):
    return jnp.concatenate(parts, axis=axis)


def cost():
    return pl.CostEstimate(flops=1, bytes_accessed=1, transcendentals=0)


def params():
    return pltpu.CompilerParams(vmem_limit_bytes=VMEM_BYTES)


def head_masks(scale):
    lane = lax.broadcasted_iota(jnp.int32, (1, PAIR), 1)
    first = jnp.where(lane < HD, scale, 0.0).astype(F32)
    second = jnp.where(lane < HD, 0.0, scale).astype(F32)
    return first.astype(BF16), second.astype(BF16)


def stacked(values, masks):
    return cat([values * masks[0], values * masks[1]], 0)


def strip(i, tokens):
    return slice(ROWS * i, ROWS * i + tokens + ROWS)


def put_rows(ref, cols, pair):
    head = lax.broadcasted_iota(jnp.int32, (H, 1), 0) - 2 * pl.program_id(0)
    ref[:, cols] = jnp.where(head == 0, pair[0], jnp.where(head == 1, pair[1], ref[:, cols]))


def far_first(p, pairs):
    return lax.rem(p + pairs // 2, pairs)


def take_row(values, h, pair=None):
    head = lax.broadcasted_iota(jnp.int32, (H, 1), 0) - 2 * (pl.program_id(0) if pair is None else pair)
    return jnp.sum(jnp.where(head == h, values, 0.0), axis=0, keepdims=True)


def attend_kernel(q_ref, ko_ref, kp_ref, kn_ref, vo_ref, vp_ref, vn_ref, bo_ref, bh_ref, out_ref, lse_ref, kh, vh):
    tokens = q_ref.shape[0]
    kh[:tokens] = kp_ref[...]
    kh[tokens:] = kn_ref[...]
    ones = head_masks(1.0)
    vh[:tokens] = vp_ref[...]
    vh[tokens:] = vn_ref[...]
    vo = stacked(vo_ref[...], ones)
    scaled = head_masks(HD ** -0.5)
    lane = lax.broadcasted_iota(jnp.int32, (ROWS, PAIR), 1)
    for i in range(tokens // ROWS):
        rows = slice(ROWS * i, ROWS * i + ROWS)
        window = strip(i, tokens)
        q = q_ref[rows]
        own_parts, halo_parts, totals, logs = [], [], [], []
        for mask in scaled:
            qm = q * mask
            so = nt(qm, ko_ref[...]) + bo_ref[rows]
            sh = nt(qm, kh[window]) + bh_ref[i]
            peak = jnp.maximum(jnp.max(so, axis=1, keepdims=True), jnp.max(sh, axis=1, keepdims=True))
            po = jnp.exp(so - peak)
            ph = jnp.exp(sh - peak)
            total = jnp.sum(po, axis=1, keepdims=True) + jnp.sum(ph, axis=1, keepdims=True)
            own_parts.append(po.astype(BF16))
            halo_parts.append(ph.astype(BF16))
            totals.append(1.0 / total)
            logs.append((peak + jnp.log(total)).T)
        out = nn(cat(own_parts, 1), vo) + nn(cat(halo_parts, 1), stacked(vh[window], ones))
        out = out * jnp.where(lane < HD, totals[0], totals[1])
        out_ref[rows] = out.astype(BF16)
        put_rows(lse_ref, rows, logs)


def attend(mixed, before, after, bias_own, bias_halo):
    tokens, width = mixed.shape[0], mixed.shape[1] // 3
    pairs = width // PAIR

    near = pairs // 2

    def column(part):
        return pl.BlockSpec((tokens, PAIR), lambda p: (0, (p // near * 3 + part) * near + p % near))

    whole = lambda shape: pl.BlockSpec(shape, lambda p: (0,) * len(shape))
    return pl.pallas_call(
        attend_kernel,
        grid=(pairs,),
        in_specs=[column(0), column(1), column(1), column(1), column(2), column(2), column(2), whole(bias_own.shape), whole(bias_halo.shape)],
        out_specs=[pl.BlockSpec((tokens, PAIR), lambda p: (0, p)), whole((H, tokens))],
        out_shape=[jax.ShapeDtypeStruct((tokens, width), BF16), jax.ShapeDtypeStruct((H, tokens), F32)],
        scratch_shapes=[pltpu.VMEM((2 * tokens, PAIR), BF16), pltpu.VMEM((2 * tokens, PAIR), BF16)],
        compiler_params=params(),
        cost_estimate=cost(),
        name="attend",
    )(mixed, mixed, before, after, mixed, before, after, bias_own, bias_halo)


def own_grad_kernel(q_ref, ko_ref, kp_ref, kn_ref, vo_ref, vp_ref, vn_ref, do_ref, log_ref, mean_ref, bo_ref, bh_ref, dq_ref, dkv_ref, sum_ref, kh, vh):
    tokens = q_ref.shape[0]
    kh[:tokens] = kp_ref[...]
    kh[tokens:] = kn_ref[...]
    vh[:tokens] = vp_ref[...]
    vh[tokens:] = vn_ref[...]
    ones = head_masks(1.0)
    scaled = head_masks(HD ** -0.5)
    k_own = ko_ref[...]
    v_own = vo_ref[...]
    k_pair = stacked(k_own, scaled)
    log_rows = [take_row(log_ref[...], h) for h in range(2)]
    mean_rows = [take_row(mean_ref[...], h) for h in range(2)]
    chunk = 2 * ROWS
    for c in range(tokens // chunk):
        cols = slice(chunk * c, chunk * c + chunk)
        q = q_ref[cols]
        do = do_ref[cols]
        probs, grads, qs, dos = [], [], [], []
        for h in range(2):
            qm = q * scaled[h]
            dm = do * ones[h]
            st = nt(k_own, qm) + bo_ref[:, cols]
            pt = jnp.exp(st - log_rows[h][:, cols])
            gt = pt * (nt(v_own, dm) - mean_rows[h][:, cols])
            probs.append(pt.astype(BF16))
            grads.append(gt.astype(BF16))
            qs.append(qm)
            dos.append(dm)
        dv = nn(cat(probs, 1), cat(dos, 0))
        dk = nn(cat(grads, 1), cat(qs, 0))
        if c == 0:
            dkv_ref[0, 0] = dk
            dkv_ref[0, 1] = dv
        else:
            dkv_ref[0, 0] += dk
            dkv_ref[0, 1] += dv
        dq_own = tn(cat(grads, 0), k_pair)
        for r in range(chunk // ROWS):
            i = c * (chunk // ROWS) + r
            rows = slice(ROWS * i, ROWS * i + ROWS)
            window = strip(i, tokens)
            halo = []
            for h in range(2):
                qm = q[ROWS * r : ROWS * r + ROWS] * scaled[h]
                dm = do[ROWS * r : ROWS * r + ROWS] * ones[h]
                s = nt(qm, kh[window]) + bh_ref[i]
                p = jnp.exp(s - log_rows[h][:, rows].T)
                halo.append((p * (nt(dm, vh[window]) - mean_rows[h][:, rows].T)).astype(BF16))
            dq = dq_own[ROWS * r : ROWS * r + ROWS] + nn(cat(halo, 1), stacked(kh[window], scaled))
            dq = dq.astype(BF16)
            dq_ref[0, rows] = dq
            sum_ref[...] = column_sum(dq.astype(F32)) + (sum_ref[...] if i else 0.0)


def own_grads(mixed, before, after, payload, logs, means, bias_own, bias_halo):
    tokens, width = mixed.shape[0], payload.shape[1]
    pairs = width // PAIR

    near = pairs // 2

    def column(part):
        return pl.BlockSpec((tokens, PAIR), lambda p: (0, (p // near * 3 + part) * near + p % near))

    whole = lambda shape: pl.BlockSpec(shape, lambda p: (0,) * len(shape))
    block = pl.BlockSpec((tokens, PAIR), lambda p: (0, p))
    return pl.pallas_call(
        own_grad_kernel,
        grid=(pairs,),
        in_specs=[column(0), column(1), column(1), column(1), column(2), column(2), column(2), block, whole(logs.shape), whole(means.shape), whole(bias_own.shape), whole(bias_halo.shape)],
        out_specs=[
            pl.BlockSpec((1, tokens, PAIR), lambda p: (p // near, 0, p % near)),
            pl.BlockSpec((1, 2, tokens, PAIR), lambda p: (p // near, 0, 0, p % near)),
            pl.BlockSpec((1, PAIR), lambda p: (0, p)),
        ],
        out_shape=[
            jax.ShapeDtypeStruct((2, tokens, width // 2), BF16),
            jax.ShapeDtypeStruct((2, 2, tokens, width // 2), F32),
            jax.ShapeDtypeStruct((1, width), F32),
        ],
        scratch_shapes=[pltpu.VMEM((2 * tokens, PAIR), BF16), pltpu.VMEM((2 * tokens, PAIR), BF16)],
        compiler_params=params(),
        cost_estimate=cost(),
        name="own_grads",
    )(mixed, mixed, before, after, mixed, before, after, payload, logs, means, bias_own, bias_halo)


def halo_grad_kernel(ko_ref, vo_ref, qp_ref, qn_ref, dp_ref, dn_ref, lp0, lp1, lp2, ln0, ln1, ln2, bh_ref, dq_in, dkv_in, keep_ref, send_ref, sum_ref, qh, dh, lh, made):
    tokens = ko_ref.shape[0]
    qh[:tokens] = qp_ref[...]
    qh[tokens:] = qn_ref[...]
    dh[:tokens] = dp_ref[...]
    dh[tokens:] = dn_ref[...]
    for first, refs in ((0, (lp0, lp1, lp2)), (tokens, (ln0, ln1, ln2))):
        table = refs[0][...].astype(F32) + refs[1][...].astype(F32) + refs[2][...].astype(F32)
        for h in range(2):
            row = take_row(table, h, far_first(pl.program_id(0), pl.num_programs(0)))
            lh[0, h : h + 1, first : first + tokens] = row[:, :tokens]
            lh[1, h : h + 1, first : first + tokens] = row[:, tokens:]
    ones = head_masks(1.0)
    scaled = head_masks(HD ** -0.5)
    for j in range(tokens // ROWS):
        rows = slice(ROWS * j, ROWS * j + ROWS)
        window = strip(j, tokens)
        q = qh[window]
        do = dh[window]
        k = ko_ref[rows]
        v = vo_ref[rows]
        probs, grads, qs, dos = [], [], [], []
        for h in range(2):
            qm = q * scaled[h]
            dm = do * ones[h]
            st = nt(k, qm) + bh_ref[j]
            pt = jnp.exp(st - lh[0, h : h + 1, window])
            gt = pt * (nt(v, dm) - lh[1, h : h + 1, window])
            probs.append(pt.astype(BF16))
            grads.append(gt.astype(BF16))
            qs.append(qm)
            dos.append(dm)
        made[1, rows] = (dkv_in[0, 0, rows] + nn(cat(grads, 1), cat(qs, 0))).astype(BF16)
        dv = (dkv_in[0, 1, rows] + nn(cat(probs, 1), cat(dos, 0))).astype(BF16)
        made[2, rows] = dv
        sum_ref[...] = column_sum(dv.astype(F32)) + (sum_ref[...] if j else 0.0)
    made[0] = dq_in[0]
    put_half(pl.program_id(0), pl.num_programs(0), send_ref, keep_ref, made[...])


def halo_grads(mixed, before, after, grad_before, grad_after, bias_halo, dq, dkv):
    tokens, width = dkv.shape[2], 2 * dkv.shape[3]
    pairs = width // PAIR
    near = pairs // 2

    def column(part):
        return pl.BlockSpec((tokens, PAIR), lambda p: (0, (far_first(p, pairs) // near * 3 + part) * near + p % near))

    whole = lambda shape: pl.BlockSpec(shape, lambda p: (0,) * len(shape))
    both = pl.BlockSpec((1, 2, tokens, PAIR), lambda p: (far_first(p, pairs) // near, 0, 0, p % near))
    one = pl.BlockSpec((1, tokens, PAIR), lambda p: (far_first(p, pairs) // near, 0, p % near))
    tables = [pl.BlockSpec((H, width), lambda p, k=k: (tokens // H + k, 0)) for k in range(3)]
    block = pl.BlockSpec((tokens, PAIR), lambda p: (0, far_first(p, pairs)))
    half = jax.ShapeDtypeStruct((3, tokens, width // 2), BF16)
    return pl.pallas_call(
        halo_grad_kernel,
        grid=(pairs,),
        in_specs=[column(1), column(2), column(0), column(0), block, block] + tables + tables + [whole(bias_halo.shape), one, both],
        out_specs=[
            pl.BlockSpec((3, tokens, PAIR), lambda p: (0, 0, jnp.maximum(p - near, 0))),
            pl.BlockSpec((3, tokens, PAIR), lambda p: (0, 0, jnp.minimum(p, near - 1))),
            pl.BlockSpec((1, PAIR), lambda p: (0, far_first(p, pairs))),
        ],
        out_shape=[half, half, jax.ShapeDtypeStruct((1, width), F32)],
        scratch_shapes=[
            pltpu.VMEM((2 * tokens, PAIR), BF16),
            pltpu.VMEM((2 * tokens, PAIR), BF16),
            pltpu.VMEM((2, 2, 2 * tokens), F32),
            pltpu.VMEM((3, tokens, PAIR), BF16),
        ],
        compiler_params=params(),
        cost_estimate=cost(),
        name="halo_grads",
    )(mixed, mixed, before, after, grad_before, grad_after, *[grad_before] * 3, *[grad_after] * 3, bias_halo, dq, dkv)


def mask_biases(segments, place, blocks, tokens):
    line = cat([jnp.full((tokens,), -1, jnp.int32), segments, jnp.full((tokens,), -1, jnp.int32)], 0)
    near = lax.dynamic_slice_in_dim(line, place * tokens, 3 * tokens)
    own = near[tokens : 2 * tokens]
    bias_own = jnp.where(own[:, None] == own[None, :], 0.0, FILL).astype(F32)
    halo = cat([near[:tokens], near[2 * tokens :]], 0)
    at = jnp.arange(tokens, dtype=jnp.int32)
    halo_at = cat([at - tokens, at + tokens], 0)
    allowed = (own[:, None] == halo[None, :]) & (jnp.abs(halo_at[None, :] - at[:, None]) < HALF)
    bias = jnp.where(allowed, 0.0, FILL).astype(F32)
    bias_halo = jnp.stack([bias[ROWS * i : ROWS * i + ROWS, strip(i, tokens)] for i in range(tokens // ROWS)])
    return bias_own, bias_halo


def normalized(values):
    average = jnp.mean(values, axis=1, keepdims=True)
    centered = values - average
    spread = jnp.mean(centered * centered, axis=1, keepdims=True)
    inverse = lax.rsqrt(spread + EPS)
    return centered * inverse, inverse


def norm_back(grad, gain, hat, inverse):
    scaled = grad * gain
    return inverse * (
        scaled
        - jnp.mean(scaled, axis=1, keepdims=True)
        - hat * jnp.mean(scaled * hat, axis=1, keepdims=True)
    )


def column_sum(values):
    return jnp.sum(values, axis=0, keepdims=True)


def part_blocks(at_ref, order, second, far):
    for first in range(2):
        rel = {order[-2]: first, order[-1]: second}
        y = jnp.bitwise_xor(at_ref[0], rel["y"])
        x = jnp.bitwise_xor(at_ref[1], rel["x"])
        for i in range(far):
            z = jnp.bitwise_xor(at_ref[3], (i % 2) * 2 + i // 2) if order[0] == "z" else i
            yield first, i, (z * 2 + y) * 2 + x


def start_all(copies):
    for copy in copies:
        copy.start()


def wait_all(copies):
    for copy in copies:
        copy.wait()


def block_place(at_ref, order, z, y, x, far):
    where = {"z": (z, far), "y": (jnp.bitwise_xor(at_ref[0], y), 2), "x": (jnp.bitwise_xor(at_ref[1], x), 2)}
    to = 0
    for axis in order:
        to = to * where[axis][1] + where[axis][0]
    return to


def prepare_kernel(at_ref, qkv_ref, out_ref, up_ref, *refs):
    vectors, mine_ref, send_ref, note_ref = refs[:-3], *refs[-3:]
    width = out_ref.shape[1]
    place = 0
    for ref, piece in ((qkv_ref, width // 2), (out_ref, width // 2), (up_ref, HIDDEN_BLOCK)):
        for i in range(0, ref.shape[1], 2 * piece):
            mine_ref[:, place : place + piece] = ref[:, pl.ds(pl.multiple_of(i + at_ref[2] * piece, piece), piece)]
            send_ref[:, place : place + piece] = ref[:, pl.ds(pl.multiple_of(i + (1 - at_ref[2]) * piece, piece), piece)]
            place += piece
    line = cat([v[...].astype(F32) for v in vectors], 1).astype(BF16)
    note_ref[...] = jnp.zeros_like(note_ref)
    for i in range(line.shape[1] // 128):
        note_ref[i : i + 1] = line[:, i * 128 : i * 128 + 128]


def prepare(at, qkv, out, up, vectors):
    rows = qkv.shape[0]
    columns = (qkv.shape[1] + out.shape[1] + up.shape[1]) // 2
    half = jax.ShapeDtypeStruct((rows, columns), BF16)
    return pl.pallas_call(
        prepare_kernel,
        in_specs=[SMEM] + [VMEM] * (3 + len(vectors)),
        out_shape=[half, half, jax.ShapeDtypeStruct((rows, 128), BF16)],
        compiler_params=params(),
        cost_estimate=cost(),
        name="prepare",
    )(at, qkv, out, up, *[v[None] for v in vectors])


def arrange_kernel(at_ref, mine_ref, got_ref, note_ref, block_ref, up_ref):
    rows, cut = mine_ref.shape[0], block_ref.shape[2] - 128
    block_ref[0, :, cut:] = note_ref[...]
    block_ref[1, :, cut:] = jnp.zeros_like(note_ref)

    def lay(first, second):
        for i, ref in ((0, first), (1, second)):
            block_ref[i, :, :cut] = ref[:, :cut]
            up_ref[i * rows : i * rows + rows] = ref[:, cut:]

    @pl.when(at_ref[2] == 0)
    def _():
        lay(mine_ref, got_ref)

    @pl.when(at_ref[2] != 0)
    def _():
        lay(got_ref, mine_ref)


def arrange(at, mine, got, note, hidden):
    rows, columns = mine.shape
    return pl.pallas_call(
        arrange_kernel,
        in_specs=[SMEM] + [VMEM] * 3,
        out_shape=[
            jax.ShapeDtypeStruct((2, rows, columns - hidden // 2 + 128), BF16),
            jax.ShapeDtypeStruct((2 * rows, hidden // 2), BF16),
        ],
        compiler_params=params(),
        cost_estimate=cost(),
        name="arrange",
    )(at, mine, got, note)


def first_copies(refs, qkv, out, sems, at_ref, far):
    width, columns = qkv.shape
    half, near = width // 2, columns // 2
    copies = []

    def add(source, target):
        copies.append(pltpu.make_async_copy(source, target, sems.at[len(copies)]))

    def column(core):
        return pl.ds(pl.multiple_of(jnp.bitwise_xor(at_ref[2], core) * half, half), half)

    for core in range(2):
        if far is None:
            add(refs[core], qkv.at[:, pl.ds(core * near, near)])
            for part in range(2):
                row = pl.ds(pl.multiple_of(jnp.bitwise_xor(at_ref[2], part) * half, half), half)
                add(refs[2 + core].at[pl.ds(part * half, half)], out.at[row, column(core)])
            continue
        rows = width // (8 * far)
        for color, order in enumerate(("zyx", "zxy")):
            for second in range(2):
                ref = refs[core * 4 + color * 2 + second]
                for first, z, block in part_blocks(at_ref, order, second, far):
                    row = (block * 2 + color) * rows
                    add(ref.at[first, z, :, pl.ds(0, near)], qkv.at[pl.ds(pl.multiple_of(row, rows), rows), pl.ds(core * near, near)])
                    row = jnp.bitwise_xor(row, at_ref[2] * half)
                    add(ref.at[first, z, :, pl.ds(near, half)], out.at[pl.ds(pl.multiple_of(row, rows), rows), column(core)])
    return copies


def project_kernel(far, parts, *refs):
    at_ref, refs = refs[0], refs[1:]
    part_refs, refs = refs[:parts], refs[parts:]
    own_ref, before_ref, row_ref, own_out, before_out, qkv_out, out_out, qkv, out, sems, out_sems = refs
    copies = first_copies(part_refs, qkv, out, sems, at_ref, far)
    start_all(copies)
    wait_all(copies)
    keep = [pltpu.make_async_copy(qkv, qkv_out, out_sems.at[0]), pltpu.make_async_copy(out, out_out, out_sems.at[1])]
    start_all(keep)
    chunk = 512
    for source, target in ((own_ref, own_out), (before_ref, before_out)):

        def body(j, carry, source=source, target=target):
            cols = pl.ds(pl.multiple_of(j * chunk, chunk), chunk)
            target[:, cols] = (nn(source[...], qkv[:, cols]) + row_ref[:, cols]).astype(BF16)
            return carry

        lax.fori_loop(0, qkv.shape[1] // chunk, body, 0)
    wait_all(keep)


def copy_count(far, each):
    return 2 if far is None else 8 * far * each


def project(far, at, parts, x, before, row):
    tokens, width = x.shape
    columns = row.shape[1]
    mixed = jax.ShapeDtypeStruct((tokens, columns), BF16)
    return pl.pallas_call(
        functools.partial(project_kernel, far, len(parts)),
        in_specs=[SMEM] + [ANY] * len(parts) + [VMEM] * 3,
        out_specs=[VMEM, VMEM, ANY, ANY],
        out_shape=[mixed, mixed, jax.ShapeDtypeStruct((width, columns), BF16), jax.ShapeDtypeStruct((width, width), BF16)],
        scratch_shapes=[
            pltpu.VMEM((width, columns), BF16),
            pltpu.VMEM((width, width), BF16),
            pltpu.SemaphoreType.DMA((6 if far is None else 64 * far,)),
            pltpu.SemaphoreType.DMA((2,)),
        ],
        compiler_params=params(),
        cost_estimate=cost(),
        name="project",
    )(at, *parts, x, before, row)


def project_more_kernel(x_ref, w_ref, row_ref, out_ref):
    out_ref[...] = (nn(x_ref[...], w_ref[...]) + row_ref[...]).astype(BF16)


def project_more(x, full, row, chunk=512):
    tokens, width = x.shape
    columns = full.shape[1]
    return pl.pallas_call(
        project_more_kernel,
        grid=(columns // chunk,),
        in_specs=[
            pl.BlockSpec((tokens, width), lambda i: (0, 0)),
            pl.BlockSpec((width, chunk), lambda i: (0, i)),
            pl.BlockSpec((1, chunk), lambda i: (0, i)),
        ],
        out_specs=pl.BlockSpec((tokens, chunk), lambda i: (0, i)),
        out_shape=jax.ShapeDtypeStruct((tokens, columns), BF16),
        compiler_params=params(),
        cost_estimate=cost(),
        name="project_more",
    )(x, full, row)


def out_kernel(heads_ref, w_ref, x_ref, vec_ref, hat_ref, inv_ref, first_ref, low_ref):
    branch = nn(heads_ref[...], w_ref[...]) + vec_ref[0:1]
    hat, inverse = normalized(x_ref[...].astype(F32) + branch)
    first = hat * vec_ref[1:2] + vec_ref[2:3]
    hat_ref[...] = hat
    inv_ref[...] = inverse
    first_ref[...] = first
    low_ref[...] = first.astype(BF16)


def out_project(heads, out_full, x, vectors):
    tokens, width = heads.shape
    rows = tokens // 2
    block = pl.BlockSpec((rows, width), lambda i: (i, 0))
    return pl.pallas_call(
        out_kernel,
        grid=(2,),
        in_specs=[block, pl.BlockSpec(out_full.shape, lambda i: (0, 0)), block, pl.BlockSpec(vectors.shape, lambda i: (0, 0))],
        out_specs=[block, pl.BlockSpec((rows, 1), lambda i: (i, 0)), block, block],
        out_shape=[
            jax.ShapeDtypeStruct((tokens, width), F32),
            jax.ShapeDtypeStruct((tokens, 1), F32),
            jax.ShapeDtypeStruct((tokens, width), F32),
            jax.ShapeDtypeStruct((tokens, width), BF16),
        ],
        compiler_params=params(),
        cost_estimate=cost(),
        name="out_project",
    )(heads, out_full, x, vectors)


def up_copies(refs, full, sems, at_ref, far):
    width, half = full.shape[0], full.shape[1] // 2
    copies = []
    for core in range(2):
        cols = pl.ds(core * half, half)
        if far is None:
            copies.append(pltpu.make_async_copy(refs[core], full.at[:, cols], sems.at[core]))
            continue
        rows = width // (4 * far)
        for second in range(2):
            ref = refs[core * 2 + second]
            for first, z, block in part_blocks(at_ref, "zyx", second, far):
                to = full.at[pl.ds(pl.multiple_of(block * rows, rows), rows), cols]
                copies.append(pltpu.make_async_copy(ref.at[first, z], to, sems.at[len(copies)]))
    return copies


def down_copies(refs, full, sems, at_ref, far):
    half = full.shape[0] // 2
    copies = []
    for core in range(2):
        if far is None:
            copies.append(pltpu.make_async_copy(refs[core], full.at[pl.ds(core * half, half)], sems.at[core]))
            continue
        rows = half // (4 * far)
        for second in range(2):
            ref = refs[core * 2 + second]
            for first, z, block in part_blocks(at_ref, "xy", second, far):
                to = full.at[pl.ds(pl.multiple_of(core * half + block * rows, rows), rows)]
                copies.append(pltpu.make_async_copy(ref.at[first, z], to, sems.at[len(copies)]))
    return copies


def put_half(step, steps, keep_ref, send_ref, value):
    @pl.when(step < steps // 2)
    def _():
        keep_ref[...] = value

    @pl.when(step >= steps // 2)
    def _():
        send_ref[...] = value


def take_half(step, steps, keep_ref, send_ref):
    return jnp.where(step < steps // 2, keep_ref[...], send_ref[...])


def half_blocks(rows, chunk, steps):
    last = steps // 2 - 1
    return [
        pl.BlockSpec((rows, chunk), lambda i: (0, jnp.minimum(i, last))),
        pl.BlockSpec((rows, chunk), lambda i: (0, jnp.maximum(i - last - 1, 0))),
    ]


def lift_kernel(far, parts, *refs):
    at_ref, refs = refs[0], refs[1:]
    part_refs, refs = refs[:parts], refs[parts:]
    low_ref, row_ref, act_ref, act_send, slope_ref, full_out, full, sems, out_sem = refs
    step = pl.program_id(0)
    chunk = act_ref.shape[1]
    copies = up_copies(part_refs, full, sems, at_ref, far)
    keep = pltpu.make_async_copy(full, full_out, out_sem)

    @pl.when(step == 0)
    def _():
        start_all(copies)
        wait_all(copies)
        keep.start()

    lifted = nn(low_ref[...], full[:, pl.ds(pl.multiple_of(step * chunk, chunk), chunk)]) + row_ref[...]
    phi = 0.5 * (1.0 + lax.erf(lifted * (0.5 ** 0.5)))
    density = jnp.exp(lifted * lifted * -0.5) * 0.3989422804014327
    put_half(step, pl.num_programs(0), act_ref, act_send, (lifted * phi).astype(BF16))
    slope_ref[...] = phi + lifted * density

    @pl.when(step == pl.num_programs(0) - 1)
    def _():
        keep.wait()


def lift(far, at, parts, low, row, chunk=512):
    tokens, width = low.shape
    hidden = row.shape[1]
    block = pl.BlockSpec((tokens, chunk), lambda i: (0, i))
    return pl.pallas_call(
        functools.partial(lift_kernel, far, len(parts)),
        grid=(hidden // chunk,),
        in_specs=[SMEM] + [ANY] * len(parts) + [pl.BlockSpec((tokens, width), lambda i: (0, 0)), pl.BlockSpec((1, chunk), lambda i: (0, i))],
        out_specs=half_blocks(tokens, chunk, hidden // chunk) + [block, ANY],
        out_shape=[
            jax.ShapeDtypeStruct((tokens, hidden // 2), BF16),
            jax.ShapeDtypeStruct((tokens, hidden // 2), BF16),
            jax.ShapeDtypeStruct((tokens, hidden), F32),
            jax.ShapeDtypeStruct((width, hidden), BF16),
        ],
        scratch_shapes=[pltpu.VMEM((width, hidden), BF16), pltpu.SemaphoreType.DMA((copy_count(far, 2),)), pltpu.SemaphoreType.DMA],
        compiler_params=params(),
        cost_estimate=cost(),
        name="lift",
    )(at, *parts, low, row)


def settle_kernel(far, parts, *refs):
    at_ref, refs = refs[0], refs[1:]
    part_refs, refs = refs[:parts], refs[parts:]
    act_ref, act_send, first_ref, vec_ref, dy_ref, result_ref, grad_ref, glow_ref, sums_ref, full_out, total, full, sems, out_sem = refs
    step = pl.program_id(0)
    chunk = act_ref.shape[1]
    copies = down_copies(part_refs, full, sems, at_ref, far)
    keep = pltpu.make_async_copy(full, full_out, out_sem)

    @pl.when(step == 0)
    def _():
        start_all(copies)
        wait_all(copies)
        keep.start()

    active = take_half(step, pl.num_programs(0), act_ref, act_send)
    part = nn(active, full[pl.ds(pl.multiple_of(step * chunk, chunk), chunk)])

    @pl.when(step == 0)
    def _():
        total[...] = part

    @pl.when(step > 0)
    def _():
        total[...] += part

    @pl.when(step == pl.num_programs(0) - 1)
    def _():
        rows = total.shape[0] // 4
        sums = None
        for i in range(4):
            at = slice(rows * i, rows * i + rows)
            hat, inverse = normalized(first_ref[at] + (total[at] + vec_ref[0:1]))
            result_ref[at] = (hat * vec_ref[1:2] + vec_ref[2:3]).astype(BF16)
            dy = dy_ref[at].astype(F32)
            grad = norm_back(dy, vec_ref[1:2], hat, inverse)
            low = grad.astype(BF16)
            grad_ref[at] = grad
            glow_ref[at] = low
            part = cat([column_sum(dy * hat), column_sum(dy), column_sum(low.astype(F32))], 0)
            sums = part if sums is None else sums + part
        sums_ref[...] = sums
        keep.wait()


def settle(far, at, parts, active, act_send, first, vectors, dy, chunk=1024):
    tokens, hidden = active.shape[0], 2 * active.shape[1]
    width = first.shape[1]
    whole = lambda shape: pl.BlockSpec(shape, lambda i: (0, 0))
    return pl.pallas_call(
        functools.partial(settle_kernel, far, len(parts)),
        grid=(hidden // chunk,),
        in_specs=[SMEM]
        + [ANY] * len(parts)
        + half_blocks(tokens, chunk, hidden // chunk)
        + [whole((tokens, width)), whole(vectors.shape), whole((tokens, width))],
        out_specs=[whole((tokens, width)), whole((tokens, width)), whole((tokens, width)), whole((3, width)), ANY],
        out_shape=[
            jax.ShapeDtypeStruct((tokens, width), BF16),
            jax.ShapeDtypeStruct((tokens, width), F32),
            jax.ShapeDtypeStruct((tokens, width), BF16),
            jax.ShapeDtypeStruct((3, width), F32),
            jax.ShapeDtypeStruct((hidden, width), BF16),
        ],
        scratch_shapes=[
            pltpu.VMEM((tokens, width), F32),
            pltpu.VMEM((hidden, width), BF16),
            pltpu.SemaphoreType.DMA((copy_count(far, 2),)),
            pltpu.SemaphoreType.DMA,
        ],
        compiler_params=params(),
        cost_estimate=cost(),
        name="settle",
    )(at, *parts, active, act_send, first, vectors, dy)


def lift_grad_kernel(glow_ref, down_ref, slope_ref, keep_ref, send_ref, sum_ref):
    value = (nt(glow_ref[...], down_ref[...]) * slope_ref[...]).astype(BF16)
    put_half(pl.program_id(0), pl.num_programs(0), keep_ref, send_ref, value)
    sum_ref[...] = column_sum(value.astype(F32))


def lift_grads(glow, down_full, slope, chunk=512):
    tokens, width = glow.shape
    hidden = down_full.shape[0]
    half = jax.ShapeDtypeStruct((tokens, hidden // 2), BF16)
    return pl.pallas_call(
        lift_grad_kernel,
        grid=(hidden // chunk,),
        in_specs=[
            pl.BlockSpec((tokens, width), lambda i: (0, 0)),
            pl.BlockSpec((chunk, width), lambda i: (i, 0)),
            pl.BlockSpec((tokens, chunk), lambda i: (0, i)),
        ],
        out_specs=half_blocks(tokens, chunk, hidden // chunk) + [pl.BlockSpec((1, chunk), lambda i: (0, i))],
        out_shape=[half, half, jax.ShapeDtypeStruct((1, hidden), F32)],
        compiler_params=params(),
        cost_estimate=cost(),
        name="lift_grads",
    )(glow, down_full, slope)


def down_grad_kernel(far, at_ref, act_ref, act_got, glow_ref, glow_got, dw_ref, glows):
    tokens = glow_ref.shape[0]

    @pl.when(pl.program_id(0) == 0)
    def _():
        glows[:tokens] = glow_ref[...]
        glows[tokens:] = glow_got[...]

    dw = tn(cat([act_ref[...], act_got[...]], 0), glows[...]).astype(BF16)
    if far is None:
        dw_ref[...] = dw
        return
    rows = dw.shape[0] // 4
    for j in range(4):
        to = block_place(at_ref, "yx", 0, j // 2, j % 2, far)
        dw_ref[pl.ds(pl.multiple_of(to * rows, rows), rows)] = dw[j * rows : j * rows + rows]


def down_grads(far, at, active, act_got, glow, glow_got):
    tokens, half = active.shape
    width = glow.shape[1]
    chunk = half // 4
    whole = pl.BlockSpec((tokens, width), lambda i: (0, 0))
    block = pl.BlockSpec((tokens, chunk), lambda i: (0, i))
    return pl.pallas_call(
        functools.partial(down_grad_kernel, far),
        grid=(4,),
        in_specs=[SMEM, block, block, whole, whole],
        out_specs=pl.BlockSpec((chunk, width), lambda i: (i, 0)),
        out_shape=jax.ShapeDtypeStruct((half, width), BF16),
        scratch_shapes=[pltpu.VMEM((2 * tokens, width), BF16)],
        compiler_params=params(),
        cost_estimate=cost(),
        name="down_grads",
    )(at, active, act_got, glow, glow_got)


def first_grad_kernel(at_ref, lift_ref, lift_send, up_ref, grad_ref, hat_ref, inv_ref, gain_ref, one_ref, branch_ref, mine_ref, send_ref, sums_ref, total):
    step = pl.program_id(0)
    part = nt(take_half(step, pl.num_programs(0), lift_ref, lift_send), up_ref[...])

    @pl.when(step == 0)
    def _():
        total[...] = grad_ref[...] + part

    @pl.when(step > 0)
    def _():
        total[...] += part

    @pl.when(step == pl.num_programs(0) - 1)
    def _():
        rows = total.shape[0] // 4
        sums = None
        for i in range(4):
            at = slice(rows * i, rows * i + rows)
            grad = total[at]
            hat = hat_ref[at]
            one = norm_back(grad, gain_ref[...], hat, inv_ref[at])
            branch = one.astype(BF16)
            one_ref[at] = one
            branch_ref[at] = branch
            part = cat([column_sum(grad * hat), column_sum(grad), column_sum(branch.astype(F32))], 0)
            sums = part if sums is None else sums + part
        sums_ref[...] = sums
        half = mine_ref.shape[1]
        mine_ref[...] = branch_ref[:, pl.ds(pl.multiple_of(at_ref[2] * half, half), half)]
        send_ref[...] = branch_ref[:, pl.ds(pl.multiple_of((1 - at_ref[2]) * half, half), half)]


def first_grads(at, lift, lift_send, up_full, grad_two, hat, inverse, gain, chunk=1024):
    tokens, width = hat.shape
    hidden = up_full.shape[1]
    whole = lambda shape: pl.BlockSpec(shape, lambda i: (0, 0))
    half = whole((tokens, width // 2))
    return pl.pallas_call(
        first_grad_kernel,
        grid=(hidden // chunk,),
        in_specs=[SMEM]
        + half_blocks(tokens, chunk, hidden // chunk)
        + [
            pl.BlockSpec((width, chunk), lambda i: (0, i)),
            whole((tokens, width)),
            whole((tokens, width)),
            whole((tokens, 1)),
            whole((1, width)),
        ],
        out_specs=[whole((tokens, width)), whole((tokens, width)), half, half, whole((3, width))],
        out_shape=[
            jax.ShapeDtypeStruct((tokens, width), F32),
            jax.ShapeDtypeStruct((tokens, width), BF16),
            jax.ShapeDtypeStruct((tokens, width // 2), BF16),
            jax.ShapeDtypeStruct((tokens, width // 2), BF16),
            jax.ShapeDtypeStruct((3, width), F32),
        ],
        scratch_shapes=[pltpu.VMEM((tokens, width), F32)],
        compiler_params=params(),
        cost_estimate=cost(),
        name="first_grads",
    )(at, lift, lift_send, up_full, grad_two, hat, inverse, gain)


def pay_kernel(branch_ref, w_ref, heads_ref, log_ref, pay_ref, mean_ref):
    tokens, width = branch_ref.shape
    grad = nt(branch_ref[...], w_ref[...]).astype(BF16)
    pay_ref[:tokens] = grad
    product = grad.astype(F32) * heads_ref[...].astype(F32)
    head = lax.broadcasted_iota(jnp.int32, (H, width), 1) // HD
    pick = jnp.where(head == lax.broadcasted_iota(jnp.int32, (H, width), 0), 1.0, 0.0).astype(F32)
    means = lax.dot_general(pick, product, (((1,), (1,)), ((), ())), precision=lax.Precision.HIGHEST, preferred_element_type=F32)
    mean_ref[...] = means
    rest = cat([log_ref[...], means], 1)
    for k in range(3):
        term = rest.astype(BF16)
        rest = rest - term.astype(F32)
        pay_ref[tokens + H * k : tokens + H * k + H] = term


def pay(branch, out_full, heads, logs):
    tokens, width = branch.shape
    return pl.pallas_call(
        pay_kernel,
        out_shape=[jax.ShapeDtypeStruct((tokens + 3 * H, width), BF16), jax.ShapeDtypeStruct((H, tokens), F32)],
        compiler_params=params(),
        cost_estimate=cost(),
        name="pay",
    )(branch, out_full, heads, logs)


def both_flipped(at_ref, mine_ref, got_ref, flipped, far, heads=False):
    tokens = mine_ref.shape[0]
    for core, ref in ((0, mine_ref), (1, got_ref)):
        turned = ref[...].T
        cols = slice(core * tokens, core * tokens + tokens)
        flip = jnp.bitwise_xor(at_ref[2], core) if heads else 0
        half = turned.shape[0] // 2
        if far is None:
            for part in range(2):
                to = jnp.bitwise_xor(flip, part) * half
                flipped[pl.ds(pl.multiple_of(to, half), half), cols] = turned[part * half : part * half + half]
            continue
        rows = turned.shape[0] // (8 * far)
        for z in range(far):
            at_z = jnp.bitwise_xor(z, flip * (far // 2))
            for y in range(2):
                for x in range(2):
                    a = ((z * 2 + y) * 2 + x) * 2 * rows
                    to_y, to_x = jnp.bitwise_xor(at_ref[0], y), jnp.bitwise_xor(at_ref[1], x)
                    first = ((1 - to_x) * 2 + to_y) * far + at_z
                    second = ((3 - to_y) * 2 + to_x) * far + at_z
                    for i, to in enumerate((first, second)):
                        to = pl.ds(pl.multiple_of(to * rows, rows), rows)
                        flipped[to, cols] = turned[a + i * rows : a + i * rows + rows]


def quarter_specs(rows, columns, index):
    return [pl.BlockSpec((rows // 4, columns), index)] * 4


def put_quarters(refs, cols, value):
    rows = value.shape[0] // 4
    for i, ref in enumerate(refs):
        ref[:, cols] = value[i * rows : i * rows + rows]


def late_grad_kernel(far, at_ref, low_ref, low_got, heads_ref, heads_got, lift_ref, lift_got, branch_ref, branch_got, *refs):
    quarters, flipped = refs[:4], refs[4]
    step = pl.program_id(0)
    last = pl.num_programs(0) - 1

    @pl.when(step == 0)
    def _():
        both_flipped(at_ref, low_ref, low_got, flipped, far)

    @pl.when(step < last)
    def _():
        put_quarters(quarters, slice(None), nn(flipped[...], cat([lift_ref[...], lift_got[...]], 0)).astype(BF16))

    @pl.when(step == last)
    def _():
        both_flipped(at_ref, heads_ref, heads_got, flipped, far, heads=True)
        put_quarters(quarters, slice(None), nn(flipped[...], cat([branch_ref[...], branch_got[...]], 0)).astype(BF16))


def late_grads(far, at, low, low_got, heads, heads_got, lift, lift_got, branch, branch_got):
    tokens, width = low.shape
    chunk = branch.shape[1]
    steps = lift.shape[1] // chunk
    whole = lambda shape: pl.BlockSpec(shape, lambda i: (0, 0))
    block = pl.BlockSpec((tokens, chunk), lambda i: (0, jnp.minimum(i, steps - 1)))
    return pl.pallas_call(
        functools.partial(late_grad_kernel, far),
        grid=(steps + 1,),
        in_specs=[SMEM] + [whole((tokens, width))] * 4 + [block, block] + [whole((tokens, chunk))] * 2,
        out_specs=quarter_specs(width, chunk, lambda i: (0, i)),
        out_shape=[jax.ShapeDtypeStruct((width // 4, (steps + 1) * chunk), BF16)] * 4,
        scratch_shapes=[pltpu.VMEM((width, 2 * tokens), BF16)],
        compiler_params=params(),
        cost_estimate=cost(),
        name="late_grads",
    )(at, low, low_got, heads, heads_got, lift, lift_got, branch, branch_got)


def qkv_grad_kernel(far, at_ref, x_ref, x_got, keep_ref, got_ref, *refs):
    note_refs, quarters, flipped = refs[:-5], refs[-5:-1], refs[-1]
    both_flipped(at_ref, x_ref, x_got, flipped, far)
    chunk = keep_ref.shape[2]
    for n in range(3):
        dw = nn(flipped[...], cat([keep_ref[n], got_ref[n]], 0)).astype(BF16)
        put_quarters(quarters, slice(n * chunk, n * chunk + chunk), dw)
    for ref in note_refs:
        put_quarters(quarters, slice(3 * chunk, 3 * chunk + ref.shape[1]), ref[...])


def qkv_grads(far, at, x, x_got, keep, got, notes=()):
    tokens, width = x.shape
    columns = 3 * keep.shape[2] + sum(v.shape[1] for v in notes)
    return pl.pallas_call(
        functools.partial(qkv_grad_kernel, far),
        in_specs=[SMEM] + [VMEM] * (4 + len(notes)),
        out_shape=[jax.ShapeDtypeStruct((width // 4, columns), BF16)] * 4,
        scratch_shapes=[pltpu.VMEM((width, 2 * tokens), BF16)],
        compiler_params=params(),
        cost_estimate=cost(),
        name="qkv_grads",
    )(at, x, x_got, keep, got, *notes)


FAR, Y, X, CORE = "far", "y", "x", "fsdp"
CTX = (FAR, Y, X)
ALL = CTX + (CORE,)


def swap(values, axis):
    return lax.ppermute(values, axis, [(0, 1), (1, 0)])


def swap_far(values, step):
    return lax.ppermute(values, FAR, [(i, i ^ step) for i in range(lax.axis_size(FAR))])


def together(*arrays):
    return lax.optimization_barrier(arrays)


def choose(core, left, right):
    return jnp.where(core == 0, left, right), jnp.where(core == 0, right, left)


def added(*terms):
    total = terms[0].astype(F32)
    for term in terms[1:]:
        total = total + term.astype(F32)
    return total.astype(BF16)


def own_rows(core, summed):
    mine, send = choose(core, summed[0], summed[1])
    return choose(core, mine, swap(send, CORE))


def color_nexts(keep_x, keep_y, there_x, there_y):
    return added(keep_x[1], there_x[1]), added(keep_y[1], there_y[1])


def color_sums(keep_x, keep_y, there_x, there_y, there_xy, there_yx):
    return jnp.stack([added(keep_x[0], there_x[0], there_xy), added(keep_y[0], there_y[0], there_yx)], 1)


def shards(inputs, segments, cotangent, qkv_weight, query_bias, value_bias, out_weight, out_bias, first_gain, first_shift, up_weight, up_bias, down_weight, down_bias, second_gain, second_shift):
    tokens, width = inputs.shape[1:]
    rows, hidden = up_weight.shape
    piece = down_weight.shape[0]
    near = width // 2
    blocks = lax.axis_size(CTX)
    place = lax.axis_index(CTX)
    core = lax.axis_index(CORE)
    at = jnp.stack([lax.axis_index(Y), lax.axis_index(X), core, lax.axis_index(FAR)]).astype(jnp.int32)
    far = 4 if rows % 32 == 0 and lax.axis_size(FAR) == 4 and piece == HIDDEN_BLOCK else None
    onward = [(i, i + 1) for i in range(blocks - 1)]
    back = [(i + 1, i) for i in range(blocks - 1)]

    def from_before(v):
        return lax.ppermute(v, CTX, onward)

    def from_after(v):
        return lax.ppermute(v, CTX, back)

    def own_first(v):
        return cat(choose(core, v[:, :near], v[:, near:]), 1)

    x = inputs[0]
    vectors = (query_bias, value_bias, out_bias, first_gain, first_shift, down_bias, second_gain, second_shift, up_bias)
    each = query_bias.shape[0]
    if far is None:
        split = lambda w, size: w.reshape(rows, -1, 2, size).swapaxes(0, 2).swapaxes(1, 2).reshape(2, rows, -1)
        sides = cat([split(qkv_weight, near), split(out_weight, near), split(up_weight, piece)], 2)
        mine, send = choose(core, sides[0], sides[1])
        both = cat(choose(core, mine, swap(send, CORE)), 0)
        whole = lambda v: lax.all_gather(v, CTX, axis=0, tiled=True)
        pair = lambda v: [v, swap(v, CORE)]
        qkv_parts = pair(whole(both[:, : 3 * near])) + pair(whole(both[:, 3 * near : 4 * near]))
        up_parts, down_parts = pair(whole(both[:, 4 * near :])), pair(whole(down_weight))
        x_before, x_after = from_before(x), from_after(x)
        table = lax.all_gather(cat(vectors, 0)[None], ALL, axis=0, tiled=True)
    else:
        mine, send, note = prepare(at, qkv_weight, out_weight, up_weight, vectors)
        block, up_block = arrange(at, mine, swap(send, CORE), note, hidden)
        cut = 4 * near
        lines = sum(v.shape[0] for v in vectors) // 128
        pair = jnp.stack([block, swap_far(block, 2)])
        down_pair = jnp.stack([down_weight, swap(down_weight, X)])
        pair, x_before, x_two = together(pair, from_before(x), x)
        wide = jnp.stack([pair, swap_far(pair, 1)]).reshape((4,) + block.shape)
        x_after = from_after(x_two)
        wide, up_block, down_pair, x_after = together(wide, up_block, down_pair, x_after)
        a1, b1, up_hi = swap(wide[:, 0], Y), swap(wide[:, 1], X), swap_far(up_block, 2)
        a1, b1, up_hi = together(a1, b1, up_hi)
        pair_a, pair_b, up_pair = jnp.stack([wide[:, 0], a1]), jnp.stack([wide[:, 1], b1]), jnp.stack([up_block, up_hi])
        a2, b2, up_lo = swap(pair_a, X), swap(pair_b, Y), swap_far(up_pair, 1)
        up_lo, down_pair = together(up_lo, down_pair)
        down_wide = lax.all_gather(down_pair, FAR, axis=1)
        a2, b2, up_lo = together(a2, b2, up_lo)
        first_parts = [pair_a, a2, pair_b, b2]
        qkv_parts = first_parts + [swap(p, CORE) for p in first_parts]
        up_wide = jnp.stack([up_pair, up_lo]).reshape((4,) + up_block.shape)
        up_y = swap(up_wide, Y)
        notes = jnp.stack([jnp.stack([qkv_parts[4 * c + s][:, :, :lines, cut:] for s in range(2)]) for c in range(2)])
        notes = notes.reshape(2, 2, 2, 2, 2, -1).swapaxes(3, 4)
        for axis, index in ((0, core), (1, at[1]), (2, at[0]), (3, at[3] // 2), (4, at[3] % 2)):
            notes = jnp.where(index == 0, notes, jnp.flip(notes, axis))
        table = notes.transpose(3, 4, 2, 1, 0, 5).reshape(2 * blocks, -1)

    rows_of = [table[:, each * i : each * i + each].reshape(1, width).astype(F32) for i in range(8)]
    query_row, value_row, out_row, gain_one, shift_one, down_row, gain_two, shift_two = rows_of
    up_row = table[:, 8 * each :].reshape(blocks, 2, piece).astype(F32)
    up_row = cat(choose(core, up_row[:, 0].reshape(1, -1), up_row[:, 1].reshape(1, -1)), 1)
    bias_own, bias_halo = mask_biases(segments[0], place, blocks, tokens)
    query_row, value_row, gap = own_first(query_row), own_first(value_row), jnp.zeros((1, near), F32)
    qkv_row = cat([query_row[:, :near], gap, value_row[:, :near], query_row[:, near:], gap, value_row[:, near:]], 1)

    mixed, before, qkv_full, out_full = project(far, at, qkv_parts, x, x_before, qkv_row)
    if far is not None:
        qkv_full, up_y = together(qkv_full, up_y)
        up_pair = jnp.stack([up_wide, up_y])
        up_x, up_pair_core = swap(up_pair, X), swap(up_pair, CORE)
    after = project_more(x_after, qkv_full, qkv_row)
    if far is not None:
        after, down_wide = together(after, down_wide)
        down_y, down_wide_core = swap(down_wide, Y), swap(down_wide, CORE)
    heads, logs = attend(mixed, before, after, bias_own, bias_halo)
    hat, inverse, first, low = out_project(heads, out_full, x, cat([out_row, gain_one, shift_one], 0))
    if far is not None:
        low, up_x, up_pair_core, down_wide_core, down_y = together(low, up_x, up_pair_core, down_wide_core, down_y)
        up_parts = [up_pair, up_x, up_pair_core, swap(up_x, CORE)]
        down_parts = [down_wide, down_y, down_wide_core, swap(down_y, CORE)]
    x_got, heads_got, low_got = swap(x, CORE), swap(heads, CORE), swap(low, CORE)
    active, act_send, slope, up_full = lift(far, at, up_parts, low, up_row)
    act_got = swap(act_send, CORE)
    active, x_got, heads_got, low_got = together(active, x_got, heads_got, low_got)
    result, grad_two, glow, sums_two, down_full = settle(
        far, at, down_parts, active, act_send, first, cat([down_row, gain_two, shift_two], 0), cotangent[0]
    )
    glow_got = swap(glow, CORE)
    lift_keep, lift_send, up_bias_part = lift_grads(glow, down_full, slope)
    lift_got = swap(lift_send, CORE)
    grad_one, branch, branch_mine, branch_send, sums_one = first_grads(at, lift_keep, lift_send, up_full, grad_two, hat, inverse, gain_one)
    branch_got = swap(branch_send, CORE)
    payload, means = pay(branch, out_full, heads, logs)
    pay_before, pay_after = from_before(payload), from_after(payload)
    down_part = down_grads(far, at, active, act_got, glow, glow_got)
    late = late_grads(far, at, low, low_got, heads, heads_got, lift_keep, lift_got, branch_mine, branch_got)
    dq, dkv, dq_sum = own_grads(mixed, before, after, payload, logs, means, bias_own, bias_halo)
    if far is not None:
        down_part = lax.psum_scatter(down_part.reshape(far, 2, 2, piece, width), FAR, scatter_dimension=0, tiled=False)
        by = lambda parts: [v.reshape(2, far, rows, v.shape[1]) for v in parts]
        late_send_x, late_keep_x, late_send_y, late_keep_y = by(late)
        late_x, late_y, pay_before, pay_after = together(late_send_x, late_send_y, pay_before, pay_after)
        late_x, late_y = swap(late_x, X), swap(late_y, Y)
    keep, send, dv_sum = halo_grads(mixed, before, after, pay_before, pay_after, bias_halo, dq, dkv)
    got = swap(send, CORE)
    if far is not None:
        got, late_x, late_y = together(got, late_x, late_y)
        late_xy, late_yx = color_nexts(late_keep_x, late_keep_y, late_x, late_y)
        late_xy, late_yx, got = together(late_xy, late_yx, got)
        late_xy, late_yx = swap(late_xy, Y), swap(late_yx, X)
    features = (own_first(dq_sum), own_first(dv_sum), sums_one[2], sums_one[0], sums_one[1], sums_two[2], sums_two[0], sums_two[1])
    small = jnp.stack([v.reshape(blocks, 2, each) for v in features], 2)
    small = small.reshape(blocks, 2, -1)
    small = choose(core, small[:, 0], small[:, 1])
    small = [cat([v, up_bias_part[:, hidden // 2 * i : hidden // 2 * (i + 1)].reshape(blocks, piece)], 1) for i, v in enumerate(small)]
    small = small[0] + swap(small[1], CORE)
    if far is None:
        qkv = qkv_grads(far, at, x, x_got, keep, got)
        total = lambda v: lax.psum_scatter(v, CTX, scatter_dimension=0, tiled=True)
        down_sum, small_sum = total(down_part).astype(F32), total(small)[0]
        late_sum, qkv_sum = [total(cat(v, 0)).reshape(2, rows, -1) for v in (late, qkv)]
    else:
        small = small.reshape(far, 2, 2, lines, 128).transpose(2, 1, 0, 3, 4)
        for axis, index in ((0, at[1]), (1, at[0])):
            small = jnp.where(index == 0, small, jnp.flip(small, axis))
        small = jnp.flip(small, 0).reshape(2 * 2 * far, lines, 128).astype(BF16)
        note = jnp.zeros((8 * far, rows, 128), BF16).at[: 4 * far, :lines].set(small).reshape(width, 128)
        qkv_send_x, qkv_keep_x, qkv_send_y, qkv_keep_y = by(qkv_grads(far, at, x, x_got, keep, got, (note,)))
        qkv_send_x, qkv_send_y, late_xy, late_yx = together(qkv_send_x, qkv_send_y, late_xy, late_yx)
        qkv_x, qkv_y = swap(qkv_send_x, X), swap(qkv_send_y, Y)
        late_sum = color_sums(late_keep_x, late_keep_y, late_x, late_y, late_xy, late_yx)
        late_sum, down_part = together(late_sum, down_part)
        late_sum = lax.psum_scatter(late_sum, FAR, scatter_dimension=0, tiled=False)
        down_y = swap(down_part[1], Y)
        qkv_x, qkv_y, grad_one, down_y = together(qkv_x, qkv_y, grad_one, down_y)
        qkv_xy, qkv_yx = color_nexts(qkv_keep_x, qkv_keep_y, qkv_x, qkv_y)
        qkv_xy, qkv_yx = swap(qkv_xy, Y), swap(qkv_yx, X)
        down_part = added(down_part[0], down_y)
        down_x = swap(down_part[1], X)
        qkv_xy, qkv_yx, late_sum, down_x = together(qkv_xy, qkv_yx, late_sum, down_x)
        qkv_sum = lax.psum_scatter(color_sums(qkv_keep_x, qkv_keep_y, qkv_x, qkv_y, qkv_xy, qkv_yx), FAR, scatter_dimension=0, tiled=False)
        down_sum = down_part[0].astype(F32) + down_x.astype(F32)
        small_sum = qkv_sum[0, :lines, 3 * near :].reshape(-1).astype(F32)
    inputs_grad = nt(cat([*keep, *send], 1), qkv_full)
    inputs_grad = (grad_one + inputs_grad).astype(BF16)[None]
    wide = hidden // 2
    left, right = own_rows(core, late_sum)
    up_sum = jnp.stack([v[:, :wide].reshape(rows, blocks, piece) for v in (left, right)], 2).reshape(rows, hidden).astype(F32)
    out_sum = cat([left[:, wide:], right[:, wide:]], 1).astype(F32)
    left, right = own_rows(core, qkv_sum[:, :, : 3 * near])
    qkv_sum = jnp.stack([v.reshape(rows, 3, near) for v in (left, right)], 2).reshape(rows, 3 * width).astype(F32)
    s = [small_sum[each * i : each * i + each] for i in range(8)]
    return (
        result[None], inputs_grad, qkv_sum, s[0], s[1], out_sum, s[2], s[3], s[4], up_sum, small_sum[8 * each :], down_sum, s[5], s[6], s[7],
    )


def solution(mesh):
    devices = mesh.devices
    split = jax.sharding.Mesh(devices.reshape(devices.shape[0] // 4, 2, 2, devices.shape[1]), ALL)
    rows, vec = P(ALL, None), P(ALL)
    tokens = P(CORE, CTX, None)
    return jax.shard_map(
        shards,
        mesh=split,
        in_specs=(tokens, P(CORE, None), tokens, rows, vec, vec, rows, vec, vec, vec, rows, vec, rows, vec, vec, vec),
        out_specs=(tokens, tokens, rows, vec, vec, rows, vec, vec, vec, rows, vec, rows, vec, vec, vec),
        check_vma=False,
    )
```

time: 689 us -> 507 us (0.74)
  waiting for transfers between devices: 306 us -> 157 us
  blocking collectives: 30.1 us -> 0 us
  other arithmetic: 49.6 us -> 35.1 us
  Pallas kernels: 199 us -> 208 us
    ppermute x32 -> x38, waiting for transfers between devices: 181 us -> 86.5 us  [swap(): return lax.ppermute(values, axis, [(0, 1), (1, 0)])]
    ppermute x3 -> x2, waiting for transfers between devices: 54.1 us -> 0.7 us  [from_before(): return lax.ppermute(v, CTX, onward)]
    ppermute x0 -> x4, waiting for transfers between devices: none -> 48.4 us  [swap_far(): lax.ppermute(values, FAR, [(i, i ^ step) for i in range(lax.axis_size(FAR...]
    all_gather x2 -> x1, waiting for transfers between devices: 41.7 us -> 2.26 us  [shards(): down_wide = lax.all_gather(down_pair, FAR, axis=1)]
    all_gather x1 -> x0, blocking collectives: 30.1 us -> none  [gather_first(): wide = lax.all_gather(block, FAR, axis=0)]
    ppermute x3 -> x2, waiting for transfers between devices: 13.2 us -> 0.01 us  [from_after(): return lax.ppermute(v, CTX, back)]
    pallas_call x5 -> x11, Pallas kernels: 95 us -> 106 us  [the longest x1 18 us: lift(): pl.pallas_call(functools.partial(lift_kernel, far, len(parts)), grid=(hid...]
    add x2, other arithmetic: 8.1 us -> 0.86 us  [the longest x1 0.86 us: shards(): down_sum = down_part[0].astype(F32) + down_x.astype(F32)]
  transfers between devices with their start and end apart: 43 -> 50, of which waited for: 17 -> 24; matrix products, arithmetic and copies ran while one was open for 10% -> 9% of each run, Pallas kernels for 12% -> 42%
where the time goes in v2:
time: 507 us; the launch traced here: 500 us
  Pallas kernels  208 us (41%)
  waiting for transfers between devices  157 us (31%)
  starting transfers between devices  55.5 us (11%)
  other arithmetic  35.1 us (7%)
  local copies, waits for them, and re-layouts  23.5 us (5%)
  between operations  15.2 us (3%)
  matrix products  5.85 us (1%)
    ppermute x38, waiting for transfers between devices, swap(): return lax.ppermute(values, axis, [(0, 1), (1, 0)])  86.5 us
    ppermute x4, waiting for transfers between devices, swap_far(): lax.ppermute(values, FAR, [(i, i ^ step) for i in range(lax.axis_size(FAR...  48.4 us
    ppermute x38, starting transfers between devices, swap(): return lax.ppermute(values, axis, [(0, 1), (1, 0)])  30 us
    pallas_call x1, Pallas kernels, own_grads(): pl.pallas_call(own_grad_kernel, grid=(pairs,), in_specs=[column(0), colum...  29.4 us
    pallas_call x1, Pallas kernels, attend(): pl.pallas_call(attend_kernel, grid=(pairs,), in_specs=[column(0), column(...  24.1 us
    pallas_call x1, Pallas kernels, halo_grads(): pl.pallas_call(halo_grad_kernel, grid=(pairs,), in_specs=[column(1), colu...  21.5 us
    pallas_call x1, Pallas kernels, project(): pl.pallas_call(functools.partial(project_kernel, far, len(parts)), in_spe...  18.8 us
    reduce_scatter x1, waiting for transfers between devices, shards(): lax.psum_scatter(color_sums(qkv_keep_x, qkv_keep_y, qkv_x, qkv_y, qkv_xy,...  18.8 us
  transfers between devices with their start and end apart: 50, of which 24 were waited for; matrix products, arithmetic and copies ran while one was open for 9% of the time, Pallas kernels for 42%

profile of v2, /device:TPU:25, one launch (start us, length us, event | category | flops | bytes accessed | tf_op | source)
XLA Modules:
  0.0 499.6 jit_solution(8820311470047265147)
XLA Ops:
  18.1 15.5 %collective-permute-done.1 = bf16[2,32,2176]{2,1,0:T(8,128)(2,1)S(1)} collective-permute-done((bf16[2,32,2176]{2,1,0:T(8,128)(2,1)}, bf16[2,32,2176]{2,1,0:T(8,128)(2,1)S(1)}, u32[]{:S(2)}, u32[]{:S(2)}) %collective-permute-start.1) | collective-permute-done | bytes 278560 | tf_op jit(solution)/shard_map/ppermute | solution.py:997
  35.3 9.0 %collective-permute-start.5 = (bf16[512,1024]{1,0:T(8,128)(2,1)S(1)}, bf16[512,1024]{1,0:T(8,128)(2,1)}, u32[]{:S(2)}, u32[]{:S(2)}) collective-permute-start(bf16[512,1024]{1,0:T(8,128)(2,1)S(1)} %bitcast.179), channel_id=1, source_target_pairs={{2,0},{4,2},{6,4},{8,6},{10,8},{12,10},{14,12},{16,14},{18,16},{20... | collective-permute-start | bytes 3145736 | tf_op jit(solution)/shard_map/ppermute | solution.py:1045
  44.3 5.5 %collective-permute-start.3 = (bf16[2,2,32,2176]{3,2,1,0:T(8,128)(2,1)S(1)}, bf16[2,2,32,2176]{3,2,1,0:T(8,128)(2,1)S(1)}, u32[]{:S(2)}, u32[]{:S(2)}) collective-permute-start(bf16[2,2,32,2176]{3,2,1,0:T(8,128)(2,1)S(1)} %pad_maximum_fusion.8), channel_id=1, source_target_pairs={{0,8},{8,0},{16,24},{24,16},{1,9},{9,1},{17,25},{25,17},{2,10},{10... | collective-permute-start | bytes 1671176 | tf_op jit(solution)/shard_map/ppermute | solution.py:997
  49.8 15.7 %collective-permute-done.4 = bf16[128,1024]{1,0:T(8,128)(2,1)S(1)} collective-permute-done((bf16[128,1024]{1,0:T(8,128)(2,1)S(1)}, bf16[128,1024]{1,0:T(8,128)(2,1)S(1)}, u32[]{:S(2)}, u32[]{:S(2)}) %collective-permute-start.4) | collective-permute-done | bytes 262176 | tf_op jit(solution)/shard_map/ppermute | solution.py:993
  66.4 10.8 %collective-permute-done.3 = bf16[2,2,32,2176]{3,2,1,0:T(8,128)(2,1)S(1)} collective-permute-done((bf16[2,2,32,2176]{3,2,1,0:T(8,128)(2,1)S(1)}, bf16[2,2,32,2176]{3,2,1,0:T(8,128)(2,1)S(1)}, u32[]{:S(2)}, u32[]{:S(2)}) %collective-permute-start.3) | collective-permute-done | bytes 557088 | tf_op jit(solution)/shard_map/ppermute | solution.py:997
  78.9 13.3 %collective-permute-done.8 = bf16[64,2048]{1,0:T(8,128)(2,1)S(1)} collective-permute-done((bf16[64,2048]{1,0:T(8,128)(2,1)S(1)}, bf16[64,2048]{1,0:T(8,128)(2,1)S(1)}, u32[]{:S(2)}, u32[]{:S(2)}) %collective-permute-start.8) | collective-permute-done | bytes 262176 | tf_op jit(solution)/shard_map/ppermute | solution.py:997
  98.6 8.8 %collective-permute-done.11 = bf16[2,64,2048]{2,1,0:T(8,128)(2,1)S(1)} collective-permute-done((bf16[2,64,2048]{2,1,0:T(8,128)(2,1)S(1)}, bf16[2,64,2048]{2,1,0:T(8,128)(2,1)S(1)}, u32[]{:S(2)}, u32[]{:S(2)}) %collective-permute-start.11) | collective-permute-done | bytes 524320 | tf_op jit(solution)/shard_map/ppermute | solution.py:997
  107.3 10.6 %collective-permute-done.9.refs_2_ = bf16[2,4,32,2176]{3,2,1,0:T(8,128)(2,1)} collective-permute-done((bf16[2,4,32,2176]{3,2,1,0:T(8,128)(2,1)S(1)}, bf16[2,4,32,2176]{3,2,1,0:T(8,128)(2,1)}, u32[]{:S(2)}, u32[]{:S(2)}) %collective-permute-start.9) | collective-permute-done | bytes 1114144 | tf_op jit(solution)/shard_map/ppermute | solution.py:993
  129.7 18.8 %project.1 = (bf16[512,3072]{1,0:T(8,128)(2,1)}, bf16[512,3072]{1,0:T(8,128)(2,1)}, bf16[1024,3072]{1,0:T(8,128)(2,1)}, bf16[1024,1024]{1,0:T(8,128)(2,1)}) custom-call(s32[4]{0:T(128)} %pad_add_fusion.2.at_ref.refs_0_, bf16[2,4,32,2176]{3,2,1,0:T(8,128)(2,1)} %copy-done.6, bf16[2,4,32,2176]{3,2,1,0:T(8,128)(2,1)} %collective-permute-done.9.refs_2_, ...), custom_call_target="tpu_custom_call" | custom-call | flops 1 | bytes 1 | tf_op jit(solution)/shard_map/project/pallas_call | solution.py:484
  154.9 8.3 %project_more.1.kn_ref.vn_ref.qn_ref = bf16[512,3072]{1,0:T(8,128)(2,1)} custom-call(bf16[512,1024]{1,0:T(8,128)(2,1)} %collective-permute-done.5.x_ref, bf16[1024,3072]{1,0:T(8,128)(2,1)} %get-tuple-element.147.w_ref, f32[1,3072]{1,0:T(1,128)} %copy-done.31), custom_call_target="tpu_custom_call" | custom-call | flops 1 | bytes 1 | tf_op jit(solution)/shard_map/project_more/pallas_call | solution.py:508
  171.3 24.1 %attend.1 = (bf16[512,1024]{1,0:T(8,128)(2,1)}, f32[16,512]{1,0:T(8,128)}) custom-call(bf16[512,3072]{1,0:T(8,128)(2,1)} %get-tuple-element.150.q_ref.ko_ref.vo_ref, bf16[512,3072]{1,0:T(8,128)(2,1)} %get-tuple-element.150.q_ref.ko_ref.vo_ref, bf16[512,3072]{1,0:T(8,128)(2,1)} %get-tuple-element.151.kp_ref.vp_ref.qp_ref, ...), custom_call_target="tpu_custom_call" | custom-call | flops 1 | bytes 1 | tf_op jit(solution)/shard_map/attend/pallas_call | solution.py:123
  195.4 5.7 %out_project.1 = (f32[512,1024]{1,0:T(8,128)}, f32[512,1]{1,0:T(8,128)}, f32[512,1024]{1,0:T(8,128)}, bf16[512,1024]{1,0:T(8,128)(2,1)}) custom-call(bf16[512,1024]{1,0:T(8,128)(2,1)} %get-tuple-element.153.heads_ref, bf16[1024,1024]{1,0:T(8,128)(2,1)} %get-tuple-element.154.w_ref, bf16[512,1024]{1,0:T(8,128)(2,1)} %bitcast.177, ...), custom_call_target="tpu_custom_call" | custom-call | flops 1 | bytes 1 | tf_op jit(solution)/shard_map/out_project/pallas_call | solution.py:538
  202.4 10.1 %collective-permute-done.20.refs_2_ = bf16[2,4,128,1024]{3,2,1,0:T(8,128)(2,1)} collective-permute-done((bf16[2,4,128,1024]{3,2,1,0:T(8,128)(2,1)}, bf16[2,4,128,1024]{3,2,1,0:T(8,128)(2,1)}, u32[]{:S(2)}, u32[]{:S(2)}) %collective-permute-start.20) | collective-permute-done | bytes 2097184 | tf_op jit(solution)/shard_map/ppermute | solution.py:993
  215.5 5.2 %collective-permute-done.22.refs_4_ = bf16[2,4,64,2048]{3,2,1,0:T(8,128)(2,1)S(1)} collective-permute-done((bf16[2,4,64,2048]{3,2,1,0:T(8,128)(2,1)}, bf16[2,4,64,2048]{3,2,1,0:T(8,128)(2,1)S(1)}, u32[]{:S(2)}, u32[]{:S(2)}) %collective-permute-start.22) | collective-permute-done | bytes 2097184 | tf_op jit(solution)/shard_map/ppermute | solution.py:993
  222.1 18.0 %lift.1 = (bf16[512,2048]{1,0:T(8,128)(2,1)}, bf16[512,2048]{1,0:T(8,128)(2,1)}, f32[512,4096]{1,0:T(8,128)}, bf16[1024,4096]{1,0:T(8,128)(2,1)}) custom-call(s32[4]{0:T(128)} %pad_add_fusion.2.at_ref.refs_0_, bf16[2,4,64,2048]{3,2,1,0:T(8,128)(2,1)} %pad_maximum_fusion.refs_1_, bf16[2,4,64,2048]{3,2,1,0:T(8,128)(2,1)} %collective-permute-done.17.refs_2_, ...), custom_call_target="tpu_custom_call" | custom-call | flops 1 | bytes 1 | tf_op jit(solution)/shard_map/lift/pallas_call | solution.py:640
  241.4 17.0 %settle.1 = (bf16[512,1024]{1,0:T(8,128)(2,1)}, f32[512,1024]{1,0:T(8,128)}, bf16[512,1024]{1,0:T(8,128)(2,1)}, f32[3,1024]{1,0:T(4,128)}, bf16[4096,1024]{1,0:T(8,128)(2,1)}) custom-call(s32[4]{0:T(128)} %pad_add_fusion.2.at_ref.refs_0_, bf16[2,4,128,1024]{3,2,1,0:T(8,128)(2,1)} %bitcast.193, bf16[2,4,128,1024]{3,2,1,0:T(8,128)(2,1)} %collective-permute-done.20.refs_2_, ...), custom_call_target="tpu_custom_call" | custom-call | flops 1 | bytes 1 | tf_op jit(solution)/shard_map/settle/pallas_call | solution.py:707
  258.4 12.7 %lift_grads.1 = (bf16[512,2048]{1,0:T(8,128)(2,1)}, bf16[512,2048]{1,0:T(8,128)(2,1)}, f32[1,4096]{1,0:T(1,128)}) custom-call(bf16[512,1024]{1,0:T(8,128)(2,1)} %get-tuple-element.170.glow_ref, bf16[4096,1024]{1,0:T(8,128)(2,1)} %get-tuple-element.171.down_ref, f32[512,4096]{1,0:T(8,128)} %get-tuple-element.172.slope_ref), custom_call_target="tpu_custom_call" | custom-call | flops 1 | bytes 1 | tf_op jit(solution)/shard_map/lift_grads/pallas_call | solution.py:744
  271.7 13.4 %first_grads.1 = (f32[512,1024]{1,0:T(8,128)}, bf16[512,1024]{1,0:T(8,128)(2,1)}, bf16[512,512]{1,0:T(8,128)(2,1)}, bf16[512,512]{1,0:T(8,128)(2,1)}, f32[3,1024]{1,0:T(4,128)}) custom-call(s32[4]{0:T(128)} %pad_add_fusion.2.at_ref.refs_0_, bf16[512,2048]{1,0:T(8,128)(2,1)} %get-tuple-element.173.lift_ref, bf16[512,2048]{1,0:T(8,128)(2,1)} %get-tuple-element.174.lift_send, ...), custom_call_target="tpu_custom_call" | custom-call | flops 1 | bytes 1 | tf_op jit(solution)/shard_map/first_grads/pallas_call | solution.py:834
  285.1 6.2 %pay.1 = (bf16[560,1024]{1,0:T(8,128)(2,1)}, f32[16,512]{1,0:T(8,128)}) custom-call(bf16[512,1024]{1,0:T(8,128)(2,1)} %get-tuple-element.183.branch_ref, bf16[1024,1024]{1,0:T(8,128)(2,1)} %get-tuple-element.154.w_ref, bf16[512,1024]{1,0:T(8,128)(2,1)} %get-tuple-element.153.heads_ref, f32[16,512]{1,0:T(8,128)} %get-tuple-element.184.log_ref), custom_call_target="tpu_custom_call" | custom-call | flops 1 | bytes 1 | tf_op jit(solution)/shard_map/pay/pallas_call | solution.py:879
  291.2 5.1 %collective-permute-start.29 = (bf16[560,1024]{1,0:T(8,128)(2,1)}, bf16[560,1024]{1,0:T(8,128)(2,1)S(1)}, u32[]{:S(2)}, u32[]{:S(2)}) collective-permute-start(bf16[560,1024]{1,0:T(8,128)(2,1)} %get-tuple-element.185.do_ref), channel_id=1, source_target_pairs={{2,0},{4,2},{6,4},{8,6},{10,8},{12,10},{14,12},{16,14},{18,16},{20... | collective-permute-start | bytes 3440648 | tf_op jit(solution)/shard_map/ppermute | solution.py:1045
  299.2 8.6 %down_grads.1 = bf16[2048,1024]{1,0:T(8,128)(2,1)} custom-call(s32[4]{0:T(128)} %pad_add_fusion.2.at_ref.refs_0_, bf16[512,2048]{1,0:T(8,128)(2,1)} %get-tuple-element.163.refs_5_.act_ref, bf16[512,2048]{1,0:T(8,128)(2,1)} %collective-permute-done.38.act_got, bf16[512,1024]{1,0:T(8,128)(2,1)} %get-tuple-element.170.glow_ref, bf16[512,1024]{1,0:T(8,128)(2,1)} %copy-done.21), custom_call_target="tpu_custom_call" | custom-call | flops 1 | bytes 1 | tf_op jit(solution)/shard_map/down_grads/pallas_call | solution.py:784
  309.1 29.4 %own_grads.1 = (bf16[2,512,512]{2,1,0:T(8,128)(2,1)}, f32[2,2,512,512]{3,2,1,0:T(8,128)}, f32[1,1024]{1,0:T(1,128)}) custom-call(bf16[512,3072]{1,0:T(8,128)(2,1)} %get-tuple-element.150.q_ref.ko_ref.vo_ref, bf16[512,3072]{1,0:T(8,128)(2,1)} %get-tuple-element.150.q_ref.ko_ref.vo_ref, bf16[512,3072]{1,0:T(8,128)(2,1)} %get-tuple-element.151.kp_ref.vp_ref.qp_ref, ...), custom_call_target="tpu_custom_call" | custom-call | flops 1 | bytes 1 | tf_op jit(solution)/shard_map/own_grads/pallas_call | solution.py:202
  340.0 12.0 %late_grads.1 = (bf16[256,2560]{1,0:T(8,128)(2,1)}, bf16[256,2560]{1,0:T(8,128)(2,1)}, bf16[256,2560]{1,0:T(8,128)(2,1)}, bf16[256,2560]{1,0:T(8,128)(2,1)}) custom-call(s32[4]{0:T(128)} %pad_add_fusion.2.at_ref.refs_0_, bf16[512,1024]{1,0:T(8,128)(2,1)} %get-tuple-element.161.refs_5_.low_ref, bf16[512,1024]{1,0:T(8,128)(2,1)} %collective-permute-done.25.low_got, ...), custom_call_target="tpu_custom_call" | custom-call | flops 1 | bytes 1 | tf_op jit(solution)/shard_map/late_grads/pallas_call | solution.py:949
  353.4 21.5 %halo_grads.1 = (bf16[3,512,512]{2,1,0:T(8,128)(2,1)}, bf16[3,512,512]{2,1,0:T(8,128)(2,1)}, f32[1,1024]{1,0:T(1,128)}) custom-call(bf16[512,3072]{1,0:T(8,128)(2,1)} %get-tuple-element.150.q_ref.ko_ref.vo_ref, bf16[512,3072]{1,0:T(8,128)(2,1)} %get-tuple-element.150.q_ref.ko_ref.vo_ref, bf16[512,3072]{1,0:T(8,128)(2,1)} %get-tuple-element.151.kp_ref.vp_ref.qp_ref, ...), custom_call_target="tpu_custom_call" | custom-call | flops 1 | bytes 1 | tf_op jit(solution)/shard_map/halo_grads/pallas_call | solution.py:277
  380.4 5.8 %fusion.35 = f32[512,1024]{1,0:T(8,128)S(1)} fusion(bf16[512,3072]{1,0:T(8,128)(2,1)S(1)} %bitcast_dynamic-update-slice_fusion, bf16[1024,3072]{1,0:T(8,128)(2,1)} %get-tuple-element.147.w_ref), kind=kOutput, calls=%fused_computation.145 | convolution fusion | flops 3221225472 | bytes 11534336 | tf_op jit(solution)/shard_map/dot_general | solution.py:32
  393.8 8.3 %qkv_grads.1 = (bf16[256,1664]{1,0:T(8,128)(2,1)}, bf16[256,1664]{1,0:T(8,128)(2,1)}, bf16[256,1664]{1,0:T(8,128)(2,1)}, bf16[256,1664]{1,0:T(8,128)(2,1)}) custom-call(s32[4]{0:T(128)} %pad_add_fusion.2.at_ref.refs_0_, bf16[512,1024]{1,0:T(8,128)(2,1)} %bitcast.178, bf16[512,1024]{1,0:T(8,128)(2,1)} %collective-permute-done.23.x_got, ...), custom_call_target="tpu_custom_call" | custom-call | flops 1 | bytes 1 | tf_op jit(solution)/shard_map/qkv_grads/pallas_call | solution.py:976
  402.1 5.6 %collective-permute-done.34 = bf16[4,32,2560]{2,1,0:T(8,128)(2,1)} collective-permute-done((bf16[4,32,2560]{2,1,0:T(8,128)(2,1)}, bf16[4,32,2560]{2,1,0:T(8,128)(2,1)}, u32[]{:S(2)}, u32[]{:S(2)}) %collective-permute-start.34) | collective-permute-done | bytes 655392 | tf_op jit(solution)/shard_map/ppermute | solution.py:993
  417.2 10.1 %collective-permute-done.36 = bf16[2,4,32,1664]{3,2,1,0:T(8,128)(2,1)} collective-permute-done((bf16[2,4,32,1664]{3,2,1,0:T(8,128)(2,1)}, bf16[2,4,32,1664]{3,2,1,0:T(8,128)(2,1)}, u32[]{:S(2)}, u32[]{:S(2)}) %collective-permute-start.36) | collective-permute-done | bytes 852000 | tf_op jit(solution)/shard_map/ppermute | solution.py:993
  427.7 11.2 %collective-permute-done.40 = bf16[2,128,1024]{2,1,0:T(8,128)(2,1)S(1)} collective-permute-done((bf16[2,128,1024]{2,1,0:T(8,128)(2,1)S(1)}, bf16[2,128,1024]{2,1,0:T(8,128)(2,1)S(1)}, u32[]{:S(2)}, u32[]{:S(2)}) %collective-permute-start.40) | collective-permute-done | bytes 524320 | tf_op jit(solution)/shard_map/ppermute | solution.py:993
  445.1 9.3 %collective-permute-done.43 = bf16[128,1024]{1,0:T(8,128)(2,1)S(1)} collective-permute-done((bf16[128,1024]{1,0:T(8,128)(2,1)S(1)}, bf16[128,1024]{1,0:T(8,128)(2,1)S(1)}, u32[]{:S(2)}, u32[]{:S(2)}) %collective-permute-start.43) | collective-permute-done | bytes 262176 | tf_op jit(solution)/shard_map/ppermute | solution.py:993
  459.6 3.7 collective-permute-start.45
  467.3 18.8 %reduce-scatter.8.cloned.1.call-done = bf16[1,2,32,1664]{3,2,1,0:T(8,128)(2,1)} async-done(((bf16[4,2,32,1664]{3,2,1,0:T(8,128)(2,1)}), bf16[1,2,32,1664]{3,2,1,0:T(8,128)(2,1)}) %reduce-scatter.8.cloned.1.call-update) | async-done | bytes 213008 | tf_op jit(solution)/shard_map/reduce_scatter | solution.py:1175
  (307 shorter events, 106.5 us)
Async XLA Ops:
  7.2 158.2 %all-gather.3.cloned.1.call-start = ((), (), s32[]{:S(2)}) async-start(), calls=%async_computation.6 | async-start | bytes 2621440 | tf_op jit(solution)/shard_map/all_gather | solution.py:1080
  7.2 28.1 %collective-permute-start.2 = (bf16[512,1024]{1,0:T(8,128)(2,1)}, bf16[512,1024]{1,0:T(8,128)(2,1)S(1)}, u32[]{:S(2)}, u32[]{:S(2)}) collective-permute-start(bf16[512,1024]{1,0:T(8,128)(2,1)} %bitcast.175), channel_id=1, source_target_pairs={{0,2},{2,4},{4,6},{6,8},{8,10},{10,12},{12,14},{14,16},{16,18},{18... | collective-permute-start | bytes 3145736 | tf_op jit(solution)/shard_map/ppermute | solution.py:1042
  35.3 42.1 %collective-permute-start.5 = (bf16[512,1024]{1,0:T(8,128)(2,1)S(1)}, bf16[512,1024]{1,0:T(8,128)(2,1)}, u32[]{:S(2)}, u32[]{:S(2)}) collective-permute-start(bf16[512,1024]{1,0:T(8,128)(2,1)S(1)} %bitcast.179), channel_id=1, source_target_pairs={{2,0},{4,2},{6,4},{8,6},{10,8},{12,10},{14,12},{16,14},{18,16},{20... | collective-permute-start | bytes 3145736 | tf_op jit(solution)/shard_map/ppermute | solution.py:1045
  44.3 32.8 %collective-permute-start.3 = (bf16[2,2,32,2176]{3,2,1,0:T(8,128)(2,1)S(1)}, bf16[2,2,32,2176]{3,2,1,0:T(8,128)(2,1)S(1)}, u32[]{:S(2)}, u32[]{:S(2)}) collective-permute-start(bf16[2,2,32,2176]{3,2,1,0:T(8,128)(2,1)S(1)} %pad_maximum_fusion.8), channel_id=1, source_target_pairs={{0,8},{8,0},{16,24},{24,16},{1,9},{9,1},{17,25},{25,17},{2,10},{10... | collective-permute-start | bytes 1671176 | tf_op jit(solution)/shard_map/ppermute | solution.py:997
  92.4 25.5 %collective-permute-start.9 = (bf16[2,4,32,2176]{3,2,1,0:T(8,128)(2,1)S(1)}, bf16[2,4,32,2176]{3,2,1,0:T(8,128)(2,1)}, u32[]{:S(2)}, u32[]{:S(2)}) collective-permute-start(bf16[2,4,32,2176]{3,2,1,0:T(8,128)(2,1)S(1)} %pad_maximum_fusion.3.refs_1_), channel_id=1, source_target_pairs={{0,2},{2,0},{1,3},{3,1},{4,6},{6,4},{5,7},{7,5},{8,10},{10,8},{9,1... | collective-permute-start | bytes 3342344 | tf_op jit(solution)/shard_map/ppermute | solution.py:993
  94.6 24.6 %collective-permute-start.10 = (bf16[2,4,32,2176]{3,2,1,0:T(8,128)(2,1)S(1)}, bf16[2,4,32,2176]{3,2,1,0:T(8,128)(2,1)S(1)}, u32[]{:S(2)}, u32[]{:S(2)}) collective-permute-start(bf16[2,4,32,2176]{3,2,1,0:T(8,128)(2,1)S(1)} %pad_maximum_fusion.5.refs_3_), channel_id=1, source_target_pairs={{0,4},{4,0},{1,5},{5,1},{2,6},{6,2},{3,7},{7,3},{8,12},{12,8},{9,1... | collective-permute-start | bytes 3342344 | tf_op jit(solution)/shard_map/ppermute | solution.py:993
  95.7 28.4 %collective-permute-start.12 = (bf16[2,4,32,2176]{3,2,1,0:T(8,128)(2,1)S(1)}, bf16[2,4,32,2176]{3,2,1,0:T(8,128)(2,1)}, u32[]{:S(2)}, u32[]{:S(2)}) collective-permute-start(bf16[2,4,32,2176]{3,2,1,0:T(8,128)(2,1)S(1)} %pad_maximum_fusion.3.refs_1_), channel_id=1, source_target_pairs={{0,1},{1,0},{2,3},{3,2},{4,5},{5,4},{6,7},{7,6},{8,9},{9,8},{10,11... | collective-permute-start | bytes 3342344 | tf_op jit(solution)/shard_map/ppermute | solution.py:993
  122.7 290.7 %reduce-scatter.4.cloned.1.call-start = ((), (), s32[]{:S(2)}) async-start(), calls=%async_computation.3 | async-start | bytes 5242880 | tf_op jit(solution)/shard_map/reduce_scatter | solution.py:1133
  126.3 24.4 %collective-permute-start.16 = (bf16[4,64,2048]{2,1,0:T(8,128)(2,1)S(1)}, bf16[4,64,2048]{2,1,0:T(8,128)(2,1)}, u32[]{:S(2)}, u32[]{:S(2)}) collective-permute-start(bf16[4,64,2048]{2,1,0:T(8,128)(2,1)S(1)} %bitcast.182), channel_id=1, source_target_pairs={{0,4},{4,0},{1,5},{5,1},{2,6},{6,2},{3,7},{7,3},{8,12},{12,8},{9,1... | collective-permute-start | bytes 3145736 | tf_op jit(solution)/shard_map/ppermute | solution.py:993
  153.5 47.7 %collective-permute-start.18 = (bf16[2,4,64,2048]{3,2,1,0:T(8,128)(2,1)}, bf16[2,4,64,2048]{3,2,1,0:T(8,128)(2,1)}, u32[]{:S(2)}, u32[]{:S(2)}) collective-permute-start(bf16[2,4,64,2048]{3,2,1,0:T(8,128)(2,1)} %pad_maximum_fusion.refs_1_), channel_id=1, source_target_pairs={{0,1},{1,0},{2,3},{3,2},{4,5},{5,4},{6,7},{7,6},{8,9},{9,8},{10,11... | collective-permute-start | bytes 6291464 | tf_op jit(solution)/shard_map/ppermute | solution.py:993
  154.9 47.6 %collective-permute-start.17 = (bf16[2,4,64,2048]{3,2,1,0:T(8,128)(2,1)}, bf16[2,4,64,2048]{3,2,1,0:T(8,128)(2,1)}, u32[]{:S(2)}, u32[]{:S(2)}) collective-permute-start(bf16[2,4,64,2048]{3,2,1,0:T(8,128)(2,1)} %pad_maximum_fusion.refs_1_), channel_id=1, source_target_pairs={{0,2},{2,0},{1,3},{3,1},{4,6},{6,4},{5,7},{7,5},{8,10},{10,8},{9,1... | collective-permute-start | bytes 6291464 | tf_op jit(solution)/shard_map/ppermute | solution.py:993
  165.4 47.1 %collective-permute-start.20 = (bf16[2,4,128,1024]{3,2,1,0:T(8,128)(2,1)}, bf16[2,4,128,1024]{3,2,1,0:T(8,128)(2,1)}, u32[]{:S(2)}, u32[]{:S(2)}) collective-permute-start(bf16[2,4,128,1024]{3,2,1,0:T(8,128)(2,1)} %bitcast.191), channel_id=1, source_target_pairs={{0,4},{4,0},{1,5},{5,1},{2,6},{6,2},{3,7},{7,3},{8,12},{12,8},{9,1... | collective-permute-start | bytes 6291464 | tf_op jit(solution)/shard_map/ppermute | solution.py:993
  166.6 45.9 %collective-permute-start.19 = (bf16[2,4,128,1024]{3,2,1,0:T(8,128)(2,1)}, bf16[2,4,128,1024]{3,2,1,0:T(8,128)(2,1)}, u32[]{:S(2)}, u32[]{:S(2)}) collective-permute-start(bf16[2,4,128,1024]{3,2,1,0:T(8,128)(2,1)} %bitcast.192), channel_id=1, source_target_pairs={{0,1},{1,0},{2,3},{3,2},{4,5},{5,4},{6,7},{7,6},{8,9},{9,8},{10,11... | collective-permute-start | bytes 6291464 | tf_op jit(solution)/shard_map/ppermute | solution.py:993
  213.8 27.6 %collective-permute-start.21 = (bf16[2,4,128,1024]{3,2,1,0:T(8,128)(2,1)}, bf16[2,4,128,1024]{3,2,1,0:T(8,128)(2,1)}, u32[]{:S(2)}, u32[]{:S(2)}) collective-permute-start(bf16[2,4,128,1024]{3,2,1,0:T(8,128)(2,1)} %collective-permute-done.20.refs_2_), channel_id=1, source_target_pairs={{0,1},{1,0},{2,3},{3,2},{4,5},{5,4},{6,7},{7,6},{8,9},{9,8},{10,11... | collective-permute-start | bytes 6291464 | tf_op jit(solution)/shard_map/ppermute | solution.py:993
  213.8 27.6 %collective-permute-start.23 = (bf16[512,1024]{1,0:T(8,128)(2,1)S(1)}, bf16[512,1024]{1,0:T(8,128)(2,1)}, u32[]{:S(2)}, u32[]{:S(2)}) collective-permute-start(bf16[512,1024]{1,0:T(8,128)(2,1)S(1)} %bitcast.180), channel_id=1, source_target_pairs={{0,1},{1,0},{2,3},{3,2},{4,5},{5,4},{6,7},{7,6},{8,9},{9,8},{10,11... | collective-permute-start | bytes 3145736 | tf_op jit(solution)/shard_map/ppermute | solution.py:993
  214.3 27.0 %collective-permute-start.24 = (bf16[512,1024]{1,0:T(8,128)(2,1)S(1)}, bf16[512,1024]{1,0:T(8,128)(2,1)S(1)}, u32[]{:S(2)}, u32[]{:S(2)}) collective-permute-start(bf16[512,1024]{1,0:T(8,128)(2,1)S(1)} %copy-done.4), channel_id=1, source_target_pairs={{0,1},{1,0},{2,3},{3,2},{4,5},{5,4},{6,7},{7,6},{8,9},{9,8},{10,11... | collective-permute-start | bytes 3145736 | tf_op jit(solution)/shard_map/ppermute | solution.py:993
  214.4 27.0 %collective-permute-start.25 = (bf16[512,1024]{1,0:T(8,128)(2,1)}, bf16[512,1024]{1,0:T(8,128)(2,1)}, u32[]{:S(2)}, u32[]{:S(2)}) collective-permute-start(bf16[512,1024]{1,0:T(8,128)(2,1)} %get-tuple-element.161.refs_5_.low_ref), channel_id=1, source_target_pairs={{0,1},{1,0},{2,3},{3,2},{4,5},{5,4},{6,7},{7,6},{8,9},{9,8},{10,11... | collective-permute-start | bytes 3145736 | tf_op jit(solution)/shard_map/ppermute | solution.py:993
  240.0 58.2 %collective-permute-start.38 = (bf16[512,2048]{1,0:T(8,128)(2,1)}, bf16[512,2048]{1,0:T(8,128)(2,1)}, u32[]{:S(2)}, u32[]{:S(2)}) collective-permute-start(bf16[512,2048]{1,0:T(8,128)(2,1)} %get-tuple-element.164.refs_6_), channel_id=1, source_target_pairs={{0,1},{1,0},{2,3},{3,2},{4,5},{5,4},{6,7},{7,6},{8,9},{9,8},{10,11... | collective-permute-start | bytes 6291464 | tf_op jit(solution)/shard_map/ppermute | solution.py:993
  271.2 68.0 %collective-permute-start.26 = (bf16[512,2048]{1,0:T(8,128)(2,1)}, bf16[512,2048]{1,0:T(8,128)(2,1)}, u32[]{:S(2)}, u32[]{:S(2)}) collective-permute-start(bf16[512,2048]{1,0:T(8,128)(2,1)} %get-tuple-element.174.lift_send), channel_id=1, source_target_pairs={{0,1},{1,0},{2,3},{3,2},{4,5},{5,4},{6,7},{7,6},{8,9},{9,8},{10,11... | collective-permute-start | bytes 6291464 | tf_op jit(solution)/shard_map/ppermute | solution.py:993
  271.3 27.0 %collective-permute-start.39 = (bf16[512,1024]{1,0:T(8,128)(2,1)S(1)}, bf16[512,1024]{1,0:T(8,128)(2,1)S(1)}, u32[]{:S(2)}, u32[]{:S(2)}) collective-permute-start(bf16[512,1024]{1,0:T(8,128)(2,1)S(1)} %copy-done.8), channel_id=1, source_target_pairs={{0,1},{1,0},{2,3},{3,2},{4,5},{5,4},{6,7},{7,6},{8,9},{9,8},{10,11... | collective-permute-start | bytes 3145736 | tf_op jit(solution)/shard_map/ppermute | solution.py:993
  291.2 60.7 %collective-permute-start.29 = (bf16[560,1024]{1,0:T(8,128)(2,1)}, bf16[560,1024]{1,0:T(8,128)(2,1)S(1)}, u32[]{:S(2)}, u32[]{:S(2)}) collective-permute-start(bf16[560,1024]{1,0:T(8,128)(2,1)} %get-tuple-element.185.do_ref), channel_id=1, source_target_pairs={{2,0},{4,2},{6,4},{8,6},{10,8},{12,10},{14,12},{16,14},{18,16},{20... | collective-permute-start | bytes 3440648 | tf_op jit(solution)/shard_map/ppermute | solution.py:1045
  296.3 55.7 %collective-permute-start.28 = (bf16[560,1024]{1,0:T(8,128)(2,1)}, bf16[560,1024]{1,0:T(8,128)(2,1)S(1)}, u32[]{:S(2)}, u32[]{:S(2)}) collective-permute-start(bf16[560,1024]{1,0:T(8,128)(2,1)} %get-tuple-element.185.do_ref), channel_id=1, source_target_pairs={{0,2},{2,4},{4,6},{6,8},{8,10},{10,12},{12,14},{14,16},{16,18},{18... | collective-permute-start | bytes 3440648 | tf_op jit(solution)/shard_map/ppermute | solution.py:1042
  307.8 148.0 %reduce-scatter.6.cloned.1.call-start = ((), (), s32[]{:S(2)}) async-start(), calls=%async_computation.4 | async-start | bytes 1638400 | tf_op jit(solution)/shard_map/reduce_scatter | solution.py:1167
  308.6 30.6 %collective-permute-start.27 = (bf16[512,512]{1,0:T(8,128)(2,1)}, bf16[512,512]{1,0:T(8,128)(2,1)S(1)}, u32[]{:S(2)}, u32[]{:S(2)}) collective-permute-start(bf16[512,512]{1,0:T(8,128)(2,1)} %get-tuple-element.180), channel_id=1, source_target_pairs={{0,1},{1,0},{2,3},{3,2},{4,5},{5,4},{6,7},{7,6},{8,9},{9,8},{10,11... | collective-permute-start | bytes 1572872 | tf_op jit(solution)/shard_map/ppermute | solution.py:993
  352.0 34.3 %collective-permute-start.31 = (bf16[2,4,32,2560]{3,2,1,0:T(8,128)(2,1)}, bf16[2,4,32,2560]{3,2,1,0:T(8,128)(2,1)}, u32[]{:S(2)}, u32[]{:S(2)}) collective-permute-start(bf16[2,4,32,2560]{3,2,1,0:T(8,128)(2,1)} %bitcast.236), channel_id=1, source_target_pairs={{0,2},{2,0},{1,3},{3,1},{4,6},{6,4},{5,7},{7,5},{8,10},{10,8},{9,1... | collective-permute-start | bytes 3932168 | tf_op jit(solution)/shard_map/ppermute | solution.py:993
  352.7 33.6 %collective-permute-start.32 = (bf16[2,4,32,2560]{3,2,1,0:T(8,128)(2,1)}, bf16[2,4,32,2560]{3,2,1,0:T(8,128)(2,1)}, u32[]{:S(2)}, u32[]{:S(2)}) collective-permute-start(bf16[2,4,32,2560]{3,2,1,0:T(8,128)(2,1)} %bitcast.235), channel_id=1, source_target_pairs={{0,4},{4,0},{1,5},{5,1},{2,6},{6,2},{3,7},{7,3},{8,12},{12,8},{9,1... | collective-permute-start | bytes 3932168 | tf_op jit(solution)/shard_map/ppermute | solution.py:993
  376.3 16.7 %collective-permute-start.33 = (f32[16,384]{1,0:T(8,128)S(1)}, f32[16,384]{1,0:T(8,128)S(1)}, u32[]{:S(2)}, u32[]{:S(2)}) collective-permute-start(f32[16,384]{1,0:T(8,128)S(1)} %pad_maximum_fusion.11), channel_id=1, source_target_pairs={{0,1},{1,0},{2,3},{3,2},{4,5},{5,4},{6,7},{7,6},{8,9},{9,8},{10,11... | collective-permute-start | bytes 73736 | tf_op jit(solution)/shard_map/ppermute | solution.py:993
  391.1 16.6 %collective-permute-start.34 = (bf16[4,32,2560]{2,1,0:T(8,128)(2,1)}, bf16[4,32,2560]{2,1,0:T(8,128)(2,1)}, u32[]{:S(2)}, u32[]{:S(2)}) collective-permute-start(bf16[4,32,2560]{2,1,0:T(8,128)(2,1)} %fusion.7), channel_id=1, source_target_pairs={{0,4},{4,0},{1,5},{5,1},{2,6},{6,2},{3,7},{7,3},{8,12},{12,8},{9,1... | collective-permute-start | bytes 1966088 | tf_op jit(solution)/shard_map/ppermute | solution.py:993
  408.1 19.2 %collective-permute-start.36 = (bf16[2,4,32,1664]{3,2,1,0:T(8,128)(2,1)}, bf16[2,4,32,1664]{3,2,1,0:T(8,128)(2,1)}, u32[]{:S(2)}, u32[]{:S(2)}) collective-permute-start(bf16[2,4,32,1664]{3,2,1,0:T(8,128)(2,1)} %bitcast.239), channel_id=1, source_target_pairs={{0,2},{2,0},{1,3},{3,1},{4,6},{6,4},{5,7},{7,5},{8,10},{10,8},{9,1... | collective-permute-start | bytes 2555912 | tf_op jit(solution)/shard_map/ppermute | solution.py:993
  408.8 18.9 %collective-permute-start.37 = (bf16[2,4,32,1664]{3,2,1,0:T(8,128)(2,1)}, bf16[2,4,32,1664]{3,2,1,0:T(8,128)(2,1)}, u32[]{:S(2)}, u32[]{:S(2)}) collective-permute-start(bf16[2,4,32,1664]{3,2,1,0:T(8,128)(2,1)} %bitcast.238), channel_id=1, source_target_pairs={{0,4},{4,0},{1,5},{5,1},{2,6},{6,2},{3,7},{7,3},{8,12},{12,8},{9,1... | collective-permute-start | bytes 2555912 | tf_op jit(solution)/shard_map/ppermute | solution.py:993
  413.5 72.6 %reduce-scatter.8.cloned.1.call-start = ((), (), s32[]{:S(2)}) async-start(), calls=%async_computation.5 | async-start | bytes 1064960 | tf_op jit(solution)/shard_map/reduce_scatter | solution.py:1175
  414.7 24.3 %collective-permute-start.40 = (bf16[2,128,1024]{2,1,0:T(8,128)(2,1)S(1)}, bf16[2,128,1024]{2,1,0:T(8,128)(2,1)S(1)}, u32[]{:S(2)}, u32[]{:S(2)}) collective-permute-start(bf16[2,128,1024]{2,1,0:T(8,128)(2,1)S(1)} %slice_bitcast_fusion), channel_id=1, source_target_pairs={{0,4},{4,0},{1,5},{5,1},{2,6},{6,2},{3,7},{7,3},{8,12},{12,8},{9,1... | collective-permute-start | bytes 1572872 | tf_op jit(solution)/shard_map/ppermute | solution.py:993
  (56 other events, 589.4 us)
Sparse Core Ops, SparseCore 0:
  122.8 42.5 all-gather.2
  308.0 82.9 reduce-scatter.3
  413.6 31.7 reduce-scatter.5
  459.6 26.3 reduce-scatter.7

commit v3 on v2

--- a/solution.py
+++ b/solution.py
@@ -11,7 +11,8 @@
 HD = 64
 WINDOW = 1024
 HALF = WINDOW // 2
-ROWS = 128
+ROWS = 256
+NARROW = 128
 PAIR = 2 * HD
 FILL = -1e30
 EPS = 1e-05
@@ -40,8 +41,8 @@
     return jnp.concatenate(parts, axis=axis)
 
 
-def cost():
-    return pl.CostEstimate(flops=1, bytes_accessed=1, transcendentals=0)
+def cost(us):
+    return pl.CostEstimate(flops=int(us * 1.0e9), bytes_accessed=int(us * 3.5e6), transcendentals=0)
 
 
 def params():
@@ -59,17 +60,13 @@
     return cat([values * masks[0], values * masks[1]], 0)
 
 
-def strip(i, tokens):
-    return slice(ROWS * i, ROWS * i + tokens + ROWS)
+def strip(i, tokens, rows=ROWS):
+    return slice(rows * i, rows * i + tokens + rows)
 
 
 def put_rows(ref, cols, pair):
     head = lax.broadcasted_iota(jnp.int32, (H, 1), 0) - 2 * pl.program_id(0)
     ref[:, cols] = jnp.where(head == 0, pair[0], jnp.where(head == 1, pair[1], ref[:, cols]))
-
-
-def far_first(p, pairs):
-    return lax.rem(p + pairs // 2, pairs)
 
 
 def take_row(values, h, pair=None):
@@ -128,7 +125,7 @@
         out_shape=[jax.ShapeDtypeStruct((tokens, width), BF16), jax.ShapeDtypeStruct((H, tokens), F32)],
         scratch_shapes=[pltpu.VMEM((2 * tokens, PAIR), BF16), pltpu.VMEM((2 * tokens, PAIR), BF16)],
         compiler_params=params(),
-        cost_estimate=cost(),
+        cost_estimate=cost(0.48),
         name="attend",
     )(mixed, mixed, before, after, mixed, before, after, bias_own, bias_halo)
 
@@ -146,7 +143,7 @@
     k_pair = stacked(k_own, scaled)
     log_rows = [take_row(log_ref[...], h) for h in range(2)]
     mean_rows = [take_row(mean_ref[...], h) for h in range(2)]
-    chunk = 2 * ROWS
+    chunk = ROWS
     for c in range(tokens // chunk):
         cols = slice(chunk * c, chunk * c + chunk)
         q = q_ref[cols]
@@ -215,12 +212,12 @@
         ],
         scratch_shapes=[pltpu.VMEM((2 * tokens, PAIR), BF16), pltpu.VMEM((2 * tokens, PAIR), BF16)],
         compiler_params=params(),
-        cost_estimate=cost(),
+        cost_estimate=cost(29.5),
         name="own_grads",
     )(mixed, mixed, before, after, mixed, before, after, payload, logs, means, bias_own, bias_halo)
 
 
-def halo_grad_kernel(ko_ref, vo_ref, qp_ref, qn_ref, dp_ref, dn_ref, lp0, lp1, lp2, ln0, ln1, ln2, bh_ref, dq_in, dkv_in, keep_ref, send_ref, sum_ref, qh, dh, lh, made):
+def halo_grad_kernel(half, ko_ref, vo_ref, qp_ref, qn_ref, dp_ref, dn_ref, lp0, lp1, lp2, ln0, ln1, ln2, bh_ref, dkv_in, dk_ref, dv_ref, sum_ref, qh, dh, lh):
     tokens = ko_ref.shape[0]
     qh[:tokens] = qp_ref[...]
     qh[tokens:] = qn_ref[...]
@@ -229,14 +226,14 @@
     for first, refs in ((0, (lp0, lp1, lp2)), (tokens, (ln0, ln1, ln2))):
         table = refs[0][...].astype(F32) + refs[1][...].astype(F32) + refs[2][...].astype(F32)
         for h in range(2):
-            row = take_row(table, h, far_first(pl.program_id(0), pl.num_programs(0)))
+            row = take_row(table, h, pl.program_id(0) + half * pl.num_programs(0))
             lh[0, h : h + 1, first : first + tokens] = row[:, :tokens]
             lh[1, h : h + 1, first : first + tokens] = row[:, tokens:]
     ones = head_masks(1.0)
     scaled = head_masks(HD ** -0.5)
-    for j in range(tokens // ROWS):
-        rows = slice(ROWS * j, ROWS * j + ROWS)
-        window = strip(j, tokens)
+    for j in range(tokens // NARROW):
+        rows = slice(NARROW * j, NARROW * j + NARROW)
+        window = strip(j, tokens, NARROW)
         q = qh[window]
         do = dh[window]
         k = ko_ref[rows]
@@ -252,48 +249,39 @@
             grads.append(gt.astype(BF16))
             qs.append(qm)
             dos.append(dm)
-        made[1, rows] = (dkv_in[0, 0, rows] + nn(cat(grads, 1), cat(qs, 0))).astype(BF16)
+        dk_ref[rows] = (dkv_in[0, 0, rows] + nn(cat(grads, 1), cat(qs, 0))).astype(BF16)
         dv = (dkv_in[0, 1, rows] + nn(cat(probs, 1), cat(dos, 0))).astype(BF16)
-        made[2, rows] = dv
+        dv_ref[rows] = dv
         sum_ref[...] = column_sum(dv.astype(F32)) + (sum_ref[...] if j else 0.0)
-    made[0] = dq_in[0]
-    put_half(pl.program_id(0), pl.num_programs(0), send_ref, keep_ref, made[...])
-
-
-def halo_grads(mixed, before, after, grad_before, grad_after, bias_halo, dq, dkv):
+
+
+def halo_grads(mixed, before, after, grad_before, grad_after, bias_halo, dkv, half):
     tokens, width = dkv.shape[2], 2 * dkv.shape[3]
-    pairs = width // PAIR
-    near = pairs // 2
+    near = width // PAIR // 2
 
     def column(part):
-        return pl.BlockSpec((tokens, PAIR), lambda p: (0, (far_first(p, pairs) // near * 3 + part) * near + p % near))
+        return pl.BlockSpec((tokens, PAIR), lambda p: (0, (half * 3 + part) * near + p))
 
     whole = lambda shape: pl.BlockSpec(shape, lambda p: (0,) * len(shape))
-    both = pl.BlockSpec((1, 2, tokens, PAIR), lambda p: (far_first(p, pairs) // near, 0, 0, p % near))
-    one = pl.BlockSpec((1, tokens, PAIR), lambda p: (far_first(p, pairs) // near, 0, p % near))
+    both = pl.BlockSpec((1, 2, tokens, PAIR), lambda p: (half, 0, 0, p))
     tables = [pl.BlockSpec((H, width), lambda p, k=k: (tokens // H + k, 0)) for k in range(3)]
-    block = pl.BlockSpec((tokens, PAIR), lambda p: (0, far_first(p, pairs)))
-    half = jax.ShapeDtypeStruct((3, tokens, width // 2), BF16)
+    block = pl.BlockSpec((tokens, PAIR), lambda p: (0, half * near + p))
+    made = pl.BlockSpec((tokens, PAIR), lambda p: (0, p))
     return pl.pallas_call(
-        halo_grad_kernel,
-        grid=(pairs,),
-        in_specs=[column(1), column(2), column(0), column(0), block, block] + tables + tables + [whole(bias_halo.shape), one, both],
-        out_specs=[
-            pl.BlockSpec((3, tokens, PAIR), lambda p: (0, 0, jnp.maximum(p - near, 0))),
-            pl.BlockSpec((3, tokens, PAIR), lambda p: (0, 0, jnp.minimum(p, near - 1))),
-            pl.BlockSpec((1, PAIR), lambda p: (0, far_first(p, pairs))),
-        ],
-        out_shape=[half, half, jax.ShapeDtypeStruct((1, width), F32)],
+        functools.partial(halo_grad_kernel, half),
+        grid=(near,),
+        in_specs=[column(1), column(2), column(0), column(0), block, block] + tables + tables + [whole(bias_halo.shape), both],
+        out_specs=[made, made, pl.BlockSpec((1, PAIR), lambda p: (0, p))],
+        out_shape=[jax.ShapeDtypeStruct((tokens, width // 2), BF16)] * 2 + [jax.ShapeDtypeStruct((1, width // 2), F32)],
         scratch_shapes=[
             pltpu.VMEM((2 * tokens, PAIR), BF16),
             pltpu.VMEM((2 * tokens, PAIR), BF16),
             pltpu.VMEM((2, 2, 2 * tokens), F32),
-            pltpu.VMEM((3, tokens, PAIR), BF16),
         ],
         compiler_params=params(),
-        cost_estimate=cost(),
+        cost_estimate=cost(0.05),
         name="halo_grads",
-    )(mixed, mixed, before, after, grad_before, grad_after, *[grad_before] * 3, *[grad_after] * 3, bias_halo, dq, dkv)
+    )(mixed, mixed, before, after, grad_before, grad_after, *[grad_before] * 3, *[grad_after] * 3, bias_halo, dkv)
 
 
 def mask_biases(segments, place, blocks, tokens):
@@ -306,8 +294,8 @@
     halo_at = cat([at - tokens, at + tokens], 0)
     allowed = (own[:, None] == halo[None, :]) & (jnp.abs(halo_at[None, :] - at[:, None]) < HALF)
     bias = jnp.where(allowed, 0.0, FILL).astype(F32)
-    bias_halo = jnp.stack([bias[ROWS * i : ROWS * i + ROWS, strip(i, tokens)] for i in range(tokens // ROWS)])
-    return bias_own, bias_halo
+    strips = [jnp.stack([bias[r * i : r * i + r, strip(i, tokens, r)] for i in range(tokens // r)]) for r in (ROWS, NARROW)]
+    return bias_own, *strips
 
 
 def normalized(values):
@@ -383,7 +371,7 @@
         in_specs=[SMEM] + [VMEM] * (3 + len(vectors)),
         out_shape=[half, half, jax.ShapeDtypeStruct((rows, 128), BF16)],
         compiler_params=params(),
-        cost_estimate=cost(),
+        cost_estimate=cost(0.04),
         name="prepare",
     )(at, qkv, out, up, *[v[None] for v in vectors])
 
@@ -417,7 +405,7 @@
             jax.ShapeDtypeStruct((2 * rows, hidden // 2), BF16),
         ],
         compiler_params=params(),
-        cost_estimate=cost(),
+        cost_estimate=cost(0.04),
         name="arrange",
     )(at, mine, got, note)
 
@@ -455,21 +443,20 @@
 def project_kernel(far, parts, *refs):
     at_ref, refs = refs[0], refs[1:]
     part_refs, refs = refs[:parts], refs[parts:]
-    own_ref, before_ref, row_ref, own_out, before_out, qkv_out, out_out, qkv, out, sems, out_sems = refs
+    own_ref, row_ref, own_out, qkv_out, out_out, qkv, out, sems, out_sems = refs
     copies = first_copies(part_refs, qkv, out, sems, at_ref, far)
     start_all(copies)
     wait_all(copies)
     keep = [pltpu.make_async_copy(qkv, qkv_out, out_sems.at[0]), pltpu.make_async_copy(out, out_out, out_sems.at[1])]
     start_all(keep)
     chunk = 512
-    for source, target in ((own_ref, own_out), (before_ref, before_out)):
-
-        def body(j, carry, source=source, target=target):
-            cols = pl.ds(pl.multiple_of(j * chunk, chunk), chunk)
-            target[:, cols] = (nn(source[...], qkv[:, cols]) + row_ref[:, cols]).astype(BF16)
-            return carry
-
-        lax.fori_loop(0, qkv.shape[1] // chunk, body, 0)
+
+    def body(j, carry):
+        cols = pl.ds(pl.multiple_of(j * chunk, chunk), chunk)
+        own_out[:, cols] = (nn(own_ref[...], qkv[:, cols]) + row_ref[:, cols]).astype(BF16)
+        return carry
+
+    lax.fori_loop(0, qkv.shape[1] // chunk, body, 0)
     wait_all(keep)
 
 
@@ -477,15 +464,15 @@
     return 2 if far is None else 8 * far * each
 
 
-def project(far, at, parts, x, before, row):
+def project(far, at, parts, x, row):
     tokens, width = x.shape
     columns = row.shape[1]
     mixed = jax.ShapeDtypeStruct((tokens, columns), BF16)
     return pl.pallas_call(
         functools.partial(project_kernel, far, len(parts)),
-        in_specs=[SMEM] + [ANY] * len(parts) + [VMEM] * 3,
-        out_specs=[VMEM, VMEM, ANY, ANY],
-        out_shape=[mixed, mixed, jax.ShapeDtypeStruct((width, columns), BF16), jax.ShapeDtypeStruct((width, width), BF16)],
+        in_specs=[SMEM] + [ANY] * len(parts) + [VMEM] * 2,
+        out_specs=[VMEM, ANY, ANY],
+        out_shape=[mixed, jax.ShapeDtypeStruct((width, columns), BF16), jax.ShapeDtypeStruct((width, width), BF16)],
         scratch_shapes=[
             pltpu.VMEM((width, columns), BF16),
             pltpu.VMEM((width, width), BF16),
@@ -493,42 +480,39 @@
             pltpu.SemaphoreType.DMA((2,)),
         ],
         compiler_params=params(),
-        cost_estimate=cost(),
+        cost_estimate=cost(0.26),
         name="project",
-    )(at, *parts, x, before, row)
-
-
-def project_more_kernel(x_ref, w_ref, row_ref, out_ref):
-    out_ref[...] = (nn(x_ref[...], w_ref[...]) + row_ref[...]).astype(BF16)
-
-
-def project_more(x, full, row, chunk=512):
-    tokens, width = x.shape
+    )(at, *parts, x, row)
+
+
+def project_more_kernel(before_ref, after_ref, w_ref, row_ref, before_out, after_out):
+    for source, target in ((before_ref, before_out), (after_ref, after_out)):
+        target[...] = (nn(source[...], w_ref[...]) + row_ref[...]).astype(BF16)
+
+
+def project_more(before, after, full, row, chunk=512):
+    tokens, width = before.shape
     columns = full.shape[1]
+    whole = pl.BlockSpec((tokens, width), lambda i: (0, 0))
+    block = pl.BlockSpec((tokens, chunk), lambda i: (0, i))
     return pl.pallas_call(
         project_more_kernel,
         grid=(columns // chunk,),
-        in_specs=[
-            pl.BlockSpec((tokens, width), lambda i: (0, 0)),
-            pl.BlockSpec((width, chunk), lambda i: (0, i)),
-            pl.BlockSpec((1, chunk), lambda i: (0, i)),
-        ],
-        out_specs=pl.BlockSpec((tokens, chunk), lambda i: (0, i)),
-        out_shape=jax.ShapeDtypeStruct((tokens, columns), BF16),
+        in_specs=[whole, whole, pl.BlockSpec((width, chunk), lambda i: (0, i)), pl.BlockSpec((1, chunk), lambda i: (0, i))],
+        out_specs=[block, block],
+        out_shape=[jax.ShapeDtypeStruct((tokens, columns), BF16)] * 2,
         compiler_params=params(),
-        cost_estimate=cost(),
+        cost_estimate=cost(0.214),
         name="project_more",
-    )(x, full, row)
-
-
-def out_kernel(heads_ref, w_ref, x_ref, vec_ref, hat_ref, inv_ref, first_ref, low_ref):
+    )(before, after, full, row)
+
+
+def out_kernel(heads_ref, w_ref, x_ref, vec_ref, hat_ref, inv_ref, low_ref):
     branch = nn(heads_ref[...], w_ref[...]) + vec_ref[0:1]
     hat, inverse = normalized(x_ref[...].astype(F32) + branch)
-    first = hat * vec_ref[1:2] + vec_ref[2:3]
     hat_ref[...] = hat
     inv_ref[...] = inverse
-    first_ref[...] = first
-    low_ref[...] = first.astype(BF16)
+    low_ref[...] = (hat * vec_ref[1:2] + vec_ref[2:3]).astype(BF16)
 
 
 def out_project(heads, out_full, x, vectors):
@@ -539,15 +523,14 @@
         out_kernel,
         grid=(2,),
         in_specs=[block, pl.BlockSpec(out_full.shape, lambda i: (0, 0)), block, pl.BlockSpec(vectors.shape, lambda i: (0, 0))],
-        out_specs=[block, pl.BlockSpec((rows, 1), lambda i: (i, 0)), block, block],
+        out_specs=[block, pl.BlockSpec((rows, 1), lambda i: (i, 0)), block],
         out_shape=[
             jax.ShapeDtypeStruct((tokens, width), F32),
             jax.ShapeDtypeStruct((tokens, 1), F32),
-            jax.ShapeDtypeStruct((tokens, width), F32),
             jax.ShapeDtypeStruct((tokens, width), BF16),
         ],
         compiler_params=params(),
-        cost_estimate=cost(),
+        cost_estimate=cost(0.114),
         name="out_project",
     )(heads, out_full, x, vectors)
 
@@ -585,176 +568,186 @@
     return copies
 
 
-def put_half(step, steps, keep_ref, send_ref, value):
-    @pl.when(step < steps // 2)
-    def _():
-        keep_ref[...] = value
-
-    @pl.when(step >= steps // 2)
-    def _():
-        send_ref[...] = value
-
-
-def take_half(step, steps, keep_ref, send_ref):
-    return jnp.where(step < steps // 2, keep_ref[...], send_ref[...])
-
-
-def half_blocks(rows, chunk, steps):
-    last = steps // 2 - 1
-    return [
-        pl.BlockSpec((rows, chunk), lambda i: (0, jnp.minimum(i, last))),
-        pl.BlockSpec((rows, chunk), lambda i: (0, jnp.maximum(i - last - 1, 0))),
-    ]
-
-
-def lift_kernel(far, parts, *refs):
+def middle_kernel(far, ups, downs, *refs):
     at_ref, refs = refs[0], refs[1:]
-    part_refs, refs = refs[:parts], refs[parts:]
-    low_ref, row_ref, act_ref, act_send, slope_ref, full_out, full, sems, out_sem = refs
-    step = pl.program_id(0)
-    chunk = act_ref.shape[1]
-    copies = up_copies(part_refs, full, sems, at_ref, far)
-    keep = pltpu.make_async_copy(full, full_out, out_sem)
-
-    @pl.when(step == 0)
-    def _():
-        start_all(copies)
-        wait_all(copies)
-        keep.start()
-
-    lifted = nn(low_ref[...], full[:, pl.ds(pl.multiple_of(step * chunk, chunk), chunk)]) + row_ref[...]
-    phi = 0.5 * (1.0 + lax.erf(lifted * (0.5 ** 0.5)))
-    density = jnp.exp(lifted * lifted * -0.5) * 0.3989422804014327
-    put_half(step, pl.num_programs(0), act_ref, act_send, (lifted * phi).astype(BF16))
-    slope_ref[...] = phi + lifted * density
-
-    @pl.when(step == pl.num_programs(0) - 1)
-    def _():
-        keep.wait()
-
-
-def lift(far, at, parts, low, row, chunk=512):
+    up_refs, down_refs, refs = refs[:ups], refs[ups : ups + downs], refs[ups + downs :]
+    low_ref, row_ref, vec_ref, log_ref, inv_ref, hat_in, dy_in, heads_in, out_in = refs[:9]
+    act_out, act_send, result_out, glow_out, lift_out, lift_send, one_out, mine_out, send_out, pay_out, mean_ref, row_sums, two_sums, one_sums = refs[9:23]
+    up, down, out, hat, dy, heads, act, slope, result, glow, total, branch, sides, payload, up_sems, down_sems, in_sems, out_sems = refs[23:]
+    tokens, width = low_ref.shape
+    half = up.shape[1] // 2
+    chunk = 512
+    steps = 2 * half // chunk
+    from_up = up_copies(up_refs, up, up_sems, at_ref, far)
+    from_down = down_copies(down_refs, down, down_sems, at_ref, far)
+    loads = [pltpu.make_async_copy(*pair, in_sems.at[i]) for i, pair in enumerate(((hat_in, hat), (dy_in, dy), (out_in, out), (heads_in, heads)))]
+    start_all(from_up)
+    start_all(from_down)
+    start_all(loads)
+    stores = []
+
+    def store(source, target):
+        copy = pltpu.make_async_copy(source, target, out_sems.at[len(stores)])
+        stores.append(copy)
+        copy.start()
+
+    def cols(i):
+        return pl.ds(pl.multiple_of(i * chunk, chunk), chunk)
+
+    def raise_one(i):
+        lifted = nn(low_ref[...], up[:, cols(i)]) + row_ref[:, cols(i)]
+        phi = 0.5 * (1.0 + lax.erf(lifted * (0.5 ** 0.5)))
+        density = jnp.exp(lifted * lifted * -0.5) * 0.3989422804014327
+        act[:, cols(i)] = (lifted * phi).astype(BF16)
+        slope[:, cols(i)] = (phi + lifted * density).astype(BF16)
+
+    def settle_one(i):
+        total[...] += nn(act[:, cols(i)], down[cols(i)])
+
+    half_up, half_down = len(from_up) // 2, len(from_down) // 2
+    wait_all(from_up[:half_up])
+    total[...] = jnp.zeros_like(total)
+    raise_one(0)
+    wait_all(from_down[:half_down])
+
+    def both(i, carry):
+        raise_one(i)
+        settle_one(i - 1)
+        return carry
+
+    lax.fori_loop(1, steps // 2, both, 0)
+    wait_all(from_up[half_up:])
+    both(steps // 2, 0)
+    wait_all(from_down[half_down:])
+    lax.fori_loop(steps // 2 + 1, steps, both, 0)
+    settle_one(steps - 1)
+    store(act.at[:, pl.ds(0, half)], act_out)
+    store(act.at[:, pl.ds(half, half)], act_send)
+    wait_all(loads)
+
+    rows = 128
+    for n in range(tokens // rows):
+        at = slice(rows * n, rows * n + rows)
+        first = hat[at] * vec_ref[3:4] + vec_ref[4:5]
+        hat_two, inverse = normalized(first + (total[at] + vec_ref[0:1]))
+        result[at] = (hat_two * vec_ref[1:2] + vec_ref[2:3]).astype(BF16)
+        grad = dy[at].astype(F32)
+        part = [column_sum(grad * hat_two), column_sum(grad)]
+        grad = norm_back(grad, vec_ref[1:2], hat_two, inverse)
+        low = grad.astype(BF16)
+        total[at] = grad
+        glow[at] = low
+        part = cat(part + [column_sum(low.astype(F32))], 0)
+        two_sums[...] = part if n == 0 else two_sums[...] + part
+    store(result, result_out)
+    store(glow, glow_out)
+
+    def lower_one(i):
+        value = (nt(glow[...], down[cols(i)]) * slope[:, cols(i)].astype(F32)).astype(BF16)
+        slope[:, cols(i)] = value
+        row_sums[:, cols(i)] = column_sum(value.astype(F32))
+
+    def first_one(i):
+        total[...] += nt(slope[:, cols(i)], up[:, cols(i)])
+
+    lower_one(0)
+
+    def back(i, carry):
+        lower_one(i)
+        first_one(i - 1)
+        return carry
+
+    lax.fori_loop(1, steps, back, 0)
+    store(slope.at[:, pl.ds(0, half)], lift_out)
+    store(slope.at[:, pl.ds(half, half)], lift_send)
+    first_one(steps - 1)
+
+    for n in range(tokens // rows):
+        at = slice(rows * n, rows * n + rows)
+        grad = total[at]
+        one = norm_back(grad, vec_ref[3:4], hat[at], inv_ref[at])
+        low = one.astype(BF16)
+        total[at] = one
+        branch[at] = low
+        part = cat([column_sum(grad * hat[at]), column_sum(grad), column_sum(low.astype(F32))], 0)
+        one_sums[...] = part if n == 0 else one_sums[...] + part
+    store(total, one_out)
+    middle = width // 2
+    for n in range(2):
+        side = pl.multiple_of(jnp.bitwise_xor(at_ref[2], n) * middle, middle)
+        sides[n] = branch[:, pl.ds(side, middle)]
+    store(sides.at[0], mine_out)
+    store(sides.at[1], send_out)
+
+    head = lax.broadcasted_iota(jnp.int32, (H, width), 1) // HD
+    pick = jnp.where(head == lax.broadcasted_iota(jnp.int32, (H, width), 0), 1.0, 0.0).astype(F32)
+    for n in range(tokens // rows):
+        at = slice(rows * n, rows * n + rows)
+        grad = nt(branch[at], out[...]).astype(BF16)
+        payload[at] = grad
+        product = grad.astype(F32) * heads[at].astype(F32)
+        mean_ref[:, at] = lax.dot_general(
+            pick, product, (((1,), (1,)), ((), ())), precision=lax.Precision.HIGHEST, preferred_element_type=F32
+        )
+    rest = cat([log_ref[...], mean_ref[...]], 1)
+    for n in range(3):
+        term = rest.astype(BF16)
+        rest = rest - term.astype(F32)
+        payload[tokens + H * n : tokens + H * n + H] = term
+    store(payload, pay_out)
+    wait_all(stores)
+
+
+def middle(far, at, up_parts, down_parts, low, row, vectors, logs, inverse, hat, dy, heads, out_full):
     tokens, width = low.shape
     hidden = row.shape[1]
-    block = pl.BlockSpec((tokens, chunk), lambda i: (0, i))
+    half = hidden // 2
+    shape = jax.ShapeDtypeStruct
+    pay_shape = (tokens + 3 * H, width)
     return pl.pallas_call(
-        functools.partial(lift_kernel, far, len(parts)),
-        grid=(hidden // chunk,),
-        in_specs=[SMEM] + [ANY] * len(parts) + [pl.BlockSpec((tokens, width), lambda i: (0, 0)), pl.BlockSpec((1, chunk), lambda i: (0, i))],
-        out_specs=half_blocks(tokens, chunk, hidden // chunk) + [block, ANY],
+        functools.partial(middle_kernel, far, len(up_parts), len(down_parts)),
+        in_specs=[SMEM] + [ANY] * (len(up_parts) + len(down_parts)) + [VMEM] * 5 + [ANY] * 4,
+        out_specs=[ANY] * 10 + [VMEM] * 4,
         out_shape=[
-            jax.ShapeDtypeStruct((tokens, hidden // 2), BF16),
-            jax.ShapeDtypeStruct((tokens, hidden // 2), BF16),
-            jax.ShapeDtypeStruct((tokens, hidden), F32),
-            jax.ShapeDtypeStruct((width, hidden), BF16),
-        ],
-        scratch_shapes=[pltpu.VMEM((width, hidden), BF16), pltpu.SemaphoreType.DMA((copy_count(far, 2),)), pltpu.SemaphoreType.DMA],
-        compiler_params=params(),
-        cost_estimate=cost(),
-        name="lift",
-    )(at, *parts, low, row)
-
-
-def settle_kernel(far, parts, *refs):
-    at_ref, refs = refs[0], refs[1:]
-    part_refs, refs = refs[:parts], refs[parts:]
-    act_ref, act_send, first_ref, vec_ref, dy_ref, result_ref, grad_ref, glow_ref, sums_ref, full_out, total, full, sems, out_sem = refs
-    step = pl.program_id(0)
-    chunk = act_ref.shape[1]
-    copies = down_copies(part_refs, full, sems, at_ref, far)
-    keep = pltpu.make_async_copy(full, full_out, out_sem)
-
-    @pl.when(step == 0)
-    def _():
-        start_all(copies)
-        wait_all(copies)
-        keep.start()
-
-    active = take_half(step, pl.num_programs(0), act_ref, act_send)
-    part = nn(active, full[pl.ds(pl.multiple_of(step * chunk, chunk), chunk)])
-
-    @pl.when(step == 0)
-    def _():
-        total[...] = part
-
-    @pl.when(step > 0)
-    def _():
-        total[...] += part
-
-    @pl.when(step == pl.num_programs(0) - 1)
-    def _():
-        rows = total.shape[0] // 4
-        sums = None
-        for i in range(4):
-            at = slice(rows * i, rows * i + rows)
-            hat, inverse = normalized(first_ref[at] + (total[at] + vec_ref[0:1]))
-            result_ref[at] = (hat * vec_ref[1:2] + vec_ref[2:3]).astype(BF16)
-            dy = dy_ref[at].astype(F32)
-            grad = norm_back(dy, vec_ref[1:2], hat, inverse)
-            low = grad.astype(BF16)
-            grad_ref[at] = grad
-            glow_ref[at] = low
-            part = cat([column_sum(dy * hat), column_sum(dy), column_sum(low.astype(F32))], 0)
-            sums = part if sums is None else sums + part
-        sums_ref[...] = sums
-        keep.wait()
-
-
-def settle(far, at, parts, active, act_send, first, vectors, dy, chunk=1024):
-    tokens, hidden = active.shape[0], 2 * active.shape[1]
-    width = first.shape[1]
-    whole = lambda shape: pl.BlockSpec(shape, lambda i: (0, 0))
-    return pl.pallas_call(
-        functools.partial(settle_kernel, far, len(parts)),
-        grid=(hidden // chunk,),
-        in_specs=[SMEM]
-        + [ANY] * len(parts)
-        + half_blocks(tokens, chunk, hidden // chunk)
-        + [whole((tokens, width)), whole(vectors.shape), whole((tokens, width))],
-        out_specs=[whole((tokens, width)), whole((tokens, width)), whole((tokens, width)), whole((3, width)), ANY],
-        out_shape=[
-            jax.ShapeDtypeStruct((tokens, width), BF16),
-            jax.ShapeDtypeStruct((tokens, width), F32),
-            jax.ShapeDtypeStruct((tokens, width), BF16),
-            jax.ShapeDtypeStruct((3, width), F32),
-            jax.ShapeDtypeStruct((hidden, width), BF16),
+            shape((tokens, half), BF16),
+            shape((tokens, half), BF16),
+            shape((tokens, width), BF16),
+            shape((tokens, width), BF16),
+            shape((tokens, half), BF16),
+            shape((tokens, half), BF16),
+            shape((tokens, width), F32),
+            shape((tokens, width // 2), BF16),
+            shape((tokens, width // 2), BF16),
+            shape(pay_shape, BF16),
+            shape((H, tokens), F32),
+            shape((1, hidden), F32),
+            shape((3, width), F32),
+            shape((3, width), F32),
         ],
         scratch_shapes=[
+            pltpu.VMEM((width, hidden), BF16),
+            pltpu.VMEM((hidden, width), BF16),
+            pltpu.VMEM((width, width), BF16),
             pltpu.VMEM((tokens, width), F32),
-            pltpu.VMEM((hidden, width), BF16),
+            pltpu.VMEM((tokens, width), BF16),
+            pltpu.VMEM((tokens, width), BF16),
+            pltpu.VMEM((tokens, hidden), BF16),
+            pltpu.VMEM((tokens, hidden), BF16),
+            pltpu.VMEM((tokens, width), BF16),
+            pltpu.VMEM((tokens, width), BF16),
+            pltpu.VMEM((tokens, width), F32),
+            pltpu.VMEM((tokens, width), BF16),
+            pltpu.VMEM((2, tokens, width // 2), BF16),
+            pltpu.VMEM(pay_shape, BF16),
             pltpu.SemaphoreType.DMA((copy_count(far, 2),)),
-            pltpu.SemaphoreType.DMA,
+            pltpu.SemaphoreType.DMA((copy_count(far, 2),)),
+            pltpu.SemaphoreType.DMA((4,)),
+            pltpu.SemaphoreType.DMA((10,)),
         ],
         compiler_params=params(),
-        cost_estimate=cost(),
-        name="settle",
-    )(at, *parts, active, act_send, first, vectors, dy)
-
-
-def lift_grad_kernel(glow_ref, down_ref, slope_ref, keep_ref, send_ref, sum_ref):
-    value = (nt(glow_ref[...], down_ref[...]) * slope_ref[...]).astype(BF16)
-    put_half(pl.program_id(0), pl.num_programs(0), keep_ref, send_ref, value)
-    sum_ref[...] = column_sum(value.astype(F32))
-
-
-def lift_grads(glow, down_full, slope, chunk=512):
-    tokens, width = glow.shape
-    hidden = down_full.shape[0]
-    half = jax.ShapeDtypeStruct((tokens, hidden // 2), BF16)
-    return pl.pallas_call(
-        lift_grad_kernel,
-        grid=(hidden // chunk,),
-        in_specs=[
-            pl.BlockSpec((tokens, width), lambda i: (0, 0)),
-            pl.BlockSpec((chunk, width), lambda i: (i, 0)),
-            pl.BlockSpec((tokens, chunk), lambda i: (0, i)),
-        ],
-        out_specs=half_blocks(tokens, chunk, hidden // chunk) + [pl.BlockSpec((1, chunk), lambda i: (0, i))],
-        out_shape=[half, half, jax.ShapeDtypeStruct((1, hidden), F32)],
-        compiler_params=params(),
-        cost_estimate=cost(),
-        name="lift_grads",
-    )(glow, down_full, slope)
+        cost_estimate=cost(45),
+        name="middle",
+    )(at, *up_parts, *down_parts, low, row, vectors, logs, inverse, hat, dy, heads, out_full)
 
 
 def down_grad_kernel(far, at_ref, act_ref, act_got, glow_ref, glow_got, dw_ref, glows):
@@ -789,100 +782,9 @@
         out_shape=jax.ShapeDtypeStruct((half, width), BF16),
         scratch_shapes=[pltpu.VMEM((2 * tokens, width), BF16)],
         compiler_params=params(),
-        cost_estimate=cost(),
+        cost_estimate=cost(8.5),
         name="down_grads",
     )(at, active, act_got, glow, glow_got)
-
-
-def first_grad_kernel(at_ref, lift_ref, lift_send, up_ref, grad_ref, hat_ref, inv_ref, gain_ref, one_ref, branch_ref, mine_ref, send_ref, sums_ref, total):
-    step = pl.program_id(0)
-    part = nt(take_half(step, pl.num_programs(0), lift_ref, lift_send), up_ref[...])
-
-    @pl.when(step == 0)
-    def _():
-        total[...] = grad_ref[...] + part
-
-    @pl.when(step > 0)
-    def _():
-        total[...] += part
-
-    @pl.when(step == pl.num_programs(0) - 1)
-    def _():
-        rows = total.shape[0] // 4
-        sums = None
-        for i in range(4):
-            at = slice(rows * i, rows * i + rows)
-            grad = total[at]
-            hat = hat_ref[at]
-            one = norm_back(grad, gain_ref[...], hat, inv_ref[at])
-            branch = one.astype(BF16)
-            one_ref[at] = one
-            branch_ref[at] = branch
-            part = cat([column_sum(grad * hat), column_sum(grad), column_sum(branch.astype(F32))], 0)
-            sums = part if sums is None else sums + part
-        sums_ref[...] = sums
-        half = mine_ref.shape[1]
-        mine_ref[...] = branch_ref[:, pl.ds(pl.multiple_of(at_ref[2] * half, half), half)]
-        send_ref[...] = branch_ref[:, pl.ds(pl.multiple_of((1 - at_ref[2]) * half, half), half)]
-
-
-def first_grads(at, lift, lift_send, up_full, grad_two, hat, inverse, gain, chunk=1024):
-    tokens, width = hat.shape
-    hidden = up_full.shape[1]
-    whole = lambda shape: pl.BlockSpec(shape, lambda i: (0, 0))
-    half = whole((tokens, width // 2))
-    return pl.pallas_call(
-        first_grad_kernel,
-        grid=(hidden // chunk,),
-        in_specs=[SMEM]
-        + half_blocks(tokens, chunk, hidden // chunk)
-        + [
-            pl.BlockSpec((width, chunk), lambda i: (0, i)),
-            whole((tokens, width)),
-            whole((tokens, width)),
-            whole((tokens, 1)),
-            whole((1, width)),
-        ],
-        out_specs=[whole((tokens, width)), whole((tokens, width)), half, half, whole((3, width))],
-        out_shape=[
-            jax.ShapeDtypeStruct((tokens, width), F32),
-            jax.ShapeDtypeStruct((tokens, width), BF16),
-            jax.ShapeDtypeStruct((tokens, width // 2), BF16),
-            jax.ShapeDtypeStruct((tokens, width // 2), BF16),
-            jax.ShapeDtypeStruct((3, width), F32),
-        ],
-        scratch_shapes=[pltpu.VMEM((tokens, width), F32)],
-        compiler_params=params(),
-        cost_estimate=cost(),
-        name="first_grads",
-    )(at, lift, lift_send, up_full, grad_two, hat, inverse, gain)
-
-
-def pay_kernel(branch_ref, w_ref, heads_ref, log_ref, pay_ref, mean_ref):
-    tokens, width = branch_ref.shape
-    grad = nt(branch_ref[...], w_ref[...]).astype(BF16)
-    pay_ref[:tokens] = grad
-    product = grad.astype(F32) * heads_ref[...].astype(F32)
-    head = lax.broadcasted_iota(jnp.int32, (H, width), 1) // HD
-    pick = jnp.where(head == lax.broadcasted_iota(jnp.int32, (H, width), 0), 1.0, 0.0).astype(F32)
-    means = lax.dot_general(pick, product, (((1,), (1,)), ((), ())), precision=lax.Precision.HIGHEST, preferred_element_type=F32)
-    mean_ref[...] = means
-    rest = cat([log_ref[...], means], 1)
-    for k in range(3):
-        term = rest.astype(BF16)
-        rest = rest - term.astype(F32)
-        pay_ref[tokens + H * k : tokens + H * k + H] = term
-
-
-def pay(branch, out_full, heads, logs):
-    tokens, width = branch.shape
-    return pl.pallas_call(
-        pay_kernel,
-        out_shape=[jax.ShapeDtypeStruct((tokens + 3 * H, width), BF16), jax.ShapeDtypeStruct((H, tokens), F32)],
-        compiler_params=params(),
-        cost_estimate=cost(),
-        name="pay",
-    )(branch, out_full, heads, logs)
 
 
 def both_flipped(at_ref, mine_ref, got_ref, flipped, far, heads=False):
@@ -954,17 +856,18 @@
         out_shape=[jax.ShapeDtypeStruct((width // 4, (steps + 1) * chunk), BF16)] * 4,
         scratch_shapes=[pltpu.VMEM((width, 2 * tokens), BF16)],
         compiler_params=params(),
-        cost_estimate=cost(),
+        cost_estimate=cost(12),
         name="late_grads",
     )(at, low, low_got, heads, heads_got, lift, lift_got, branch, branch_got)
 
 
-def qkv_grad_kernel(far, at_ref, x_ref, x_got, keep_ref, got_ref, *refs):
+def qkv_grad_kernel(far, at_ref, x_ref, x_got, *refs):
+    keeps, gots, refs = refs[:3], refs[3:6], refs[6:]
     note_refs, quarters, flipped = refs[:-5], refs[-5:-1], refs[-1]
     both_flipped(at_ref, x_ref, x_got, flipped, far)
-    chunk = keep_ref.shape[2]
+    chunk = keeps[0].shape[1]
     for n in range(3):
-        dw = nn(flipped[...], cat([keep_ref[n], got_ref[n]], 0)).astype(BF16)
+        dw = nn(flipped[...], cat([keeps[n][...], gots[n][...]], 0)).astype(BF16)
         put_quarters(quarters, slice(n * chunk, n * chunk + chunk), dw)
     for ref in note_refs:
         put_quarters(quarters, slice(3 * chunk, 3 * chunk + ref.shape[1]), ref[...])
@@ -972,16 +875,16 @@
 
 def qkv_grads(far, at, x, x_got, keep, got, notes=()):
     tokens, width = x.shape
-    columns = 3 * keep.shape[2] + sum(v.shape[1] for v in notes)
+    columns = 3 * keep[0].shape[1] + sum(v.shape[1] for v in notes)
     return pl.pallas_call(
         functools.partial(qkv_grad_kernel, far),
-        in_specs=[SMEM] + [VMEM] * (4 + len(notes)),
+        in_specs=[SMEM] + [VMEM] * (8 + len(notes)),
         out_shape=[jax.ShapeDtypeStruct((width // 4, columns), BF16)] * 4,
         scratch_shapes=[pltpu.VMEM((width, 2 * tokens), BF16)],
         compiler_params=params(),
-        cost_estimate=cost(),
+        cost_estimate=cost(8.3),
         name="qkv_grads",
-    )(at, x, x_got, keep, got, *notes)
+    )(at, x, x_got, *keep, *got, *notes)
 
 
 FAR, Y, X, CORE = "far", "y", "x", "fsdp"
@@ -991,6 +894,10 @@
 
 def swap(values, axis):
     return lax.ppermute(values, axis, [(0, 1), (1, 0)])
+
+
+def swap_both(values):
+    return lax.ppermute(values, (Y, X), [(i, 3 - i) for i in range(4)])
 
 
 def swap_far(values, step):
@@ -1093,95 +1000,100 @@
     query_row, value_row, out_row, gain_one, shift_one, down_row, gain_two, shift_two = rows_of
     up_row = table[:, 8 * each :].reshape(blocks, 2, piece).astype(F32)
     up_row = cat(choose(core, up_row[:, 0].reshape(1, -1), up_row[:, 1].reshape(1, -1)), 1)
-    bias_own, bias_halo = mask_biases(segments[0], place, blocks, tokens)
+    bias_own, bias_halo, bias_narrow = mask_biases(segments[0], place, blocks, tokens)
     query_row, value_row, gap = own_first(query_row), own_first(value_row), jnp.zeros((1, near), F32)
     qkv_row = cat([query_row[:, :near], gap, value_row[:, :near], query_row[:, near:], gap, value_row[:, near:]], 1)
 
-    mixed, before, qkv_full, out_full = project(far, at, qkv_parts, x, x_before, qkv_row)
+    mixed, qkv_full, out_full = project(far, at, qkv_parts, x, qkv_row)
     if far is not None:
         qkv_full, up_y = together(qkv_full, up_y)
         up_pair = jnp.stack([up_wide, up_y])
         up_x, up_pair_core = swap(up_pair, X), swap(up_pair, CORE)
-    after = project_more(x_after, qkv_full, qkv_row)
+    before, after = project_more(x_before, x_after, qkv_full, qkv_row)
     if far is not None:
-        after, down_wide = together(after, down_wide)
+        before, down_wide = together(before, down_wide)
         down_y, down_wide_core = swap(down_wide, Y), swap(down_wide, CORE)
     heads, logs = attend(mixed, before, after, bias_own, bias_halo)
-    hat, inverse, first, low = out_project(heads, out_full, x, cat([out_row, gain_one, shift_one], 0))
+    hat, inverse, low = out_project(heads, out_full, x, cat([out_row, gain_one, shift_one], 0))
+    low, x_got, heads_got = together(low, swap(x, CORE), swap(heads, CORE))
     if far is not None:
         low, up_x, up_pair_core, down_wide_core, down_y = together(low, up_x, up_pair_core, down_wide_core, down_y)
         up_parts = [up_pair, up_x, up_pair_core, swap(up_x, CORE)]
         down_parts = [down_wide, down_y, down_wide_core, swap(down_y, CORE)]
-    x_got, heads_got, low_got = swap(x, CORE), swap(heads, CORE), swap(low, CORE)
-    active, act_send, slope, up_full = lift(far, at, up_parts, low, up_row)
-    act_got = swap(act_send, CORE)
-    active, x_got, heads_got, low_got = together(active, x_got, heads_got, low_got)
-    result, grad_two, glow, sums_two, down_full = settle(
-        far, at, down_parts, active, act_send, first, cat([down_row, gain_two, shift_two], 0), cotangent[0]
+    low_got = swap(low, CORE)
+    (
+        active, act_send, result, glow, lift_keep, lift_send, grad_one, branch_mine, branch_send, payload, means, up_bias_part, sums_two, sums_one,
+    ) = middle(
+        far, at, up_parts, down_parts, low, up_row, cat([down_row, gain_two, shift_two, gain_one, shift_one], 0),
+        logs, inverse, hat, cotangent[0], heads, out_full,
     )
-    glow_got = swap(glow, CORE)
-    lift_keep, lift_send, up_bias_part = lift_grads(glow, down_full, slope)
-    lift_got = swap(lift_send, CORE)
-    grad_one, branch, branch_mine, branch_send, sums_one = first_grads(at, lift_keep, lift_send, up_full, grad_two, hat, inverse, gain_one)
-    branch_got = swap(branch_send, CORE)
-    payload, means = pay(branch, out_full, heads, logs)
+    payload, low_got = together(payload, low_got)
     pay_before, pay_after = from_before(payload), from_after(payload)
+    act_got, glow_got, lift_got, branch_got = swap(act_send, CORE), swap(glow, CORE), swap(lift_send, CORE), swap(branch_send, CORE)
     down_part = down_grads(far, at, active, act_got, glow, glow_got)
     late = late_grads(far, at, low, low_got, heads, heads_got, lift_keep, lift_got, branch_mine, branch_got)
     dq, dkv, dq_sum = own_grads(mixed, before, after, payload, logs, means, bias_own, bias_halo)
+    dq_keep, dq_send = dq[0], dq[1]
     if far is not None:
         down_part = lax.psum_scatter(down_part.reshape(far, 2, 2, piece, width), FAR, scatter_dimension=0, tiled=False)
         by = lambda parts: [v.reshape(2, far, rows, v.shape[1]) for v in parts]
         late_send_x, late_keep_x, late_send_y, late_keep_y = by(late)
-        late_x, late_y, pay_before, pay_after = together(late_send_x, late_send_y, pay_before, pay_after)
+        late_x, late_y, pay_before, pay_after, dkv = together(late_send_x, late_send_y, pay_before, pay_after, dkv)
         late_x, late_y = swap(late_x, X), swap(late_y, Y)
-    keep, send, dv_sum = halo_grads(mixed, before, after, pay_before, pay_after, bias_halo, dq, dkv)
-    got = swap(send, CORE)
+    *send, sum_send = halo_grads(mixed, before, after, pay_before, pay_after, bias_narrow, dkv, 1)
+    send = [dq_send] + send
+    *keep, sum_keep = halo_grads(mixed, before, after, pay_before, pay_after, bias_narrow, dkv, 0)
     if far is not None:
-        got, late_x, late_y = together(got, late_x, late_y)
+        late_x, late_y, sum_keep = together(late_x, late_y, sum_keep)
+    keep, dv_sum = [dq_keep] + keep, cat([sum_keep, sum_send], 1)
+    got = [swap(v, CORE) for v in send]
+    if far is not None:
         late_xy, late_yx = color_nexts(late_keep_x, late_keep_y, late_x, late_y)
-        late_xy, late_yx, got = together(late_xy, late_yx, got)
+        late_xy, late_yx, *got = together(late_xy, late_yx, *got)
         late_xy, late_yx = swap(late_xy, Y), swap(late_yx, X)
     features = (own_first(dq_sum), own_first(dv_sum), sums_one[2], sums_one[0], sums_one[1], sums_two[2], sums_two[0], sums_two[1])
-    small = jnp.stack([v.reshape(blocks, 2, each) for v in features], 2)
-    small = small.reshape(blocks, 2, -1)
-    small = choose(core, small[:, 0], small[:, 1])
-    small = [cat([v, up_bias_part[:, hidden // 2 * i : hidden // 2 * (i + 1)].reshape(blocks, piece)], 1) for i, v in enumerate(small)]
-    small = small[0] + swap(small[1], CORE)
+    small = jnp.stack([v.reshape(blocks, 2, each) for v in features], 2).reshape(blocks, 2, -1)
+    sides = choose(core, up_bias_part[:, : hidden // 2], up_bias_part[:, hidden // 2 :])
+    small = cat([small, jnp.stack([v.reshape(blocks, piece) for v in sides], 1)], 2)
     if far is None:
         qkv = qkv_grads(far, at, x, x_got, keep, got)
         total = lambda v: lax.psum_scatter(v, CTX, scatter_dimension=0, tiled=True)
-        down_sum, small_sum = total(down_part).astype(F32), total(small)[0]
+        down_sum = total(down_part).astype(F32)
+        small_sum = lax.psum_scatter(small.reshape(2 * blocks, -1), ALL, scatter_dimension=0, tiled=True)[0]
         late_sum, qkv_sum = [total(cat(v, 0)).reshape(2, rows, -1) for v in (late, qkv)]
     else:
-        small = small.reshape(far, 2, 2, lines, 128).transpose(2, 1, 0, 3, 4)
-        for axis, index in ((0, at[1]), (1, at[0])):
+        small = small.astype(BF16).reshape(far, 2, 2, 2, lines, 128).transpose(3, 2, 1, 0, 4, 5)
+        for axis, index in ((1, at[1]), (2, at[0])):
             small = jnp.where(index == 0, small, jnp.flip(small, axis))
-        small = jnp.flip(small, 0).reshape(2 * 2 * far, lines, 128).astype(BF16)
-        note = jnp.zeros((8 * far, rows, 128), BF16).at[: 4 * far, :lines].set(small).reshape(width, 128)
+        small = jnp.stack([jnp.flip(small[0], 0), jnp.flip(small[1].swapaxes(0, 1), 0)])
+        small = small.reshape(8 * far, lines, 128)
+        note = jnp.zeros((8 * far, rows, 128), BF16).at[:, :lines].set(small).reshape(width, 128)
         qkv_send_x, qkv_keep_x, qkv_send_y, qkv_keep_y = by(qkv_grads(far, at, x, x_got, keep, got, (note,)))
         qkv_send_x, qkv_send_y, late_xy, late_yx = together(qkv_send_x, qkv_send_y, late_xy, late_yx)
         qkv_x, qkv_y = swap(qkv_send_x, X), swap(qkv_send_y, Y)
         late_sum = color_sums(late_keep_x, late_keep_y, late_x, late_y, late_xy, late_yx)
-        late_sum, down_part = together(late_sum, down_part)
         late_sum = lax.psum_scatter(late_sum, FAR, scatter_dimension=0, tiled=False)
-        down_y = swap(down_part[1], Y)
-        qkv_x, qkv_y, grad_one, down_y = together(qkv_x, qkv_y, grad_one, down_y)
+        qkv_x, qkv_y, down_part = together(qkv_x, qkv_y, down_part)
         qkv_xy, qkv_yx = color_nexts(qkv_keep_x, qkv_keep_y, qkv_x, qkv_y)
+        qkv_xy, qkv_yx, down_part, *both = together(qkv_xy, qkv_yx, down_part, *keep, *send)
+        keep, send = both[:3], both[3:]
         qkv_xy, qkv_yx = swap(qkv_xy, Y), swap(qkv_yx, X)
-        down_part = added(down_part[0], down_y)
-        down_x = swap(down_part[1], X)
-        qkv_xy, qkv_yx, late_sum, down_x = together(qkv_xy, qkv_yx, late_sum, down_x)
+        down_y, down_x, down_xy = swap(down_part[1, 0], Y), swap(down_part[0, 1], X), swap_both(down_part[1, 1])
+        qkv_xy, qkv_yx, late_sum = together(qkv_xy, qkv_yx, late_sum)
         qkv_sum = lax.psum_scatter(color_sums(qkv_keep_x, qkv_keep_y, qkv_x, qkv_y, qkv_xy, qkv_yx), FAR, scatter_dimension=0, tiled=False)
-        down_sum = down_part[0].astype(F32) + down_x.astype(F32)
-        small_sum = qkv_sum[0, :lines, 3 * near :].reshape(-1).astype(F32)
+        qkv_sum, down_y, down_x, down_xy, late_sum = together(qkv_sum, down_y, down_x, down_xy, late_sum)
+        down_sum = down_part[0, 0].astype(F32) + down_y.astype(F32) + down_x.astype(F32) + down_xy.astype(F32)
     inputs_grad = nt(cat([*keep, *send], 1), qkv_full)
     inputs_grad = (grad_one + inputs_grad).astype(BF16)[None]
     wide = hidden // 2
     left, right = own_rows(core, late_sum)
     up_sum = jnp.stack([v[:, :wide].reshape(rows, blocks, piece) for v in (left, right)], 2).reshape(rows, hidden).astype(F32)
     out_sum = cat([left[:, wide:], right[:, wide:]], 1).astype(F32)
-    left, right = own_rows(core, qkv_sum[:, :, : 3 * near])
+    mine, send = choose(core, qkv_sum[0], qkv_sum[1])
+    got = swap(send, CORE)
+    left, right = choose(core, mine[:, : 3 * near], got[:, : 3 * near])
+    if far is not None:
+        small_sum = (mine[:lines, 3 * near :].astype(F32) + got[:lines, 3 * near :].astype(F32)).reshape(-1)
     qkv_sum = jnp.stack([v.reshape(rows, 3, near) for v in (left, right)], 2).reshape(rows, 3 * width).astype(F32)
     s = [small_sum[each * i : each * i + each] for i in range(8)]
     return (

time: 507 us -> 472 us (0.931)
  Pallas kernels: 208 us -> 175 us
  waiting for transfers between devices: 157 us -> 151 us
    pallas_call x7 -> x4, Pallas kernels: 97.1 us -> 74.1 us  [the longest x1 41.4 us: middle(): pl.pallas_call(functools.partial(middle_kernel, far, len(up_parts), len(d...]
    reduce_scatter x1, waiting for transfers between devices: 0.01 us -> 11.2 us  [shards(): late_sum = lax.psum_scatter(late_sum, FAR, scatter_dimension=0, tiled=False)]
    ppermute x38 -> x39, waiting for transfers between devices: 86.5 us -> 79.2 us  [swap(): return lax.ppermute(values, axis, [(0, 1), (1, 0)])]
    reduce_scatter x1, waiting for transfers between devices: 18.8 us -> 11.5 us  [shards(): lax.psum_scatter(color_sums(qkv_keep_x, qkv_keep_y, qkv_x, qkv_y, qkv_xy,...]
    pallas_call x1, Pallas kernels: 18.8 us -> 13.3 us  [project(): pl.pallas_call(functools.partial(project_kernel, far, len(parts)), in_spe...]
    unnamed x84 -> x83, local copies, waits for them, and re-layouts: 10.6 us -> 11.8 us
    ppermute x38 -> x39, starting transfers between devices: 30 us -> 29.9 us  [swap(): return lax.ppermute(values, axis, [(0, 1), (1, 0)])]
  transfers between devices with their start and end apart: 50 -> 52, of which waited for: 24 -> 22; matrix products, arithmetic and copies ran while one was open for 9% -> 12% of each run, Pallas kernels for 42% -> 38%
where the time goes in v3:
time: 472 us; the launch traced here: 464 us
  Pallas kernels  175 us (37%)
  waiting for transfers between devices  151 us (32%)
  starting transfers between devices  57 us (12%)
  other arithmetic  32.4 us (7%)
  local copies, waits for them, and re-layouts  26.7 us (6%)
  between operations  15 us (3%)
  matrix products  6.66 us (1%)
    ppermute x39, waiting for transfers between devices, swap(): return lax.ppermute(values, axis, [(0, 1), (1, 0)])  79.2 us
    ppermute x4, waiting for transfers between devices, swap_far(): lax.ppermute(values, FAR, [(i, i ^ step) for i in range(lax.axis_size(FAR...  48.3 us
    pallas_call x1, Pallas kernels, middle(): pl.pallas_call(functools.partial(middle_kernel, far, len(up_parts), len(d...  41.4 us
    ppermute x39, starting transfers between devices, swap(): return lax.ppermute(values, axis, [(0, 1), (1, 0)])  29.9 us
    pallas_call x1, Pallas kernels, own_grads(): pl.pallas_call(own_grad_kernel, grid=(pairs,), in_specs=[column(0), colum...  27.5 us
    pallas_call x1, Pallas kernels, attend(): pl.pallas_call(attend_kernel, grid=(pairs,), in_specs=[column(0), column(...  22.4 us
    pallas_call x2, Pallas kernels, halo_grads(): pl.pallas_call(functools.partial(halo_grad_kernel, half), grid=(near,), i...  22 us
    pallas_call x1, Pallas kernels, project(): pl.pallas_call(functools.partial(project_kernel, far, len(parts)), in_spe...  13.3 us
  transfers between devices with their start and end apart: 52, of which 22 were waited for; matrix products, arithmetic and copies ran while one was open for 12% of the time, Pallas kernels for 38%

profile of v3, /device:TPU:25, one launch (start us, length us, event | category | flops | bytes accessed | tf_op | source)
XLA Modules:
  0.0 464.4 jit_solution(11790074667572222086)
XLA Ops:
  7.2 3.3 collective-permute-start.2
  18.1 15.5 %collective-permute-done.1 = bf16[2,32,2176]{2,1,0:T(8,128)(2,1)S(1)} collective-permute-done((bf16[2,32,2176]{2,1,0:T(8,128)(2,1)}, bf16[2,32,2176]{2,1,0:T(8,128)(2,1)S(1)}, u32[]{:S(2)}, u32[]{:S(2)}) %collective-permute-start.1) | collective-permute-done | bytes 278560 | tf_op jit(solution)/shard_map/ppermute | solution.py:904
  35.3 9.0 %collective-permute-start.5 = (bf16[512,1024]{1,0:T(8,128)(2,1)}, bf16[512,1024]{1,0:T(8,128)(2,1)S(1)}, u32[]{:S(2)}, u32[]{:S(2)}) collective-permute-start(bf16[512,1024]{1,0:T(8,128)(2,1)} %bitcast.15.refs_9_.x_ref), channel_id=1, source_target_pairs={{2,0},{4,2},{6,4},{8,6},{10,8},{12,10},{14,12},{16,14},{18,16},{20... | collective-permute-start | bytes 3145736 | tf_op jit(solution)/shard_map/ppermute | solution.py:952
  44.3 5.5 %collective-permute-start.3 = (bf16[2,2,32,2176]{3,2,1,0:T(8,128)(2,1)S(1)}, bf16[2,2,32,2176]{3,2,1,0:T(8,128)(2,1)S(1)}, u32[]{:S(2)}, u32[]{:S(2)}) collective-permute-start(bf16[2,2,32,2176]{3,2,1,0:T(8,128)(2,1)S(1)} %pad_maximum_fusion.9), channel_id=1, source_target_pairs={{0,8},{8,0},{16,24},{24,16},{1,9},{9,1},{17,25},{25,17},{2,10},{10... | collective-permute-start | bytes 1671176 | tf_op jit(solution)/shard_map/ppermute | solution.py:904
  49.8 15.9 %collective-permute-done.4 = bf16[128,1024]{1,0:T(8,128)(2,1)S(1)} collective-permute-done((bf16[128,1024]{1,0:T(8,128)(2,1)S(1)}, bf16[128,1024]{1,0:T(8,128)(2,1)S(1)}, u32[]{:S(2)}, u32[]{:S(2)}) %collective-permute-start.4) | collective-permute-done | bytes 262176 | tf_op jit(solution)/shard_map/ppermute | solution.py:896
  66.6 10.7 %collective-permute-done.3 = bf16[2,2,32,2176]{3,2,1,0:T(8,128)(2,1)S(1)} collective-permute-done((bf16[2,2,32,2176]{3,2,1,0:T(8,128)(2,1)S(1)}, bf16[2,2,32,2176]{3,2,1,0:T(8,128)(2,1)S(1)}, u32[]{:S(2)}, u32[]{:S(2)}) %collective-permute-start.3) | collective-permute-done | bytes 557088 | tf_op jit(solution)/shard_map/ppermute | solution.py:904
  80.1 13.3 %collective-permute-done.8 = bf16[64,2048]{1,0:T(8,128)(2,1)S(1)} collective-permute-done((bf16[64,2048]{1,0:T(8,128)(2,1)S(1)}, bf16[64,2048]{1,0:T(8,128)(2,1)S(1)}, u32[]{:S(2)}, u32[]{:S(2)}) %collective-permute-start.8) | collective-permute-done | bytes 262176 | tf_op jit(solution)/shard_map/ppermute | solution.py:904
  99.6 8.7 %collective-permute-done.11 = bf16[2,64,2048]{2,1,0:T(8,128)(2,1)S(1)} collective-permute-done((bf16[2,64,2048]{2,1,0:T(8,128)(2,1)S(1)}, bf16[2,64,2048]{2,1,0:T(8,128)(2,1)S(1)}, u32[]{:S(2)}, u32[]{:S(2)}) %collective-permute-start.11) | collective-permute-done | bytes 524320 | tf_op jit(solution)/shard_map/ppermute | solution.py:904
  108.3 9.5 %collective-permute-done.10.refs_4_ = bf16[2,4,32,2176]{3,2,1,0:T(8,128)(2,1)S(1)} collective-permute-done((bf16[2,4,32,2176]{3,2,1,0:T(8,128)(2,1)S(1)}, bf16[2,4,32,2176]{3,2,1,0:T(8,128)(2,1)S(1)}, u32[]{:S(2)}, u32[]{:S(2)}) %collective-permute-start.10) | collective-permute-done | bytes 1114144 | tf_op jit(solution)/shard_map/ppermute | solution.py:896
  130.6 13.3 %project.1 = (bf16[512,3072]{1,0:T(8,128)(2,1)}, bf16[1024,3072]{1,0:T(8,128)(2,1)}, bf16[1024,1024]{1,0:T(8,128)(2,1)}) custom-call(s32[4]{0:T(128)} %pad_add_fusion.2.at_ref.refs_0_, bf16[2,4,32,2176]{3,2,1,0:T(8,128)(2,1)} %copy-done.3, bf16[2,4,32,2176]{3,2,1,0:T(8,128)(2,1)} %collective-permute-done.9.refs_2_, bf16[2,4,32,2176]{3,2,1,0:T(8,128)(2,1)} %copy-done.2, ...), custom_call_target="tpu_custom_call" | custom-call | flops 260000000 | bytes 910000 | tf_op jit(solution)/shard_map/project/pallas_call | solution.py:471
  143.9 6.2 %collective-permute-done.16 = bf16[4,64,2048]{2,1,0:T(8,128)(2,1)} collective-permute-done((bf16[4,64,2048]{2,1,0:T(8,128)(2,1)S(1)}, bf16[4,64,2048]{2,1,0:T(8,128)(2,1)}, u32[]{:S(2)}, u32[]{:S(2)}) %collective-permute-start.16) | collective-permute-done | bytes 1048608 | tf_op jit(solution)/shard_map/ppermute | solution.py:896
  150.2 2.8 pad_maximum_fusion.refs_1_
  156.2 10.7 %project_more.1 = (bf16[512,3072]{1,0:T(8,128)(2,1)}, bf16[512,3072]{1,0:T(8,128)(2,1)}) custom-call(bf16[512,1024]{1,0:T(8,128)(2,1)} %copy-done.11, bf16[512,1024]{1,0:T(8,128)(2,1)} %copy-done.12, bf16[1024,3072]{1,0:T(8,128)(2,1)} %get-tuple-element.161.w_ref, f32[1,3072]{1,0:T(1,128)} %copy-done.24), custom_call_target="tpu_custom_call" | custom-call | flops 214000000 | bytes 749000 | tf_op jit(solution)/shard_map/project_more/pallas_call | solution.py:498
  172.1 22.4 %attend.1 = (bf16[512,1024]{1,0:T(8,128)(2,1)}, f32[16,512]{1,0:T(8,128)}) custom-call(bf16[512,3072]{1,0:T(8,128)(2,1)} %get-tuple-element.158.q_ref.ko_ref.vo_ref, bf16[512,3072]{1,0:T(8,128)(2,1)} %get-tuple-element.158.q_ref.ko_ref.vo_ref, bf16[512,3072]{1,0:T(8,128)(2,1)} %get-tuple-element.164.kp_ref.vp_ref.qp_ref, ...), custom_call_target="tpu_custom_call" | custom-call | flops 480000000 | bytes 1680000 | tf_op jit(solution)/shard_map/attend/pallas_call | solution.py:120
  195.7 5.2 %out_project.1 = (f32[512,1024]{1,0:T(8,128)}, f32[512,1]{1,0:T(8,128)}, bf16[512,1024]{1,0:T(8,128)(2,1)}) custom-call(bf16[512,1024]{1,0:T(8,128)(2,1)} %get-tuple-element.166.heads_ref.refs_16_, bf16[1024,1024]{1,0:T(8,128)(2,1)} %get-tuple-element.167.w_ref.refs_17_, bf16[512,1024]{1,0:T(8,128)(2,1)} %bitcast.15.refs_9_.x_ref, ...), custom_call_target="tpu_custom_call" | custom-call | flops 114000000 | bytes 399000 | tf_op jit(solution)/shard_map/out_project/pallas_call | solution.py:522
  201.0 14.3 %collective-permute-done.22.refs_6_ = bf16[2,4,128,1024]{3,2,1,0:T(8,128)(2,1)} collective-permute-done((bf16[2,4,128,1024]{3,2,1,0:T(8,128)(2,1)}, bf16[2,4,128,1024]{3,2,1,0:T(8,128)(2,1)}, u32[]{:S(2)}, u32[]{:S(2)}) %collective-permute-start.22) | collective-permute-done | bytes 2097184 | tf_op jit(solution)/shard_map/ppermute | solution.py:896
  220.3 3.0 collective-permute-done.24.refs_8_
  223.3 41.4 %middle.1 = (bf16[512,2048]{1,0:T(8,128)(2,1)}, bf16[512,2048]{1,0:T(8,128)(2,1)}, bf16[512,1024]{1,0:T(8,128)(2,1)}, bf16[512,1024]{1,0:T(8,128)(2,1)}, bf16[51...) custom-call(s32[4]{0:T(128)} %pad_add_fusion.2.at_ref.refs_0_, ...), custom_call_target="tpu_custom_call" | custom-call | flops 44999999488 | bytes 157500000 | tf_op jit(solution)/shard_map/middle/pallas_call | solution.py:707
  264.7 3.1 collective-permute-start.28
  267.8 4.0 collective-permute-start.29
  273.3 27.5 %own_grads.1 = (bf16[2,512,512]{2,1,0:T(8,128)(2,1)}, f32[2,2,512,512]{3,2,1,0:T(8,128)}, f32[1,1024]{1,0:T(1,128)}) custom-call(bf16[512,3072]{1,0:T(8,128)(2,1)} %get-tuple-element.158.q_ref.ko_ref.vo_ref, bf16[512,3072]{1,0:T(8,128)(2,1)} %get-tuple-element.158.q_ref.ko_ref.vo_ref, bf16[512,3072]{1,0:T(8,128)(2,1)} %get-tuple-element.164.kp_ref.vp_ref.qp_ref, ...), custom_call_target="tpu_custom_call" | custom-call | flops 29500000256 | bytes 103250000 | tf_op jit(solution)/shard_map/own_grads/pallas_call | solution.py:199
  304.8 8.6 %down_grads.1 = bf16[2048,1024]{1,0:T(8,128)(2,1)} custom-call(s32[4]{0:T(128)} %pad_add_fusion.2.at_ref.refs_0_, bf16[512,2048]{1,0:T(8,128)(2,1)} %get-tuple-element.225.act_ref, bf16[512,2048]{1,0:T(8,128)(2,1)} %copy-done.32, bf16[512,1024]{1,0:T(8,128)(2,1)} %get-tuple-element.227.glow_ref, bf16[512,1024]{1,0:T(8,128)(2,1)} %copy-done.36), custom_call_target="tpu_custom_call" | custom-call | flops 8499999744 | bytes 29750000 | tf_op jit(solution)/shard_map/down_grads/pallas_call | solution.py:777
  315.1 12.0 %late_grads.1 = (bf16[256,2560]{1,0:T(8,128)(2,1)}, bf16[256,2560]{1,0:T(8,128)(2,1)}, bf16[256,2560]{1,0:T(8,128)(2,1)}, bf16[256,2560]{1,0:T(8,128)(2,1)}) custom-call(s32[4]{0:T(128)} %pad_add_fusion.2.at_ref.refs_0_, bf16[512,1024]{1,0:T(8,128)(2,1)} %get-tuple-element.175.refs_9_.low_ref, bf16[512,1024]{1,0:T(8,128)(2,1)} %copy-done.35, ...), custom_call_target="tpu_custom_call" | custom-call | flops 12000000000 | bytes 42000000 | tf_op jit(solution)/shard_map/late_grads/pallas_call | solution.py:851
  328.5 11.0 %halo_grads.3 = (bf16[512,512]{1,0:T(8,128)(2,1)}, bf16[512,512]{1,0:T(8,128)(2,1)}, f32[1,512]{1,0:T(1,128)}) custom-call(bf16[512,3072]{1,0:T(8,128)(2,1)} %get-tuple-element.158.q_ref.ko_ref.vo_ref, bf16[512,3072]{1,0:T(8,128)(2,1)} %get-tuple-element.158.q_ref.ko_ref.vo_ref, bf16[512,3072]{1,0:T(8,128)(2,1)} %get-tuple-element.164.kp_ref.vp_ref.qp_ref, ...), custom_call_target="tpu_custom_call" | custom-call | flops 50000000 | bytes 175000 | tf_op jit(solution)/shard_map/halo_grads/pallas_call | solution.py:270
  340.1 11.0 %halo_grads.2 = (bf16[512,512]{1,0:T(8,128)(2,1)}, bf16[512,512]{1,0:T(8,128)(2,1)}, f32[1,512]{1,0:T(1,128)}) custom-call(bf16[512,3072]{1,0:T(8,128)(2,1)} %get-tuple-element.158.q_ref.ko_ref.vo_ref, bf16[512,3072]{1,0:T(8,128)(2,1)} %get-tuple-element.158.q_ref.ko_ref.vo_ref, bf16[512,3072]{1,0:T(8,128)(2,1)} %get-tuple-element.164.kp_ref.vp_ref.qp_ref, ...), custom_call_target="tpu_custom_call" | custom-call | flops 50000000 | bytes 175000 | tf_op jit(solution)/shard_map/halo_grads/pallas_call | solution.py:270
  352.5 5.1 %collective-permute-done.30 = bf16[2,4,32,2560]{3,2,1,0:T(8,128)(2,1)} collective-permute-done((bf16[2,4,32,2560]{3,2,1,0:T(8,128)(2,1)}, bf16[2,4,32,2560]{3,2,1,0:T(8,128)(2,1)}, u32[]{:S(2)}, u32[]{:S(2)}) %collective-permute-start.30) | collective-permute-done | bytes 1310752 | tf_op jit(solution)/shard_map/ppermute | solution.py:896
  363.1 8.3 %qkv_grads.1 = (bf16[256,1664]{1,0:T(8,128)(2,1)}, bf16[256,1664]{1,0:T(8,128)(2,1)}, bf16[256,1664]{1,0:T(8,128)(2,1)}, bf16[256,1664]{1,0:T(8,128)(2,1)}) custom-call(s32[4]{0:T(128)} %pad_add_fusion.2.at_ref.refs_0_, bf16[512,1024]{1,0:T(8,128)(2,1)} %bitcast.15.refs_9_.x_ref, bf16[512,1024]{1,0:T(8,128)(2,1)} %collective-permute-done.17.x_got, ...), custom_call_target="tpu_custom_call" | custom-call | flops 8300000256 | bytes 29050000 | tf_op jit(solution)/shard_map/qkv_grads/pallas_call | solution.py:879
  371.4 4.7 %collective-permute-done.35 = bf16[4,32,2560]{2,1,0:T(8,128)(2,1)S(1)} collective-permute-done((bf16[4,32,2560]{2,1,0:T(8,128)(2,1)S(1)}, bf16[4,32,2560]{2,1,0:T(8,128)(2,1)S(1)}, u32[]{:S(2)}, u32[]{:S(2)}) %collective-permute-start.35) | collective-permute-done | bytes 655392 | tf_op jit(solution)/shard_map/ppermute | solution.py:896
  382.4 16.3 %collective-permute-done.37 = bf16[2,4,32,1664]{3,2,1,0:T(8,128)(2,1)} collective-permute-done((bf16[2,4,32,1664]{3,2,1,0:T(8,128)(2,1)}, bf16[2,4,32,1664]{3,2,1,0:T(8,128)(2,1)}, u32[]{:S(2)}, u32[]{:S(2)}) %collective-permute-start.37) | collective-permute-done | bytes 852000 | tf_op jit(solution)/shard_map/ppermute | solution.py:896
  409.7 11.2 %reduce-scatter.6.cloned.1.call-done = bf16[1,2,32,2560]{3,2,1,0:T(8,128)(2,1)} async-done(((bf16[4,2,32,2560]{3,2,1,0:T(8,128)(2,1)}), bf16[1,2,32,2560]{3,2,1,0:T(8,128)(2,1)}) %reduce-scatter.6.cloned.1.call-update) | async-done | bytes 327696 | tf_op jit(solution)/shard_map/reduce_scatter | solution.py:1075
  428.2 6.7 %fusion.43 = f32[512,1024]{1,0:T(8,128)S(1)} fusion(bf16[512,3072]{1,0:T(8,128)(2,1)} %constant_dynamic-update-slice_fusion.6, bf16[1024,3072]{1,0:T(8,128)(2,1)} %get-tuple-element.161.w_ref), kind=kOutput, calls=%fused_computation.161 | convolution fusion | flops 3221225472 | bytes 11534336 | tf_op jit(solution)/shard_map/dot_general | solution.py:33
  436.2 11.5 %reduce-scatter.8.cloned.1.call-done = bf16[1,2,32,1664]{3,2,1,0:T(8,128)(2,1)} async-done(((bf16[4,2,32,1664]{3,2,1,0:T(8,128)(2,1)}), bf16[1,2,32,1664]{3,2,1,0:T(8,128)(2,1)}) %reduce-scatter.8.cloned.1.call-update) | async-done | bytes 213008 | tf_op jit(solution)/shard_map/reduce_scatter | solution.py:1083
  (311 shorter events, 97.6 us)
Async XLA Ops:
  7.2 160.2 %all-gather.3.cloned.1.call-start = ((), (), s32[]{:S(2)}) async-start(), calls=%async_computation.6 | async-start | bytes 2621440 | tf_op jit(solution)/shard_map/all_gather | solution.py:987
  7.2 28.1 %collective-permute-start.2 = (bf16[512,1024]{1,0:T(8,128)(2,1)}, bf16[512,1024]{1,0:T(8,128)(2,1)S(1)}, u32[]{:S(2)}, u32[]{:S(2)}) collective-permute-start(bf16[512,1024]{1,0:T(8,128)(2,1)} %bitcast.15.refs_9_.x_ref), channel_id=1, source_target_pairs={{0,2},{2,4},{4,6},{6,8},{8,10},{10,12},{12,14},{14,16},{16,18},{18... | collective-permute-start | bytes 3145736 | tf_op jit(solution)/shard_map/ppermute | solution.py:949
  35.3 42.3 %collective-permute-start.5 = (bf16[512,1024]{1,0:T(8,128)(2,1)}, bf16[512,1024]{1,0:T(8,128)(2,1)S(1)}, u32[]{:S(2)}, u32[]{:S(2)}) collective-permute-start(bf16[512,1024]{1,0:T(8,128)(2,1)} %bitcast.15.refs_9_.x_ref), channel_id=1, source_target_pairs={{2,0},{4,2},{6,4},{8,6},{10,8},{12,10},{14,12},{16,14},{18,16},{20... | collective-permute-start | bytes 3145736 | tf_op jit(solution)/shard_map/ppermute | solution.py:952
  44.3 33.0 %collective-permute-start.3 = (bf16[2,2,32,2176]{3,2,1,0:T(8,128)(2,1)S(1)}, bf16[2,2,32,2176]{3,2,1,0:T(8,128)(2,1)S(1)}, u32[]{:S(2)}, u32[]{:S(2)}) collective-permute-start(bf16[2,2,32,2176]{3,2,1,0:T(8,128)(2,1)S(1)} %pad_maximum_fusion.9), channel_id=1, source_target_pairs={{0,8},{8,0},{16,24},{24,16},{1,9},{9,1},{17,25},{25,17},{2,10},{10... | collective-permute-start | bytes 1671176 | tf_op jit(solution)/shard_map/ppermute | solution.py:904
  93.5 24.3 %collective-permute-start.10 = (bf16[2,4,32,2176]{3,2,1,0:T(8,128)(2,1)S(1)}, bf16[2,4,32,2176]{3,2,1,0:T(8,128)(2,1)S(1)}, u32[]{:S(2)}, u32[]{:S(2)}) collective-permute-start(bf16[2,4,32,2176]{3,2,1,0:T(8,128)(2,1)S(1)} %pad_maximum_fusion.6.refs_3_), channel_id=1, source_target_pairs={{0,4},{4,0},{1,5},{5,1},{2,6},{6,2},{3,7},{7,3},{8,12},{12,8},{9,1... | collective-permute-start | bytes 3342344 | tf_op jit(solution)/shard_map/ppermute | solution.py:896
  94.4 24.0 %collective-permute-start.9 = (bf16[2,4,32,2176]{3,2,1,0:T(8,128)(2,1)S(1)}, bf16[2,4,32,2176]{3,2,1,0:T(8,128)(2,1)}, u32[]{:S(2)}, u32[]{:S(2)}) collective-permute-start(bf16[2,4,32,2176]{3,2,1,0:T(8,128)(2,1)S(1)} %pad_maximum_fusion.4.refs_1_), channel_id=1, source_target_pairs={{0,2},{2,0},{1,3},{3,1},{4,6},{6,4},{5,7},{7,5},{8,10},{10,8},{9,1... | collective-permute-start | bytes 3342344 | tf_op jit(solution)/shard_map/ppermute | solution.py:896
  96.8 26.4 %collective-permute-start.12 = (bf16[2,4,32,2176]{3,2,1,0:T(8,128)(2,1)S(1)}, bf16[2,4,32,2176]{3,2,1,0:T(8,128)(2,1)}, u32[]{:S(2)}, u32[]{:S(2)}) collective-permute-start(bf16[2,4,32,2176]{3,2,1,0:T(8,128)(2,1)S(1)} %pad_maximum_fusion.4.refs_1_), channel_id=1, source_target_pairs={{0,1},{1,0},{2,3},{3,2},{4,5},{5,4},{6,7},{7,6},{8,9},{9,8},{10,11... | collective-permute-start | bytes 3342344 | tf_op jit(solution)/shard_map/ppermute | solution.py:896
  121.6 72.8 %collective-permute-start.17 = (bf16[512,1024]{1,0:T(8,128)(2,1)}, bf16[512,1024]{1,0:T(8,128)(2,1)}, u32[]{:S(2)}, u32[]{:S(2)}) collective-permute-start(bf16[512,1024]{1,0:T(8,128)(2,1)} %bitcast.15.refs_9_.x_ref), channel_id=1, source_target_pairs={{0,1},{1,0},{2,3},{3,2},{4,5},{5,4},{6,7},{7,6},{8,9},{9,8},{10,11... | collective-permute-start | bytes 3145736 | tf_op jit(solution)/shard_map/ppermute | solution.py:896
  122.4 276.7 %reduce-scatter.4.cloned.1.call-start = ((), (), s32[]{:S(2)}) async-start(), calls=%async_computation.3 | async-start | bytes 5242880 | tf_op jit(solution)/shard_map/reduce_scatter | solution.py:1038
  125.2 24.9 %collective-permute-start.16 = (bf16[4,64,2048]{2,1,0:T(8,128)(2,1)S(1)}, bf16[4,64,2048]{2,1,0:T(8,128)(2,1)}, u32[]{:S(2)}, u32[]{:S(2)}) collective-permute-start(bf16[4,64,2048]{2,1,0:T(8,128)(2,1)S(1)} %bitcast.175), channel_id=1, source_target_pairs={{0,4},{4,0},{1,5},{5,1},{2,6},{6,2},{3,7},{7,3},{8,12},{12,8},{9,1... | collective-permute-start | bytes 3145736 | tf_op jit(solution)/shard_map/ppermute | solution.py:896
  153.0 48.0 %collective-permute-start.19 = (bf16[2,4,64,2048]{3,2,1,0:T(8,128)(2,1)}, bf16[2,4,64,2048]{3,2,1,0:T(8,128)(2,1)}, u32[]{:S(2)}, u32[]{:S(2)}) collective-permute-start(bf16[2,4,64,2048]{3,2,1,0:T(8,128)(2,1)} %pad_maximum_fusion.refs_1_), channel_id=1, source_target_pairs={{0,2},{2,0},{1,3},{3,1},{4,6},{6,4},{5,7},{7,5},{8,10},{10,8},{9,1... | collective-permute-start | bytes 6291464 | tf_op jit(solution)/shard_map/ppermute | solution.py:896
  155.1 45.9 %collective-permute-start.20 = (bf16[2,4,64,2048]{3,2,1,0:T(8,128)(2,1)}, bf16[2,4,64,2048]{3,2,1,0:T(8,128)(2,1)}, u32[]{:S(2)}, u32[]{:S(2)}) collective-permute-start(bf16[2,4,64,2048]{3,2,1,0:T(8,128)(2,1)} %pad_maximum_fusion.refs_1_), channel_id=1, source_target_pairs={{0,1},{1,0},{2,3},{3,2},{4,5},{5,4},{6,7},{7,6},{8,9},{9,8},{10,11... | collective-permute-start | bytes 6291464 | tf_op jit(solution)/shard_map/ppermute | solution.py:896
  167.3 33.6 %collective-permute-start.21 = (bf16[2,4,128,1024]{3,2,1,0:T(8,128)(2,1)}, bf16[2,4,128,1024]{3,2,1,0:T(8,128)(2,1)}, u32[]{:S(2)}, u32[]{:S(2)}) collective-permute-start(bf16[2,4,128,1024]{3,2,1,0:T(8,128)(2,1)} %bitcast.223), channel_id=1, source_target_pairs={{0,1},{1,0},{2,3},{3,2},{4,5},{5,4},{6,7},{7,6},{8,9},{9,8},{10,11... | collective-permute-start | bytes 6291464 | tf_op jit(solution)/shard_map/ppermute | solution.py:896
  167.8 47.5 %collective-permute-start.22 = (bf16[2,4,128,1024]{3,2,1,0:T(8,128)(2,1)}, bf16[2,4,128,1024]{3,2,1,0:T(8,128)(2,1)}, u32[]{:S(2)}, u32[]{:S(2)}) collective-permute-start(bf16[2,4,128,1024]{3,2,1,0:T(8,128)(2,1)} %bitcast.224), channel_id=1, source_target_pairs={{0,4},{4,0},{1,5},{5,1},{2,6},{6,2},{3,7},{7,3},{8,12},{12,8},{9,1... | collective-permute-start | bytes 6291464 | tf_op jit(solution)/shard_map/ppermute | solution.py:896
  219.0 45.8 %collective-permute-start.25 = (bf16[512,1024]{1,0:T(8,128)(2,1)S(1)}, bf16[512,1024]{1,0:T(8,128)(2,1)S(1)}, u32[]{:S(2)}, u32[]{:S(2)}) collective-permute-start(bf16[512,1024]{1,0:T(8,128)(2,1)S(1)} %copy-done.34), channel_id=1, source_target_pairs={{0,1},{1,0},{2,3},{3,2},{4,5},{5,4},{6,7},{7,6},{8,9},{9,8},{10,11... | collective-permute-start | bytes 3145736 | tf_op jit(solution)/shard_map/ppermute | solution.py:896
  264.7 62.4 %collective-permute-start.28 = (bf16[560,1024]{1,0:T(8,128)(2,1)}, bf16[560,1024]{1,0:T(8,128)(2,1)S(1)}, u32[]{:S(2)}, u32[]{:S(2)}) collective-permute-start(bf16[560,1024]{1,0:T(8,128)(2,1)} %get-tuple-element.183.do_ref), channel_id=1, source_target_pairs={{0,2},{2,4},{4,6},{6,8},{8,10},{10,12},{12,14},{14,16},{16,18},{18... | collective-permute-start | bytes 3440648 | tf_op jit(solution)/shard_map/ppermute | solution.py:949
  267.8 59.3 %collective-permute-start.29 = (bf16[560,1024]{1,0:T(8,128)(2,1)}, bf16[560,1024]{1,0:T(8,128)(2,1)S(1)}, u32[]{:S(2)}, u32[]{:S(2)}) collective-permute-start(bf16[560,1024]{1,0:T(8,128)(2,1)} %get-tuple-element.183.do_ref), channel_id=1, source_target_pairs={{2,0},{4,2},{6,4},{8,6},{10,8},{12,10},{14,12},{16,14},{18,16},{20... | collective-permute-start | bytes 3440648 | tf_op jit(solution)/shard_map/ppermute | solution.py:952
  271.8 43.2 %collective-permute-start.26 = (bf16[512,2048]{1,0:T(8,128)(2,1)}, bf16[512,2048]{1,0:T(8,128)(2,1)}, u32[]{:S(2)}, u32[]{:S(2)}) collective-permute-start(bf16[512,2048]{1,0:T(8,128)(2,1)} %get-tuple-element.189), channel_id=1, source_target_pairs={{0,1},{1,0},{2,3},{3,2},{4,5},{5,4},{6,7},{7,6},{8,9},{9,8},{10,11... | collective-permute-start | bytes 6291464 | tf_op jit(solution)/shard_map/ppermute | solution.py:896
  272.8 30.4 %collective-permute-start.39 = (bf16[512,2048]{1,0:T(8,128)(2,1)}, bf16[512,2048]{1,0:T(8,128)(2,1)S(1)}, u32[]{:S(2)}, u32[]{:S(2)}) collective-permute-start(bf16[512,2048]{1,0:T(8,128)(2,1)} %get-tuple-element.226), channel_id=1, source_target_pairs={{0,1},{1,0},{2,3},{3,2},{4,5},{5,4},{6,7},{7,6},{8,9},{9,8},{10,11... | collective-permute-start | bytes 6291464 | tf_op jit(solution)/shard_map/ppermute | solution.py:896
  272.9 30.2 %collective-permute-start.40 = (bf16[512,1024]{1,0:T(8,128)(2,1)}, bf16[512,1024]{1,0:T(8,128)(2,1)S(1)}, u32[]{:S(2)}, u32[]{:S(2)}) collective-permute-start(bf16[512,1024]{1,0:T(8,128)(2,1)} %get-tuple-element.227.glow_ref), channel_id=1, source_target_pairs={{0,1},{1,0},{2,3},{3,2},{4,5},{5,4},{6,7},{7,6},{8,9},{9,8},{10,11... | collective-permute-start | bytes 3145736 | tf_op jit(solution)/shard_map/ppermute | solution.py:896
  313.4 107.6 %reduce-scatter.6.cloned.1.call-start = ((), (), s32[]{:S(2)}) async-start(), calls=%async_computation.4 | async-start | bytes 1638400 | tf_op jit(solution)/shard_map/reduce_scatter | solution.py:1075
  314.8 46.0 %collective-permute-start.32 = (bf16[512,512]{1,0:T(8,128)(2,1)S(1)}, bf16[512,512]{1,0:T(8,128)(2,1)}, u32[]{:S(2)}, u32[]{:S(2)}) collective-permute-start(bf16[512,512]{1,0:T(8,128)(2,1)S(1)} %get-tuple-element.235), channel_id=1, source_target_pairs={{0,1},{1,0},{2,3},{3,2},{4,5},{5,4},{6,7},{7,6},{8,9},{9,8},{10,11... | collective-permute-start | bytes 1572872 | tf_op jit(solution)/shard_map/ppermute | solution.py:896
  327.1 30.4 %collective-permute-start.30 = (bf16[2,4,32,2560]{3,2,1,0:T(8,128)(2,1)}, bf16[2,4,32,2560]{3,2,1,0:T(8,128)(2,1)}, u32[]{:S(2)}, u32[]{:S(2)}) collective-permute-start(bf16[2,4,32,2560]{3,2,1,0:T(8,128)(2,1)} %bitcast.227), channel_id=1, source_target_pairs={{0,2},{2,0},{1,3},{3,1},{4,6},{6,4},{5,7},{7,5},{8,10},{10,8},{9,1... | collective-permute-start | bytes 3932168 | tf_op jit(solution)/shard_map/ppermute | solution.py:896
  327.2 30.4 %collective-permute-start.31 = (bf16[2,4,32,2560]{3,2,1,0:T(8,128)(2,1)}, bf16[2,4,32,2560]{3,2,1,0:T(8,128)(2,1)}, u32[]{:S(2)}, u32[]{:S(2)}) collective-permute-start(bf16[2,4,32,2560]{3,2,1,0:T(8,128)(2,1)} %bitcast.226), channel_id=1, source_target_pairs={{0,4},{4,0},{1,5},{5,1},{2,6},{6,2},{3,7},{7,3},{8,12},{12,8},{9,1... | collective-permute-start | bytes 3932168 | tf_op jit(solution)/shard_map/ppermute | solution.py:896
  339.5 21.3 %collective-permute-start.33 = (bf16[512,512]{1,0:T(8,128)(2,1)}, bf16[512,512]{1,0:T(8,128)(2,1)}, u32[]{:S(2)}, u32[]{:S(2)}) collective-permute-start(bf16[512,512]{1,0:T(8,128)(2,1)} %get-tuple-element.236), channel_id=1, source_target_pairs={{0,1},{1,0},{2,3},{3,2},{4,5},{5,4},{6,7},{7,6},{8,9},{9,8},{10,11... | collective-permute-start | bytes 1572872 | tf_op jit(solution)/shard_map/ppermute | solution.py:896
  340.0 20.8 %collective-permute-start.34 = (bf16[512,512]{1,0:T(8,128)(2,1)}, bf16[512,512]{1,0:T(8,128)(2,1)}, u32[]{:S(2)}, u32[]{:S(2)}) collective-permute-start(bf16[512,512]{1,0:T(8,128)(2,1)} %get-tuple-element.237), channel_id=1, source_target_pairs={{0,1},{1,0},{2,3},{3,2},{4,5},{5,4},{6,7},{7,6},{8,9},{9,8},{10,11... | collective-permute-start | bytes 1572872 | tf_op jit(solution)/shard_map/ppermute | solution.py:896
  380.0 67.6 %reduce-scatter.8.cloned.1.call-start = ((), (), s32[]{:S(2)}) async-start(), calls=%async_computation.5 | async-start | bytes 1064960 | tf_op jit(solution)/shard_map/reduce_scatter | solution.py:1083
  380.3 18.5 %collective-permute-start.37 = (bf16[2,4,32,1664]{3,2,1,0:T(8,128)(2,1)}, bf16[2,4,32,1664]{3,2,1,0:T(8,128)(2,1)}, u32[]{:S(2)}, u32[]{:S(2)}) collective-permute-start(bf16[2,4,32,1664]{3,2,1,0:T(8,128)(2,1)} %bitcast.230), channel_id=1, source_target_pairs={{0,2},{2,0},{1,3},{3,1},{4,6},{6,4},{5,7},{7,5},{8,10},{10,8},{9,1... | collective-permute-start | bytes 2555912 | tf_op jit(solution)/shard_map/ppermute | solution.py:896
  402.2 18.7 %collective-permute-start.41 = (bf16[4,32,1664]{2,1,0:T(8,128)(2,1)S(1)}, bf16[4,32,1664]{2,1,0:T(8,128)(2,1)}, u32[]{:S(2)}, u32[]{:S(2)}) collective-permute-start(bf16[4,32,1664]{2,1,0:T(8,128)(2,1)S(1)} %fusion.14), channel_id=1, source_target_pairs={{0,4},{4,0},{1,5},{5,1},{2,6},{6,2},{3,7},{7,3},{8,12},{12,8},{9,1... | collective-permute-start | bytes 1277960 | tf_op jit(solution)/shard_map/ppermute | solution.py:896
  405.3 30.8 %collective-permute-start.43 = (bf16[128,1024]{1,0:T(8,128)(2,1)}, bf16[128,1024]{1,0:T(8,128)(2,1)S(1)}, u32[]{:S(2)}, u32[]{:S(2)}) collective-permute-start(bf16[128,1024]{1,0:T(8,128)(2,1)} %get-tuple-element.275), channel_id=1, source_target_pairs={{0,4},{4,0},{1,5},{5,1},{2,6},{6,2},{3,7},{7,3},{8,12},{12,8},{9,1... | collective-permute-start | bytes 786440 | tf_op jit(solution)/shard_map/ppermute | solution.py:896
  405.5 30.7 %collective-permute-start.44 = (bf16[128,1024]{1,0:T(8,128)(2,1)}, bf16[128,1024]{1,0:T(8,128)(2,1)}, u32[]{:S(2)}, u32[]{:S(2)}) collective-permute-start(bf16[128,1024]{1,0:T(8,128)(2,1)} %get-tuple-element.274), channel_id=1, source_target_pairs={{0,2},{2,0},{1,3},{3,1},{4,6},{6,4},{5,7},{7,5},{8,10},{10,8},{9,1... | collective-permute-start | bytes 786440 | tf_op jit(solution)/shard_map/ppermute | solution.py:896
  406.1 30.0 %collective-permute-start.45 = (bf16[128,1024]{1,0:T(8,128)(2,1)}, bf16[128,1024]{1,0:T(8,128)(2,1)}, u32[]{:S(2)}, u32[]{:S(2)}) collective-permute-start(bf16[128,1024]{1,0:T(8,128)(2,1)} %get-tuple-element.273), channel_id=1, source_target_pairs={{0,6},{2,4},{4,2},{6,0},{1,7},{3,5},{5,3},{7,1},{8,14},{10,12},{12... | collective-permute-start | bytes 786440 | tf_op jit(solution)/shard_map/ppermute | solution.py:900
  (57 other events, 588.5 us)
Sparse Core Ops, SparseCore 0:
  122.5 44.8 all-gather.2
  313.5 74.9 reduce-scatter.3
  390.9 30.0 reduce-scatter.5
  424.6 23.0 reduce-scatter.7

commit v4 on v3

--- a/solution.py
+++ b/solution.py
@@ -130,7 +130,7 @@
     )(mixed, mixed, before, after, mixed, before, after, bias_own, bias_halo)
 
 
-def own_grad_kernel(q_ref, ko_ref, kp_ref, kn_ref, vo_ref, vp_ref, vn_ref, do_ref, log_ref, mean_ref, bo_ref, bh_ref, dq_ref, dkv_ref, sum_ref, kh, vh):
+def own_grad_kernel(q_ref, ko_ref, kp_ref, kn_ref, vo_ref, vp_ref, vn_ref, do_ref, log_ref, mean_ref, bo_ref, bh_ref, dq_keep, dq_send, dkv_ref, sum_ref, kh, vh, dq_ref):
     tokens = q_ref.shape[0]
     kh[:tokens] = kp_ref[...]
     kh[tokens:] = kn_ref[...]
@@ -181,8 +181,16 @@
                 halo.append((p * (nt(dm, vh[window]) - mean_rows[h][:, rows].T)).astype(BF16))
             dq = dq_own[ROWS * r : ROWS * r + ROWS] + nn(cat(halo, 1), stacked(kh[window], scaled))
             dq = dq.astype(BF16)
-            dq_ref[0, rows] = dq
+            dq_ref[rows] = dq
             sum_ref[...] = column_sum(dq.astype(F32)) + (sum_ref[...] if i else 0.0)
+
+    @pl.when(pl.program_id(0) < pl.num_programs(0) // 2)
+    def _():
+        dq_keep[...] = dq_ref[...]
+
+    @pl.when(pl.program_id(0) >= pl.num_programs(0) // 2)
+    def _():
+        dq_send[...] = dq_ref[...]
 
 
 def own_grads(mixed, before, after, payload, logs, means, bias_own, bias_halo):
@@ -201,18 +209,20 @@
         grid=(pairs,),
         in_specs=[column(0), column(1), column(1), column(1), column(2), column(2), column(2), block, whole(logs.shape), whole(means.shape), whole(bias_own.shape), whole(bias_halo.shape)],
         out_specs=[
-            pl.BlockSpec((1, tokens, PAIR), lambda p: (p // near, 0, p % near)),
+            pl.BlockSpec((tokens, PAIR), lambda p: (0, jnp.minimum(p, near - 1))),
+            pl.BlockSpec((tokens, PAIR), lambda p: (0, jnp.maximum(p - near, 0))),
             pl.BlockSpec((1, 2, tokens, PAIR), lambda p: (p // near, 0, 0, p % near)),
             pl.BlockSpec((1, PAIR), lambda p: (0, p)),
         ],
         out_shape=[
-            jax.ShapeDtypeStruct((2, tokens, width // 2), BF16),
+            jax.ShapeDtypeStruct((tokens, width // 2), BF16),
+            jax.ShapeDtypeStruct((tokens, width // 2), BF16),
             jax.ShapeDtypeStruct((2, 2, tokens, width // 2), F32),
             jax.ShapeDtypeStruct((1, width), F32),
         ],
-        scratch_shapes=[pltpu.VMEM((2 * tokens, PAIR), BF16), pltpu.VMEM((2 * tokens, PAIR), BF16)],
+        scratch_shapes=[pltpu.VMEM((2 * tokens, PAIR), BF16), pltpu.VMEM((2 * tokens, PAIR), BF16), pltpu.VMEM((tokens, PAIR), BF16)],
         compiler_params=params(),
-        cost_estimate=cost(29.5),
+        cost_estimate=cost(27.5),
         name="own_grads",
     )(mixed, mixed, before, after, mixed, before, after, payload, logs, means, bias_own, bias_halo)
 
@@ -576,8 +586,7 @@
     up, down, out, hat, dy, heads, act, slope, result, glow, total, branch, sides, payload, up_sems, down_sems, in_sems, out_sems = refs[23:]
     tokens, width = low_ref.shape
     half = up.shape[1] // 2
-    chunk = 512
-    steps = 2 * half // chunk
+    chunk = half
     from_up = up_copies(up_refs, up, up_sems, at_ref, far)
     from_down = down_copies(down_refs, down, down_sems, at_ref, far)
     loads = [pltpu.make_async_copy(*pair, in_sems.at[i]) for i, pair in enumerate(((hat_in, hat), (dy_in, dy), (out_in, out), (heads_in, heads)))]
@@ -592,7 +601,7 @@
         copy.start()
 
     def cols(i):
-        return pl.ds(pl.multiple_of(i * chunk, chunk), chunk)
+        return slice(i * chunk, i * chunk + chunk)
 
     def raise_one(i):
         lifted = nn(low_ref[...], up[:, cols(i)]) + row_ref[:, cols(i)]
@@ -606,21 +615,13 @@
 
     half_up, half_down = len(from_up) // 2, len(from_down) // 2
     wait_all(from_up[:half_up])
-    total[...] = jnp.zeros_like(total)
     raise_one(0)
+    wait_all(from_up[half_up:])
     wait_all(from_down[:half_down])
-
-    def both(i, carry):
-        raise_one(i)
-        settle_one(i - 1)
-        return carry
-
-    lax.fori_loop(1, steps // 2, both, 0)
-    wait_all(from_up[half_up:])
-    both(steps // 2, 0)
+    raise_one(1)
+    total[...] = nn(act[:, cols(0)], down[cols(0)])
     wait_all(from_down[half_down:])
-    lax.fori_loop(steps // 2 + 1, steps, both, 0)
-    settle_one(steps - 1)
+    settle_one(1)
     store(act.at[:, pl.ds(0, half)], act_out)
     store(act.at[:, pl.ds(half, half)], act_send)
     wait_all(loads)
@@ -651,16 +652,11 @@
         total[...] += nt(slope[:, cols(i)], up[:, cols(i)])
 
     lower_one(0)
-
-    def back(i, carry):
-        lower_one(i)
-        first_one(i - 1)
-        return carry
-
-    lax.fori_loop(1, steps, back, 0)
     store(slope.at[:, pl.ds(0, half)], lift_out)
+    lower_one(1)
     store(slope.at[:, pl.ds(half, half)], lift_send)
-    first_one(steps - 1)
+    first_one(0)
+    first_one(1)
 
     for n in range(tokens // rows):
         at = slice(rows * n, rows * n + rows)
@@ -681,14 +677,15 @@
 
     head = lax.broadcasted_iota(jnp.int32, (H, width), 1) // HD
     pick = jnp.where(head == lax.broadcasted_iota(jnp.int32, (H, width), 0), 1.0, 0.0).astype(F32)
-    for n in range(tokens // rows):
-        at = slice(rows * n, rows * n + rows)
-        grad = nt(branch[at], out[...]).astype(BF16)
-        payload[at] = grad
-        product = grad.astype(F32) * heads[at].astype(F32)
-        mean_ref[:, at] = lax.dot_general(
-            pick, product, (((1,), (1,)), ((), ())), precision=lax.Precision.HIGHEST, preferred_element_type=F32
+    for n in range(4):
+        part = slice(width // 4 * n, width // 4 * (n + 1))
+        grad = nt(branch[...], out[part]).astype(BF16)
+        payload[:tokens, part] = grad
+        product = grad.astype(F32) * heads[:, part].astype(F32)
+        means = lax.dot_general(
+            pick[:, part], product, (((1,), (1,)), ((), ())), precision=lax.Precision.HIGHEST, preferred_element_type=F32
         )
+        mean_ref[...] = means if n == 0 else mean_ref[...] + means
     rest = cat([log_ref[...], mean_ref[...]], 1)
     for n in range(3):
         term = rest.astype(BF16)
@@ -787,7 +784,7 @@
     )(at, active, act_got, glow, glow_got)
 
 
-def both_flipped(at_ref, mine_ref, got_ref, flipped, far, heads=False):
+def both_flipped(at_ref, mine_ref, got_ref, flipped, far, heads=False, distant=False):
     tokens = mine_ref.shape[0]
     for core, ref in ((0, mine_ref), (1, got_ref)):
         turned = ref[...].T
@@ -802,6 +799,9 @@
         rows = turned.shape[0] // (8 * far)
         for z in range(far):
             at_z = jnp.bitwise_xor(z, flip * (far // 2))
+            if distant:
+                away = jnp.bitwise_xor(at_z, at_ref[3])
+                at_z = away % 2 * 2 + away // 2
             for y in range(2):
                 for x in range(2):
                     a = ((z * 2 + y) * 2 + x) * 2 * rows
@@ -830,7 +830,7 @@
 
     @pl.when(step == 0)
     def _():
-        both_flipped(at_ref, low_ref, low_got, flipped, far)
+        both_flipped(at_ref, low_ref, low_got, flipped, far, distant=True)
 
     @pl.when(step < last)
     def _():
@@ -838,7 +838,7 @@
 
     @pl.when(step == last)
     def _():
-        both_flipped(at_ref, heads_ref, heads_got, flipped, far, heads=True)
+        both_flipped(at_ref, heads_ref, heads_got, flipped, far, heads=True, distant=True)
         put_quarters(quarters, slice(None), nn(flipped[...], cat([branch_ref[...], branch_got[...]], 0)).astype(BF16))
 
 
@@ -856,7 +856,7 @@
         out_shape=[jax.ShapeDtypeStruct((width // 4, (steps + 1) * chunk), BF16)] * 4,
         scratch_shapes=[pltpu.VMEM((width, 2 * tokens), BF16)],
         compiler_params=params(),
-        cost_estimate=cost(12),
+        cost_estimate=cost(9),
         name="late_grads",
     )(at, low, low_got, heads, heads_got, lift, lift_got, branch, branch_got)
 
@@ -1032,8 +1032,7 @@
     act_got, glow_got, lift_got, branch_got = swap(act_send, CORE), swap(glow, CORE), swap(lift_send, CORE), swap(branch_send, CORE)
     down_part = down_grads(far, at, active, act_got, glow, glow_got)
     late = late_grads(far, at, low, low_got, heads, heads_got, lift_keep, lift_got, branch_mine, branch_got)
-    dq, dkv, dq_sum = own_grads(mixed, before, after, payload, logs, means, bias_own, bias_halo)
-    dq_keep, dq_send = dq[0], dq[1]
+    dq_keep, dq_send, dkv, dq_sum = own_grads(mixed, before, after, payload, logs, means, bias_own, bias_halo)
     if far is not None:
         down_part = lax.psum_scatter(down_part.reshape(far, 2, 2, piece, width), FAR, scatter_dimension=0, tiled=False)
         by = lambda parts: [v.reshape(2, far, rows, v.shape[1]) for v in parts]
@@ -1072,16 +1071,19 @@
         qkv_send_x, qkv_send_y, late_xy, late_yx = together(qkv_send_x, qkv_send_y, late_xy, late_yx)
         qkv_x, qkv_y = swap(qkv_send_x, X), swap(qkv_send_y, Y)
         late_sum = color_sums(late_keep_x, late_keep_y, late_x, late_y, late_xy, late_yx)
-        late_sum = lax.psum_scatter(late_sum, FAR, scatter_dimension=0, tiled=False)
+        late_lo = swap_far(late_sum[2:], 1)
         qkv_x, qkv_y, down_part = together(qkv_x, qkv_y, down_part)
         qkv_xy, qkv_yx = color_nexts(qkv_keep_x, qkv_keep_y, qkv_x, qkv_y)
         qkv_xy, qkv_yx, down_part, *both = together(qkv_xy, qkv_yx, down_part, *keep, *send)
         keep, send = both[:3], both[3:]
         qkv_xy, qkv_yx = swap(qkv_xy, Y), swap(qkv_yx, X)
         down_y, down_x, down_xy = swap(down_part[1, 0], Y), swap(down_part[0, 1], X), swap_both(down_part[1, 1])
-        qkv_xy, qkv_yx, late_sum = together(qkv_xy, qkv_yx, late_sum)
-        qkv_sum = lax.psum_scatter(color_sums(qkv_keep_x, qkv_keep_y, qkv_x, qkv_y, qkv_xy, qkv_yx), FAR, scatter_dimension=0, tiled=False)
-        qkv_sum, down_y, down_x, down_xy, late_sum = together(qkv_sum, down_y, down_x, down_xy, late_sum)
+        qkv_xy, qkv_yx, late_lo = together(qkv_xy, qkv_yx, late_lo)
+        qkv_sum = color_sums(qkv_keep_x, qkv_keep_y, qkv_x, qkv_y, qkv_xy, qkv_yx)
+        qkv_sum, late_sum = together(qkv_sum, added(late_sum[:2], late_lo))
+        qkv_sum = lax.psum_scatter(qkv_sum, FAR, scatter_dimension=0, tiled=False)
+        late_sum = added(late_sum[0], swap_far(late_sum[1], 2))
+        late_sum, down_y, down_x, down_xy = together(late_sum, down_y, down_x, down_xy)
         down_sum = down_part[0, 0].astype(F32) + down_y.astype(F32) + down_x.astype(F32) + down_xy.astype(F32)
     inputs_grad = nt(cat([*keep, *send], 1), qkv_full)
     inputs_grad = (grad_one + inputs_grad).astype(BF16)[None]

time: 472 us -> 464 us (0.983)
  the two profiles are of different devices: /device:TPU:25 before, /device:TPU:0 now
where the time goes in v4:
time: 464 us; the launch traced here: 455 us
  Pallas kernels  171 us (37%)
  waiting for transfers between devices  153 us (33%)
  starting transfers between devices  54 us (12%)
  other arithmetic  35.3 us (8%)
  local copies, waits for them, and re-layouts  21.1 us (5%)
  between operations  15.1 us (3%)
  matrix products  4.75 us (1%)
    ppermute x39, waiting for transfers between devices, swap(): return lax.ppermute(values, axis, [(0, 1), (1, 0)])  89.2 us
    ppermute x6, waiting for transfers between devices, swap_far(): lax.ppermute(values, FAR, [(i, i ^ step) for i in range(lax.axis_size(FAR...  57.3 us
    pallas_call x1, Pallas kernels, middle(): pl.pallas_call(functools.partial(middle_kernel, far, len(up_parts), len(d...  35.8 us
    pallas_call x1, Pallas kernels, own_grads(): pl.pallas_call(own_grad_kernel, grid=(pairs,), in_specs=[column(0), colum...  28.6 us
    ppermute x39, starting transfers between devices, swap(): return lax.ppermute(values, axis, [(0, 1), (1, 0)])  23.5 us
    pallas_call x1, Pallas kernels, attend(): pl.pallas_call(attend_kernel, grid=(pairs,), in_specs=[column(0), column(...  22.4 us
    pallas_call x2, Pallas kernels, halo_grads(): pl.pallas_call(functools.partial(halo_grad_kernel, half), grid=(near,), i...  22.1 us
    ppermute x6, starting transfers between devices, swap_far(): lax.ppermute(values, FAR, [(i, i ^ step) for i in range(lax.axis_size(FAR...  18.6 us
  transfers between devices with their start and end apart: 53, of which 24 were waited for; matrix products, arithmetic and copies ran while one was open for 12% of the time, Pallas kernels for 38%

profile of v4, /device:TPU:0, one launch (start us, length us, event | category | flops | bytes accessed | tf_op | source)
XLA Modules:
  0.0 454.7 jit_solution(8011511709837258312)
XLA Ops:
  7.2 5.0 %collective-permute-start.2 = (bf16[512,1024]{1,0:T(8,128)(2,1)}, bf16[512,1024]{1,0:T(8,128)(2,1)S(1)}, u32[]{:S(2)}, u32[]{:S(2)}) collective-permute-start(bf16[512,1024]{1,0:T(8,128)(2,1)} %bitcast.15.refs_9_.x_ref), channel_id=1, source_target_pairs={{0,2},{2,4},{4,6},{6,8},{8,10},{10,12},{12,14},{14,16},{16,18},{18... | collective-permute-start | bytes 3145736 | tf_op jit(solution)/shard_map/ppermute | solution.py:949
  21.8 13.2 %collective-permute-done.1 = bf16[2,32,2176]{2,1,0:T(8,128)(2,1)S(1)} collective-permute-done((bf16[2,32,2176]{2,1,0:T(8,128)(2,1)}, bf16[2,32,2176]{2,1,0:T(8,128)(2,1)S(1)}, u32[]{:S(2)}, u32[]{:S(2)}) %collective-permute-start.1) | collective-permute-done | bytes 278560 | tf_op jit(solution)/shard_map/ppermute | solution.py:904
  37.3 10.5 %collective-permute-start.3 = (bf16[2,2,32,2176]{3,2,1,0:T(8,128)(2,1)S(1)}, bf16[2,2,32,2176]{3,2,1,0:T(8,128)(2,1)S(1)}, u32[]{:S(2)}, u32[]{:S(2)}) collective-permute-start(bf16[2,2,32,2176]{3,2,1,0:T(8,128)(2,1)S(1)} %pad_maximum_fusion.9), channel_id=1, source_target_pairs={{0,8},{8,0},{16,24},{24,16},{1,9},{9,1},{17,25},{25,17},{2,10},{10... | collective-permute-start | bytes 1671176 | tf_op jit(solution)/shard_map/ppermute | solution.py:904
  47.9 26.7 %collective-permute-done.4 = bf16[128,1024]{1,0:T(8,128)(2,1)S(1)} collective-permute-done((bf16[128,1024]{1,0:T(8,128)(2,1)S(1)}, bf16[128,1024]{1,0:T(8,128)(2,1)S(1)}, u32[]{:S(2)}, u32[]{:S(2)}) %collective-permute-start.4) | collective-permute-done | bytes 262176 | tf_op jit(solution)/shard_map/ppermute | solution.py:896
  75.5 6.5 %collective-permute-done.3 = bf16[2,2,32,2176]{3,2,1,0:T(8,128)(2,1)S(1)} collective-permute-done((bf16[2,2,32,2176]{3,2,1,0:T(8,128)(2,1)S(1)}, bf16[2,2,32,2176]{3,2,1,0:T(8,128)(2,1)S(1)}, u32[]{:S(2)}, u32[]{:S(2)}) %collective-permute-start.3) | collective-permute-done | bytes 557088 | tf_op jit(solution)/shard_map/ppermute | solution.py:904
  83.4 3.3 collective-permute-start.8
  86.7 10.1 %collective-permute-done.8 = bf16[64,2048]{1,0:T(8,128)(2,1)S(1)} collective-permute-done((bf16[64,2048]{1,0:T(8,128)(2,1)S(1)}, bf16[64,2048]{1,0:T(8,128)(2,1)S(1)}, u32[]{:S(2)}, u32[]{:S(2)}) %collective-permute-start.8) | collective-permute-done | bytes 262176 | tf_op jit(solution)/shard_map/ppermute | solution.py:904
  100.3 12.9 %collective-permute-done.11 = bf16[2,64,2048]{2,1,0:T(8,128)(2,1)S(1)} collective-permute-done((bf16[2,64,2048]{2,1,0:T(8,128)(2,1)S(1)}, bf16[2,64,2048]{2,1,0:T(8,128)(2,1)S(1)}, u32[]{:S(2)}, u32[]{:S(2)}) %collective-permute-start.11) | collective-permute-done | bytes 524320 | tf_op jit(solution)/shard_map/ppermute | solution.py:904
  113.1 10.3 %collective-permute-done.10.refs_4_ = bf16[2,4,32,2176]{3,2,1,0:T(8,128)(2,1)} collective-permute-done((bf16[2,4,32,2176]{3,2,1,0:T(8,128)(2,1)S(1)}, bf16[2,4,32,2176]{3,2,1,0:T(8,128)(2,1)}, u32[]{:S(2)}, u32[]{:S(2)}) %collective-permute-start.10) | collective-permute-done | bytes 1114144 | tf_op jit(solution)/shard_map/ppermute | solution.py:896
  132.2 13.1 %project.1 = (bf16[512,3072]{1,0:T(8,128)(2,1)}, bf16[1024,3072]{1,0:T(8,128)(2,1)}, bf16[1024,1024]{1,0:T(8,128)(2,1)}) custom-call(s32[4]{0:T(128)} %pad_add_fusion.2.at_ref.refs_0_, bf16[2,4,32,2176]{3,2,1,0:T(8,128)(2,1)} %copy-done.3, bf16[2,4,32,2176]{3,2,1,0:T(8,128)(2,1)} %collective-permute-done.9.refs_2_, bf16[2,4,32,2176]{3,2,1,0:T(8,128)(2,1)} %copy-done.2, ...), custom_call_target="tpu_custom_call" | custom-call | flops 260000000 | bytes 910000 | tf_op jit(solution)/shard_map/project/pallas_call | solution.py:481
  145.3 8.0 %collective-permute-done.16 = bf16[4,64,2048]{2,1,0:T(8,128)(2,1)} collective-permute-done((bf16[4,64,2048]{2,1,0:T(8,128)(2,1)S(1)}, bf16[4,64,2048]{2,1,0:T(8,128)(2,1)}, u32[]{:S(2)}, u32[]{:S(2)}) %collective-permute-start.16) | collective-permute-done | bytes 1048608 | tf_op jit(solution)/shard_map/ppermute | solution.py:896
  153.3 2.8 pad_maximum_fusion.refs_1_
  157.5 10.8 %project_more.1 = (bf16[512,3072]{1,0:T(8,128)(2,1)}, bf16[512,3072]{1,0:T(8,128)(2,1)}) custom-call(bf16[512,1024]{1,0:T(8,128)(2,1)} %copy-done.11, bf16[512,1024]{1,0:T(8,128)(2,1)} %copy-done.12, bf16[1024,3072]{1,0:T(8,128)(2,1)} %get-tuple-element.163.w_ref, f32[1,3072]{1,0:T(1,128)} %copy-done.24), custom_call_target="tpu_custom_call" | custom-call | flops 214000000 | bytes 749000 | tf_op jit(solution)/shard_map/project_more/pallas_call | solution.py:508
  175.4 22.4 %attend.1 = (bf16[512,1024]{1,0:T(8,128)(2,1)}, f32[16,512]{1,0:T(8,128)}) custom-call(bf16[512,3072]{1,0:T(8,128)(2,1)} %get-tuple-element.160.q_ref.ko_ref.vo_ref, bf16[512,3072]{1,0:T(8,128)(2,1)} %get-tuple-element.160.q_ref.ko_ref.vo_ref, bf16[512,3072]{1,0:T(8,128)(2,1)} %get-tuple-element.166.kp_ref.vp_ref.qp_ref, ...), custom_call_target="tpu_custom_call" | custom-call | flops 480000000 | bytes 1680000 | tf_op jit(solution)/shard_map/attend/pallas_call | solution.py:120
  198.9 5.6 %out_project.1 = (f32[512,1024]{1,0:T(8,128)}, f32[512,1]{1,0:T(8,128)}, bf16[512,1024]{1,0:T(8,128)(2,1)}) custom-call(bf16[512,1024]{1,0:T(8,128)(2,1)} %get-tuple-element.168.heads_ref.refs_16_, bf16[1024,1024]{1,0:T(8,128)(2,1)} %get-tuple-element.169.w_ref.refs_17_, bf16[512,1024]{1,0:T(8,128)(2,1)} %bitcast.15.refs_9_.x_ref, ...), custom_call_target="tpu_custom_call" | custom-call | flops 114000000 | bytes 399000 | tf_op jit(solution)/shard_map/out_project/pallas_call | solution.py:532
  204.6 14.5 %collective-permute-done.22.refs_6_ = bf16[2,4,128,1024]{3,2,1,0:T(8,128)(2,1)} collective-permute-done((bf16[2,4,128,1024]{3,2,1,0:T(8,128)(2,1)}, bf16[2,4,128,1024]{3,2,1,0:T(8,128)(2,1)}, u32[]{:S(2)}, u32[]{:S(2)}) %collective-permute-start.22) | collective-permute-done | bytes 2097184 | tf_op jit(solution)/shard_map/ppermute | solution.py:896
  223.7 3.0 collective-permute-done.24.refs_8_
  226.7 35.8 %middle.1 = (bf16[512,2048]{1,0:T(8,128)(2,1)}, bf16[512,2048]{1,0:T(8,128)(2,1)}, bf16[512,1024]{1,0:T(8,128)(2,1)}, bf16[512,1024]{1,0:T(8,128)(2,1)}, bf16[51...) custom-call(s32[4]{0:T(128)} %pad_add_fusion.2.at_ref.refs_0_, ...), custom_call_target="tpu_custom_call" | custom-call | flops 44999999488 | bytes 157500000 | tf_op jit(solution)/shard_map/middle/pallas_call | solution.py:704
  262.5 3.5 collective-permute-start.28
  267.9 28.6 %own_grads.1 = (bf16[512,512]{1,0:T(8,128)(2,1)}, bf16[512,512]{1,0:T(8,128)(2,1)}, f32[2,2,512,512]{3,2,1,0:T(8,128)}, f32[1,1024]{1,0:T(1,128)}) custom-call(bf16[512,3072]{1,0:T(8,128)(2,1)} %get-tuple-element.160.q_ref.ko_ref.vo_ref, bf16[512,3072]{1,0:T(8,128)(2,1)} %get-tuple-element.160.q_ref.ko_ref.vo_ref, ...), custom_call_target="tpu_custom_call" | custom-call | flops 27499999232 | bytes 96250000 | tf_op jit(solution)/shard_map/own_grads/pallas_call | solution.py:207
  298.8 8.5 %down_grads.1 = bf16[2048,1024]{1,0:T(8,128)(2,1)} custom-call(s32[4]{0:T(128)} %pad_add_fusion.2.at_ref.refs_0_, bf16[512,2048]{1,0:T(8,128)(2,1)} %get-tuple-element.228.act_ref, bf16[512,2048]{1,0:T(8,128)(2,1)} %collective-permute-done.39.act_got, bf16[512,1024]{1,0:T(8,128)(2,1)} %get-tuple-element.230.glow_ref, ...), custom_call_target="tpu_custom_call" | custom-call | flops 8499999744 | bytes 29750000 | tf_op jit(solution)/shard_map/down_grads/pallas_call | solution.py:774
  307.5 12.1 %late_grads.1 = (bf16[256,2560]{1,0:T(8,128)(2,1)}, bf16[256,2560]{1,0:T(8,128)(2,1)}, bf16[256,2560]{1,0:T(8,128)(2,1)}, bf16[256,2560]{1,0:T(8,128)(2,1)}) custom-call(s32[4]{0:T(128)} %pad_add_fusion.2.at_ref.refs_0_, bf16[512,1024]{1,0:T(8,128)(2,1)} %get-tuple-element.177.refs_9_.low_ref, bf16[512,1024]{1,0:T(8,128)(2,1)} %copy-done.32, ...), custom_call_target="tpu_custom_call" | custom-call | flops 8999999488 | bytes 31500000 | tf_op jit(solution)/shard_map/late_grads/pallas_call | solution.py:851
  319.6 2.7 collective-permute-start.30
  323.7 11.0 %halo_grads.3 = (bf16[512,512]{1,0:T(8,128)(2,1)}, bf16[512,512]{1,0:T(8,128)(2,1)}, f32[1,512]{1,0:T(1,128)}) custom-call(bf16[512,3072]{1,0:T(8,128)(2,1)} %get-tuple-element.160.q_ref.ko_ref.vo_ref, bf16[512,3072]{1,0:T(8,128)(2,1)} %get-tuple-element.160.q_ref.ko_ref.vo_ref, bf16[512,3072]{1,0:T(8,128)(2,1)} %get-tuple-element.166.kp_ref.vp_ref.qp_ref, ...), custom_call_target="tpu_custom_call" | custom-call | flops 50000000 | bytes 175000 | tf_op jit(solution)/shard_map/halo_grads/pallas_call | solution.py:280
  335.4 11.1 %halo_grads.2 = (bf16[512,512]{1,0:T(8,128)(2,1)}, bf16[512,512]{1,0:T(8,128)(2,1)}, f32[1,512]{1,0:T(1,128)}) custom-call(bf16[512,3072]{1,0:T(8,128)(2,1)} %get-tuple-element.160.q_ref.ko_ref.vo_ref, bf16[512,3072]{1,0:T(8,128)(2,1)} %get-tuple-element.160.q_ref.ko_ref.vo_ref, bf16[512,3072]{1,0:T(8,128)(2,1)} %get-tuple-element.166.kp_ref.vp_ref.qp_ref, ...), custom_call_target="tpu_custom_call" | custom-call | flops 50000000 | bytes 175000 | tf_op jit(solution)/shard_map/halo_grads/pallas_call | solution.py:280
  348.7 3.3 collective-permute-done.30
  360.2 8.2 %qkv_grads.1 = (bf16[256,1664]{1,0:T(8,128)(2,1)}, bf16[256,1664]{1,0:T(8,128)(2,1)}, bf16[256,1664]{1,0:T(8,128)(2,1)}, bf16[256,1664]{1,0:T(8,128)(2,1)}) custom-call(s32[4]{0:T(128)} %pad_add_fusion.2.at_ref.refs_0_, bf16[512,1024]{1,0:T(8,128)(2,1)} %bitcast.15.refs_9_.x_ref, bf16[512,1024]{1,0:T(8,128)(2,1)} %collective-permute-done.17.x_got, ...), custom_call_target="tpu_custom_call" | custom-call | flops 8300000256 | bytes 29050000 | tf_op jit(solution)/shard_map/qkv_grads/pallas_call | solution.py:879
  380.2 12.7 %collective-permute-done.37 = bf16[2,4,32,1664]{3,2,1,0:T(8,128)(2,1)} collective-permute-done((bf16[2,4,32,1664]{3,2,1,0:T(8,128)(2,1)S(1)}, bf16[2,4,32,1664]{3,2,1,0:T(8,128)(2,1)}, u32[]{:S(2)}, u32[]{:S(2)}) %collective-permute-start.37) | collective-permute-done | bytes 852000 | tf_op jit(solution)/shard_map/ppermute | solution.py:896
  404.2 4.8 %fusion.45 = f32[512,1024]{1,0:T(8,128)} fusion(bf16[512,3072]{1,0:T(8,128)(2,1)S(1)} %constant_dynamic-update-slice_fusion.6, bf16[1024,3072]{1,0:T(8,128)(2,1)S(1)} %bitcast.173), kind=kOutput, calls=%fused_computation.166 | convolution fusion | flops 3221225472 | bytes 11534336 | tf_op jit(solution)/shard_map/dot_general | solution.py:33
  416.5 2.9 fusion.8
  419.4 14.6 %collective-permute-done.45 = bf16[2,32,2560]{2,1,0:T(8,128)(2,1)S(1)} collective-permute-done((bf16[2,32,2560]{2,1,0:T(8,128)(2,1)S(1)}, bf16[2,32,2560]{2,1,0:T(8,128)(2,1)S(1)}, u32[]{:S(2)}, u32[]{:S(2)}) %collective-permute-start.45) | collective-permute-done | bytes 327712 | tf_op jit(solution)/shard_map/ppermute | solution.py:904
  438.7 4.2 reduce-scatter.5.cloned.1.call-done
  (317 shorter events, 96.8 us)
Async XLA Ops:
  7.2 163.6 %all-gather.3.cloned.1.call-start = ((), (), s32[]{:S(2)}) async-start(), calls=%async_computation.4 | async-start | bytes 2621440 | tf_op jit(solution)/shard_map/all_gather | solution.py:987
  7.2 28.8 %collective-permute-start.2 = (bf16[512,1024]{1,0:T(8,128)(2,1)}, bf16[512,1024]{1,0:T(8,128)(2,1)S(1)}, u32[]{:S(2)}, u32[]{:S(2)}) collective-permute-start(bf16[512,1024]{1,0:T(8,128)(2,1)} %bitcast.15.refs_9_.x_ref), channel_id=1, source_target_pairs={{0,2},{2,4},{4,6},{6,8},{8,10},{10,12},{12,14},{14,16},{16,18},{18... | collective-permute-start | bytes 3145736 | tf_op jit(solution)/shard_map/ppermute | solution.py:949
  36.0 46.2 %collective-permute-start.5 = (bf16[512,1024]{1,0:T(8,128)(2,1)}, bf16[512,1024]{1,0:T(8,128)(2,1)S(1)}, u32[]{:S(2)}, u32[]{:S(2)}) collective-permute-start(bf16[512,1024]{1,0:T(8,128)(2,1)} %bitcast.15.refs_9_.x_ref), channel_id=1, source_target_pairs={{2,0},{4,2},{6,4},{8,6},{10,8},{12,10},{14,12},{16,14},{18,16},{20... | collective-permute-start | bytes 3145736 | tf_op jit(solution)/shard_map/ppermute | solution.py:952
  37.3 44.6 %collective-permute-start.3 = (bf16[2,2,32,2176]{3,2,1,0:T(8,128)(2,1)S(1)}, bf16[2,2,32,2176]{3,2,1,0:T(8,128)(2,1)S(1)}, u32[]{:S(2)}, u32[]{:S(2)}) collective-permute-start(bf16[2,2,32,2176]{3,2,1,0:T(8,128)(2,1)S(1)} %pad_maximum_fusion.9), channel_id=1, source_target_pairs={{0,8},{8,0},{16,24},{24,16},{1,9},{9,1},{17,25},{25,17},{2,10},{10... | collective-permute-start | bytes 1671176 | tf_op jit(solution)/shard_map/ppermute | solution.py:904
  47.9 26.7 %collective-permute-start.4 = (bf16[128,1024]{1,0:T(8,128)(2,1)S(1)}, bf16[128,1024]{1,0:T(8,128)(2,1)S(1)}, u32[]{:S(2)}, u32[]{:S(2)}) collective-permute-start(bf16[128,1024]{1,0:T(8,128)(2,1)S(1)} %copy-done.22), channel_id=1, source_target_pairs={{0,2},{2,0},{1,3},{3,1},{4,6},{6,4},{5,7},{7,5},{8,10},{10,8},{9,1... | collective-permute-start | bytes 786440 | tf_op jit(solution)/shard_map/ppermute | solution.py:896
  96.9 26.6 %collective-permute-start.10 = (bf16[2,4,32,2176]{3,2,1,0:T(8,128)(2,1)S(1)}, bf16[2,4,32,2176]{3,2,1,0:T(8,128)(2,1)}, u32[]{:S(2)}, u32[]{:S(2)}) collective-permute-start(bf16[2,4,32,2176]{3,2,1,0:T(8,128)(2,1)S(1)} %pad_maximum_fusion.5.refs_3_), channel_id=1, source_target_pairs={{0,4},{4,0},{1,5},{5,1},{2,6},{6,2},{3,7},{7,3},{8,12},{12,8},{9,1... | collective-permute-start | bytes 3342344 | tf_op jit(solution)/shard_map/ppermute | solution.py:896
  97.9 26.0 %collective-permute-start.9 = (bf16[2,4,32,2176]{3,2,1,0:T(8,128)(2,1)S(1)}, bf16[2,4,32,2176]{3,2,1,0:T(8,128)(2,1)}, u32[]{:S(2)}, u32[]{:S(2)}) collective-permute-start(bf16[2,4,32,2176]{3,2,1,0:T(8,128)(2,1)S(1)} %pad_maximum_fusion.3.refs_1_), channel_id=1, source_target_pairs={{0,2},{2,0},{1,3},{3,1},{4,6},{6,4},{5,7},{7,5},{8,10},{10,8},{9,1... | collective-permute-start | bytes 3342344 | tf_op jit(solution)/shard_map/ppermute | solution.py:896
  100.3 25.2 %collective-permute-start.12 = (bf16[2,4,32,2176]{3,2,1,0:T(8,128)(2,1)S(1)}, bf16[2,4,32,2176]{3,2,1,0:T(8,128)(2,1)}, u32[]{:S(2)}, u32[]{:S(2)}) collective-permute-start(bf16[2,4,32,2176]{3,2,1,0:T(8,128)(2,1)S(1)} %pad_maximum_fusion.3.refs_1_), channel_id=1, source_target_pairs={{0,1},{1,0},{2,3},{3,2},{4,5},{5,4},{6,7},{7,6},{8,9},{9,8},{10,11... | collective-permute-start | bytes 3342344 | tf_op jit(solution)/shard_map/ppermute | solution.py:896
  123.9 73.9 %collective-permute-start.17 = (bf16[512,1024]{1,0:T(8,128)(2,1)}, bf16[512,1024]{1,0:T(8,128)(2,1)}, u32[]{:S(2)}, u32[]{:S(2)}) collective-permute-start(bf16[512,1024]{1,0:T(8,128)(2,1)} %bitcast.15.refs_9_.x_ref), channel_id=1, source_target_pairs={{0,1},{1,0},{2,3},{3,2},{4,5},{5,4},{6,7},{7,6},{8,9},{9,8},{10,11... | collective-permute-start | bytes 3145736 | tf_op jit(solution)/shard_map/ppermute | solution.py:896
  124.7 269.4 %reduce-scatter.3.cloned.1.call-start = ((), (), s32[]{:S(2)}) async-start(), calls=%async_computation.2 | async-start | bytes 5242880 | tf_op jit(solution)/shard_map/reduce_scatter | solution.py:1037
  127.5 25.7 %collective-permute-start.16 = (bf16[4,64,2048]{2,1,0:T(8,128)(2,1)S(1)}, bf16[4,64,2048]{2,1,0:T(8,128)(2,1)}, u32[]{:S(2)}, u32[]{:S(2)}) collective-permute-start(bf16[4,64,2048]{2,1,0:T(8,128)(2,1)S(1)} %bitcast.176), channel_id=1, source_target_pairs={{0,4},{4,0},{1,5},{5,1},{2,6},{6,2},{3,7},{7,3},{8,12},{12,8},{9,1... | collective-permute-start | bytes 3145736 | tf_op jit(solution)/shard_map/ppermute | solution.py:896
  156.1 48.5 %collective-permute-start.19 = (bf16[2,4,64,2048]{3,2,1,0:T(8,128)(2,1)}, bf16[2,4,64,2048]{3,2,1,0:T(8,128)(2,1)}, u32[]{:S(2)}, u32[]{:S(2)}) collective-permute-start(bf16[2,4,64,2048]{3,2,1,0:T(8,128)(2,1)} %pad_maximum_fusion.refs_1_), channel_id=1, source_target_pairs={{0,2},{2,0},{1,3},{3,1},{4,6},{6,4},{5,7},{7,5},{8,10},{10,8},{9,1... | collective-permute-start | bytes 6291464 | tf_op jit(solution)/shard_map/ppermute | solution.py:896
  157.5 47.1 %collective-permute-start.20 = (bf16[2,4,64,2048]{3,2,1,0:T(8,128)(2,1)}, bf16[2,4,64,2048]{3,2,1,0:T(8,128)(2,1)}, u32[]{:S(2)}, u32[]{:S(2)}) collective-permute-start(bf16[2,4,64,2048]{3,2,1,0:T(8,128)(2,1)} %pad_maximum_fusion.refs_1_), channel_id=1, source_target_pairs={{0,1},{1,0},{2,3},{3,2},{4,5},{5,4},{6,7},{7,6},{8,9},{9,8},{10,11... | collective-permute-start | bytes 6291464 | tf_op jit(solution)/shard_map/ppermute | solution.py:896
  170.8 33.8 %collective-permute-start.21 = (bf16[2,4,128,1024]{3,2,1,0:T(8,128)(2,1)}, bf16[2,4,128,1024]{3,2,1,0:T(8,128)(2,1)}, u32[]{:S(2)}, u32[]{:S(2)}) collective-permute-start(bf16[2,4,128,1024]{3,2,1,0:T(8,128)(2,1)} %bitcast.221), channel_id=1, source_target_pairs={{0,1},{1,0},{2,3},{3,2},{4,5},{5,4},{6,7},{7,6},{8,9},{9,8},{10,11... | collective-permute-start | bytes 6291464 | tf_op jit(solution)/shard_map/ppermute | solution.py:896
  170.8 48.4 %collective-permute-start.22 = (bf16[2,4,128,1024]{3,2,1,0:T(8,128)(2,1)}, bf16[2,4,128,1024]{3,2,1,0:T(8,128)(2,1)}, u32[]{:S(2)}, u32[]{:S(2)}) collective-permute-start(bf16[2,4,128,1024]{3,2,1,0:T(8,128)(2,1)} %bitcast.222), channel_id=1, source_target_pairs={{0,4},{4,0},{1,5},{5,1},{2,6},{6,2},{3,7},{7,3},{8,12},{12,8},{9,1... | collective-permute-start | bytes 6291464 | tf_op jit(solution)/shard_map/ppermute | solution.py:896
  222.5 40.0 %collective-permute-start.25 = (bf16[512,1024]{1,0:T(8,128)(2,1)S(1)}, bf16[512,1024]{1,0:T(8,128)(2,1)S(1)}, u32[]{:S(2)}, u32[]{:S(2)}) collective-permute-start(bf16[512,1024]{1,0:T(8,128)(2,1)S(1)} %copy-done.31), channel_id=1, source_target_pairs={{0,1},{1,0},{2,3},{3,2},{4,5},{5,4},{6,7},{7,6},{8,9},{9,8},{10,11... | collective-permute-start | bytes 3145736 | tf_op jit(solution)/shard_map/ppermute | solution.py:896
  262.5 57.1 %collective-permute-start.28 = (bf16[560,1024]{1,0:T(8,128)(2,1)}, bf16[560,1024]{1,0:T(8,128)(2,1)S(1)}, u32[]{:S(2)}, u32[]{:S(2)}) collective-permute-start(bf16[560,1024]{1,0:T(8,128)(2,1)} %get-tuple-element.185.do_ref), channel_id=1, source_target_pairs={{0,2},{2,4},{4,6},{6,8},{8,10},{10,12},{12,14},{14,16},{16,18},{18... | collective-permute-start | bytes 3440648 | tf_op jit(solution)/shard_map/ppermute | solution.py:949
  265.9 53.7 %collective-permute-start.29 = (bf16[560,1024]{1,0:T(8,128)(2,1)}, bf16[560,1024]{1,0:T(8,128)(2,1)S(1)}, u32[]{:S(2)}, u32[]{:S(2)}) collective-permute-start(bf16[560,1024]{1,0:T(8,128)(2,1)} %get-tuple-element.185.do_ref), channel_id=1, source_target_pairs={{2,0},{4,2},{6,4},{8,6},{10,8},{12,10},{14,12},{16,14},{18,16},{20... | collective-permute-start | bytes 3440648 | tf_op jit(solution)/shard_map/ppermute | solution.py:952
  267.2 40.2 %collective-permute-start.26 = (bf16[512,2048]{1,0:T(8,128)(2,1)}, bf16[512,2048]{1,0:T(8,128)(2,1)}, u32[]{:S(2)}, u32[]{:S(2)}) collective-permute-start(bf16[512,2048]{1,0:T(8,128)(2,1)} %get-tuple-element.191), channel_id=1, source_target_pairs={{0,1},{1,0},{2,3},{3,2},{4,5},{5,4},{6,7},{7,6},{8,9},{9,8},{10,11... | collective-permute-start | bytes 6291464 | tf_op jit(solution)/shard_map/ppermute | solution.py:896
  267.3 31.4 %collective-permute-start.39 = (bf16[512,2048]{1,0:T(8,128)(2,1)}, bf16[512,2048]{1,0:T(8,128)(2,1)}, u32[]{:S(2)}, u32[]{:S(2)}) collective-permute-start(bf16[512,2048]{1,0:T(8,128)(2,1)} %get-tuple-element.229), channel_id=1, source_target_pairs={{0,1},{1,0},{2,3},{3,2},{4,5},{5,4},{6,7},{7,6},{8,9},{9,8},{10,11... | collective-permute-start | bytes 6291464 | tf_op jit(solution)/shard_map/ppermute | solution.py:896
  267.8 30.4 %collective-permute-start.40 = (bf16[512,1024]{1,0:T(8,128)(2,1)}, bf16[512,1024]{1,0:T(8,128)(2,1)}, u32[]{:S(2)}, u32[]{:S(2)}) collective-permute-start(bf16[512,1024]{1,0:T(8,128)(2,1)} %get-tuple-element.230.glow_ref), channel_id=1, source_target_pairs={{0,1},{1,0},{2,3},{3,2},{4,5},{5,4},{6,7},{7,6},{8,9},{9,8},{10,11... | collective-permute-start | bytes 3145736 | tf_op jit(solution)/shard_map/ppermute | solution.py:896
  298.7 57.9 %collective-permute-start.32 = (bf16[512,512]{1,0:T(8,128)(2,1)}, bf16[512,512]{1,0:T(8,128)(2,1)}, u32[]{:S(2)}, u32[]{:S(2)}) collective-permute-start(bf16[512,512]{1,0:T(8,128)(2,1)} %get-tuple-element.238), channel_id=1, source_target_pairs={{0,1},{1,0},{2,3},{3,2},{4,5},{5,4},{6,7},{7,6},{8,9},{9,8},{10,11... | collective-permute-start | bytes 1572872 | tf_op jit(solution)/shard_map/ppermute | solution.py:896
  307.4 135.5 %reduce-scatter.5.cloned.1.call-start = ((), (), s32[]{:S(2)}) async-start(), calls=%async_computation.3 | async-start | bytes 1064960 | tf_op jit(solution)/shard_map/reduce_scatter | solution.py:1084
  319.6 32.3 %collective-permute-start.30 = (bf16[2,4,32,2560]{3,2,1,0:T(8,128)(2,1)}, bf16[2,4,32,2560]{3,2,1,0:T(8,128)(2,1)}, u32[]{:S(2)}, u32[]{:S(2)}) collective-permute-start(bf16[2,4,32,2560]{3,2,1,0:T(8,128)(2,1)} %bitcast.225), channel_id=1, source_target_pairs={{0,2},{2,0},{1,3},{3,1},{4,6},{6,4},{5,7},{7,5},{8,10},{10,8},{9,1... | collective-permute-start | bytes 3932168 | tf_op jit(solution)/shard_map/ppermute | solution.py:896
  322.3 31.1 %collective-permute-start.31 = (bf16[2,4,32,2560]{3,2,1,0:T(8,128)(2,1)}, bf16[2,4,32,2560]{3,2,1,0:T(8,128)(2,1)}, u32[]{:S(2)}, u32[]{:S(2)}) collective-permute-start(bf16[2,4,32,2560]{3,2,1,0:T(8,128)(2,1)} %bitcast.224), channel_id=1, source_target_pairs={{0,4},{4,0},{1,5},{5,1},{2,6},{6,2},{3,7},{7,3},{8,12},{12,8},{9,1... | collective-permute-start | bytes 3932168 | tf_op jit(solution)/shard_map/ppermute | solution.py:896
  334.8 21.8 %collective-permute-start.33 = (bf16[512,512]{1,0:T(8,128)(2,1)}, bf16[512,512]{1,0:T(8,128)(2,1)}, u32[]{:S(2)}, u32[]{:S(2)}) collective-permute-start(bf16[512,512]{1,0:T(8,128)(2,1)} %get-tuple-element.239), channel_id=1, source_target_pairs={{0,1},{1,0},{2,3},{3,2},{4,5},{5,4},{6,7},{7,6},{8,9},{9,8},{10,11... | collective-permute-start | bytes 1572872 | tf_op jit(solution)/shard_map/ppermute | solution.py:896
  334.9 21.8 %collective-permute-start.34 = (bf16[512,512]{1,0:T(8,128)(2,1)}, bf16[512,512]{1,0:T(8,128)(2,1)}, u32[]{:S(2)}, u32[]{:S(2)}) collective-permute-start(bf16[512,512]{1,0:T(8,128)(2,1)} %get-tuple-element.240), channel_id=1, source_target_pairs={{0,1},{1,0},{2,3},{3,2},{4,5},{5,4},{6,7},{7,6},{8,9},{9,8},{10,11... | collective-permute-start | bytes 1572872 | tf_op jit(solution)/shard_map/ppermute | solution.py:896
  373.8 19.1 %collective-permute-start.37 = (bf16[2,4,32,1664]{3,2,1,0:T(8,128)(2,1)S(1)}, bf16[2,4,32,1664]{3,2,1,0:T(8,128)(2,1)}, u32[]{:S(2)}, u32[]{:S(2)}) collective-permute-start(bf16[2,4,32,1664]{3,2,1,0:T(8,128)(2,1)S(1)} %bitcast.228), channel_id=1, source_target_pairs={{0,2},{2,0},{1,3},{3,1},{4,6},{6,4},{5,7},{7,5},{8,10},{10,8},{9,1... | collective-permute-start | bytes 2555912 | tf_op jit(solution)/shard_map/ppermute | solution.py:896
  379.5 29.4 %collective-permute-start.43 = (bf16[2,2,32,2560]{3,2,1,0:T(8,128)(2,1)}, bf16[2,2,32,2560]{3,2,1,0:T(8,128)(2,1)}, u32[]{:S(2)}, u32[]{:S(2)}) collective-permute-start(bf16[2,2,32,2560]{3,2,1,0:T(8,128)(2,1)} %fusion.17), channel_id=1, source_target_pairs={{0,8},{8,0},{16,24},{24,16},{1,9},{9,1},{17,25},{25,17},{2,10},{10... | collective-permute-start | bytes 1966088 | tf_op jit(solution)/shard_map/ppermute | solution.py:904
  399.0 35.0 %collective-permute-start.46 = (bf16[128,1024]{1,0:T(8,128)(2,1)}, bf16[128,1024]{1,0:T(8,128)(2,1)}, u32[]{:S(2)}, u32[]{:S(2)}) collective-permute-start(bf16[128,1024]{1,0:T(8,128)(2,1)} %get-tuple-element.279), channel_id=1, source_target_pairs={{0,4},{4,0},{1,5},{5,1},{2,6},{6,2},{3,7},{7,3},{8,12},{12,8},{9,1... | collective-permute-start | bytes 786440 | tf_op jit(solution)/shard_map/ppermute | solution.py:896
  400.3 33.7 %collective-permute-start.47 = (bf16[128,1024]{1,0:T(8,128)(2,1)}, bf16[128,1024]{1,0:T(8,128)(2,1)}, u32[]{:S(2)}, u32[]{:S(2)}) collective-permute-start(bf16[128,1024]{1,0:T(8,128)(2,1)} %get-tuple-element.278), channel_id=1, source_target_pairs={{0,2},{2,0},{1,3},{3,1},{4,6},{6,4},{5,7},{7,5},{8,10},{10,8},{9,1... | collective-permute-start | bytes 786440 | tf_op jit(solution)/shard_map/ppermute | solution.py:896
  408.9 25.1 %collective-permute-start.48 = (bf16[128,1024]{1,0:T(8,128)(2,1)}, bf16[128,1024]{1,0:T(8,128)(2,1)}, u32[]{:S(2)}, u32[]{:S(2)}) collective-permute-start(bf16[128,1024]{1,0:T(8,128)(2,1)} %get-tuple-element.277), channel_id=1, source_target_pairs={{0,6},{2,4},{4,2},{6,0},{1,7},{3,5},{5,3},{7,1},{8,14},{10,12},{12... | collective-permute-start | bytes 786440 | tf_op jit(solution)/shard_map/ppermute | solution.py:900
  (59 other events, 677.0 us)
Sparse Core Ops, SparseCore 0:
  124.8 45.9 all-gather.2
  307.5 77.1 reduce-scatter.2
  419.5 23.3 reduce-scatter.4

commit v5 on v4

--- a/solution.py
+++ b/solution.py
@@ -864,7 +864,7 @@
 def qkv_grad_kernel(far, at_ref, x_ref, x_got, *refs):
     keeps, gots, refs = refs[:3], refs[3:6], refs[6:]
     note_refs, quarters, flipped = refs[:-5], refs[-5:-1], refs[-1]
-    both_flipped(at_ref, x_ref, x_got, flipped, far)
+    both_flipped(at_ref, x_ref, x_got, flipped, far, distant=True)
     chunk = keeps[0].shape[1]
     for n in range(3):
         dw = nn(flipped[...], cat([keeps[n][...], gots[n][...]], 0)).astype(BF16)
@@ -1065,7 +1065,10 @@
         for axis, index in ((1, at[1]), (2, at[0])):
             small = jnp.where(index == 0, small, jnp.flip(small, axis))
         small = jnp.stack([jnp.flip(small[0], 0), jnp.flip(small[1].swapaxes(0, 1), 0)])
-        small = small.reshape(8 * far, lines, 128)
+        small = small.reshape(2, 2, 2, 2, 2, lines, 128)
+        for axis, index in ((3, at[3] // 2), (4, at[3] % 2)):
+            small = jnp.where(index == 0, small, jnp.flip(small, axis))
+        small = small.swapaxes(3, 4).reshape(8 * far, lines, 128)
         note = jnp.zeros((8 * far, rows, 128), BF16).at[:, :lines].set(small).reshape(width, 128)
         qkv_send_x, qkv_keep_x, qkv_send_y, qkv_keep_y = by(qkv_grads(far, at, x, x_got, keep, got, (note,)))
         qkv_send_x, qkv_send_y, late_xy, late_yx = together(qkv_send_x, qkv_send_y, late_xy, late_yx)
@@ -1081,13 +1084,18 @@
         qkv_xy, qkv_yx, late_lo = together(qkv_xy, qkv_yx, late_lo)
         qkv_sum = color_sums(qkv_keep_x, qkv_keep_y, qkv_x, qkv_y, qkv_xy, qkv_yx)
         qkv_sum, late_sum = together(qkv_sum, added(late_sum[:2], late_lo))
-        qkv_sum = lax.psum_scatter(qkv_sum, FAR, scatter_dimension=0, tiled=False)
-        late_sum = added(late_sum[0], swap_far(late_sum[1], 2))
+        qkv_lo, late_hi = swap_far(qkv_sum[2:], 1), swap_far(late_sum[1], 2)
+        qkv_lo, late_hi = together(qkv_lo, late_hi)
+        qkv_sum = added(qkv_sum[:2], qkv_lo)
+        qkv_sum = added(qkv_sum[0], swap_far(qkv_sum[1], 2))
+        late_sum = added(late_sum[0], late_hi)
         late_sum, down_y, down_x, down_xy = together(late_sum, down_y, down_x, down_xy)
         down_sum = down_part[0, 0].astype(F32) + down_y.astype(F32) + down_x.astype(F32) + down_xy.astype(F32)
     inputs_grad = nt(cat([*keep, *send], 1), qkv_full)
     inputs_grad = (grad_one + inputs_grad).astype(BF16)[None]
     wide = hidden // 2
+    if far is not None:
+        qkv_sum, late_sum = together(qkv_sum, late_sum)
     left, right = own_rows(core, late_sum)
     up_sum = jnp.stack([v[:, :wide].reshape(rows, blocks, piece) for v in (left, right)], 2).reshape(rows, hidden).astype(F32)
     out_sum = cat([left[:, wide:], right[:, wide:]], 1).astype(F32)

time: 464 us -> 460 us (level)
  the two profiles are of different devices: /device:TPU:0 before, /device:TPU:25 now
where the time goes in v5:
time: 460 us; the launch traced here: 451 us
  Pallas kernels  171 us (37%)
  waiting for transfers between devices  142 us (31%)
  starting transfers between devices  66.4 us (14%)
  other arithmetic  30.9 us (7%)
  local copies, waits for them, and re-layouts  20.9 us (5%)
  between operations  15.7 us (3%)
    ppermute x39, waiting for transfers between devices, swap(): return lax.ppermute(values, axis, [(0, 1), (1, 0)])  73.9 us
    ppermute x8, waiting for transfers between devices, swap_far(): lax.ppermute(values, FAR, [(i, i ^ step) for i in range(lax.axis_size(FAR...  66.4 us
    pallas_call x1, Pallas kernels, middle(): pl.pallas_call(functools.partial(middle_kernel, far, len(up_parts), len(d...  36 us
    ppermute x39, starting transfers between devices, swap(): return lax.ppermute(values, axis, [(0, 1), (1, 0)])  35.5 us
    pallas_call x1, Pallas kernels, own_grads(): pl.pallas_call(own_grad_kernel, grid=(pairs,), in_specs=[column(0), colum...  28.4 us
    pallas_call x1, Pallas kernels, attend(): pl.pallas_call(attend_kernel, grid=(pairs,), in_specs=[column(0), column(...  22.4 us
    pallas_call x2, Pallas kernels, halo_grads(): pl.pallas_call(functools.partial(halo_grad_kernel, half), grid=(near,), i...  22.1 us
    pallas_call x1, Pallas kernels, project(): pl.pallas_call(functools.partial(project_kernel, far, len(parts)), in_spe...  13.3 us
  transfers between devices with their start and end apart: 54, of which 24 were waited for; matrix products, arithmetic and copies ran while one was open for 11% of the time, Pallas kernels for 38%

profile of v5, /device:TPU:25, one launch (start us, length us, event | category | flops | bytes accessed | tf_op | source)
XLA Modules:
  0.0 450.6 jit_solution(905475273924498635)
XLA Ops:
  7.2 3.3 collective-permute-start.2
  18.1 15.5 %collective-permute-done.1 = bf16[2,32,2176]{2,1,0:T(8,128)(2,1)S(1)} collective-permute-done((bf16[2,32,2176]{2,1,0:T(8,128)(2,1)}, bf16[2,32,2176]{2,1,0:T(8,128)(2,1)S(1)}, u32[]{:S(2)}, u32[]{:S(2)}) %collective-permute-start.1) | collective-permute-done | bytes 278560 | tf_op jit(solution)/shard_map/ppermute | solution.py:904
  35.3 9.0 %collective-permute-start.5 = (bf16[512,1024]{1,0:T(8,128)(2,1)}, bf16[512,1024]{1,0:T(8,128)(2,1)S(1)}, u32[]{:S(2)}, u32[]{:S(2)}) collective-permute-start(bf16[512,1024]{1,0:T(8,128)(2,1)} %bitcast.15.refs_9_.x_ref), channel_id=1, source_target_pairs={{2,0},{4,2},{6,4},{8,6},{10,8},{12,10},{14,12},{16,14},{18,16},{20... | collective-permute-start | bytes 3145736 | tf_op jit(solution)/shard_map/ppermute | solution.py:952
  44.3 5.5 %collective-permute-start.3 = (bf16[2,2,32,2176]{3,2,1,0:T(8,128)(2,1)S(1)}, bf16[2,2,32,2176]{3,2,1,0:T(8,128)(2,1)S(1)}, u32[]{:S(2)}, u32[]{:S(2)}) collective-permute-start(bf16[2,2,32,2176]{3,2,1,0:T(8,128)(2,1)S(1)} %pad_maximum_fusion.9), channel_id=1, source_target_pairs={{0,8},{8,0},{16,24},{24,16},{1,9},{9,1},{17,25},{25,17},{2,10},{10... | collective-permute-start | bytes 1671176 | tf_op jit(solution)/shard_map/ppermute | solution.py:904
  49.8 15.9 %collective-permute-done.4 = bf16[128,1024]{1,0:T(8,128)(2,1)S(1)} collective-permute-done((bf16[128,1024]{1,0:T(8,128)(2,1)S(1)}, bf16[128,1024]{1,0:T(8,128)(2,1)S(1)}, u32[]{:S(2)}, u32[]{:S(2)}) %collective-permute-start.4) | collective-permute-done | bytes 262176 | tf_op jit(solution)/shard_map/ppermute | solution.py:896
  66.6 10.8 %collective-permute-done.3 = bf16[2,2,32,2176]{3,2,1,0:T(8,128)(2,1)S(1)} collective-permute-done((bf16[2,2,32,2176]{3,2,1,0:T(8,128)(2,1)S(1)}, bf16[2,2,32,2176]{3,2,1,0:T(8,128)(2,1)S(1)}, u32[]{:S(2)}, u32[]{:S(2)}) %collective-permute-start.3) | collective-permute-done | bytes 557088 | tf_op jit(solution)/shard_map/ppermute | solution.py:904
  79.8 13.8 %collective-permute-done.8 = bf16[64,2048]{1,0:T(8,128)(2,1)S(1)} collective-permute-done((bf16[64,2048]{1,0:T(8,128)(2,1)S(1)}, bf16[64,2048]{1,0:T(8,128)(2,1)S(1)}, u32[]{:S(2)}, u32[]{:S(2)}) %collective-permute-start.8) | collective-permute-done | bytes 262176 | tf_op jit(solution)/shard_map/ppermute | solution.py:904
  99.4 8.8 %collective-permute-done.11 = bf16[2,64,2048]{2,1,0:T(8,128)(2,1)} collective-permute-done((bf16[2,64,2048]{2,1,0:T(8,128)(2,1)S(1)}, bf16[2,64,2048]{2,1,0:T(8,128)(2,1)}, u32[]{:S(2)}, u32[]{:S(2)}) %collective-permute-start.11) | collective-permute-done | bytes 524320 | tf_op jit(solution)/shard_map/ppermute | solution.py:904
  108.1 10.5 %collective-permute-done.10.refs_4_ = bf16[2,4,32,2176]{3,2,1,0:T(8,128)(2,1)} collective-permute-done((bf16[2,4,32,2176]{3,2,1,0:T(8,128)(2,1)S(1)}, bf16[2,4,32,2176]{3,2,1,0:T(8,128)(2,1)}, u32[]{:S(2)}, u32[]{:S(2)}) %collective-permute-start.10) | collective-permute-done | bytes 1114144 | tf_op jit(solution)/shard_map/ppermute | solution.py:896
  129.6 13.3 %project.1 = (bf16[512,3072]{1,0:T(8,128)(2,1)}, bf16[1024,3072]{1,0:T(8,128)(2,1)}, bf16[1024,1024]{1,0:T(8,128)(2,1)}) custom-call(s32[4]{0:T(128)} %pad_add_fusion.2.at_ref.refs_0_, bf16[2,4,32,2176]{3,2,1,0:T(8,128)(2,1)} %copy-done.3, bf16[2,4,32,2176]{3,2,1,0:T(8,128)(2,1)} %collective-permute-done.9.refs_2_, bf16[2,4,32,2176]{3,2,1,0:T(8,128)(2,1)} %copy-done.2, ...), custom_call_target="tpu_custom_call" | custom-call | flops 260000000 | bytes 910000 | tf_op jit(solution)/shard_map/project/pallas_call | solution.py:481
  142.9 7.0 %collective-permute-done.16 = bf16[4,64,2048]{2,1,0:T(8,128)(2,1)} collective-permute-done((bf16[4,64,2048]{2,1,0:T(8,128)(2,1)S(1)}, bf16[4,64,2048]{2,1,0:T(8,128)(2,1)}, u32[]{:S(2)}, u32[]{:S(2)}) %collective-permute-start.16) | collective-permute-done | bytes 1048608 | tf_op jit(solution)/shard_map/ppermute | solution.py:896
  149.9 2.8 pad_maximum_fusion.refs_1_
  155.3 10.8 %project_more.1 = (bf16[512,3072]{1,0:T(8,128)(2,1)}, bf16[512,3072]{1,0:T(8,128)(2,1)}) custom-call(bf16[512,1024]{1,0:T(8,128)(2,1)} %copy-done.11, bf16[512,1024]{1,0:T(8,128)(2,1)} %copy-done.12, bf16[1024,3072]{1,0:T(8,128)(2,1)} %get-tuple-element.167.w_ref, f32[1,3072]{1,0:T(1,128)} %copy-done.23), custom_call_target="tpu_custom_call" | custom-call | flops 214000000 | bytes 749000 | tf_op jit(solution)/shard_map/project_more/pallas_call | solution.py:508
  171.8 22.4 %attend.1 = (bf16[512,1024]{1,0:T(8,128)(2,1)}, f32[16,512]{1,0:T(8,128)}) custom-call(bf16[512,3072]{1,0:T(8,128)(2,1)} %get-tuple-element.164.q_ref.ko_ref.vo_ref, bf16[512,3072]{1,0:T(8,128)(2,1)} %get-tuple-element.164.q_ref.ko_ref.vo_ref, bf16[512,3072]{1,0:T(8,128)(2,1)} %get-tuple-element.170.kp_ref.vp_ref.qp_ref, ...), custom_call_target="tpu_custom_call" | custom-call | flops 480000000 | bytes 1680000 | tf_op jit(solution)/shard_map/attend/pallas_call | solution.py:120
  195.5 5.4 %out_project.1 = (f32[512,1024]{1,0:T(8,128)}, f32[512,1]{1,0:T(8,128)}, bf16[512,1024]{1,0:T(8,128)(2,1)}) custom-call(bf16[512,1024]{1,0:T(8,128)(2,1)} %get-tuple-element.172.heads_ref.refs_16_, bf16[1024,1024]{1,0:T(8,128)(2,1)} %get-tuple-element.173.w_ref.refs_17_, bf16[512,1024]{1,0:T(8,128)(2,1)} %bitcast.15.refs_9_.x_ref, ...), custom_call_target="tpu_custom_call" | custom-call | flops 114000000 | bytes 399000 | tf_op jit(solution)/shard_map/out_project/pallas_call | solution.py:532
  200.9 14.2 %collective-permute-done.22.refs_6_ = bf16[2,4,128,1024]{3,2,1,0:T(8,128)(2,1)} collective-permute-done((bf16[2,4,128,1024]{3,2,1,0:T(8,128)(2,1)}, bf16[2,4,128,1024]{3,2,1,0:T(8,128)(2,1)}, u32[]{:S(2)}, u32[]{:S(2)}) %collective-permute-start.22) | collective-permute-done | bytes 2097184 | tf_op jit(solution)/shard_map/ppermute | solution.py:896
  220.1 3.0 collective-permute-done.24.refs_8_
  223.1 36.0 %middle.1 = (bf16[512,2048]{1,0:T(8,128)(2,1)}, bf16[512,2048]{1,0:T(8,128)(2,1)}, bf16[512,1024]{1,0:T(8,128)(2,1)}, bf16[512,1024]{1,0:T(8,128)(2,1)}, bf16[51...) custom-call(s32[4]{0:T(128)} %pad_add_fusion.2.at_ref.refs_0_, ...), custom_call_target="tpu_custom_call" | custom-call | flops 44999999488 | bytes 157500000 | tf_op jit(solution)/shard_map/middle/pallas_call | solution.py:704
  259.1 3.1 collective-permute-start.28
  262.2 4.0 collective-permute-start.29
  267.7 28.4 %own_grads.1 = (bf16[512,512]{1,0:T(8,128)(2,1)}, bf16[512,512]{1,0:T(8,128)(2,1)}, f32[2,2,512,512]{3,2,1,0:T(8,128)}, f32[1,1024]{1,0:T(1,128)}) custom-call(bf16[512,3072]{1,0:T(8,128)(2,1)} %get-tuple-element.164.q_ref.ko_ref.vo_ref, bf16[512,3072]{1,0:T(8,128)(2,1)} %get-tuple-element.164.q_ref.ko_ref.vo_ref, ...), custom_call_target="tpu_custom_call" | custom-call | flops 27499999232 | bytes 96250000 | tf_op jit(solution)/shard_map/own_grads/pallas_call | solution.py:207
  298.4 8.5 %down_grads.1 = bf16[2048,1024]{1,0:T(8,128)(2,1)} custom-call(s32[4]{0:T(128)} %pad_add_fusion.2.at_ref.refs_0_, bf16[512,2048]{1,0:T(8,128)(2,1)} %get-tuple-element.232.act_ref, bf16[512,2048]{1,0:T(8,128)(2,1)} %collective-permute-done.39.act_got, bf16[512,1024]{1,0:T(8,128)(2,1)} %get-tuple-element.234.glow_ref, ...), custom_call_target="tpu_custom_call" | custom-call | flops 8499999744 | bytes 29750000 | tf_op jit(solution)/shard_map/down_grads/pallas_call | solution.py:774
  306.9 12.1 %late_grads.1 = (bf16[256,2560]{1,0:T(8,128)(2,1)}, bf16[256,2560]{1,0:T(8,128)(2,1)}, bf16[256,2560]{1,0:T(8,128)(2,1)}, bf16[256,2560]{1,0:T(8,128)(2,1)}) custom-call(s32[4]{0:T(128)} %pad_add_fusion.2.at_ref.refs_0_, bf16[512,1024]{1,0:T(8,128)(2,1)} %get-tuple-element.181.refs_9_.low_ref, bf16[512,1024]{1,0:T(8,128)(2,1)} %copy-done.31, ...), custom_call_target="tpu_custom_call" | custom-call | flops 8999999488 | bytes 31500000 | tf_op jit(solution)/shard_map/late_grads/pallas_call | solution.py:851
  320.5 11.0 %halo_grads.3 = (bf16[512,512]{1,0:T(8,128)(2,1)}, bf16[512,512]{1,0:T(8,128)(2,1)}, f32[1,512]{1,0:T(1,128)}) custom-call(bf16[512,3072]{1,0:T(8,128)(2,1)} %get-tuple-element.164.q_ref.ko_ref.vo_ref, bf16[512,3072]{1,0:T(8,128)(2,1)} %get-tuple-element.164.q_ref.ko_ref.vo_ref, bf16[512,3072]{1,0:T(8,128)(2,1)} %get-tuple-element.170.kp_ref.vp_ref.qp_ref, ...), custom_call_target="tpu_custom_call" | custom-call | flops 50000000 | bytes 175000 | tf_op jit(solution)/shard_map/halo_grads/pallas_call | solution.py:280
  332.1 11.1 %halo_grads.2 = (bf16[512,512]{1,0:T(8,128)(2,1)}, bf16[512,512]{1,0:T(8,128)(2,1)}, f32[1,512]{1,0:T(1,128)}) custom-call(bf16[512,3072]{1,0:T(8,128)(2,1)} %get-tuple-element.164.q_ref.ko_ref.vo_ref, bf16[512,3072]{1,0:T(8,128)(2,1)} %get-tuple-element.164.q_ref.ko_ref.vo_ref, bf16[512,3072]{1,0:T(8,128)(2,1)} %get-tuple-element.170.kp_ref.vp_ref.qp_ref, ...), custom_call_target="tpu_custom_call" | custom-call | flops 50000000 | bytes 175000 | tf_op jit(solution)/shard_map/halo_grads/pallas_call | solution.py:280
  345.5 4.3 collective-permute-done.30
  355.4 8.2 %qkv_grads.1 = (bf16[256,1664]{1,0:T(8,128)(2,1)}, bf16[256,1664]{1,0:T(8,128)(2,1)}, bf16[256,1664]{1,0:T(8,128)(2,1)}, bf16[256,1664]{1,0:T(8,128)(2,1)}) custom-call(s32[4]{0:T(128)} %pad_add_fusion.2.at_ref.refs_0_, bf16[512,1024]{1,0:T(8,128)(2,1)} %bitcast.15.refs_9_.x_ref, bf16[512,1024]{1,0:T(8,128)(2,1)} %collective-permute-done.17.x_got, ...), custom_call_target="tpu_custom_call" | custom-call | flops 8300000256 | bytes 29050000 | tf_op jit(solution)/shard_map/qkv_grads/pallas_call | solution.py:879
  375.3 12.2 %collective-permute-done.37 = bf16[2,4,32,1664]{3,2,1,0:T(8,128)(2,1)} collective-permute-done((bf16[2,4,32,1664]{3,2,1,0:T(8,128)(2,1)S(1)}, bf16[2,4,32,1664]{3,2,1,0:T(8,128)(2,1)}, u32[]{:S(2)}, u32[]{:S(2)}) %collective-permute-start.37) | collective-permute-done | bytes 852000 | tf_op jit(solution)/shard_map/ppermute | solution.py:896
  396.0 3.5 fusion.46
  408.1 8.0 %collective-permute-done.45 = bf16[2,32,2560]{2,1,0:T(8,128)(2,1)S(1)} collective-permute-done((bf16[2,32,2560]{2,1,0:T(8,128)(2,1)S(1)}, bf16[2,32,2560]{2,1,0:T(8,128)(2,1)S(1)}, u32[]{:S(2)}, u32[]{:S(2)}) %collective-permute-start.45) | collective-permute-done | bytes 327712 | tf_op jit(solution)/shard_map/ppermute | solution.py:904
  419.3 9.2 %collective-permute-done.46 = bf16[2,32,1664]{2,1,0:T(8,128)(2,1)S(1)} collective-permute-done((bf16[2,32,1664]{2,1,0:T(8,128)(2,1)S(1)}, bf16[2,32,1664]{2,1,0:T(8,128)(2,1)S(1)}, u32[]{:S(2)}, u32[]{:S(2)}) %collective-permute-start.46) | collective-permute-done | bytes 213024 | tf_op jit(solution)/shard_map/ppermute | solution.py:904
  428.6 8.0 %collective-permute-start.50 = (bf16[32,1664]{1,0:T(8,128)(2,1)S(1)}, bf16[32,1664]{1,0:T(8,128)(2,1)S(1)}, u32[]{:S(2)}, u32[]{:S(2)}) collective-permute-start(bf16[32,1664]{1,0:T(8,128)(2,1)S(1)} %get-tuple-element.301), channel_id=1, source_target_pairs={{0,1},{1,0},{2,3},{3,2},{4,5},{5,4},{6,7},{7,6},{8,9},{9,8},{10,11... | collective-permute-start | bytes 319496 | tf_op jit(solution)/shard_map/ppermute | solution.py:896
  (324 shorter events, 95.4 us)
Async XLA Ops:
  7.2 159.9 %all-gather.3.cloned.1.call-start = ((), (), s32[]{:S(2)}) async-start(), calls=%async_computation.2 | async-start | bytes 2621440 | tf_op jit(solution)/shard_map/all_gather | solution.py:987
  7.2 28.1 %collective-permute-start.2 = (bf16[512,1024]{1,0:T(8,128)(2,1)}, bf16[512,1024]{1,0:T(8,128)(2,1)S(1)}, u32[]{:S(2)}, u32[]{:S(2)}) collective-permute-start(bf16[512,1024]{1,0:T(8,128)(2,1)} %bitcast.15.refs_9_.x_ref), channel_id=1, source_target_pairs={{0,2},{2,4},{4,6},{6,8},{8,10},{10,12},{12,14},{14,16},{16,18},{18... | collective-permute-start | bytes 3145736 | tf_op jit(solution)/shard_map/ppermute | solution.py:949
  35.3 42.3 %collective-permute-start.5 = (bf16[512,1024]{1,0:T(8,128)(2,1)}, bf16[512,1024]{1,0:T(8,128)(2,1)S(1)}, u32[]{:S(2)}, u32[]{:S(2)}) collective-permute-start(bf16[512,1024]{1,0:T(8,128)(2,1)} %bitcast.15.refs_9_.x_ref), channel_id=1, source_target_pairs={{2,0},{4,2},{6,4},{8,6},{10,8},{12,10},{14,12},{16,14},{18,16},{20... | collective-permute-start | bytes 3145736 | tf_op jit(solution)/shard_map/ppermute | solution.py:952
  44.3 33.0 %collective-permute-start.3 = (bf16[2,2,32,2176]{3,2,1,0:T(8,128)(2,1)S(1)}, bf16[2,2,32,2176]{3,2,1,0:T(8,128)(2,1)S(1)}, u32[]{:S(2)}, u32[]{:S(2)}) collective-permute-start(bf16[2,2,32,2176]{3,2,1,0:T(8,128)(2,1)S(1)} %pad_maximum_fusion.9), channel_id=1, source_target_pairs={{0,8},{8,0},{16,24},{24,16},{1,9},{9,1},{17,25},{25,17},{2,10},{10... | collective-permute-start | bytes 1671176 | tf_op jit(solution)/shard_map/ppermute | solution.py:904
  49.8 15.9 %collective-permute-start.4 = (bf16[128,1024]{1,0:T(8,128)(2,1)S(1)}, bf16[128,1024]{1,0:T(8,128)(2,1)S(1)}, u32[]{:S(2)}, u32[]{:S(2)}) collective-permute-start(bf16[128,1024]{1,0:T(8,128)(2,1)S(1)} %copy-done.21), channel_id=1, source_target_pairs={{0,2},{2,0},{1,3},{3,1},{4,6},{6,4},{5,7},{7,5},{8,10},{10,8},{9,1... | collective-permute-start | bytes 786440 | tf_op jit(solution)/shard_map/ppermute | solution.py:896
  93.8 24.8 %collective-permute-start.10 = (bf16[2,4,32,2176]{3,2,1,0:T(8,128)(2,1)S(1)}, bf16[2,4,32,2176]{3,2,1,0:T(8,128)(2,1)}, u32[]{:S(2)}, u32[]{:S(2)}) collective-permute-start(bf16[2,4,32,2176]{3,2,1,0:T(8,128)(2,1)S(1)} %pad_maximum_fusion.5.refs_3_), channel_id=1, source_target_pairs={{0,4},{4,0},{1,5},{5,1},{2,6},{6,2},{3,7},{7,3},{8,12},{12,8},{9,1... | collective-permute-start | bytes 3342344 | tf_op jit(solution)/shard_map/ppermute | solution.py:896
  94.0 24.7 %collective-permute-start.9 = (bf16[2,4,32,2176]{3,2,1,0:T(8,128)(2,1)S(1)}, bf16[2,4,32,2176]{3,2,1,0:T(8,128)(2,1)}, u32[]{:S(2)}, u32[]{:S(2)}) collective-permute-start(bf16[2,4,32,2176]{3,2,1,0:T(8,128)(2,1)S(1)} %pad_maximum_fusion.3.refs_1_), channel_id=1, source_target_pairs={{0,2},{2,0},{1,3},{3,1},{4,6},{6,4},{5,7},{7,5},{8,10},{10,8},{9,1... | collective-permute-start | bytes 3342344 | tf_op jit(solution)/shard_map/ppermute | solution.py:896
  96.6 26.3 %collective-permute-start.12 = (bf16[2,4,32,2176]{3,2,1,0:T(8,128)(2,1)S(1)}, bf16[2,4,32,2176]{3,2,1,0:T(8,128)(2,1)}, u32[]{:S(2)}, u32[]{:S(2)}) collective-permute-start(bf16[2,4,32,2176]{3,2,1,0:T(8,128)(2,1)S(1)} %pad_maximum_fusion.3.refs_1_), channel_id=1, source_target_pairs={{0,1},{1,0},{2,3},{3,2},{4,5},{5,4},{6,7},{7,6},{8,9},{9,8},{10,11... | collective-permute-start | bytes 3342344 | tf_op jit(solution)/shard_map/ppermute | solution.py:896
  121.3 72.9 %collective-permute-start.17 = (bf16[512,1024]{1,0:T(8,128)(2,1)}, bf16[512,1024]{1,0:T(8,128)(2,1)}, u32[]{:S(2)}, u32[]{:S(2)}) collective-permute-start(bf16[512,1024]{1,0:T(8,128)(2,1)} %bitcast.15.refs_9_.x_ref), channel_id=1, source_target_pairs={{0,1},{1,0},{2,3},{3,2},{4,5},{5,4},{6,7},{7,6},{8,9},{9,8},{10,11... | collective-permute-start | bytes 3145736 | tf_op jit(solution)/shard_map/ppermute | solution.py:896
  122.1 265.7 %reduce-scatter.2.cloned.1.call-start = ((), (), s32[]{:S(2)}) async-start(), calls=%async_computation.1 | async-start | bytes 5242880 | tf_op jit(solution)/shard_map/reduce_scatter | solution.py:1037
  125.0 24.9 %collective-permute-start.16 = (bf16[4,64,2048]{2,1,0:T(8,128)(2,1)S(1)}, bf16[4,64,2048]{2,1,0:T(8,128)(2,1)}, u32[]{:S(2)}, u32[]{:S(2)}) collective-permute-start(bf16[4,64,2048]{2,1,0:T(8,128)(2,1)S(1)} %bitcast.182), channel_id=1, source_target_pairs={{0,4},{4,0},{1,5},{5,1},{2,6},{6,2},{3,7},{7,3},{8,12},{12,8},{9,1... | collective-permute-start | bytes 3145736 | tf_op jit(solution)/shard_map/ppermute | solution.py:896
  152.7 48.2 %collective-permute-start.19 = (bf16[2,4,64,2048]{3,2,1,0:T(8,128)(2,1)}, bf16[2,4,64,2048]{3,2,1,0:T(8,128)(2,1)}, u32[]{:S(2)}, u32[]{:S(2)}) collective-permute-start(bf16[2,4,64,2048]{3,2,1,0:T(8,128)(2,1)} %pad_maximum_fusion.refs_1_), channel_id=1, source_target_pairs={{0,2},{2,0},{1,3},{3,1},{4,6},{6,4},{5,7},{7,5},{8,10},{10,8},{9,1... | collective-permute-start | bytes 6291464 | tf_op jit(solution)/shard_map/ppermute | solution.py:896
  154.2 46.8 %collective-permute-start.20 = (bf16[2,4,64,2048]{3,2,1,0:T(8,128)(2,1)}, bf16[2,4,64,2048]{3,2,1,0:T(8,128)(2,1)}, u32[]{:S(2)}, u32[]{:S(2)}) collective-permute-start(bf16[2,4,64,2048]{3,2,1,0:T(8,128)(2,1)} %pad_maximum_fusion.refs_1_), channel_id=1, source_target_pairs={{0,1},{1,0},{2,3},{3,2},{4,5},{5,4},{6,7},{7,6},{8,9},{9,8},{10,11... | collective-permute-start | bytes 6291464 | tf_op jit(solution)/shard_map/ppermute | solution.py:896
  167.1 33.8 %collective-permute-start.21 = (bf16[2,4,128,1024]{3,2,1,0:T(8,128)(2,1)}, bf16[2,4,128,1024]{3,2,1,0:T(8,128)(2,1)}, u32[]{:S(2)}, u32[]{:S(2)}) collective-permute-start(bf16[2,4,128,1024]{3,2,1,0:T(8,128)(2,1)} %bitcast.227), channel_id=1, source_target_pairs={{0,1},{1,0},{2,3},{3,2},{4,5},{5,4},{6,7},{7,6},{8,9},{9,8},{10,11... | collective-permute-start | bytes 6291464 | tf_op jit(solution)/shard_map/ppermute | solution.py:896
  167.6 47.5 %collective-permute-start.22 = (bf16[2,4,128,1024]{3,2,1,0:T(8,128)(2,1)}, bf16[2,4,128,1024]{3,2,1,0:T(8,128)(2,1)}, u32[]{:S(2)}, u32[]{:S(2)}) collective-permute-start(bf16[2,4,128,1024]{3,2,1,0:T(8,128)(2,1)} %bitcast.228), channel_id=1, source_target_pairs={{0,4},{4,0},{1,5},{5,1},{2,6},{6,2},{3,7},{7,3},{8,12},{12,8},{9,1... | collective-permute-start | bytes 6291464 | tf_op jit(solution)/shard_map/ppermute | solution.py:896
  218.7 40.3 %collective-permute-start.25 = (bf16[512,1024]{1,0:T(8,128)(2,1)S(1)}, bf16[512,1024]{1,0:T(8,128)(2,1)S(1)}, u32[]{:S(2)}, u32[]{:S(2)}) collective-permute-start(bf16[512,1024]{1,0:T(8,128)(2,1)S(1)} %copy-done.30), channel_id=1, source_target_pairs={{0,1},{1,0},{2,3},{3,2},{4,5},{5,4},{6,7},{7,6},{8,9},{9,8},{10,11... | collective-permute-start | bytes 3145736 | tf_op jit(solution)/shard_map/ppermute | solution.py:896
  259.1 60.0 %collective-permute-start.28 = (bf16[560,1024]{1,0:T(8,128)(2,1)}, bf16[560,1024]{1,0:T(8,128)(2,1)S(1)}, u32[]{:S(2)}, u32[]{:S(2)}) collective-permute-start(bf16[560,1024]{1,0:T(8,128)(2,1)} %get-tuple-element.189.do_ref), channel_id=1, source_target_pairs={{0,2},{2,4},{4,6},{6,8},{8,10},{10,12},{12,14},{14,16},{16,18},{18... | collective-permute-start | bytes 3440648 | tf_op jit(solution)/shard_map/ppermute | solution.py:949
  262.2 56.9 %collective-permute-start.29 = (bf16[560,1024]{1,0:T(8,128)(2,1)}, bf16[560,1024]{1,0:T(8,128)(2,1)S(1)}, u32[]{:S(2)}, u32[]{:S(2)}) collective-permute-start(bf16[560,1024]{1,0:T(8,128)(2,1)} %get-tuple-element.189.do_ref), channel_id=1, source_target_pairs={{2,0},{4,2},{6,4},{8,6},{10,8},{12,10},{14,12},{16,14},{18,16},{20... | collective-permute-start | bytes 3440648 | tf_op jit(solution)/shard_map/ppermute | solution.py:952
  266.2 40.8 %collective-permute-start.26 = (bf16[512,2048]{1,0:T(8,128)(2,1)}, bf16[512,2048]{1,0:T(8,128)(2,1)}, u32[]{:S(2)}, u32[]{:S(2)}) collective-permute-start(bf16[512,2048]{1,0:T(8,128)(2,1)} %get-tuple-element.195), channel_id=1, source_target_pairs={{0,1},{1,0},{2,3},{3,2},{4,5},{5,4},{6,7},{7,6},{8,9},{9,8},{10,11... | collective-permute-start | bytes 6291464 | tf_op jit(solution)/shard_map/ppermute | solution.py:896
  267.2 30.7 %collective-permute-start.39 = (bf16[512,2048]{1,0:T(8,128)(2,1)}, bf16[512,2048]{1,0:T(8,128)(2,1)}, u32[]{:S(2)}, u32[]{:S(2)}) collective-permute-start(bf16[512,2048]{1,0:T(8,128)(2,1)} %get-tuple-element.233), channel_id=1, source_target_pairs={{0,1},{1,0},{2,3},{3,2},{4,5},{5,4},{6,7},{7,6},{8,9},{9,8},{10,11... | collective-permute-start | bytes 6291464 | tf_op jit(solution)/shard_map/ppermute | solution.py:896
  267.3 30.5 %collective-permute-start.40 = (bf16[512,1024]{1,0:T(8,128)(2,1)}, bf16[512,1024]{1,0:T(8,128)(2,1)}, u32[]{:S(2)}, u32[]{:S(2)}) collective-permute-start(bf16[512,1024]{1,0:T(8,128)(2,1)} %get-tuple-element.234.glow_ref), channel_id=1, source_target_pairs={{0,1},{1,0},{2,3},{3,2},{4,5},{5,4},{6,7},{7,6},{8,9},{9,8},{10,11... | collective-permute-start | bytes 3145736 | tf_op jit(solution)/shard_map/ppermute | solution.py:896
  297.9 55.4 %collective-permute-start.32 = (bf16[512,512]{1,0:T(8,128)(2,1)}, bf16[512,512]{1,0:T(8,128)(2,1)}, u32[]{:S(2)}, u32[]{:S(2)}) collective-permute-start(bf16[512,512]{1,0:T(8,128)(2,1)} %get-tuple-element.242), channel_id=1, source_target_pairs={{0,1},{1,0},{2,3},{3,2},{4,5},{5,4},{6,7},{7,6},{8,9},{9,8},{10,11... | collective-permute-start | bytes 1572872 | tf_op jit(solution)/shard_map/ppermute | solution.py:896
  319.1 30.7 %collective-permute-start.30 = (bf16[2,4,32,2560]{3,2,1,0:T(8,128)(2,1)}, bf16[2,4,32,2560]{3,2,1,0:T(8,128)(2,1)}, u32[]{:S(2)}, u32[]{:S(2)}) collective-permute-start(bf16[2,4,32,2560]{3,2,1,0:T(8,128)(2,1)} %bitcast.231), channel_id=1, source_target_pairs={{0,2},{2,0},{1,3},{3,1},{4,6},{6,4},{5,7},{7,5},{8,10},{10,8},{9,1... | collective-permute-start | bytes 3932168 | tf_op jit(solution)/shard_map/ppermute | solution.py:896
  319.2 30.7 %collective-permute-start.31 = (bf16[2,4,32,2560]{3,2,1,0:T(8,128)(2,1)}, bf16[2,4,32,2560]{3,2,1,0:T(8,128)(2,1)}, u32[]{:S(2)}, u32[]{:S(2)}) collective-permute-start(bf16[2,4,32,2560]{3,2,1,0:T(8,128)(2,1)} %bitcast.230), channel_id=1, source_target_pairs={{0,4},{4,0},{1,5},{5,1},{2,6},{6,2},{3,7},{7,3},{8,12},{12,8},{9,1... | collective-permute-start | bytes 3932168 | tf_op jit(solution)/shard_map/ppermute | solution.py:896
  331.5 21.8 %collective-permute-start.33 = (bf16[512,512]{1,0:T(8,128)(2,1)}, bf16[512,512]{1,0:T(8,128)(2,1)}, u32[]{:S(2)}, u32[]{:S(2)}) collective-permute-start(bf16[512,512]{1,0:T(8,128)(2,1)} %get-tuple-element.243), channel_id=1, source_target_pairs={{0,1},{1,0},{2,3},{3,2},{4,5},{5,4},{6,7},{7,6},{8,9},{9,8},{10,11... | collective-permute-start | bytes 1572872 | tf_op jit(solution)/shard_map/ppermute | solution.py:896
  331.7 21.7 %collective-permute-start.34 = (bf16[512,512]{1,0:T(8,128)(2,1)}, bf16[512,512]{1,0:T(8,128)(2,1)}, u32[]{:S(2)}, u32[]{:S(2)}) collective-permute-start(bf16[512,512]{1,0:T(8,128)(2,1)} %get-tuple-element.244), channel_id=1, source_target_pairs={{0,1},{1,0},{2,3},{3,2},{4,5},{5,4},{6,7},{7,6},{8,9},{9,8},{10,11... | collective-permute-start | bytes 1572872 | tf_op jit(solution)/shard_map/ppermute | solution.py:896
  368.9 18.6 %collective-permute-start.37 = (bf16[2,4,32,1664]{3,2,1,0:T(8,128)(2,1)S(1)}, bf16[2,4,32,1664]{3,2,1,0:T(8,128)(2,1)}, u32[]{:S(2)}, u32[]{:S(2)}) collective-permute-start(bf16[2,4,32,1664]{3,2,1,0:T(8,128)(2,1)S(1)} %bitcast.234), channel_id=1, source_target_pairs={{0,2},{2,0},{1,3},{3,1},{4,6},{6,4},{5,7},{7,5},{8,10},{10,8},{9,1... | collective-permute-start | bytes 2555912 | tf_op jit(solution)/shard_map/ppermute | solution.py:896
  369.7 18.1 %collective-permute-start.38 = (bf16[2,4,32,1664]{3,2,1,0:T(8,128)(2,1)S(1)}, bf16[2,4,32,1664]{3,2,1,0:T(8,128)(2,1)}, u32[]{:S(2)}, u32[]{:S(2)}) collective-permute-start(bf16[2,4,32,1664]{3,2,1,0:T(8,128)(2,1)S(1)} %bitcast.233), channel_id=1, source_target_pairs={{0,4},{4,0},{1,5},{5,1},{2,6},{6,2},{3,7},{7,3},{8,12},{12,8},{9,1... | collective-permute-start | bytes 2555912 | tf_op jit(solution)/shard_map/ppermute | solution.py:896
  374.6 24.9 %collective-permute-start.43 = (bf16[2,2,32,2560]{3,2,1,0:T(8,128)(2,1)}, bf16[2,2,32,2560]{3,2,1,0:T(8,128)(2,1)}, u32[]{:S(2)}, u32[]{:S(2)}) collective-permute-start(bf16[2,2,32,2560]{3,2,1,0:T(8,128)(2,1)} %fusion.17), channel_id=1, source_target_pairs={{0,8},{8,0},{16,24},{24,16},{1,9},{9,1},{17,25},{25,17},{2,10},{10... | collective-permute-start | bytes 1966088 | tf_op jit(solution)/shard_map/ppermute | solution.py:904
  392.6 23.8 %collective-permute-start.47 = (bf16[128,1024]{1,0:T(8,128)(2,1)S(1)}, bf16[128,1024]{1,0:T(8,128)(2,1)S(1)}, u32[]{:S(2)}, u32[]{:S(2)}) collective-permute-start(bf16[128,1024]{1,0:T(8,128)(2,1)S(1)} %get-tuple-element.287), channel_id=1, source_target_pairs={{0,4},{4,0},{1,5},{5,1},{2,6},{6,2},{3,7},{7,3},{8,12},{12,8},{9,1... | collective-permute-start | bytes 786440 | tf_op jit(solution)/shard_map/ppermute | solution.py:896
  393.0 23.4 %collective-permute-start.48 = (bf16[128,1024]{1,0:T(8,128)(2,1)S(1)}, bf16[128,1024]{1,0:T(8,128)(2,1)S(1)}, u32[]{:S(2)}, u32[]{:S(2)}) collective-permute-start(bf16[128,1024]{1,0:T(8,128)(2,1)S(1)} %get-tuple-element.286), channel_id=1, source_target_pairs={{0,2},{2,0},{1,3},{3,1},{4,6},{6,4},{5,7},{7,5},{8,10},{10,8},{9,1... | collective-permute-start | bytes 786440 | tf_op jit(solution)/shard_map/ppermute | solution.py:896
  399.5 17.0 %collective-permute-start.49 = (bf16[128,1024]{1,0:T(8,128)(2,1)S(1)}, bf16[128,1024]{1,0:T(8,128)(2,1)S(1)}, u32[]{:S(2)}, u32[]{:S(2)}) collective-permute-start(bf16[128,1024]{1,0:T(8,128)(2,1)S(1)} %get-tuple-element.285), channel_id=1, source_target_pairs={{0,6},{2,4},{4,2},{6,0},{1,7},{3,5},{5,3},{7,1},{8,14},{10,12},{12... | collective-permute-start | bytes 786440 | tf_op jit(solution)/shard_map/ppermute | solution.py:900
  (59 other events, 656.5 us)
Sparse Core Ops, SparseCore 0:
  122.2 44.8 all-gather.2
  307.0 76.5 reduce-scatter.1

commit v6 on v5

--- a/solution.py
+++ b/solution.py
@@ -586,7 +586,8 @@
     up, down, out, hat, dy, heads, act, slope, result, glow, total, branch, sides, payload, up_sems, down_sems, in_sems, out_sems = refs[23:]
     tokens, width = low_ref.shape
     half = up.shape[1] // 2
-    chunk = half
+    chunk = half // 2
+    steps = 2 * half // chunk
     from_up = up_copies(up_refs, up, up_sems, at_ref, far)
     from_down = down_copies(down_refs, down, down_sems, at_ref, far)
     loads = [pltpu.make_async_copy(*pair, in_sems.at[i]) for i, pair in enumerate(((hat_in, hat), (dy_in, dy), (out_in, out), (heads_in, heads)))]
@@ -601,7 +602,7 @@
         copy.start()
 
     def cols(i):
-        return slice(i * chunk, i * chunk + chunk)
+        return pl.ds(pl.multiple_of(i * chunk, chunk), chunk)
 
     def raise_one(i):
         lifted = nn(low_ref[...], up[:, cols(i)]) + row_ref[:, cols(i)]
@@ -616,12 +617,20 @@
     half_up, half_down = len(from_up) // 2, len(from_down) // 2
     wait_all(from_up[:half_up])
     raise_one(0)
+    raise_one(1)
     wait_all(from_up[half_up:])
     wait_all(from_down[:half_down])
-    raise_one(1)
     total[...] = nn(act[:, cols(0)], down[cols(0)])
+
+    def both(i, carry):
+        raise_one(i)
+        settle_one(i - 1)
+        return carry
+
+    both(2, 0)
     wait_all(from_down[half_down:])
-    settle_one(1)
+    both(3, 0)
+    settle_one(steps - 1)
     store(act.at[:, pl.ds(0, half)], act_out)
     store(act.at[:, pl.ds(half, half)], act_send)
     wait_all(loads)
@@ -652,11 +661,16 @@
         total[...] += nt(slope[:, cols(i)], up[:, cols(i)])
 
     lower_one(0)
+
+    def back(i, carry):
+        lower_one(i)
+        first_one(i - 1)
+        return carry
+
+    lax.fori_loop(1, steps, back, 0)
     store(slope.at[:, pl.ds(0, half)], lift_out)
-    lower_one(1)
     store(slope.at[:, pl.ds(half, half)], lift_send)
-    first_one(0)
-    first_one(1)
+    first_one(steps - 1)
 
     for n in range(tokens // rows):
         at = slice(rows * n, rows * n + rows)

time: 460 us -> 461 us (level)
  transfers between devices with their start and end apart: 54 -> 54, of which waited for: 24 -> 24; matrix products, arithmetic and copies ran while one was open for 11% -> 10% of each run, Pallas kernels for 38% -> 38%
where the time goes in v6:
time: 461 us; the launch traced here: 452 us
  Pallas kernels  173 us (38%)
  waiting for transfers between devices  142 us (31%)
  starting transfers between devices  66.3 us (14%)
  other arithmetic  30.9 us (7%)
  local copies, waits for them, and re-layouts  20.8 us (5%)
  between operations  15.7 us (3%)
    ppermute x39, waiting for transfers between devices, swap(): return lax.ppermute(values, axis, [(0, 1), (1, 0)])  74 us
    ppermute x8, waiting for transfers between devices, swap_far(): lax.ppermute(values, FAR, [(i, i ^ step) for i in range(lax.axis_size(FAR...  66.4 us
    pallas_call x1, Pallas kernels, middle(): pl.pallas_call(functools.partial(middle_kernel, far, len(up_parts), len(d...  37.8 us
    ppermute x39, starting transfers between devices, swap(): return lax.ppermute(values, axis, [(0, 1), (1, 0)])  35.5 us
    pallas_call x1, Pallas kernels, own_grads(): pl.pallas_call(own_grad_kernel, grid=(pairs,), in_specs=[column(0), colum...  28.4 us
    pallas_call x1, Pallas kernels, attend(): pl.pallas_call(attend_kernel, grid=(pairs,), in_specs=[column(0), column(...  22.4 us
    pallas_call x2, Pallas kernels, halo_grads(): pl.pallas_call(functools.partial(halo_grad_kernel, half), grid=(near,), i...  22.1 us
    pallas_call x1, Pallas kernels, project(): pl.pallas_call(functools.partial(project_kernel, far, len(parts)), in_spe...  13.3 us
  transfers between devices with their start and end apart: 54, of which 24 were waited for; matrix products, arithmetic and copies ran while one was open for 10% of the time, Pallas kernels for 38%

profile of v6, /device:TPU:25, one launch (start us, length us, event | category | flops | bytes accessed | tf_op | source)
XLA Modules:
  0.0 452.4 jit_solution(13088293281674294187)
XLA Ops:
  7.2 3.3 collective-permute-start.2
  18.1 15.5 %collective-permute-done.1 = bf16[2,32,2176]{2,1,0:T(8,128)(2,1)S(1)} collective-permute-done((bf16[2,32,2176]{2,1,0:T(8,128)(2,1)}, bf16[2,32,2176]{2,1,0:T(8,128)(2,1)S(1)}, u32[]{:S(2)}, u32[]{:S(2)}) %collective-permute-start.1) | collective-permute-done | bytes 278560 | tf_op jit(solution)/shard_map/ppermute | solution.py:918
  35.3 9.0 %collective-permute-start.5 = (bf16[512,1024]{1,0:T(8,128)(2,1)}, bf16[512,1024]{1,0:T(8,128)(2,1)S(1)}, u32[]{:S(2)}, u32[]{:S(2)}) collective-permute-start(bf16[512,1024]{1,0:T(8,128)(2,1)} %bitcast.15.refs_9_.x_ref), channel_id=1, source_target_pairs={{2,0},{4,2},{6,4},{8,6},{10,8},{12,10},{14,12},{16,14},{18,16},{20... | collective-permute-start | bytes 3145736 | tf_op jit(solution)/shard_map/ppermute | solution.py:966
  44.3 5.5 %collective-permute-start.3 = (bf16[2,2,32,2176]{3,2,1,0:T(8,128)(2,1)S(1)}, bf16[2,2,32,2176]{3,2,1,0:T(8,128)(2,1)S(1)}, u32[]{:S(2)}, u32[]{:S(2)}) collective-permute-start(bf16[2,2,32,2176]{3,2,1,0:T(8,128)(2,1)S(1)} %pad_maximum_fusion.9), channel_id=1, source_target_pairs={{0,8},{8,0},{16,24},{24,16},{1,9},{9,1},{17,25},{25,17},{2,10},{10... | collective-permute-start | bytes 1671176 | tf_op jit(solution)/shard_map/ppermute | solution.py:918
  49.8 15.9 %collective-permute-done.4 = bf16[128,1024]{1,0:T(8,128)(2,1)S(1)} collective-permute-done((bf16[128,1024]{1,0:T(8,128)(2,1)S(1)}, bf16[128,1024]{1,0:T(8,128)(2,1)S(1)}, u32[]{:S(2)}, u32[]{:S(2)}) %collective-permute-start.4) | collective-permute-done | bytes 262176 | tf_op jit(solution)/shard_map/ppermute | solution.py:910
  66.6 10.8 %collective-permute-done.3 = bf16[2,2,32,2176]{3,2,1,0:T(8,128)(2,1)S(1)} collective-permute-done((bf16[2,2,32,2176]{3,2,1,0:T(8,128)(2,1)S(1)}, bf16[2,2,32,2176]{3,2,1,0:T(8,128)(2,1)S(1)}, u32[]{:S(2)}, u32[]{:S(2)}) %collective-permute-start.3) | collective-permute-done | bytes 557088 | tf_op jit(solution)/shard_map/ppermute | solution.py:918
  79.8 13.8 %collective-permute-done.8 = bf16[64,2048]{1,0:T(8,128)(2,1)S(1)} collective-permute-done((bf16[64,2048]{1,0:T(8,128)(2,1)S(1)}, bf16[64,2048]{1,0:T(8,128)(2,1)S(1)}, u32[]{:S(2)}, u32[]{:S(2)}) %collective-permute-start.8) | collective-permute-done | bytes 262176 | tf_op jit(solution)/shard_map/ppermute | solution.py:918
  99.4 8.8 %collective-permute-done.11 = bf16[2,64,2048]{2,1,0:T(8,128)(2,1)} collective-permute-done((bf16[2,64,2048]{2,1,0:T(8,128)(2,1)S(1)}, bf16[2,64,2048]{2,1,0:T(8,128)(2,1)}, u32[]{:S(2)}, u32[]{:S(2)}) %collective-permute-start.11) | collective-permute-done | bytes 524320 | tf_op jit(solution)/shard_map/ppermute | solution.py:918
  108.1 10.5 %collective-permute-done.10.refs_4_ = bf16[2,4,32,2176]{3,2,1,0:T(8,128)(2,1)} collective-permute-done((bf16[2,4,32,2176]{3,2,1,0:T(8,128)(2,1)S(1)}, bf16[2,4,32,2176]{3,2,1,0:T(8,128)(2,1)}, u32[]{:S(2)}, u32[]{:S(2)}) %collective-permute-start.10) | collective-permute-done | bytes 1114144 | tf_op jit(solution)/shard_map/ppermute | solution.py:910
  129.6 13.3 %project.1 = (bf16[512,3072]{1,0:T(8,128)(2,1)}, bf16[1024,3072]{1,0:T(8,128)(2,1)}, bf16[1024,1024]{1,0:T(8,128)(2,1)}) custom-call(s32[4]{0:T(128)} %pad_add_fusion.2.at_ref.refs_0_, bf16[2,4,32,2176]{3,2,1,0:T(8,128)(2,1)} %copy-done.3, bf16[2,4,32,2176]{3,2,1,0:T(8,128)(2,1)} %collective-permute-done.9.refs_2_, bf16[2,4,32,2176]{3,2,1,0:T(8,128)(2,1)} %copy-done.2, ...), custom_call_target="tpu_custom_call" | custom-call | flops 260000000 | bytes 910000 | tf_op jit(solution)/shard_map/project/pallas_call | solution.py:481
  142.9 7.0 %collective-permute-done.16 = bf16[4,64,2048]{2,1,0:T(8,128)(2,1)} collective-permute-done((bf16[4,64,2048]{2,1,0:T(8,128)(2,1)S(1)}, bf16[4,64,2048]{2,1,0:T(8,128)(2,1)}, u32[]{:S(2)}, u32[]{:S(2)}) %collective-permute-start.16) | collective-permute-done | bytes 1048608 | tf_op jit(solution)/shard_map/ppermute | solution.py:910
  149.9 2.8 pad_maximum_fusion.refs_1_
  155.3 10.8 %project_more.1 = (bf16[512,3072]{1,0:T(8,128)(2,1)}, bf16[512,3072]{1,0:T(8,128)(2,1)}) custom-call(bf16[512,1024]{1,0:T(8,128)(2,1)} %copy-done.11, bf16[512,1024]{1,0:T(8,128)(2,1)} %copy-done.12, bf16[1024,3072]{1,0:T(8,128)(2,1)} %get-tuple-element.167.w_ref, f32[1,3072]{1,0:T(1,128)} %copy-done.23), custom_call_target="tpu_custom_call" | custom-call | flops 214000000 | bytes 749000 | tf_op jit(solution)/shard_map/project_more/pallas_call | solution.py:508
  171.8 22.4 %attend.1 = (bf16[512,1024]{1,0:T(8,128)(2,1)}, f32[16,512]{1,0:T(8,128)}) custom-call(bf16[512,3072]{1,0:T(8,128)(2,1)} %get-tuple-element.164.q_ref.ko_ref.vo_ref, bf16[512,3072]{1,0:T(8,128)(2,1)} %get-tuple-element.164.q_ref.ko_ref.vo_ref, bf16[512,3072]{1,0:T(8,128)(2,1)} %get-tuple-element.170.kp_ref.vp_ref.qp_ref, ...), custom_call_target="tpu_custom_call" | custom-call | flops 480000000 | bytes 1680000 | tf_op jit(solution)/shard_map/attend/pallas_call | solution.py:120
  195.5 5.4 %out_project.1 = (f32[512,1024]{1,0:T(8,128)}, f32[512,1]{1,0:T(8,128)}, bf16[512,1024]{1,0:T(8,128)(2,1)}) custom-call(bf16[512,1024]{1,0:T(8,128)(2,1)} %get-tuple-element.172.heads_ref.refs_16_, bf16[1024,1024]{1,0:T(8,128)(2,1)} %get-tuple-element.173.w_ref.refs_17_, bf16[512,1024]{1,0:T(8,128)(2,1)} %bitcast.15.refs_9_.x_ref, ...), custom_call_target="tpu_custom_call" | custom-call | flops 114000000 | bytes 399000 | tf_op jit(solution)/shard_map/out_project/pallas_call | solution.py:532
  200.9 14.2 %collective-permute-done.22.refs_6_ = bf16[2,4,128,1024]{3,2,1,0:T(8,128)(2,1)} collective-permute-done((bf16[2,4,128,1024]{3,2,1,0:T(8,128)(2,1)}, bf16[2,4,128,1024]{3,2,1,0:T(8,128)(2,1)}, u32[]{:S(2)}, u32[]{:S(2)}) %collective-permute-start.22) | collective-permute-done | bytes 2097184 | tf_op jit(solution)/shard_map/ppermute | solution.py:910
  220.1 3.0 collective-permute-done.24.refs_8_
  223.1 37.8 %middle.1 = (bf16[512,2048]{1,0:T(8,128)(2,1)}, bf16[512,2048]{1,0:T(8,128)(2,1)}, bf16[512,1024]{1,0:T(8,128)(2,1)}, bf16[512,1024]{1,0:T(8,128)(2,1)}, bf16[51...) custom-call(s32[4]{0:T(128)} %pad_add_fusion.2.at_ref.refs_0_, ...), custom_call_target="tpu_custom_call" | custom-call | flops 44999999488 | bytes 157500000 | tf_op jit(solution)/shard_map/middle/pallas_call | solution.py:718
  260.9 3.1 collective-permute-start.28
  264.0 4.0 collective-permute-start.29
  269.5 28.4 %own_grads.1 = (bf16[512,512]{1,0:T(8,128)(2,1)}, bf16[512,512]{1,0:T(8,128)(2,1)}, f32[2,2,512,512]{3,2,1,0:T(8,128)}, f32[1,1024]{1,0:T(1,128)}) custom-call(bf16[512,3072]{1,0:T(8,128)(2,1)} %get-tuple-element.164.q_ref.ko_ref.vo_ref, bf16[512,3072]{1,0:T(8,128)(2,1)} %get-tuple-element.164.q_ref.ko_ref.vo_ref, ...), custom_call_target="tpu_custom_call" | custom-call | flops 27499999232 | bytes 96250000 | tf_op jit(solution)/shard_map/own_grads/pallas_call | solution.py:207
  300.1 8.5 %down_grads.1 = bf16[2048,1024]{1,0:T(8,128)(2,1)} custom-call(s32[4]{0:T(128)} %pad_add_fusion.2.at_ref.refs_0_, bf16[512,2048]{1,0:T(8,128)(2,1)} %get-tuple-element.232.act_ref, bf16[512,2048]{1,0:T(8,128)(2,1)} %collective-permute-done.39.act_got, bf16[512,1024]{1,0:T(8,128)(2,1)} %get-tuple-element.234.glow_ref, ...), custom_call_target="tpu_custom_call" | custom-call | flops 8499999744 | bytes 29750000 | tf_op jit(solution)/shard_map/down_grads/pallas_call | solution.py:788
  308.7 12.1 %late_grads.1 = (bf16[256,2560]{1,0:T(8,128)(2,1)}, bf16[256,2560]{1,0:T(8,128)(2,1)}, bf16[256,2560]{1,0:T(8,128)(2,1)}, bf16[256,2560]{1,0:T(8,128)(2,1)}) custom-call(s32[4]{0:T(128)} %pad_add_fusion.2.at_ref.refs_0_, bf16[512,1024]{1,0:T(8,128)(2,1)} %get-tuple-element.181.refs_9_.low_ref, bf16[512,1024]{1,0:T(8,128)(2,1)} %copy-done.31, ...), custom_call_target="tpu_custom_call" | custom-call | flops 8999999488 | bytes 31500000 | tf_op jit(solution)/shard_map/late_grads/pallas_call | solution.py:865
  322.3 11.0 %halo_grads.3 = (bf16[512,512]{1,0:T(8,128)(2,1)}, bf16[512,512]{1,0:T(8,128)(2,1)}, f32[1,512]{1,0:T(1,128)}) custom-call(bf16[512,3072]{1,0:T(8,128)(2,1)} %get-tuple-element.164.q_ref.ko_ref.vo_ref, bf16[512,3072]{1,0:T(8,128)(2,1)} %get-tuple-element.164.q_ref.ko_ref.vo_ref, bf16[512,3072]{1,0:T(8,128)(2,1)} %get-tuple-element.170.kp_ref.vp_ref.qp_ref, ...), custom_call_target="tpu_custom_call" | custom-call | flops 50000000 | bytes 175000 | tf_op jit(solution)/shard_map/halo_grads/pallas_call | solution.py:280
  333.9 11.1 %halo_grads.2 = (bf16[512,512]{1,0:T(8,128)(2,1)}, bf16[512,512]{1,0:T(8,128)(2,1)}, f32[1,512]{1,0:T(1,128)}) custom-call(bf16[512,3072]{1,0:T(8,128)(2,1)} %get-tuple-element.164.q_ref.ko_ref.vo_ref, bf16[512,3072]{1,0:T(8,128)(2,1)} %get-tuple-element.164.q_ref.ko_ref.vo_ref, bf16[512,3072]{1,0:T(8,128)(2,1)} %get-tuple-element.170.kp_ref.vp_ref.qp_ref, ...), custom_call_target="tpu_custom_call" | custom-call | flops 50000000 | bytes 175000 | tf_op jit(solution)/shard_map/halo_grads/pallas_call | solution.py:280
  347.3 4.3 collective-permute-done.30
  357.2 8.2 %qkv_grads.1 = (bf16[256,1664]{1,0:T(8,128)(2,1)}, bf16[256,1664]{1,0:T(8,128)(2,1)}, bf16[256,1664]{1,0:T(8,128)(2,1)}, bf16[256,1664]{1,0:T(8,128)(2,1)}) custom-call(s32[4]{0:T(128)} %pad_add_fusion.2.at_ref.refs_0_, bf16[512,1024]{1,0:T(8,128)(2,1)} %bitcast.15.refs_9_.x_ref, bf16[512,1024]{1,0:T(8,128)(2,1)} %collective-permute-done.17.x_got, ...), custom_call_target="tpu_custom_call" | custom-call | flops 8300000256 | bytes 29050000 | tf_op jit(solution)/shard_map/qkv_grads/pallas_call | solution.py:893
  377.1 12.2 %collective-permute-done.37 = bf16[2,4,32,1664]{3,2,1,0:T(8,128)(2,1)} collective-permute-done((bf16[2,4,32,1664]{3,2,1,0:T(8,128)(2,1)S(1)}, bf16[2,4,32,1664]{3,2,1,0:T(8,128)(2,1)}, u32[]{:S(2)}, u32[]{:S(2)}) %collective-permute-start.37) | collective-permute-done | bytes 852000 | tf_op jit(solution)/shard_map/ppermute | solution.py:910
  397.8 3.5 fusion.46
  409.9 7.9 %collective-permute-done.45 = bf16[2,32,2560]{2,1,0:T(8,128)(2,1)S(1)} collective-permute-done((bf16[2,32,2560]{2,1,0:T(8,128)(2,1)S(1)}, bf16[2,32,2560]{2,1,0:T(8,128)(2,1)S(1)}, u32[]{:S(2)}, u32[]{:S(2)}) %collective-permute-start.45) | collective-permute-done | bytes 327712 | tf_op jit(solution)/shard_map/ppermute | solution.py:918
  421.0 9.2 %collective-permute-done.46 = bf16[2,32,1664]{2,1,0:T(8,128)(2,1)S(1)} collective-permute-done((bf16[2,32,1664]{2,1,0:T(8,128)(2,1)S(1)}, bf16[2,32,1664]{2,1,0:T(8,128)(2,1)S(1)}, u32[]{:S(2)}, u32[]{:S(2)}) %collective-permute-start.46) | collective-permute-done | bytes 213024 | tf_op jit(solution)/shard_map/ppermute | solution.py:918
  430.3 8.0 %collective-permute-start.50 = (bf16[32,1664]{1,0:T(8,128)(2,1)S(1)}, bf16[32,1664]{1,0:T(8,128)(2,1)S(1)}, u32[]{:S(2)}, u32[]{:S(2)}) collective-permute-start(bf16[32,1664]{1,0:T(8,128)(2,1)S(1)} %get-tuple-element.301), channel_id=1, source_target_pairs={{0,1},{1,0},{2,3},{3,2},{4,5},{5,4},{6,7},{7,6},{8,9},{9,8},{10,11... | collective-permute-start | bytes 319496 | tf_op jit(solution)/shard_map/ppermute | solution.py:910
  (324 shorter events, 95.4 us)
Async XLA Ops:
  7.2 159.9 %all-gather.3.cloned.1.call-start = ((), (), s32[]{:S(2)}) async-start(), calls=%async_computation.2 | async-start | bytes 2621440 | tf_op jit(solution)/shard_map/all_gather | solution.py:1001
  7.2 28.1 %collective-permute-start.2 = (bf16[512,1024]{1,0:T(8,128)(2,1)}, bf16[512,1024]{1,0:T(8,128)(2,1)S(1)}, u32[]{:S(2)}, u32[]{:S(2)}) collective-permute-start(bf16[512,1024]{1,0:T(8,128)(2,1)} %bitcast.15.refs_9_.x_ref), channel_id=1, source_target_pairs={{0,2},{2,4},{4,6},{6,8},{8,10},{10,12},{12,14},{14,16},{16,18},{18... | collective-permute-start | bytes 3145736 | tf_op jit(solution)/shard_map/ppermute | solution.py:963
  35.3 42.3 %collective-permute-start.5 = (bf16[512,1024]{1,0:T(8,128)(2,1)}, bf16[512,1024]{1,0:T(8,128)(2,1)S(1)}, u32[]{:S(2)}, u32[]{:S(2)}) collective-permute-start(bf16[512,1024]{1,0:T(8,128)(2,1)} %bitcast.15.refs_9_.x_ref), channel_id=1, source_target_pairs={{2,0},{4,2},{6,4},{8,6},{10,8},{12,10},{14,12},{16,14},{18,16},{20... | collective-permute-start | bytes 3145736 | tf_op jit(solution)/shard_map/ppermute | solution.py:966
  44.3 33.0 %collective-permute-start.3 = (bf16[2,2,32,2176]{3,2,1,0:T(8,128)(2,1)S(1)}, bf16[2,2,32,2176]{3,2,1,0:T(8,128)(2,1)S(1)}, u32[]{:S(2)}, u32[]{:S(2)}) collective-permute-start(bf16[2,2,32,2176]{3,2,1,0:T(8,128)(2,1)S(1)} %pad_maximum_fusion.9), channel_id=1, source_target_pairs={{0,8},{8,0},{16,24},{24,16},{1,9},{9,1},{17,25},{25,17},{2,10},{10... | collective-permute-start | bytes 1671176 | tf_op jit(solution)/shard_map/ppermute | solution.py:918
  49.8 15.9 %collective-permute-start.4 = (bf16[128,1024]{1,0:T(8,128)(2,1)S(1)}, bf16[128,1024]{1,0:T(8,128)(2,1)S(1)}, u32[]{:S(2)}, u32[]{:S(2)}) collective-permute-start(bf16[128,1024]{1,0:T(8,128)(2,1)S(1)} %copy-done.21), channel_id=1, source_target_pairs={{0,2},{2,0},{1,3},{3,1},{4,6},{6,4},{5,7},{7,5},{8,10},{10,8},{9,1... | collective-permute-start | bytes 786440 | tf_op jit(solution)/shard_map/ppermute | solution.py:910
  93.8 24.8 %collective-permute-start.10 = (bf16[2,4,32,2176]{3,2,1,0:T(8,128)(2,1)S(1)}, bf16[2,4,32,2176]{3,2,1,0:T(8,128)(2,1)}, u32[]{:S(2)}, u32[]{:S(2)}) collective-permute-start(bf16[2,4,32,2176]{3,2,1,0:T(8,128)(2,1)S(1)} %pad_maximum_fusion.5.refs_3_), channel_id=1, source_target_pairs={{0,4},{4,0},{1,5},{5,1},{2,6},{6,2},{3,7},{7,3},{8,12},{12,8},{9,1... | collective-permute-start | bytes 3342344 | tf_op jit(solution)/shard_map/ppermute | solution.py:910
  94.0 24.7 %collective-permute-start.9 = (bf16[2,4,32,2176]{3,2,1,0:T(8,128)(2,1)S(1)}, bf16[2,4,32,2176]{3,2,1,0:T(8,128)(2,1)}, u32[]{:S(2)}, u32[]{:S(2)}) collective-permute-start(bf16[2,4,32,2176]{3,2,1,0:T(8,128)(2,1)S(1)} %pad_maximum_fusion.3.refs_1_), channel_id=1, source_target_pairs={{0,2},{2,0},{1,3},{3,1},{4,6},{6,4},{5,7},{7,5},{8,10},{10,8},{9,1... | collective-permute-start | bytes 3342344 | tf_op jit(solution)/shard_map/ppermute | solution.py:910
  96.6 26.3 %collective-permute-start.12 = (bf16[2,4,32,2176]{3,2,1,0:T(8,128)(2,1)S(1)}, bf16[2,4,32,2176]{3,2,1,0:T(8,128)(2,1)}, u32[]{:S(2)}, u32[]{:S(2)}) collective-permute-start(bf16[2,4,32,2176]{3,2,1,0:T(8,128)(2,1)S(1)} %pad_maximum_fusion.3.refs_1_), channel_id=1, source_target_pairs={{0,1},{1,0},{2,3},{3,2},{4,5},{5,4},{6,7},{7,6},{8,9},{9,8},{10,11... | collective-permute-start | bytes 3342344 | tf_op jit(solution)/shard_map/ppermute | solution.py:910
  121.3 72.9 %collective-permute-start.17 = (bf16[512,1024]{1,0:T(8,128)(2,1)}, bf16[512,1024]{1,0:T(8,128)(2,1)}, u32[]{:S(2)}, u32[]{:S(2)}) collective-permute-start(bf16[512,1024]{1,0:T(8,128)(2,1)} %bitcast.15.refs_9_.x_ref), channel_id=1, source_target_pairs={{0,1},{1,0},{2,3},{3,2},{4,5},{5,4},{6,7},{7,6},{8,9},{9,8},{10,11... | collective-permute-start | bytes 3145736 | tf_op jit(solution)/shard_map/ppermute | solution.py:910
  122.1 267.5 %reduce-scatter.2.cloned.1.call-start = ((), (), s32[]{:S(2)}) async-start(), calls=%async_computation.1 | async-start | bytes 5242880 | tf_op jit(solution)/shard_map/reduce_scatter | solution.py:1051
  125.0 24.9 %collective-permute-start.16 = (bf16[4,64,2048]{2,1,0:T(8,128)(2,1)S(1)}, bf16[4,64,2048]{2,1,0:T(8,128)(2,1)}, u32[]{:S(2)}, u32[]{:S(2)}) collective-permute-start(bf16[4,64,2048]{2,1,0:T(8,128)(2,1)S(1)} %bitcast.182), channel_id=1, source_target_pairs={{0,4},{4,0},{1,5},{5,1},{2,6},{6,2},{3,7},{7,3},{8,12},{12,8},{9,1... | collective-permute-start | bytes 3145736 | tf_op jit(solution)/shard_map/ppermute | solution.py:910
  152.7 48.2 %collective-permute-start.19 = (bf16[2,4,64,2048]{3,2,1,0:T(8,128)(2,1)}, bf16[2,4,64,2048]{3,2,1,0:T(8,128)(2,1)}, u32[]{:S(2)}, u32[]{:S(2)}) collective-permute-start(bf16[2,4,64,2048]{3,2,1,0:T(8,128)(2,1)} %pad_maximum_fusion.refs_1_), channel_id=1, source_target_pairs={{0,2},{2,0},{1,3},{3,1},{4,6},{6,4},{5,7},{7,5},{8,10},{10,8},{9,1... | collective-permute-start | bytes 6291464 | tf_op jit(solution)/shard_map/ppermute | solution.py:910
  154.2 46.8 %collective-permute-start.20 = (bf16[2,4,64,2048]{3,2,1,0:T(8,128)(2,1)}, bf16[2,4,64,2048]{3,2,1,0:T(8,128)(2,1)}, u32[]{:S(2)}, u32[]{:S(2)}) collective-permute-start(bf16[2,4,64,2048]{3,2,1,0:T(8,128)(2,1)} %pad_maximum_fusion.refs_1_), channel_id=1, source_target_pairs={{0,1},{1,0},{2,3},{3,2},{4,5},{5,4},{6,7},{7,6},{8,9},{9,8},{10,11... | collective-permute-start | bytes 6291464 | tf_op jit(solution)/shard_map/ppermute | solution.py:910
  167.1 33.8 %collective-permute-start.21 = (bf16[2,4,128,1024]{3,2,1,0:T(8,128)(2,1)}, bf16[2,4,128,1024]{3,2,1,0:T(8,128)(2,1)}, u32[]{:S(2)}, u32[]{:S(2)}) collective-permute-start(bf16[2,4,128,1024]{3,2,1,0:T(8,128)(2,1)} %bitcast.227), channel_id=1, source_target_pairs={{0,1},{1,0},{2,3},{3,2},{4,5},{5,4},{6,7},{7,6},{8,9},{9,8},{10,11... | collective-permute-start | bytes 6291464 | tf_op jit(solution)/shard_map/ppermute | solution.py:910
  167.6 47.5 %collective-permute-start.22 = (bf16[2,4,128,1024]{3,2,1,0:T(8,128)(2,1)}, bf16[2,4,128,1024]{3,2,1,0:T(8,128)(2,1)}, u32[]{:S(2)}, u32[]{:S(2)}) collective-permute-start(bf16[2,4,128,1024]{3,2,1,0:T(8,128)(2,1)} %bitcast.228), channel_id=1, source_target_pairs={{0,4},{4,0},{1,5},{5,1},{2,6},{6,2},{3,7},{7,3},{8,12},{12,8},{9,1... | collective-permute-start | bytes 6291464 | tf_op jit(solution)/shard_map/ppermute | solution.py:910
  218.7 42.1 %collective-permute-start.25 = (bf16[512,1024]{1,0:T(8,128)(2,1)S(1)}, bf16[512,1024]{1,0:T(8,128)(2,1)S(1)}, u32[]{:S(2)}, u32[]{:S(2)}) collective-permute-start(bf16[512,1024]{1,0:T(8,128)(2,1)S(1)} %copy-done.30), channel_id=1, source_target_pairs={{0,1},{1,0},{2,3},{3,2},{4,5},{5,4},{6,7},{7,6},{8,9},{9,8},{10,11... | collective-permute-start | bytes 3145736 | tf_op jit(solution)/shard_map/ppermute | solution.py:910
  260.9 60.0 %collective-permute-start.28 = (bf16[560,1024]{1,0:T(8,128)(2,1)}, bf16[560,1024]{1,0:T(8,128)(2,1)S(1)}, u32[]{:S(2)}, u32[]{:S(2)}) collective-permute-start(bf16[560,1024]{1,0:T(8,128)(2,1)} %get-tuple-element.189.do_ref), channel_id=1, source_target_pairs={{0,2},{2,4},{4,6},{6,8},{8,10},{10,12},{12,14},{14,16},{16,18},{18... | collective-permute-start | bytes 3440648 | tf_op jit(solution)/shard_map/ppermute | solution.py:963
  264.0 56.9 %collective-permute-start.29 = (bf16[560,1024]{1,0:T(8,128)(2,1)}, bf16[560,1024]{1,0:T(8,128)(2,1)S(1)}, u32[]{:S(2)}, u32[]{:S(2)}) collective-permute-start(bf16[560,1024]{1,0:T(8,128)(2,1)} %get-tuple-element.189.do_ref), channel_id=1, source_target_pairs={{2,0},{4,2},{6,4},{8,6},{10,8},{12,10},{14,12},{16,14},{18,16},{20... | collective-permute-start | bytes 3440648 | tf_op jit(solution)/shard_map/ppermute | solution.py:966
  268.0 40.7 %collective-permute-start.26 = (bf16[512,2048]{1,0:T(8,128)(2,1)}, bf16[512,2048]{1,0:T(8,128)(2,1)}, u32[]{:S(2)}, u32[]{:S(2)}) collective-permute-start(bf16[512,2048]{1,0:T(8,128)(2,1)} %get-tuple-element.195), channel_id=1, source_target_pairs={{0,1},{1,0},{2,3},{3,2},{4,5},{5,4},{6,7},{7,6},{8,9},{9,8},{10,11... | collective-permute-start | bytes 6291464 | tf_op jit(solution)/shard_map/ppermute | solution.py:910
  269.0 30.7 %collective-permute-start.39 = (bf16[512,2048]{1,0:T(8,128)(2,1)}, bf16[512,2048]{1,0:T(8,128)(2,1)}, u32[]{:S(2)}, u32[]{:S(2)}) collective-permute-start(bf16[512,2048]{1,0:T(8,128)(2,1)} %get-tuple-element.233), channel_id=1, source_target_pairs={{0,1},{1,0},{2,3},{3,2},{4,5},{5,4},{6,7},{7,6},{8,9},{9,8},{10,11... | collective-permute-start | bytes 6291464 | tf_op jit(solution)/shard_map/ppermute | solution.py:910
  269.0 30.5 %collective-permute-start.40 = (bf16[512,1024]{1,0:T(8,128)(2,1)}, bf16[512,1024]{1,0:T(8,128)(2,1)}, u32[]{:S(2)}, u32[]{:S(2)}) collective-permute-start(bf16[512,1024]{1,0:T(8,128)(2,1)} %get-tuple-element.234.glow_ref), channel_id=1, source_target_pairs={{0,1},{1,0},{2,3},{3,2},{4,5},{5,4},{6,7},{7,6},{8,9},{9,8},{10,11... | collective-permute-start | bytes 3145736 | tf_op jit(solution)/shard_map/ppermute | solution.py:910
  299.7 55.4 %collective-permute-start.32 = (bf16[512,512]{1,0:T(8,128)(2,1)}, bf16[512,512]{1,0:T(8,128)(2,1)}, u32[]{:S(2)}, u32[]{:S(2)}) collective-permute-start(bf16[512,512]{1,0:T(8,128)(2,1)} %get-tuple-element.242), channel_id=1, source_target_pairs={{0,1},{1,0},{2,3},{3,2},{4,5},{5,4},{6,7},{7,6},{8,9},{9,8},{10,11... | collective-permute-start | bytes 1572872 | tf_op jit(solution)/shard_map/ppermute | solution.py:910
  320.9 30.7 %collective-permute-start.30 = (bf16[2,4,32,2560]{3,2,1,0:T(8,128)(2,1)}, bf16[2,4,32,2560]{3,2,1,0:T(8,128)(2,1)}, u32[]{:S(2)}, u32[]{:S(2)}) collective-permute-start(bf16[2,4,32,2560]{3,2,1,0:T(8,128)(2,1)} %bitcast.231), channel_id=1, source_target_pairs={{0,2},{2,0},{1,3},{3,1},{4,6},{6,4},{5,7},{7,5},{8,10},{10,8},{9,1... | collective-permute-start | bytes 3932168 | tf_op jit(solution)/shard_map/ppermute | solution.py:910
  321.0 30.7 %collective-permute-start.31 = (bf16[2,4,32,2560]{3,2,1,0:T(8,128)(2,1)}, bf16[2,4,32,2560]{3,2,1,0:T(8,128)(2,1)}, u32[]{:S(2)}, u32[]{:S(2)}) collective-permute-start(bf16[2,4,32,2560]{3,2,1,0:T(8,128)(2,1)} %bitcast.230), channel_id=1, source_target_pairs={{0,4},{4,0},{1,5},{5,1},{2,6},{6,2},{3,7},{7,3},{8,12},{12,8},{9,1... | collective-permute-start | bytes 3932168 | tf_op jit(solution)/shard_map/ppermute | solution.py:910
  333.3 21.8 %collective-permute-start.33 = (bf16[512,512]{1,0:T(8,128)(2,1)}, bf16[512,512]{1,0:T(8,128)(2,1)}, u32[]{:S(2)}, u32[]{:S(2)}) collective-permute-start(bf16[512,512]{1,0:T(8,128)(2,1)} %get-tuple-element.243), channel_id=1, source_target_pairs={{0,1},{1,0},{2,3},{3,2},{4,5},{5,4},{6,7},{7,6},{8,9},{9,8},{10,11... | collective-permute-start | bytes 1572872 | tf_op jit(solution)/shard_map/ppermute | solution.py:910
  333.5 21.7 %collective-permute-start.34 = (bf16[512,512]{1,0:T(8,128)(2,1)}, bf16[512,512]{1,0:T(8,128)(2,1)}, u32[]{:S(2)}, u32[]{:S(2)}) collective-permute-start(bf16[512,512]{1,0:T(8,128)(2,1)} %get-tuple-element.244), channel_id=1, source_target_pairs={{0,1},{1,0},{2,3},{3,2},{4,5},{5,4},{6,7},{7,6},{8,9},{9,8},{10,11... | collective-permute-start | bytes 1572872 | tf_op jit(solution)/shard_map/ppermute | solution.py:910
  370.7 18.6 %collective-permute-start.37 = (bf16[2,4,32,1664]{3,2,1,0:T(8,128)(2,1)S(1)}, bf16[2,4,32,1664]{3,2,1,0:T(8,128)(2,1)}, u32[]{:S(2)}, u32[]{:S(2)}) collective-permute-start(bf16[2,4,32,1664]{3,2,1,0:T(8,128)(2,1)S(1)} %bitcast.234), channel_id=1, source_target_pairs={{0,2},{2,0},{1,3},{3,1},{4,6},{6,4},{5,7},{7,5},{8,10},{10,8},{9,1... | collective-permute-start | bytes 2555912 | tf_op jit(solution)/shard_map/ppermute | solution.py:910
  371.5 18.1 %collective-permute-start.38 = (bf16[2,4,32,1664]{3,2,1,0:T(8,128)(2,1)S(1)}, bf16[2,4,32,1664]{3,2,1,0:T(8,128)(2,1)}, u32[]{:S(2)}, u32[]{:S(2)}) collective-permute-start(bf16[2,4,32,1664]{3,2,1,0:T(8,128)(2,1)S(1)} %bitcast.233), channel_id=1, source_target_pairs={{0,4},{4,0},{1,5},{5,1},{2,6},{6,2},{3,7},{7,3},{8,12},{12,8},{9,1... | collective-permute-start | bytes 2555912 | tf_op jit(solution)/shard_map/ppermute | solution.py:910
  376.4 24.9 %collective-permute-start.43 = (bf16[2,2,32,2560]{3,2,1,0:T(8,128)(2,1)}, bf16[2,2,32,2560]{3,2,1,0:T(8,128)(2,1)}, u32[]{:S(2)}, u32[]{:S(2)}) collective-permute-start(bf16[2,2,32,2560]{3,2,1,0:T(8,128)(2,1)} %fusion.17), channel_id=1, source_target_pairs={{0,8},{8,0},{16,24},{24,16},{1,9},{9,1},{17,25},{25,17},{2,10},{10... | collective-permute-start | bytes 1966088 | tf_op jit(solution)/shard_map/ppermute | solution.py:918
  394.4 23.9 %collective-permute-start.47 = (bf16[128,1024]{1,0:T(8,128)(2,1)S(1)}, bf16[128,1024]{1,0:T(8,128)(2,1)S(1)}, u32[]{:S(2)}, u32[]{:S(2)}) collective-permute-start(bf16[128,1024]{1,0:T(8,128)(2,1)S(1)} %get-tuple-element.287), channel_id=1, source_target_pairs={{0,4},{4,0},{1,5},{5,1},{2,6},{6,2},{3,7},{7,3},{8,12},{12,8},{9,1... | collective-permute-start | bytes 786440 | tf_op jit(solution)/shard_map/ppermute | solution.py:910
  394.8 23.5 %collective-permute-start.48 = (bf16[128,1024]{1,0:T(8,128)(2,1)S(1)}, bf16[128,1024]{1,0:T(8,128)(2,1)S(1)}, u32[]{:S(2)}, u32[]{:S(2)}) collective-permute-start(bf16[128,1024]{1,0:T(8,128)(2,1)S(1)} %get-tuple-element.286), channel_id=1, source_target_pairs={{0,2},{2,0},{1,3},{3,1},{4,6},{6,4},{5,7},{7,5},{8,10},{10,8},{9,1... | collective-permute-start | bytes 786440 | tf_op jit(solution)/shard_map/ppermute | solution.py:910
  401.3 17.1 %collective-permute-start.49 = (bf16[128,1024]{1,0:T(8,128)(2,1)S(1)}, bf16[128,1024]{1,0:T(8,128)(2,1)S(1)}, u32[]{:S(2)}, u32[]{:S(2)}) collective-permute-start(bf16[128,1024]{1,0:T(8,128)(2,1)S(1)} %get-tuple-element.285), channel_id=1, source_target_pairs={{0,6},{2,4},{4,2},{6,0},{1,7},{3,5},{5,3},{7,1},{8,14},{10,12},{12... | collective-permute-start | bytes 786440 | tf_op jit(solution)/shard_map/ppermute | solution.py:914
  (59 other events, 656.6 us)
Sparse Core Ops, SparseCore 0:
  122.2 44.8 all-gather.2
  308.8 76.5 reduce-scatter.1
